TPU v7x, 512 devices: a whole 4x4x16 slice. The times are simulated.
512 devices in a mesh: loop: 64 (over z_lo, x, core), grp: 8 (over y, z_hi).
Axes of the slice: x: 4, y: 4, z: 16 (z_hi: 2, z_lo: 8; z = z_hi * 8 + z_lo), core: 2. Of those that a mesh axis runs over, the one named last changes fastest.
Arguments:
- picture_vectors: float32 [12288, 1152], P(('loop', 'grp')), may hold values from -0.8249579 to 0.8249579, as said below
- caption_vectors: float32 [12288, 1152], P(('loop', 'grp')), may hold values from -0.8249579 to 0.8249579, as said below
- heat_exponent: float32 [1], replicated, may hold values from 2 to 2.6
- offset_added: float32 [1], replicated, may hold values from -9 to -7
Outputs:
- loss_mean: float32 [1], replicated
- image_grads: float32 [12288, 1152], P(('loop', 'grp'))
- text_grads: float32 [12288, 1152], P(('loop', 'grp'))
Inputs may be any that keep to these rules, and one draw needn't show every extreme that they name: `picture_vectors`: entries of image embeddings lie within the stated bounds. `caption_vectors`: entries of text embeddings lie within the stated bounds.
All inputs are finite; a program needn't handle non-finite values.
Results may differ from a plain program's by a relative error of at most 0.0031.
Values may be sent and summed in bfloat16 or wider, within the bound.
No kernel may reach another device: no remote copies, remote signals or barrier semaphores. Data moves between devices by JAX's collectives and lax.ppermute only.
A program may use at most 64 MiB of HBM per device.

v0:
```python
import jax
import jax.numpy as jnp
from jax import lax
from jax.sharding import PartitionSpec as P

epsilon = 1e-06


def shifted(value, axis, steps):
    count = lax.axis_size(axis)
    pairs = [(source, (source + steps) % count) for source in range(count)]
    return lax.ppermute(value, axis, pairs)


def normalize(raw_rows):
    row_norm = jnp.sqrt(jnp.sum(raw_rows * raw_rows, axis=1, keepdims=True) + epsilon)
    return (raw_rows / row_norm, row_norm)


def back_norm(unit_rows, row_norm, gradient):
    return (gradient - unit_rows * jnp.sum(unit_rows * gradient, axis=1, keepdims=True)) / row_norm


def pairwise_terms(
    text_portion,
    text_identifiers,
    image_block_rows,
    image_identifiers,
    heat_multiplier,
    cyclic_shift_count,
):
    match_logits = lax.dot_general(
        text_portion, image_block_rows, (((1,), (1,)), ((), ())), preferred_element_type=jnp.float32
    )
    match_logits = match_logits * heat_multiplier + cyclic_shift_count
    match_targets = jnp.where(
        text_identifiers[:, None] == image_identifiers[None, :], 1.0, -1.0
    ).astype(jnp.float32)
    loss_part = jnp.sum(jax.nn.softplus(-match_targets * match_logits))
    match_factors = (
        -match_targets * jax.nn.sigmoid(-match_targets * match_logits) * heat_multiplier
    ).astype(jnp.bfloat16)
    text_grad = jnp.dot(match_factors, image_block_rows, preferred_element_type=jnp.float32)
    image_grad = lax.dot_general(
        match_factors, text_portion, (((0,), (0,)), ((), ())), preferred_element_type=jnp.float32
    )
    return (loss_part, text_grad, image_grad)


def shards(picture_vectors, caption_vectors, heat_exponent, offset_added):
    row_count = picture_vectors.shape[0]
    loop_size = lax.axis_size("loop")
    group_size = lax.axis_size("grp")
    loop_place = lax.axis_index("loop")
    group_place = lax.axis_index("grp")
    heat_multiplier = jnp.exp(heat_exponent[0])
    cyclic_shift_count = offset_added[0]
    image_unit, image_norm = normalize(picture_vectors)
    text_unit, text_norm = normalize(caption_vectors)
    image_block_rows = lax.all_gather(image_unit.astype(jnp.bfloat16), "grp", axis=0, tiled=True)
    image_identifiers = loop_place * group_size * row_count + jnp.arange(
        group_size * row_count, dtype=jnp.int32
    )
    caption_start_index = text_unit.astype(jnp.bfloat16)
    offsets = jnp.arange(row_count, dtype=jnp.int32)
    image_start = jnp.zeros(image_block_rows.shape, jnp.float32)
    loss_start = jnp.zeros((), jnp.float32)

    def one_hop(hop_index, state_tuple):
        text_portion, grad_carry, image_sum, loss_sum = state_tuple
        anchor = (loop_place - hop_index) % loop_size
        text_identifiers = (anchor * group_size + group_place) * row_count + offsets
        loss_part, text_grad, image_grad = pairwise_terms(
            text_portion,
            text_identifiers,
            image_block_rows,
            image_identifiers,
            heat_multiplier,
            cyclic_shift_count,
        )
        grad_carry = shifted(grad_carry + text_grad, "loop", 1)
        text_portion = shifted(text_portion, "loop", 1)
        return (text_portion, grad_carry, image_sum + image_grad, loss_sum + loss_part)

    start_state = (
        caption_start_index,
        jnp.zeros(caption_vectors.shape, jnp.float32),
        image_start,
        loss_start,
    )
    text_portion, text_sum, image_sum, loss_sum = lax.fori_loop(0, loop_size, one_hop, start_state)
    image_share = lax.psum_scatter(image_sum, "grp", scatter_dimension=0, tiled=True)
    loss_total = lax.psum(loss_sum, ("loop", "grp"))
    batch_total = row_count * loop_size * group_size
    loss_mean = (loss_total / batch_total).reshape(1)
    return (
        loss_mean,
        back_norm(image_unit, image_norm, image_share),
        back_norm(text_unit, text_norm, text_sum),
    )


def solution(mesh):
    in_specs = (P(("loop", "grp"), None), P(("loop", "grp"), None), P(), P())
    out_specs = (P(), P(("loop", "grp"), None), P(("loop", "grp"), None))
    return jax.shard_map(shards, mesh=mesh, in_specs=in_specs, out_specs=out_specs, check_vma=False)
```

profile of v0, /device:TPU:1, one launch (start us, length us, event | category | flops | bytes accessed | tf_op | source)
XLA Modules:
  0.0 1407.9 jit_solution(11607071521492080053)
XLA Ops:
  10.1 79.2 %all_gather.3 = bf16[192,1152]{1,0:T(8,128)(2,1)S(1)} all-gather(bf16[24,1152]{1,0:T(8,128)(2,1)S(1)} %fusion.8), channel_id=1, replica_groups=mesh['loop'=64,'grp'=8] {'grp'}, dimensions={0}, use_global_device_ids=true | all-gather | bytes 497664 | tf_op jit(solution)/shard_map/all_gather | solution.py:60
  89.3 1184.5 %while.22 = (s32[]{:T(128)}, bf16[24,1152]{1,0:T(8,128)(2,1)S(1)}, f32[24,1152]{1,0:T(8,128)S(1)}, f32[192,1152]{1,0:T(8,128)S(1)}, f32[]{:T(128)}, /*index=5*/s...) while((s32[]{:T(128)}, bf16[24,1152]{1,0:T(8,128)(2,1)S(1)}, ...), condition=%wide.region_4.5_spmd.clone, body=%wide.region_2.4_spmd.clone.sunk | while | flops 32463592 | bytes 3819324 | solution.py:91
  89.3 11.2 collective-permute-start
  128.1 7.7 collective-permute-done
  146.7 7.7 collective-permute-done
  165.3 7.7 collective-permute-done
  183.9 7.7 collective-permute-done
  202.5 7.7 collective-permute-done
  221.1 7.7 collective-permute-done
  239.6 7.7 collective-permute-done
  258.2 7.7 collective-permute-done
  276.8 7.7 collective-permute-done
  295.4 7.7 collective-permute-done
  314.0 7.7 collective-permute-done
  332.6 7.7 collective-permute-done
  351.2 7.7 collective-permute-done
  369.8 7.7 collective-permute-done
  388.4 7.7 collective-permute-done
  407.0 7.7 collective-permute-done
  425.6 7.7 collective-permute-done
  444.2 7.7 collective-permute-done
  462.7 7.7 collective-permute-done
  481.3 7.7 collective-permute-done
  499.9 7.7 collective-permute-done
  518.5 7.7 collective-permute-done
  537.1 7.7 collective-permute-done
  555.7 7.7 collective-permute-done
  574.3 7.7 collective-permute-done
  592.9 7.7 collective-permute-done
  611.5 7.7 collective-permute-done
  630.1 7.7 collective-permute-done
  648.7 7.7 collective-permute-done
  667.3 7.7 collective-permute-done
  685.8 7.7 collective-permute-done
  704.4 7.7 collective-permute-done
  723.0 7.7 collective-permute-done
  741.6 7.7 collective-permute-done
  760.2 7.7 collective-permute-done
  778.8 7.7 collective-permute-done
  797.4 7.7 collective-permute-done
  816.0 7.7 collective-permute-done
  834.6 7.7 collective-permute-done
  853.2 7.7 collective-permute-done
  871.8 7.7 collective-permute-done
  890.4 7.7 collective-permute-done
  908.9 7.7 collective-permute-done
  927.5 7.7 collective-permute-done
  946.1 7.7 collective-permute-done
  964.7 7.7 collective-permute-done
  983.3 7.7 collective-permute-done
  1001.9 7.7 collective-permute-done
  1020.5 7.7 collective-permute-done
  1039.1 7.7 collective-permute-done
  1076.3 7.7 collective-permute-done
  1094.9 7.7 collective-permute-done
  1113.5 7.7 collective-permute-done
  1150.6 7.7 collective-permute-done
  1169.2 7.7 collective-permute-done
  1187.8 7.7 collective-permute-done
  1206.4 7.7 collective-permute-done
  1225.0 7.7 collective-permute-done
  1243.6 7.7 collective-permute-done
  1262.2 7.7 collective-permute-done
  1274.7 114.9 %psum.7 = f32[]{:T(128)} all-reduce(f32[]{:T(128)} %get-tuple-element.292), channel_id=1, replica_groups=mesh['loop'=64,'grp'=8] {'loop','grp'}, use_global_device_ids=true, to_apply=%region_5.6 | all-reduce | flops 1 | bytes 8 | tf_op jit(solution)/shard_map/psum | solution.py:93
  (602 shorter events, 678.2 us)
Async XLA Ops:
  7.2 1390.9 %reduce-scatter.4.cloned.1.call-start = ((), (), s32[]{:S(2)}) async-start(), calls=%async_computation.1 | async-start | bytes 995328
  89.3 16.3 %collective-permute-start = (bf16[24,1152]{1,0:T(8,128)(2,1)S(1)}, bf16[24,1152]{1,0:T(8,128)(2,1)S(1)}, u32[]{:S(2)}, u32[]{:S(2)}) collective-permute-start(bf16[24,1152]{1,0:T(8,128)(2,1)S(1)} %copy.13), channel_id=1, source_target_pairs={{0,8},{8,16},{16,24},{24,32},{32,40},{40,48},{48,56},{56,64},{64,7... | collective-permute-start | bytes 165896 | tf_op jit(solution)/shard_map/while/body/eval_jaxpr/ppermute | solution.py:12
  124.9 14.8 %collective-permute-start.1 = (f32[24,1152]{1,0:T(8,128)S(1)}, f32[24,1152]{1,0:T(8,128)S(1)}, u32[]{:S(2)}, u32[]{:S(2)}) collective-permute-start(f32[24,1152]{1,0:T(8,128)S(1)} %convolution_add_fusion.4), channel_id=1, source_target_pairs={{0,8},{8,16},{16,24},{24,32},{32,40},{40,48},{48,56},{56,64},{64,7... | collective-permute-start | bytes 331784 | tf_op jit(solution)/shard_map/while/body/eval_jaxpr/ppermute | solution.py:12
  143.5 14.8 %collective-permute-start.1 = (f32[24,1152]{1,0:T(8,128)S(1)}, f32[24,1152]{1,0:T(8,128)S(1)}, u32[]{:S(2)}, u32[]{:S(2)}) collective-permute-start(f32[24,1152]{1,0:T(8,128)S(1)} %convolution_add_fusion.4), channel_id=1, source_target_pairs={{0,8},{8,16},{16,24},{24,32},{32,40},{40,48},{48,56},{56,64},{64,7... | collective-permute-start | bytes 331784 | tf_op jit(solution)/shard_map/while/body/eval_jaxpr/ppermute | solution.py:12
  162.1 14.8 %collective-permute-start.1 = (f32[24,1152]{1,0:T(8,128)S(1)}, f32[24,1152]{1,0:T(8,128)S(1)}, u32[]{:S(2)}, u32[]{:S(2)}) collective-permute-start(f32[24,1152]{1,0:T(8,128)S(1)} %convolution_add_fusion.4), channel_id=1, source_target_pairs={{0,8},{8,16},{16,24},{24,32},{32,40},{40,48},{48,56},{56,64},{64,7... | collective-permute-start | bytes 331784 | tf_op jit(solution)/shard_map/while/body/eval_jaxpr/ppermute | solution.py:12
  180.7 14.8 %collective-permute-start.1 = (f32[24,1152]{1,0:T(8,128)S(1)}, f32[24,1152]{1,0:T(8,128)S(1)}, u32[]{:S(2)}, u32[]{:S(2)}) collective-permute-start(f32[24,1152]{1,0:T(8,128)S(1)} %convolution_add_fusion.4), channel_id=1, source_target_pairs={{0,8},{8,16},{16,24},{24,32},{32,40},{40,48},{48,56},{56,64},{64,7... | collective-permute-start | bytes 331784 | tf_op jit(solution)/shard_map/while/body/eval_jaxpr/ppermute | solution.py:12
  199.3 14.8 %collective-permute-start.1 = (f32[24,1152]{1,0:T(8,128)S(1)}, f32[24,1152]{1,0:T(8,128)S(1)}, u32[]{:S(2)}, u32[]{:S(2)}) collective-permute-start(f32[24,1152]{1,0:T(8,128)S(1)} %convolution_add_fusion.4), channel_id=1, source_target_pairs={{0,8},{8,16},{16,24},{24,32},{32,40},{40,48},{48,56},{56,64},{64,7... | collective-permute-start | bytes 331784 | tf_op jit(solution)/shard_map/while/body/eval_jaxpr/ppermute | solution.py:12
  217.9 14.8 %collective-permute-start.1 = (f32[24,1152]{1,0:T(8,128)S(1)}, f32[24,1152]{1,0:T(8,128)S(1)}, u32[]{:S(2)}, u32[]{:S(2)}) collective-permute-start(f32[24,1152]{1,0:T(8,128)S(1)} %convolution_add_fusion.4), channel_id=1, source_target_pairs={{0,8},{8,16},{16,24},{24,32},{32,40},{40,48},{48,56},{56,64},{64,7... | collective-permute-start | bytes 331784 | tf_op jit(solution)/shard_map/while/body/eval_jaxpr/ppermute | solution.py:12
  236.5 14.8 %collective-permute-start.1 = (f32[24,1152]{1,0:T(8,128)S(1)}, f32[24,1152]{1,0:T(8,128)S(1)}, u32[]{:S(2)}, u32[]{:S(2)}) collective-permute-start(f32[24,1152]{1,0:T(8,128)S(1)} %convolution_add_fusion.4), channel_id=1, source_target_pairs={{0,8},{8,16},{16,24},{24,32},{32,40},{40,48},{48,56},{56,64},{64,7... | collective-permute-start | bytes 331784 | tf_op jit(solution)/shard_map/while/body/eval_jaxpr/ppermute | solution.py:12
  255.1 14.8 %collective-permute-start.1 = (f32[24,1152]{1,0:T(8,128)S(1)}, f32[24,1152]{1,0:T(8,128)S(1)}, u32[]{:S(2)}, u32[]{:S(2)}) collective-permute-start(f32[24,1152]{1,0:T(8,128)S(1)} %convolution_add_fusion.4), channel_id=1, source_target_pairs={{0,8},{8,16},{16,24},{24,32},{32,40},{40,48},{48,56},{56,64},{64,7... | collective-permute-start | bytes 331784 | tf_op jit(solution)/shard_map/while/body/eval_jaxpr/ppermute | solution.py:12
  273.7 14.8 %collective-permute-start.1 = (f32[24,1152]{1,0:T(8,128)S(1)}, f32[24,1152]{1,0:T(8,128)S(1)}, u32[]{:S(2)}, u32[]{:S(2)}) collective-permute-start(f32[24,1152]{1,0:T(8,128)S(1)} %convolution_add_fusion.4), channel_id=1, source_target_pairs={{0,8},{8,16},{16,24},{24,32},{32,40},{40,48},{48,56},{56,64},{64,7... | collective-permute-start | bytes 331784 | tf_op jit(solution)/shard_map/while/body/eval_jaxpr/ppermute | solution.py:12
  292.2 14.8 %collective-permute-start.1 = (f32[24,1152]{1,0:T(8,128)S(1)}, f32[24,1152]{1,0:T(8,128)S(1)}, u32[]{:S(2)}, u32[]{:S(2)}) collective-permute-start(f32[24,1152]{1,0:T(8,128)S(1)} %convolution_add_fusion.4), channel_id=1, source_target_pairs={{0,8},{8,16},{16,24},{24,32},{32,40},{40,48},{48,56},{56,64},{64,7... | collective-permute-start | bytes 331784 | tf_op jit(solution)/shard_map/while/body/eval_jaxpr/ppermute | solution.py:12
  310.8 14.8 %collective-permute-start.1 = (f32[24,1152]{1,0:T(8,128)S(1)}, f32[24,1152]{1,0:T(8,128)S(1)}, u32[]{:S(2)}, u32[]{:S(2)}) collective-permute-start(f32[24,1152]{1,0:T(8,128)S(1)} %convolution_add_fusion.4), channel_id=1, source_target_pairs={{0,8},{8,16},{16,24},{24,32},{32,40},{40,48},{48,56},{56,64},{64,7... | collective-permute-start | bytes 331784 | tf_op jit(solution)/shard_map/while/body/eval_jaxpr/ppermute | solution.py:12
  329.4 14.8 %collective-permute-start.1 = (f32[24,1152]{1,0:T(8,128)S(1)}, f32[24,1152]{1,0:T(8,128)S(1)}, u32[]{:S(2)}, u32[]{:S(2)}) collective-permute-start(f32[24,1152]{1,0:T(8,128)S(1)} %convolution_add_fusion.4), channel_id=1, source_target_pairs={{0,8},{8,16},{16,24},{24,32},{32,40},{40,48},{48,56},{56,64},{64,7... | collective-permute-start | bytes 331784 | tf_op jit(solution)/shard_map/while/body/eval_jaxpr/ppermute | solution.py:12
  348.0 14.8 %collective-permute-start.1 = (f32[24,1152]{1,0:T(8,128)S(1)}, f32[24,1152]{1,0:T(8,128)S(1)}, u32[]{:S(2)}, u32[]{:S(2)}) collective-permute-start(f32[24,1152]{1,0:T(8,128)S(1)} %convolution_add_fusion.4), channel_id=1, source_target_pairs={{0,8},{8,16},{16,24},{24,32},{32,40},{40,48},{48,56},{56,64},{64,7... | collective-permute-start | bytes 331784 | tf_op jit(solution)/shard_map/while/body/eval_jaxpr/ppermute | solution.py:12
  366.6 14.8 %collective-permute-start.1 = (f32[24,1152]{1,0:T(8,128)S(1)}, f32[24,1152]{1,0:T(8,128)S(1)}, u32[]{:S(2)}, u32[]{:S(2)}) collective-permute-start(f32[24,1152]{1,0:T(8,128)S(1)} %convolution_add_fusion.4), channel_id=1, source_target_pairs={{0,8},{8,16},{16,24},{24,32},{32,40},{40,48},{48,56},{56,64},{64,7... | collective-permute-start | bytes 331784 | tf_op jit(solution)/shard_map/while/body/eval_jaxpr/ppermute | solution.py:12
  385.2 14.8 %collective-permute-start.1 = (f32[24,1152]{1,0:T(8,128)S(1)}, f32[24,1152]{1,0:T(8,128)S(1)}, u32[]{:S(2)}, u32[]{:S(2)}) collective-permute-start(f32[24,1152]{1,0:T(8,128)S(1)} %convolution_add_fusion.4), channel_id=1, source_target_pairs={{0,8},{8,16},{16,24},{24,32},{32,40},{40,48},{48,56},{56,64},{64,7... | collective-permute-start | bytes 331784 | tf_op jit(solution)/shard_map/while/body/eval_jaxpr/ppermute | solution.py:12
  403.8 14.8 %collective-permute-start.1 = (f32[24,1152]{1,0:T(8,128)S(1)}, f32[24,1152]{1,0:T(8,128)S(1)}, u32[]{:S(2)}, u32[]{:S(2)}) collective-permute-start(f32[24,1152]{1,0:T(8,128)S(1)} %convolution_add_fusion.4), channel_id=1, source_target_pairs={{0,8},{8,16},{16,24},{24,32},{32,40},{40,48},{48,56},{56,64},{64,7... | collective-permute-start | bytes 331784 | tf_op jit(solution)/shard_map/while/body/eval_jaxpr/ppermute | solution.py:12
  422.4 14.8 %collective-permute-start.1 = (f32[24,1152]{1,0:T(8,128)S(1)}, f32[24,1152]{1,0:T(8,128)S(1)}, u32[]{:S(2)}, u32[]{:S(2)}) collective-permute-start(f32[24,1152]{1,0:T(8,128)S(1)} %convolution_add_fusion.4), channel_id=1, source_target_pairs={{0,8},{8,16},{16,24},{24,32},{32,40},{40,48},{48,56},{56,64},{64,7... | collective-permute-start | bytes 331784 | tf_op jit(solution)/shard_map/while/body/eval_jaxpr/ppermute | solution.py:12
  441.0 14.8 %collective-permute-start.1 = (f32[24,1152]{1,0:T(8,128)S(1)}, f32[24,1152]{1,0:T(8,128)S(1)}, u32[]{:S(2)}, u32[]{:S(2)}) collective-permute-start(f32[24,1152]{1,0:T(8,128)S(1)} %convolution_add_fusion.4), channel_id=1, source_target_pairs={{0,8},{8,16},{16,24},{24,32},{32,40},{40,48},{48,56},{56,64},{64,7... | collective-permute-start | bytes 331784 | tf_op jit(solution)/shard_map/while/body/eval_jaxpr/ppermute | solution.py:12
  459.6 14.8 %collective-permute-start.1 = (f32[24,1152]{1,0:T(8,128)S(1)}, f32[24,1152]{1,0:T(8,128)S(1)}, u32[]{:S(2)}, u32[]{:S(2)}) collective-permute-start(f32[24,1152]{1,0:T(8,128)S(1)} %convolution_add_fusion.4), channel_id=1, source_target_pairs={{0,8},{8,16},{16,24},{24,32},{32,40},{40,48},{48,56},{56,64},{64,7... | collective-permute-start | bytes 331784 | tf_op jit(solution)/shard_map/while/body/eval_jaxpr/ppermute | solution.py:12
  478.2 14.8 %collective-permute-start.1 = (f32[24,1152]{1,0:T(8,128)S(1)}, f32[24,1152]{1,0:T(8,128)S(1)}, u32[]{:S(2)}, u32[]{:S(2)}) collective-permute-start(f32[24,1152]{1,0:T(8,128)S(1)} %convolution_add_fusion.4), channel_id=1, source_target_pairs={{0,8},{8,16},{16,24},{24,32},{32,40},{40,48},{48,56},{56,64},{64,7... | collective-permute-start | bytes 331784 | tf_op jit(solution)/shard_map/while/body/eval_jaxpr/ppermute | solution.py:12
  496.8 14.8 %collective-permute-start.1 = (f32[24,1152]{1,0:T(8,128)S(1)}, f32[24,1152]{1,0:T(8,128)S(1)}, u32[]{:S(2)}, u32[]{:S(2)}) collective-permute-start(f32[24,1152]{1,0:T(8,128)S(1)} %convolution_add_fusion.4), channel_id=1, source_target_pairs={{0,8},{8,16},{16,24},{24,32},{32,40},{40,48},{48,56},{56,64},{64,7... | collective-permute-start | bytes 331784 | tf_op jit(solution)/shard_map/while/body/eval_jaxpr/ppermute | solution.py:12
  515.3 14.8 %collective-permute-start.1 = (f32[24,1152]{1,0:T(8,128)S(1)}, f32[24,1152]{1,0:T(8,128)S(1)}, u32[]{:S(2)}, u32[]{:S(2)}) collective-permute-start(f32[24,1152]{1,0:T(8,128)S(1)} %convolution_add_fusion.4), channel_id=1, source_target_pairs={{0,8},{8,16},{16,24},{24,32},{32,40},{40,48},{48,56},{56,64},{64,7... | collective-permute-start | bytes 331784 | tf_op jit(solution)/shard_map/while/body/eval_jaxpr/ppermute | solution.py:12
  533.9 14.8 %collective-permute-start.1 = (f32[24,1152]{1,0:T(8,128)S(1)}, f32[24,1152]{1,0:T(8,128)S(1)}, u32[]{:S(2)}, u32[]{:S(2)}) collective-permute-start(f32[24,1152]{1,0:T(8,128)S(1)} %convolution_add_fusion.4), channel_id=1, source_target_pairs={{0,8},{8,16},{16,24},{24,32},{32,40},{40,48},{48,56},{56,64},{64,7... | collective-permute-start | bytes 331784 | tf_op jit(solution)/shard_map/while/body/eval_jaxpr/ppermute | solution.py:12
  552.5 14.8 %collective-permute-start.1 = (f32[24,1152]{1,0:T(8,128)S(1)}, f32[24,1152]{1,0:T(8,128)S(1)}, u32[]{:S(2)}, u32[]{:S(2)}) collective-permute-start(f32[24,1152]{1,0:T(8,128)S(1)} %convolution_add_fusion.4), channel_id=1, source_target_pairs={{0,8},{8,16},{16,24},{24,32},{32,40},{40,48},{48,56},{56,64},{64,7... | collective-permute-start | bytes 331784 | tf_op jit(solution)/shard_map/while/body/eval_jaxpr/ppermute | solution.py:12
  571.1 14.8 %collective-permute-start.1 = (f32[24,1152]{1,0:T(8,128)S(1)}, f32[24,1152]{1,0:T(8,128)S(1)}, u32[]{:S(2)}, u32[]{:S(2)}) collective-permute-start(f32[24,1152]{1,0:T(8,128)S(1)} %convolution_add_fusion.4), channel_id=1, source_target_pairs={{0,8},{8,16},{16,24},{24,32},{32,40},{40,48},{48,56},{56,64},{64,7... | collective-permute-start | bytes 331784 | tf_op jit(solution)/shard_map/while/body/eval_jaxpr/ppermute | solution.py:12
  589.7 14.8 %collective-permute-start.1 = (f32[24,1152]{1,0:T(8,128)S(1)}, f32[24,1152]{1,0:T(8,128)S(1)}, u32[]{:S(2)}, u32[]{:S(2)}) collective-permute-start(f32[24,1152]{1,0:T(8,128)S(1)} %convolution_add_fusion.4), channel_id=1, source_target_pairs={{0,8},{8,16},{16,24},{24,32},{32,40},{40,48},{48,56},{56,64},{64,7... | collective-permute-start | bytes 331784 | tf_op jit(solution)/shard_map/while/body/eval_jaxpr/ppermute | solution.py:12
  608.3 14.8 %collective-permute-start.1 = (f32[24,1152]{1,0:T(8,128)S(1)}, f32[24,1152]{1,0:T(8,128)S(1)}, u32[]{:S(2)}, u32[]{:S(2)}) collective-permute-start(f32[24,1152]{1,0:T(8,128)S(1)} %convolution_add_fusion.4), channel_id=1, source_target_pairs={{0,8},{8,16},{16,24},{24,32},{32,40},{40,48},{48,56},{56,64},{64,7... | collective-permute-start | bytes 331784 | tf_op jit(solution)/shard_map/while/body/eval_jaxpr/ppermute | solution.py:12
  626.9 14.8 %collective-permute-start.1 = (f32[24,1152]{1,0:T(8,128)S(1)}, f32[24,1152]{1,0:T(8,128)S(1)}, u32[]{:S(2)}, u32[]{:S(2)}) collective-permute-start(f32[24,1152]{1,0:T(8,128)S(1)} %convolution_add_fusion.4), channel_id=1, source_target_pairs={{0,8},{8,16},{16,24},{24,32},{32,40},{40,48},{48,56},{56,64},{64,7... | collective-permute-start | bytes 331784 | tf_op jit(solution)/shard_map/while/body/eval_jaxpr/ppermute | solution.py:12
  645.5 14.8 %collective-permute-start.1 = (f32[24,1152]{1,0:T(8,128)S(1)}, f32[24,1152]{1,0:T(8,128)S(1)}, u32[]{:S(2)}, u32[]{:S(2)}) collective-permute-start(f32[24,1152]{1,0:T(8,128)S(1)} %convolution_add_fusion.4), channel_id=1, source_target_pairs={{0,8},{8,16},{16,24},{24,32},{32,40},{40,48},{48,56},{56,64},{64,7... | collective-permute-start | bytes 331784 | tf_op jit(solution)/shard_map/while/body/eval_jaxpr/ppermute | solution.py:12
  664.1 14.8 %collective-permute-start.1 = (f32[24,1152]{1,0:T(8,128)S(1)}, f32[24,1152]{1,0:T(8,128)S(1)}, u32[]{:S(2)}, u32[]{:S(2)}) collective-permute-start(f32[24,1152]{1,0:T(8,128)S(1)} %convolution_add_fusion.4), channel_id=1, source_target_pairs={{0,8},{8,16},{16,24},{24,32},{32,40},{40,48},{48,56},{56,64},{64,7... | collective-permute-start | bytes 331784 | tf_op jit(solution)/shard_map/while/body/eval_jaxpr/ppermute | solution.py:12
  682.7 14.8 %collective-permute-start.1 = (f32[24,1152]{1,0:T(8,128)S(1)}, f32[24,1152]{1,0:T(8,128)S(1)}, u32[]{:S(2)}, u32[]{:S(2)}) collective-permute-start(f32[24,1152]{1,0:T(8,128)S(1)} %convolution_add_fusion.4), channel_id=1, source_target_pairs={{0,8},{8,16},{16,24},{24,32},{32,40},{40,48},{48,56},{56,64},{64,7... | collective-permute-start | bytes 331784 | tf_op jit(solution)/shard_map/while/body/eval_jaxpr/ppermute | solution.py:12
  701.3 14.8 %collective-permute-start.1 = (f32[24,1152]{1,0:T(8,128)S(1)}, f32[24,1152]{1,0:T(8,128)S(1)}, u32[]{:S(2)}, u32[]{:S(2)}) collective-permute-start(f32[24,1152]{1,0:T(8,128)S(1)} %convolution_add_fusion.4), channel_id=1, source_target_pairs={{0,8},{8,16},{16,24},{24,32},{32,40},{40,48},{48,56},{56,64},{64,7... | collective-permute-start | bytes 331784 | tf_op jit(solution)/shard_map/while/body/eval_jaxpr/ppermute | solution.py:12
  719.8 14.8 %collective-permute-start.1 = (f32[24,1152]{1,0:T(8,128)S(1)}, f32[24,1152]{1,0:T(8,128)S(1)}, u32[]{:S(2)}, u32[]{:S(2)}) collective-permute-start(f32[24,1152]{1,0:T(8,128)S(1)} %convolution_add_fusion.4), channel_id=1, source_target_pairs={{0,8},{8,16},{16,24},{24,32},{32,40},{40,48},{48,56},{56,64},{64,7... | collective-permute-start | bytes 331784 | tf_op jit(solution)/shard_map/while/body/eval_jaxpr/ppermute | solution.py:12
  738.4 14.8 %collective-permute-start.1 = (f32[24,1152]{1,0:T(8,128)S(1)}, f32[24,1152]{1,0:T(8,128)S(1)}, u32[]{:S(2)}, u32[]{:S(2)}) collective-permute-start(f32[24,1152]{1,0:T(8,128)S(1)} %convolution_add_fusion.4), channel_id=1, source_target_pairs={{0,8},{8,16},{16,24},{24,32},{32,40},{40,48},{48,56},{56,64},{64,7... | collective-permute-start | bytes 331784 | tf_op jit(solution)/shard_map/while/body/eval_jaxpr/ppermute | solution.py:12
  757.0 14.8 %collective-permute-start.1 = (f32[24,1152]{1,0:T(8,128)S(1)}, f32[24,1152]{1,0:T(8,128)S(1)}, u32[]{:S(2)}, u32[]{:S(2)}) collective-permute-start(f32[24,1152]{1,0:T(8,128)S(1)} %convolution_add_fusion.4), channel_id=1, source_target_pairs={{0,8},{8,16},{16,24},{24,32},{32,40},{40,48},{48,56},{56,64},{64,7... | collective-permute-start | bytes 331784 | tf_op jit(solution)/shard_map/while/body/eval_jaxpr/ppermute | solution.py:12
  775.6 14.8 %collective-permute-start.1 = (f32[24,1152]{1,0:T(8,128)S(1)}, f32[24,1152]{1,0:T(8,128)S(1)}, u32[]{:S(2)}, u32[]{:S(2)}) collective-permute-start(f32[24,1152]{1,0:T(8,128)S(1)} %convolution_add_fusion.4), channel_id=1, source_target_pairs={{0,8},{8,16},{16,24},{24,32},{32,40},{40,48},{48,56},{56,64},{64,7... | collective-permute-start | bytes 331784 | tf_op jit(solution)/shard_map/while/body/eval_jaxpr/ppermute | solution.py:12
  794.2 14.8 %collective-permute-start.1 = (f32[24,1152]{1,0:T(8,128)S(1)}, f32[24,1152]{1,0:T(8,128)S(1)}, u32[]{:S(2)}, u32[]{:S(2)}) collective-permute-start(f32[24,1152]{1,0:T(8,128)S(1)} %convolution_add_fusion.4), channel_id=1, source_target_pairs={{0,8},{8,16},{16,24},{24,32},{32,40},{40,48},{48,56},{56,64},{64,7... | collective-permute-start | bytes 331784 | tf_op jit(solution)/shard_map/while/body/eval_jaxpr/ppermute | solution.py:12
  812.8 14.8 %collective-permute-start.1 = (f32[24,1152]{1,0:T(8,128)S(1)}, f32[24,1152]{1,0:T(8,128)S(1)}, u32[]{:S(2)}, u32[]{:S(2)}) collective-permute-start(f32[24,1152]{1,0:T(8,128)S(1)} %convolution_add_fusion.4), channel_id=1, source_target_pairs={{0,8},{8,16},{16,24},{24,32},{32,40},{40,48},{48,56},{56,64},{64,7... | collective-permute-start | bytes 331784 | tf_op jit(solution)/shard_map/while/body/eval_jaxpr/ppermute | solution.py:12
  831.4 14.8 %collective-permute-start.1 = (f32[24,1152]{1,0:T(8,128)S(1)}, f32[24,1152]{1,0:T(8,128)S(1)}, u32[]{:S(2)}, u32[]{:S(2)}) collective-permute-start(f32[24,1152]{1,0:T(8,128)S(1)} %convolution_add_fusion.4), channel_id=1, source_target_pairs={{0,8},{8,16},{16,24},{24,32},{32,40},{40,48},{48,56},{56,64},{64,7... | collective-permute-start | bytes 331784 | tf_op jit(solution)/shard_map/while/body/eval_jaxpr/ppermute | solution.py:12
  850.0 14.8 %collective-permute-start.1 = (f32[24,1152]{1,0:T(8,128)S(1)}, f32[24,1152]{1,0:T(8,128)S(1)}, u32[]{:S(2)}, u32[]{:S(2)}) collective-permute-start(f32[24,1152]{1,0:T(8,128)S(1)} %convolution_add_fusion.4), channel_id=1, source_target_pairs={{0,8},{8,16},{16,24},{24,32},{32,40},{40,48},{48,56},{56,64},{64,7... | collective-permute-start | bytes 331784 | tf_op jit(solution)/shard_map/while/body/eval_jaxpr/ppermute | solution.py:12
  868.6 14.8 %collective-permute-start.1 = (f32[24,1152]{1,0:T(8,128)S(1)}, f32[24,1152]{1,0:T(8,128)S(1)}, u32[]{:S(2)}, u32[]{:S(2)}) collective-permute-start(f32[24,1152]{1,0:T(8,128)S(1)} %convolution_add_fusion.4), channel_id=1, source_target_pairs={{0,8},{8,16},{16,24},{24,32},{32,40},{40,48},{48,56},{56,64},{64,7... | collective-permute-start | bytes 331784 | tf_op jit(solution)/shard_map/while/body/eval_jaxpr/ppermute | solution.py:12
  887.2 14.8 %collective-permute-start.1 = (f32[24,1152]{1,0:T(8,128)S(1)}, f32[24,1152]{1,0:T(8,128)S(1)}, u32[]{:S(2)}, u32[]{:S(2)}) collective-permute-start(f32[24,1152]{1,0:T(8,128)S(1)} %convolution_add_fusion.4), channel_id=1, source_target_pairs={{0,8},{8,16},{16,24},{24,32},{32,40},{40,48},{48,56},{56,64},{64,7... | collective-permute-start | bytes 331784 | tf_op jit(solution)/shard_map/while/body/eval_jaxpr/ppermute | solution.py:12
  905.8 14.8 %collective-permute-start.1 = (f32[24,1152]{1,0:T(8,128)S(1)}, f32[24,1152]{1,0:T(8,128)S(1)}, u32[]{:S(2)}, u32[]{:S(2)}) collective-permute-start(f32[24,1152]{1,0:T(8,128)S(1)} %convolution_add_fusion.4), channel_id=1, source_target_pairs={{0,8},{8,16},{16,24},{24,32},{32,40},{40,48},{48,56},{56,64},{64,7... | collective-permute-start | bytes 331784 | tf_op jit(solution)/shard_map/while/body/eval_jaxpr/ppermute | solution.py:12
  924.4 14.8 %collective-permute-start.1 = (f32[24,1152]{1,0:T(8,128)S(1)}, f32[24,1152]{1,0:T(8,128)S(1)}, u32[]{:S(2)}, u32[]{:S(2)}) collective-permute-start(f32[24,1152]{1,0:T(8,128)S(1)} %convolution_add_fusion.4), channel_id=1, source_target_pairs={{0,8},{8,16},{16,24},{24,32},{32,40},{40,48},{48,56},{56,64},{64,7... | collective-permute-start | bytes 331784 | tf_op jit(solution)/shard_map/while/body/eval_jaxpr/ppermute | solution.py:12
  942.9 14.8 %collective-permute-start.1 = (f32[24,1152]{1,0:T(8,128)S(1)}, f32[24,1152]{1,0:T(8,128)S(1)}, u32[]{:S(2)}, u32[]{:S(2)}) collective-permute-start(f32[24,1152]{1,0:T(8,128)S(1)} %convolution_add_fusion.4), channel_id=1, source_target_pairs={{0,8},{8,16},{16,24},{24,32},{32,40},{40,48},{48,56},{56,64},{64,7... | collective-permute-start | bytes 331784 | tf_op jit(solution)/shard_map/while/body/eval_jaxpr/ppermute | solution.py:12
  961.5 14.8 %collective-permute-start.1 = (f32[24,1152]{1,0:T(8,128)S(1)}, f32[24,1152]{1,0:T(8,128)S(1)}, u32[]{:S(2)}, u32[]{:S(2)}) collective-permute-start(f32[24,1152]{1,0:T(8,128)S(1)} %convolution_add_fusion.4), channel_id=1, source_target_pairs={{0,8},{8,16},{16,24},{24,32},{32,40},{40,48},{48,56},{56,64},{64,7... | collective-permute-start | bytes 331784 | tf_op jit(solution)/shard_map/while/body/eval_jaxpr/ppermute | solution.py:12
  980.1 14.8 %collective-permute-start.1 = (f32[24,1152]{1,0:T(8,128)S(1)}, f32[24,1152]{1,0:T(8,128)S(1)}, u32[]{:S(2)}, u32[]{:S(2)}) collective-permute-start(f32[24,1152]{1,0:T(8,128)S(1)} %convolution_add_fusion.4), channel_id=1, source_target_pairs={{0,8},{8,16},{16,24},{24,32},{32,40},{40,48},{48,56},{56,64},{64,7... | collective-permute-start | bytes 331784 | tf_op jit(solution)/shard_map/while/body/eval_jaxpr/ppermute | solution.py:12
  998.7 14.8 %collective-permute-start.1 = (f32[24,1152]{1,0:T(8,128)S(1)}, f32[24,1152]{1,0:T(8,128)S(1)}, u32[]{:S(2)}, u32[]{:S(2)}) collective-permute-start(f32[24,1152]{1,0:T(8,128)S(1)} %convolution_add_fusion.4), channel_id=1, source_target_pairs={{0,8},{8,16},{16,24},{24,32},{32,40},{40,48},{48,56},{56,64},{64,7... | collective-permute-start | bytes 331784 | tf_op jit(solution)/shard_map/while/body/eval_jaxpr/ppermute | solution.py:12
  1017.3 14.8 %collective-permute-start.1 = (f32[24,1152]{1,0:T(8,128)S(1)}, f32[24,1152]{1,0:T(8,128)S(1)}, u32[]{:S(2)}, u32[]{:S(2)}) collective-permute-start(f32[24,1152]{1,0:T(8,128)S(1)} %convolution_add_fusion.4), channel_id=1, source_target_pairs={{0,8},{8,16},{16,24},{24,32},{32,40},{40,48},{48,56},{56,64},{64,7... | collective-permute-start | bytes 331784 | tf_op jit(solution)/shard_map/while/body/eval_jaxpr/ppermute | solution.py:12
  1035.9 14.8 %collective-permute-start.1 = (f32[24,1152]{1,0:T(8,128)S(1)}, f32[24,1152]{1,0:T(8,128)S(1)}, u32[]{:S(2)}, u32[]{:S(2)}) collective-permute-start(f32[24,1152]{1,0:T(8,128)S(1)} %convolution_add_fusion.4), channel_id=1, source_target_pairs={{0,8},{8,16},{16,24},{24,32},{32,40},{40,48},{48,56},{56,64},{64,7... | collective-permute-start | bytes 331784 | tf_op jit(solution)/shard_map/while/body/eval_jaxpr/ppermute | solution.py:12
  1054.5 14.8 %collective-permute-start.1 = (f32[24,1152]{1,0:T(8,128)S(1)}, f32[24,1152]{1,0:T(8,128)S(1)}, u32[]{:S(2)}, u32[]{:S(2)}) collective-permute-start(f32[24,1152]{1,0:T(8,128)S(1)} %convolution_add_fusion.4), channel_id=1, source_target_pairs={{0,8},{8,16},{16,24},{24,32},{32,40},{40,48},{48,56},{56,64},{64,7... | collective-permute-start | bytes 331784 | tf_op jit(solution)/shard_map/while/body/eval_jaxpr/ppermute | solution.py:12
  1073.1 14.8 %collective-permute-start.1 = (f32[24,1152]{1,0:T(8,128)S(1)}, f32[24,1152]{1,0:T(8,128)S(1)}, u32[]{:S(2)}, u32[]{:S(2)}) collective-permute-start(f32[24,1152]{1,0:T(8,128)S(1)} %convolution_add_fusion.4), channel_id=1, source_target_pairs={{0,8},{8,16},{16,24},{24,32},{32,40},{40,48},{48,56},{56,64},{64,7... | collective-permute-start | bytes 331784 | tf_op jit(solution)/shard_map/while/body/eval_jaxpr/ppermute | solution.py:12
  1091.7 14.8 %collective-permute-start.1 = (f32[24,1152]{1,0:T(8,128)S(1)}, f32[24,1152]{1,0:T(8,128)S(1)}, u32[]{:S(2)}, u32[]{:S(2)}) collective-permute-start(f32[24,1152]{1,0:T(8,128)S(1)} %convolution_add_fusion.4), channel_id=1, source_target_pairs={{0,8},{8,16},{16,24},{24,32},{32,40},{40,48},{48,56},{56,64},{64,7... | collective-permute-start | bytes 331784 | tf_op jit(solution)/shard_map/while/body/eval_jaxpr/ppermute | solution.py:12
  1110.3 14.8 %collective-permute-start.1 = (f32[24,1152]{1,0:T(8,128)S(1)}, f32[24,1152]{1,0:T(8,128)S(1)}, u32[]{:S(2)}, u32[]{:S(2)}) collective-permute-start(f32[24,1152]{1,0:T(8,128)S(1)} %convolution_add_fusion.4), channel_id=1, source_target_pairs={{0,8},{8,16},{16,24},{24,32},{32,40},{40,48},{48,56},{56,64},{64,7... | collective-permute-start | bytes 331784 | tf_op jit(solution)/shard_map/while/body/eval_jaxpr/ppermute | solution.py:12
  1128.9 14.8 %collective-permute-start.1 = (f32[24,1152]{1,0:T(8,128)S(1)}, f32[24,1152]{1,0:T(8,128)S(1)}, u32[]{:S(2)}, u32[]{:S(2)}) collective-permute-start(f32[24,1152]{1,0:T(8,128)S(1)} %convolution_add_fusion.4), channel_id=1, source_target_pairs={{0,8},{8,16},{16,24},{24,32},{32,40},{40,48},{48,56},{56,64},{64,7... | collective-permute-start | bytes 331784 | tf_op jit(solution)/shard_map/while/body/eval_jaxpr/ppermute | solution.py:12
  1147.5 14.8 %collective-permute-start.1 = (f32[24,1152]{1,0:T(8,128)S(1)}, f32[24,1152]{1,0:T(8,128)S(1)}, u32[]{:S(2)}, u32[]{:S(2)}) collective-permute-start(f32[24,1152]{1,0:T(8,128)S(1)} %convolution_add_fusion.4), channel_id=1, source_target_pairs={{0,8},{8,16},{16,24},{24,32},{32,40},{40,48},{48,56},{56,64},{64,7... | collective-permute-start | bytes 331784 | tf_op jit(solution)/shard_map/while/body/eval_jaxpr/ppermute | solution.py:12
  1166.0 14.8 %collective-permute-start.1 = (f32[24,1152]{1,0:T(8,128)S(1)}, f32[24,1152]{1,0:T(8,128)S(1)}, u32[]{:S(2)}, u32[]{:S(2)}) collective-permute-start(f32[24,1152]{1,0:T(8,128)S(1)} %convolution_add_fusion.4), channel_id=1, source_target_pairs={{0,8},{8,16},{16,24},{24,32},{32,40},{40,48},{48,56},{56,64},{64,7... | collective-permute-start | bytes 331784 | tf_op jit(solution)/shard_map/while/body/eval_jaxpr/ppermute | solution.py:12
  1184.6 14.8 %collective-permute-start.1 = (f32[24,1152]{1,0:T(8,128)S(1)}, f32[24,1152]{1,0:T(8,128)S(1)}, u32[]{:S(2)}, u32[]{:S(2)}) collective-permute-start(f32[24,1152]{1,0:T(8,128)S(1)} %convolution_add_fusion.4), channel_id=1, source_target_pairs={{0,8},{8,16},{16,24},{24,32},{32,40},{40,48},{48,56},{56,64},{64,7... | collective-permute-start | bytes 331784 | tf_op jit(solution)/shard_map/while/body/eval_jaxpr/ppermute | solution.py:12
  1203.2 14.8 %collective-permute-start.1 = (f32[24,1152]{1,0:T(8,128)S(1)}, f32[24,1152]{1,0:T(8,128)S(1)}, u32[]{:S(2)}, u32[]{:S(2)}) collective-permute-start(f32[24,1152]{1,0:T(8,128)S(1)} %convolution_add_fusion.4), channel_id=1, source_target_pairs={{0,8},{8,16},{16,24},{24,32},{32,40},{40,48},{48,56},{56,64},{64,7... | collective-permute-start | bytes 331784 | tf_op jit(solution)/shard_map/while/body/eval_jaxpr/ppermute | solution.py:12
  1221.8 14.8 %collective-permute-start.1 = (f32[24,1152]{1,0:T(8,128)S(1)}, f32[24,1152]{1,0:T(8,128)S(1)}, u32[]{:S(2)}, u32[]{:S(2)}) collective-permute-start(f32[24,1152]{1,0:T(8,128)S(1)} %convolution_add_fusion.4), channel_id=1, source_target_pairs={{0,8},{8,16},{16,24},{24,32},{32,40},{40,48},{48,56},{56,64},{64,7... | collective-permute-start | bytes 331784 | tf_op jit(solution)/shard_map/while/body/eval_jaxpr/ppermute | solution.py:12
  1240.4 14.8 %collective-permute-start.1 = (f32[24,1152]{1,0:T(8,128)S(1)}, f32[24,1152]{1,0:T(8,128)S(1)}, u32[]{:S(2)}, u32[]{:S(2)}) collective-permute-start(f32[24,1152]{1,0:T(8,128)S(1)} %convolution_add_fusion.4), channel_id=1, source_target_pairs={{0,8},{8,16},{16,24},{24,32},{32,40},{40,48},{48,56},{56,64},{64,7... | collective-permute-start | bytes 331784 | tf_op jit(solution)/shard_map/while/body/eval_jaxpr/ppermute | solution.py:12
  1259.0 14.8 %collective-permute-start.1 = (f32[24,1152]{1,0:T(8,128)S(1)}, f32[24,1152]{1,0:T(8,128)S(1)}, u32[]{:S(2)}, u32[]{:S(2)}) collective-permute-start(f32[24,1152]{1,0:T(8,128)S(1)} %convolution_add_fusion.4), channel_id=1, source_target_pairs={{0,8},{8,16},{16,24},{24,32},{32,40},{40,48},{48,56},{56,64},{64,7... | collective-permute-start | bytes 331784 | tf_op jit(solution)/shard_map/while/body/eval_jaxpr/ppermute | solution.py:12
  (69 other events, 939.3 us)
Sparse Core Ops, SparseCore 0:
  1274.9 123.1 reduce-scatter.3
where the time goes:
time: 1420 us; the launch traced here: 1410 us
  waiting for transfers between devices  732 us (52%)
  starting transfers between devices  257 us (18%)
  blocking collectives  194 us (14%)
  matrix products  156 us (11%)
  loops' own time  45.1 us (3%)
  between operations  16.6 us (1%)
    ppermute x128, waiting for transfers between devices, shifted(): return lax.ppermute(value, axis, pairs)  726 us
    ppermute x128, starting transfers between devices, shifted(): return lax.ppermute(value, axis, pairs)  257 us
    psum x1, blocking collectives, shards(): loss_total = lax.psum(loss_sum, ('loop', 'grp'))  115 us
    dot_general x64, matrix products, pairwise_terms(): lax.dot_general(text_portion, image_block_rows, (((1,), (1,)), ((), ())),...  103 us
    all_gather x1, blocking collectives, shards(): lax.all_gather(image_unit.astype(jnp.bfloat16), 'grp', axis=0, tiled=True)  79.2 us
    another operation x1, loops' own time, shards(): lax.fori_loop(0, loop_size, one_hop, start_state)  45.1 us
    dot_general x64, matrix products, pairwise_terms(): lax.dot_general(match_factors, text_portion, (((0,), (0,)), ((), ())), pr...  38.3 us
  transfers between devices with their start and end apart: 129, of which 128 were waited for; matrix products, arithmetic and copies ran while one was open for 11% of the time, Pallas kernels for 0%

commit v1 on v0

v1 whole, which is shorter than its diff:
```python
import functools

import jax
import jax.numpy as jnp
from jax import lax
from jax.experimental import pallas as pl
from jax.experimental.pallas import tpu as pltpu
from jax.sharding import Mesh, PartitionSpec as P

epsilon = 1e-06
AXES = ("zl", "x", "c", "y", "zh")
SIZES = (8, 4, 2, 4, 2)
RING = ("zl", "zh")
PLANE = ("x", "y")
LANES = 128
LIMIT = 48 * 1024 * 1024


def normalize(raw_rows):
    row_norm = jnp.sqrt(jnp.sum(raw_rows * raw_rows, axis=1, keepdims=True) + epsilon)
    return (raw_rows / row_norm, row_norm)


def back_norm(unit_rows, row_norm, gradient):
    return (gradient - unit_rows * jnp.sum(unit_rows * gradient, axis=1, keepdims=True)) / row_norm


def low(rows):
    return rows.astype(jnp.bfloat16).astype(jnp.float32)


def loss_and_sigmoid(values):
    small = jnp.exp(-jnp.abs(values))
    loss = jnp.maximum(values, 0.0) + jnp.log1p(small)
    return loss, jnp.where(values >= 0, 1.0, small) / (1.0 + small)


def own_pairs(image_low, text_low, heat, offset):
    return jnp.sum(image_low * text_low, axis=1, keepdims=True) * heat + offset


def unit_kernel(heat_ref, offset_ref, picture_ref, caption_ref, image_ref, text_ref, loss_ref):
    image_unit, _ = normalize(picture_ref[...])
    text_unit, _ = normalize(caption_ref[...])
    image_low, text_low = image_unit.astype(jnp.bfloat16), text_unit.astype(jnp.bfloat16)
    image_ref[...] = image_low
    text_ref[...] = text_low
    heat = jnp.exp(jnp.full((1, 1), heat_ref[0], jnp.float32))
    logits = own_pairs(image_low.astype(jnp.float32), text_low.astype(jnp.float32), heat, offset_ref[0])
    loss, _ = loss_and_sigmoid(-logits)
    loss_ref[...] = loss


def unit_rows(heat_exponent, offset_added, pictures, captions):
    rows = pictures.shape[0]
    return pl.pallas_call(
        unit_kernel,
        in_specs=[pl.BlockSpec(memory_space=pltpu.SMEM)] * 2 + [pl.BlockSpec(memory_space=pltpu.VMEM)] * 2,
        out_shape=[
            jax.ShapeDtypeStruct(pictures.shape, jnp.bfloat16),
            jax.ShapeDtypeStruct(captions.shape, jnp.bfloat16),
            jax.ShapeDtypeStruct((rows, 1), jnp.float32),
        ],
    )(heat_exponent, offset_added, pictures, captions)


def pair_kernel(
    rows, places, heat_ref, offset_ref, own_loss_ref, image_ref, text_ref,
    image_out_ref, text_out_ref, text_sum_ref, loss_sum_ref,
):
    step = pl.program_id(0)
    images = image_ref[...]
    texts = text_ref[...]
    heat = jnp.exp(jnp.full((1, 1), heat_ref[0], jnp.float32))
    logits = lax.dot_general(
        images, texts, (((1,), (1,)), ((), ())), preferred_element_type=jnp.float32
    )
    logits = logits * heat + offset_ref[0]
    image_row = lax.broadcasted_iota(jnp.int32, logits.shape, 0) - places[1] * rows
    text_row = lax.broadcasted_iota(jnp.int32, logits.shape, 1) - places[2] * rows
    match = (image_row == text_row) & (image_row >= 0) & (image_row < rows) & (step == 1)
    loss, sigmoid = loss_and_sigmoid(logits)
    weights = jnp.where(match, 0.0, heat * sigmoid).astype(jnp.bfloat16)
    loss = jnp.sum(jnp.where(match, 0.0, loss), axis=0, keepdims=True)
    image_out_ref[...] = jnp.dot(weights, texts, preferred_element_type=jnp.float32)[None]
    text_part = lax.dot_general(
        weights, images, (((0,), (0,)), ((), ())), preferred_element_type=jnp.float32
    )

    @pl.when(step == 0)
    def _():
        text_sum_ref[...] = text_part
        loss_sum_ref[...] = loss

    @pl.when(step == 1)
    def _():
        width = text_part.shape[1]
        text_out_ref[:, :width] = (text_sum_ref[...] + text_part).astype(jnp.bfloat16)
        total = jnp.sum(loss_sum_ref[...] + loss, axis=1, keepdims=True)
        total += jnp.sum(own_loss_ref[...], axis=0, keepdims=True)
        text_out_ref[:, width:] = pieces(total, (text_out_ref.shape[0], LANES))


def pieces(total, shape):
    first = low(total)
    second = low(total - first)
    third = total - first - second
    lane = lax.broadcasted_iota(jnp.int32, shape, len(shape) - 1)
    spread = jnp.where(lane == 0, first, jnp.where(lane == 1, second, jnp.where(lane == 2, third, 0.0)))
    return spread.astype(jnp.bfloat16)


def pair_terms(rows, places, heat_exponent, offset_added, own_loss, images, texts):
    half, width = images.shape[0] // 2, images.shape[1]
    count = texts.shape[0]
    return pl.pallas_call(
        functools.partial(pair_kernel, rows),
        grid_spec=pltpu.PrefetchScalarGridSpec(
            num_scalar_prefetch=1,
            grid=(2,),
            in_specs=[
                pl.BlockSpec(memory_space=pltpu.SMEM),
                pl.BlockSpec(memory_space=pltpu.SMEM),
                pl.BlockSpec((rows, 1), lambda i, p: (0, 0)),
                pl.BlockSpec((half, width), lambda i, p: (jnp.where(i == 0, 1 - p[0], p[0]), 0)),
                pl.BlockSpec((count, width), lambda i, p: (0, 0)),
            ],
            out_specs=[
                pl.BlockSpec((1, half, width), lambda i, p: (i, 0, 0)),
                pl.BlockSpec((count, width + LANES), lambda i, p: (0, 0)),
            ],
            scratch_shapes=[
                pltpu.VMEM((count, width), jnp.float32),
                pltpu.VMEM((1, count), jnp.float32),
            ],
        ),
        out_shape=[
            jax.ShapeDtypeStruct((2, half, width), jnp.float32),
            jax.ShapeDtypeStruct((count, width + LANES), jnp.bfloat16),
        ],
        compiler_params=pltpu.CompilerParams(vmem_limit_bytes=LIMIT),
        cost_estimate=pl.CostEstimate(
            flops=12 * half * count * width, bytes_accessed=16 * half * width, transcendentals=6 * half * count
        ),
    )(places, heat_exponent, offset_added, own_loss, images, texts)


def grad_kernel(heat_ref, offset_ref, picture_ref, caption_ref, image_part_ref, text_part_ref, image_ref, text_ref):
    width = picture_ref.shape[1]
    image_unit, image_norm = normalize(picture_ref[...])
    text_unit, text_norm = normalize(caption_ref[...])
    image_low, text_low = low(image_unit), low(text_unit)
    heat = jnp.exp(jnp.full((1, 1), heat_ref[0], jnp.float32))
    _, sigmoid = loss_and_sigmoid(-own_pairs(image_low, text_low, heat, offset_ref[0]))
    weights = low(-sigmoid * heat)
    image_sum = weights * text_low
    text_sum = weights * image_low
    for part in range(image_part_ref.shape[0]):
        image_sum += image_part_ref[part, :, :width].astype(jnp.float32)
    for part in range(text_part_ref.shape[0]):
        text_sum += text_part_ref[part, :, :width].astype(jnp.float32)
    image_ref[...] = back_norm(image_unit, image_norm, image_sum)
    text_ref[...] = back_norm(text_unit, text_norm, text_sum)


def gradients(heat_exponent, offset_added, pictures, captions, image_parts, text_parts):
    return pl.pallas_call(
        grad_kernel,
        in_specs=[pl.BlockSpec(memory_space=pltpu.SMEM)] * 2 + [pl.BlockSpec(memory_space=pltpu.VMEM)] * 4,
        out_shape=[jax.ShapeDtypeStruct(pictures.shape, jnp.float32)] * 2,
        compiler_params=pltpu.CompilerParams(vmem_limit_bytes=LIMIT),
    )(heat_exponent, offset_added, pictures, captions, image_parts, text_parts)


def gathered(block, axes):
    count = lax.axis_size(axes)
    return lax.all_to_all(jnp.broadcast_to(block[None], (count, *block.shape)), axes, 0, 0)


def loss_in(parts, width):
    return jnp.sum(parts[:, 0, width : width + 3].astype(jnp.float32))


def shards(picture_vectors, caption_vectors, heat_exponent, offset_added):
    rows, width = picture_vectors.shape
    ring = lax.axis_size(RING)
    plane = lax.axis_size(PLANE)
    image_low, text_low, own_loss = unit_rows(heat_exponent, offset_added, picture_vectors, caption_vectors)
    images = gathered(image_low, RING).reshape(ring * rows, width)
    images = lax.all_gather(images, "c", axis=0, tiled=True)
    texts = gathered(text_low, PLANE).reshape(plane * rows, width)
    core = lax.axis_index("c")
    places = jnp.stack([core, lax.axis_index(RING), lax.axis_index(PLANE)]).astype(jnp.int32)
    image_halves, text_part = pair_terms(rows, places, heat_exponent, offset_added, own_loss, images, texts)
    image_other = lax.ppermute(image_halves[0], "c", [(0, 1), (1, 0)])
    text_parts = lax.all_to_all(text_part.reshape(plane, rows, width + LANES), PLANE, 0, 0)
    image_part = (image_halves[1] + image_other).astype(jnp.bfloat16).reshape(ring, rows, width)
    loss_block = pieces(loss_in(text_parts, width), (ring, rows, LANES))
    image_parts = lax.all_to_all(jnp.concatenate([image_part, loss_block], axis=2), RING, 0, 0)
    loss_total = lax.psum(loss_in(image_parts, width), "c")
    loss_mean = (loss_total / (rows * lax.axis_size(AXES))).reshape(1)
    image_grads, text_grads = gradients(
        heat_exponent, offset_added, picture_vectors, caption_vectors, image_parts, text_parts
    )
    return (loss_mean, image_grads, text_grads)


def solution(mesh):
    fine = Mesh(mesh.devices.reshape(SIZES), AXES)
    in_specs = (P(AXES, None), P(AXES, None), P(), P())
    out_specs = (P(), P(AXES, None), P(AXES, None))
    return jax.shard_map(shards, mesh=fine, in_specs=in_specs, out_specs=out_specs, check_vma=False)
```

time: 1420 us -> 205 us (0.14)
  waiting for transfers between devices: 732 us -> 28.9 us
  starting transfers between devices: 257 us -> 16.8 us
  matrix products: 156 us -> 0 us
  blocking collectives: 194 us -> 120 us
  loops' own time: 45.1 us -> 0 us
    ppermute x128 -> x1, waiting for transfers between devices: 726 us -> 0.01 us  [shards(): image_other = lax.ppermute(image_halves[0], 'c', [(0, 1), (1, 0)])]
    ppermute x128 -> x1, starting transfers between devices: 257 us -> 6.32 us  [shards(): image_other = lax.ppermute(image_halves[0], 'c', [(0, 1), (1, 0)])]
    dot_general x192 -> x0, matrix products: 156 us -> none  [the longest x64 103 us: pairwise_terms(): lax.dot_general(text_portion, image_block_rows, (((1,), (1,)), ((), ())),...]
    all_to_all x0 -> x2, blocking collectives: none -> 110 us  [the longest x1 58.5 us: gathered(): lax.all_to_all(jnp.broadcast_to(block[None], (count, *block.shape)), axes...]
    psum x1, blocking collectives: 115 us -> 9.67 us  [shards(): loss_total = lax.psum(loss_in(image_parts, width), 'c')]
    all_gather x1 -> x0, blocking collectives: 79.2 us -> none  [shards(): lax.all_gather(image_unit.astype(jnp.bfloat16), 'grp', axis=0, tiled=True)]
    another operation x1 -> x0, loops' own time: 45.1 us -> none  [shards(): lax.fori_loop(0, loop_size, one_hop, start_state)]
    all_to_all x0 -> x2, waiting for transfers between devices: none -> 27.9 us  [the longest x1 17 us: shards(): lax.all_to_all(text_part.reshape(plane, rows, width + LANES), PLANE, 0, 0)]
  transfers between devices with their start and end apart: 129 -> 4, of which waited for: 128 -> 3; matrix products, arithmetic and copies ran while one was open for 11% -> 1% of each run, Pallas kernels for 0% -> 0%
where the time goes in v1:
time: 205 us; the launch traced here: 204 us
  blocking collectives  120 us (59%)
  waiting for transfers between devices  28.9 us (14%)
  between operations  18.5 us (9%)
  starting transfers between devices  16.8 us (8%)
  Pallas kernels  10.1 us (5%)
  local copies, waits for them, and re-layouts  6.18 us (3%)
  other arithmetic  3.05 us (1%)
    all_to_all x1, blocking collectives, gathered(): lax.all_to_all(jnp.broadcast_to(block[None], (count, *block.shape)), axes...  58.5 us
    all_to_all x1, blocking collectives, shards(): lax.all_to_all(jnp.concatenate([image_part, loss_block], axis=2), RING, 0...  51.8 us
    all_to_all x1, waiting for transfers between devices, shards(): lax.all_to_all(text_part.reshape(plane, rows, width + LANES), PLANE, 0, 0)  17 us
    all_to_all x1, waiting for transfers between devices, gathered(): lax.all_to_all(jnp.broadcast_to(block[None], (count, *block.shape)), axes...  10.9 us
    psum x1, blocking collectives, shards(): loss_total = lax.psum(loss_in(image_parts, width), 'c')  9.67 us
    pallas_call x1, Pallas kernels, pair_terms(): pl.pallas_call(functools.partial(pair_kernel, rows), grid_spec=pltpu.Pref...  7.04 us
    all_to_all x1, starting transfers between devices, gathered(): lax.all_to_all(jnp.broadcast_to(block[None], (count, *block.shape)), axes...  6.75 us
    ppermute x1, starting transfers between devices, shards(): image_other = lax.ppermute(image_halves[0], 'c', [(0, 1), (1, 0)])  6.32 us
  transfers between devices with their start and end apart: 4, of which 3 were waited for; matrix products, arithmetic and copies ran while one was open for 1% of the time, Pallas kernels for 0%

profile of v1, /device:TPU:1, one launch (start us, length us, event | category | flops | bytes accessed | tf_op | source)
XLA Modules:
  0.0 203.5 jit_solution(11915765262565698389)
XLA Ops:
  7.2 0.0 all-gather.2.cloned.1.call-start
  8.5 1.8 shard_map.67
  10.3 0.0 copy-start.4
  10.3 0.9 broadcast_in_dim.27
  11.2 58.5 %all_to_all.20 = bf16[16,24,1152]{2,1,0:T(8,128)(2,1)} all-to-all(bf16[16,24,1152]{2,1,0:T(8,128)(2,1)S(1)} %broadcast_in_dim.27), channel_id=1, replica_groups=mesh['zl'=8,'x'=4,'c'=2,'y'=4,'zh'=2] {'zl','zh'}, dimensions={0} | all-to-all | bytes 1769472 | tf_op jit(solution)/shard_map/all_to_all | solution.py:177
  69.7 0.0 copy-start.3
  69.7 0.0 all-gather.2.cloned.1.call-update
  69.7 0.0 copy-done.4
  69.7 1.0 broadcast_in_dim.28
  70.7 6.8 %all-to-all-start.1 = ((bf16[16,24,1152]{2,1,0:T(8,128)(2,1)}), bf16[16,24,1152]{2,1,0:T(8,128)(2,1)S(1)}, u32[]{:S(2)}, u32[]{:S(2)}) async-start(bf16[16,24,1152]{2,1,0:T(8,128)(2,1)} %broadcast_in_dim.28), calls=%async_computation.1 | async-start | bytes 1769472 | tf_op jit(solution)/shard_map/all_to_all | solution.py:177
  77.5 0.1 pad_add_fusion.places
  77.5 10.9 %all-to-all-done.1 = bf16[16,24,1152]{2,1,0:T(8,128)(2,1)S(1)} async-done(((bf16[16,24,1152]{2,1,0:T(8,128)(2,1)}), bf16[16,24,1152]{2,1,0:T(8,128)(2,1)S(1)}, u32[]{:S(2)}, u32[]{:S(2)}) %all-to-all-start.1) | async-done | bytes 884768 | tf_op jit(solution)/shard_map/all_to_all | solution.py:177
  88.5 1.0 all-gather.2.cloned.1.call-done.image_ref
  89.4 0.0 copy-done.3
  89.4 0.0 copy-start.2
  89.4 1.5 copy-done.2
  90.9 7.0 %shard_map.68 = (f32[2,384,1152]{2,1,0:T(8,128)}, bf16[384,1280]{1,0:T(8,128)(2,1)}) custom-call(s32[3]{0:T(128)S(1)} %pad_add_fusion.places, f32[1]{0:T(128)S(6)} %copy.7.heat_ref, f32[1]{0:T(128)S(6)} %copy.8.offset_ref, f32[24,1]{1,0:T(8,128)S(1)} %copy-done.3, bf16[768,1152]{1,0:T(8,128)(2,1)S(1)} %copy-done.2, bf16[384,1152]{1,0:T(8,128)(2,1)S(1)} %bitcast.14), custom_call_target="tpu_custom_call" | custom-call | flops 2038431744 | bytes 7077888 | tf_op jit(solution)/shard_map/pallas_call | solution.py:116
  97.9 2.8 %slice_bitcast_fusion = f32[384,1152]{1,0:T(8,128)} fusion(f32[2,384,1152]{2,1,0:T(8,128)} %get-tuple-element.13), kind=kLoop, calls=%fused_computation.2 | loop fusion | bytes 3538944 | tf_op jit(solution)/shard_map/squeeze | solution.py:195
  100.7 6.3 %collective-permute-start = (f32[384,1152]{1,0:T(8,128)}, f32[384,1152]{1,0:T(8,128)S(1)}, u32[]{:S(2)}, u32[]{:S(2)}) collective-permute-start(f32[384,1152]{1,0:T(8,128)} %slice_bitcast_fusion), channel_id=1, source_target_pairs={{0,8},{8,0},{1,9},{9,1},{2,10},{10,2},{3,11},{11,3},{4,12},{12,4},... | collective-permute-start | bytes 5308424 | tf_op jit(solution)/shard_map/ppermute | solution.py:195
  107.1 3.7 %all-to-all-start.2 = ((bf16[16,24,1280]{2,1,0:T(8,128)(2,1)}), bf16[16,24,1280]{2,1,0:T(8,128)(2,1)S(1)}, u32[]{:S(2)}, u32[]{:S(2)}) async-start(bf16[16,24,1280]{2,1,0:T(8,128)(2,1)} %bitcast.8), calls=%async_computation.2 | async-start | bytes 1966080 | tf_op jit(solution)/shard_map/all_to_all | solution.py:196
  110.7 17.0 %all-to-all-done.2.text_part_ref = bf16[16,24,1280]{2,1,0:T(8,128)(2,1)S(1)} async-done(((bf16[16,24,1280]{2,1,0:T(8,128)(2,1)}), bf16[16,24,1280]{2,1,0:T(8,128)(2,1)S(1)}, u32[]{:S(2)}, u32[]{:S(2)}) %all-to-all-start.2) | async-done | bytes 983072 | tf_op jit(solution)/shard_map/all_to_all | solution.py:196
  127.8 0.6 fusion.2
  129.7 0.0 collective-permute-done
  129.7 1.6 fusion
  131.4 0.0 copy-start
  131.4 0.0 copy-start.1
  131.4 0.1 pad_maximum_fusion
  131.5 51.8 %all_to_all.21.image_part_ref = bf16[16,24,1280]{2,1,0:T(8,128)(2,1)S(1)} all-to-all(bf16[16,24,1280]{2,1,0:T(8,128)(2,1)S(1)} %pad_maximum_fusion), channel_id=1, replica_groups=mesh['zl'=8,'x'=4,'c'=2,'y'=4,'zh'=2] {'zl','zh'}, dimensions={0} | all-to-all | bytes 1966080 | tf_op jit(solution)/shard_map/all_to_all | solution.py:199
  183.3 0.6 fusion.1
  183.9 9.7 %psum.7 = f32[]{:T(128)} all-reduce(f32[]{:T(128)} %fusion.1), channel_id=1, replica_groups=mesh['zl'=8,'x'=4,'c'=2,'y'=4,'zh'=2] {'c'}, use_global_device_ids=true, to_apply=%region_2.3 | all-reduce | flops 1 | bytes 8 | tf_op jit(solution)/shard_map/psum | solution.py:200
  194.3 0.0 copy-done
  194.3 0.0 copy-done.1
  194.3 1.2 shard_map.69
  (3 shorter events, 0.0 us)
Async XLA Ops:
  7.2 82.2 %all-gather.2.cloned.1.call-start = ((), (), s32[]{:S(2)}) async-start(), calls=%async_computation.4 | async-start | bytes 2654208 | tf_op jit(solution)/shard_map/all_gather | solution.py:190
  10.3 59.4 %copy-start.4 = (bf16[24,1152]{1,0:T(8,128)(2,1)S(1)}, bf16[24,1152]{1,0:T(8,128)(2,1)}, u32[]{:S(2)}) copy-start(bf16[24,1152]{1,0:T(8,128)(2,1)} %get-tuple-element.12) | copy-start | bytes 165892
  69.7 19.7 %copy-start.3 = (f32[24,1]{1,0:T(8,128)S(1)}, f32[24,1]{1,0:T(8,128)}, u32[]{:S(2)}) copy-start(f32[24,1]{1,0:T(8,128)} %get-tuple-element.10.own_loss_ref) | copy-start | bytes 292
  70.7 17.8 %all-to-all-start.1 = ((bf16[16,24,1152]{2,1,0:T(8,128)(2,1)}), bf16[16,24,1152]{2,1,0:T(8,128)(2,1)S(1)}, u32[]{:S(2)}, u32[]{:S(2)}) async-start(bf16[16,24,1152]{2,1,0:T(8,128)(2,1)} %broadcast_in_dim.28), calls=%async_computation.1 | async-start | bytes 1769472 | tf_op jit(solution)/shard_map/all_to_all | solution.py:177
  89.4 1.5 copy-start.2
  100.7 29.0 %collective-permute-start = (f32[384,1152]{1,0:T(8,128)}, f32[384,1152]{1,0:T(8,128)S(1)}, u32[]{:S(2)}, u32[]{:S(2)}) collective-permute-start(f32[384,1152]{1,0:T(8,128)} %slice_bitcast_fusion), channel_id=1, source_target_pairs={{0,8},{8,0},{1,9},{9,1},{2,10},{10,2},{3,11},{11,3},{4,12},{12,4},... | collective-permute-start | bytes 5308424 | tf_op jit(solution)/shard_map/ppermute | solution.py:195
  107.1 20.7 %all-to-all-start.2 = ((bf16[16,24,1280]{2,1,0:T(8,128)(2,1)}), bf16[16,24,1280]{2,1,0:T(8,128)(2,1)S(1)}, u32[]{:S(2)}, u32[]{:S(2)}) async-start(bf16[16,24,1280]{2,1,0:T(8,128)(2,1)} %bitcast.8), calls=%async_computation.2 | async-start | bytes 1966080 | tf_op jit(solution)/shard_map/all_to_all | solution.py:196
  131.4 62.9 %copy-start = (f32[24,1152]{1,0:T(8,128)S(1)}, f32[24,1152]{1,0:T(8,128)}, u32[]{:S(2)}) copy-start(f32[24,1152]{1,0:T(8,128)} %picture_ref.3) | copy-start | bytes 331780
  131.4 62.9 %copy-start.1 = (f32[24,1152]{1,0:T(8,128)S(1)}, f32[24,1152]{1,0:T(8,128)}, u32[]{:S(2)}) copy-start(f32[24,1152]{1,0:T(8,128)} %caption_ref.3) | copy-start | bytes 331780
Sparse Core Ops, SparseCore 0:
  69.8 19.5 all-gather.1

commit v2 on v1

v2 whole, which is shorter than its diff:
```python
import jax
import jax.numpy as jnp
from jax import lax
from jax.experimental import pallas as pl
from jax.experimental.pallas import tpu as pltpu
from jax.sharding import Mesh, PartitionSpec as P

epsilon = 1e-06
AXES = ("zl", "x", "c", "y", "zh")
SIZES = (8, 4, 2, 4, 2)
PLANE = ("x", "y")
COLUMN = ("zl", "c", "zh")
LANES = 128
CHUNK = 256
LIMIT = 48 * 1024 * 1024
HALF = 0.5


def normalize(raw_rows):
    row_norm = jnp.sqrt(jnp.sum(raw_rows * raw_rows, axis=1, keepdims=True) + epsilon)
    return (raw_rows / row_norm, row_norm)


def back_norm(unit_rows, row_norm, gradient):
    return (gradient - unit_rows * jnp.sum(unit_rows * gradient, axis=1, keepdims=True)) / row_norm


def low(rows):
    return rows.astype(jnp.bfloat16).astype(jnp.float32)


def loss_and_sigmoid(values):
    small = jnp.exp(-jnp.abs(values))
    loss = jnp.maximum(values, 0.0) + jnp.log1p(small)
    return loss, jnp.where(values >= 0, 1.0, small) / (1.0 + small)


def own_pairs(image_low, text_low, heat, offset):
    return jnp.sum(image_low * text_low, axis=1, keepdims=True) * heat + offset


def unit_kernel(heat_ref, offset_ref, picture_ref, caption_ref, image_ref, text_ref, loss_ref):
    image_unit, _ = normalize(picture_ref[...])
    text_unit, _ = normalize(caption_ref[...])
    image_low, text_low = image_unit.astype(jnp.bfloat16), text_unit.astype(jnp.bfloat16)
    image_ref[...] = image_low
    text_ref[...] = text_low
    heat = jnp.exp(jnp.full((1, 1), heat_ref[0], jnp.float32))
    logits = own_pairs(image_low.astype(jnp.float32), text_low.astype(jnp.float32), heat, offset_ref[0])
    loss, _ = loss_and_sigmoid(-logits)
    loss_ref[...] = loss


def unit_rows(heat_exponent, offset_added, pictures, captions):
    rows = pictures.shape[0]
    return pl.pallas_call(
        unit_kernel,
        in_specs=[pl.BlockSpec(memory_space=pltpu.SMEM)] * 2 + [pl.BlockSpec(memory_space=pltpu.VMEM)] * 2,
        out_shape=[
            jax.ShapeDtypeStruct(pictures.shape, jnp.bfloat16),
            jax.ShapeDtypeStruct(captions.shape, jnp.bfloat16),
            jax.ShapeDtypeStruct((rows, 1), jnp.float32),
        ],
    )(heat_exponent, offset_added, pictures, captions)


def pieces(total, shape):
    first = low(total)
    second = low(total - first)
    third = total - first - second
    lane = lax.broadcasted_iota(jnp.int32, shape, len(shape) - 1)
    spread = jnp.where(lane == 0, first, jnp.where(lane == 1, second, jnp.where(lane == 2, third, 0.0)))
    return spread.astype(jnp.bfloat16)


def pair_kernel(
    place_ref, heat_ref, offset_ref, own_loss_ref, near_ref, far_ref, text_ref,
    near_out_ref, far_out_ref, text_out_ref, loss_sum_ref,
):
    step = pl.program_id(0)
    rows = own_loss_ref.shape[0]
    half, width = near_ref.shape
    texts = text_ref[...]
    count = texts.shape[0]
    heat = jnp.exp(jnp.full((1, 1), heat_ref[0], jnp.float32))
    image_parts = []
    text_part = jnp.zeros((count, width), jnp.float32)
    loss = jnp.zeros((1, count), jnp.float32)
    for images in (near_ref[...], far_ref[...]):
        logits = lax.dot_general(
            images, texts, (((1,), (1,)), ((), ())), preferred_element_type=jnp.float32
        )
        logits = logits * heat + offset_ref[0]
        loss_part, sigmoid = loss_and_sigmoid(logits)
        weights = heat * sigmoid
        if not image_parts:
            image_row = lax.broadcasted_iota(jnp.int32, logits.shape, 0)
            text_row = lax.broadcasted_iota(jnp.int32, logits.shape, 1) + (step * count - place_ref[0])
            match = (image_row == text_row) & (image_row < rows)
            weights = jnp.where(match, 0.0, weights)
            loss_part = jnp.where(match, 0.0, loss_part)
        weights = weights.astype(jnp.bfloat16)
        loss += jnp.sum(loss_part, axis=0, keepdims=True)
        image_parts.append(jnp.dot(weights, texts, preferred_element_type=jnp.float32))
        text_part += lax.dot_general(
            weights, images, (((0,), (0,)), ((), ())), preferred_element_type=jnp.float32
        )
    start = pl.multiple_of(step * count, count)
    text_out_ref[pl.ds(start, count), :width] = text_part.astype(jnp.bfloat16)

    @pl.when(step == 0)
    def _():
        near_out_ref[...] = image_parts[0]
        far_out_ref[...] = image_parts[1]
        loss_sum_ref[...] = loss

    @pl.when(step > 0)
    def _():
        near_out_ref[...] += image_parts[0]
        far_out_ref[...] += image_parts[1]
        loss_sum_ref[...] += loss

    @pl.when(step == pl.num_programs(0) - 1)
    def _():
        total = jnp.sum(loss_sum_ref[...], axis=1, keepdims=True)
        total += jnp.sum(own_loss_ref[...], axis=0, keepdims=True)
        text_out_ref[:, width:] = pieces(total, (text_out_ref.shape[0], LANES))


def pair_terms(place, heat_exponent, offset_added, own_loss, near, far, texts):
    half, width = near.shape
    count = texts.shape[0]
    return pl.pallas_call(
        pair_kernel,
        grid=(count // CHUNK,),
        in_specs=[pl.BlockSpec(memory_space=pltpu.SMEM)] * 3
        + [
            pl.BlockSpec(own_loss.shape, lambda i: (0, 0)),
            pl.BlockSpec((half, width), lambda i: (0, 0)),
            pl.BlockSpec((half, width), lambda i: (0, 0)),
            pl.BlockSpec((CHUNK, width), lambda i: (i, 0)),
        ],
        out_specs=[
            pl.BlockSpec((half, width), lambda i: (0, 0)),
            pl.BlockSpec((half, width), lambda i: (0, 0)),
            pl.BlockSpec((count, width + LANES), lambda i: (0, 0)),
        ],
        out_shape=[
            jax.ShapeDtypeStruct((half, width), jnp.float32),
            jax.ShapeDtypeStruct((half, width), jnp.float32),
            jax.ShapeDtypeStruct((count, width + LANES), jnp.bfloat16),
        ],
        scratch_shapes=[pltpu.VMEM((1, CHUNK), jnp.float32)],
        compiler_params=pltpu.CompilerParams(vmem_limit_bytes=LIMIT),
        cost_estimate=pl.CostEstimate(
            flops=12 * half * count * width, bytes_accessed=16 * half * width, transcendentals=6 * half * count
        ),
    )(place, heat_exponent, offset_added, own_loss, near, far, texts)


def grad_kernel(heat_ref, offset_ref, picture_ref, caption_ref, image_sum_ref, text_sum_ref, image_ref, text_ref):
    image_unit, image_norm = normalize(picture_ref[...])
    text_unit, text_norm = normalize(caption_ref[...])
    image_low, text_low = low(image_unit), low(text_unit)
    heat = jnp.exp(jnp.full((1, 1), heat_ref[0], jnp.float32))
    _, sigmoid = loss_and_sigmoid(-own_pairs(image_low, text_low, heat, offset_ref[0]))
    weights = low(-sigmoid * heat)
    image_ref[...] = back_norm(image_unit, image_norm, image_sum_ref[...] + weights * text_low)
    text_ref[...] = back_norm(text_unit, text_norm, text_sum_ref[...] + weights * image_low)


def gradients(heat_exponent, offset_added, pictures, captions, image_sum, text_sum):
    return pl.pallas_call(
        grad_kernel,
        in_specs=[pl.BlockSpec(memory_space=pltpu.SMEM)] * 2 + [pl.BlockSpec(memory_space=pltpu.VMEM)] * 4,
        out_shape=[jax.ShapeDtypeStruct(pictures.shape, jnp.float32)] * 2,
    )(heat_exponent, offset_added, pictures, captions, image_sum, text_sum)


def swapped(value, axis, step):
    return lax.ppermute(value, axis, [(i, i ^ step) for i in range(lax.axis_size(axis))])


def doubled(value, axis, step):
    return jnp.concatenate([value, swapped(value, axis, step)], axis=0)


def halved(value, axis, step):
    half = value.shape[0] // 2
    sent = (value[half:] * HALF).astype(jnp.float16)
    return value[:half] + swapped(sent, axis, step).astype(jnp.float32) * (1 / HALF)


def shards(picture_vectors, caption_vectors, heat_exponent, offset_added):
    rows, width = picture_vectors.shape
    plane, column = lax.axis_size(PLANE), lax.axis_size(COLUMN)
    steps = [1 << bit for bit in range(lax.axis_size("zl").bit_length() - 1)]
    image_low, text_low, own_loss = unit_rows(heat_exponent, offset_added, picture_vectors, caption_vectors)

    texts = doubled(text_low, "zh", 1)
    texts = lax.all_to_all(jnp.broadcast_to(texts[None], (plane, *texts.shape)), PLANE, 0, 0)
    near = image_low
    for step in reversed(steps):
        near = doubled(near, "zl", step)
    far = swapped(near, "c", 1)

    place = (lax.axis_index(PLANE) * 2 * rows).astype(jnp.int32).reshape(1)
    near_part, far_part, text_part = pair_terms(
        place, heat_exponent, offset_added, own_loss, near, far, texts.reshape(plane * 2 * rows, width)
    )

    text_parts = lax.all_to_all(text_part.reshape(plane, 2 * rows, width + LANES), PLANE, 0, 0)
    image_sum = near_part + swapped(far_part, "c", 1)
    for step in steps:
        image_sum = halved(image_sum, "zl", step)
    text_sum = halved(jnp.sum(text_parts[:, :, :width].astype(jnp.float32), axis=0), "zh", 1)

    plane_loss = jnp.sum(text_parts[:, 0, width : width + 3].astype(jnp.float32))
    losses = lax.all_to_all(jnp.broadcast_to(plane_loss, (column, 8, LANES)), COLUMN, 0, 0)
    loss_mean = (jnp.sum(losses[:, 0, 0]) / (rows * lax.axis_size(AXES))).reshape(1)
    image_grads, text_grads = gradients(
        heat_exponent, offset_added, picture_vectors, caption_vectors, image_sum, text_sum
    )
    return (loss_mean, image_grads, text_grads)


def solution(mesh):
    fine = Mesh(mesh.devices.reshape(SIZES), AXES)
    in_specs = (P(AXES, None), P(AXES, None), P(), P())
    out_specs = (P(), P(AXES, None), P(AXES, None))
    return jax.shard_map(shards, mesh=fine, in_specs=in_specs, out_specs=out_specs, check_vma=False)
```

time: 205 us -> 144 us (0.70)
  blocking collectives: 120 us -> 0 us
  starting transfers between devices: 16.8 us -> 77.7 us
  between operations: 18.5 us -> 3.92 us
  waiting for transfers between devices: 28.9 us -> 43 us
  local copies, waits for them, and re-layouts: 6.18 us -> 2.71 us
    all_to_all x2 -> x0, blocking collectives: 110 us -> none  [the longest x1 58.5 us: gathered(): lax.all_to_all(jnp.broadcast_to(block[None], (count, *block.shape)), axes...]
    ppermute x1 -> x10, starting transfers between devices: 6.32 us -> 59.3 us  [swapped(): lax.ppermute(value, axis, [(i, i ^ step) for i in range(lax.axis_size(axi...]
    ppermute x1 -> x10, waiting for transfers between devices: 0.01 us -> 23.9 us  [swapped(): lax.ppermute(value, axis, [(i, i ^ step) for i in range(lax.axis_size(axi...]
    psum x1 -> x0, blocking collectives: 9.67 us -> none  [shards(): loss_total = lax.psum(loss_in(image_parts, width), 'c')]
    all_to_all x2 -> x3, waiting for transfers between devices: 27.9 us -> 19 us  [the longest x1 11.3 us: shards(): lax.all_to_all(jnp.broadcast_to(plane_loss, (column, 8, LANES)), COLUMN,...]
    all_to_all x2 -> x3, starting transfers between devices: 10.4 us -> 18.4 us  [the longest x1 7.74 us: shards(): lax.all_to_all(jnp.broadcast_to(plane_loss, (column, 8, LANES)), COLUMN,...]
    squeeze x1 -> x0, local copies, waits for them, and re-layouts: 2.81 us -> none  [shards(): image_other = lax.ppermute(image_halves[0], 'c', [(0, 1), (1, 0)])]
  transfers between devices with their start and end apart: 4 -> 13, of which waited for: 3 -> 8; matrix products, arithmetic and copies ran while one was open for 1% -> 4% of each run, Pallas kernels for 0% -> 1%
where the time goes in v2:
time: 144 us; the launch traced here: 143 us
  starting transfers between devices  77.7 us (54%)
  waiting for transfers between devices  43 us (30%)
  Pallas kernels  11.9 us (8%)
  other arithmetic  3.96 us (3%)
  between operations  3.92 us (3%)
  local copies, waits for them, and re-layouts  2.71 us (2%)
    ppermute x10, starting transfers between devices, swapped(): lax.ppermute(value, axis, [(i, i ^ step) for i in range(lax.axis_size(axi...  59.3 us
    ppermute x10, waiting for transfers between devices, swapped(): lax.ppermute(value, axis, [(i, i ^ step) for i in range(lax.axis_size(axi...  23.9 us
    all_to_all x1, waiting for transfers between devices, shards(): lax.all_to_all(jnp.broadcast_to(plane_loss, (column, 8, LANES)), COLUMN,...  11.3 us
    pallas_call x1, Pallas kernels, pair_terms(): pl.pallas_call(pair_kernel, grid=(count // CHUNK,), in_specs=[pl.BlockSpe...  8.05 us
    all_to_all x1, starting transfers between devices, shards(): lax.all_to_all(jnp.broadcast_to(plane_loss, (column, 8, LANES)), COLUMN,...  7.74 us
    all_to_all x1, waiting for transfers between devices, shards(): lax.all_to_all(text_part.reshape(plane, 2 * rows, width + LANES), PLANE,...  7.7 us
    all_to_all x1, starting transfers between devices, shards(): lax.all_to_all(jnp.broadcast_to(texts[None], (plane, *texts.shape)), PLAN...  6.89 us
    all_to_all x1, starting transfers between devices, shards(): lax.all_to_all(text_part.reshape(plane, 2 * rows, width + LANES), PLANE,...  3.73 us
  transfers between devices with their start and end apart: 13, of which 8 were waited for; matrix products, arithmetic and copies ran while one was open for 4% of the time, Pallas kernels for 1%

profile of v2, /device:TPU:1, one launch (start us, length us, event | category | flops | bytes accessed | tf_op | source)
XLA Modules:
  0.0 143.2 jit_solution(7538595943781414795)
XLA Ops:
  1.9 1.8 %shard_map.67 = (bf16[24,1152]{1,0:T(8,128)(2,1)}, bf16[24,1152]{1,0:T(8,128)(2,1)}, f32[24,1]{1,0:T(8,128)}) custom-call(f32[1]{0:T(128)S(6)} %copy.12.heat_ref, f32[1]{0:T(128)S(6)} %copy.13.offset_ref, f32[24,1152]{1,0:T(8,128)} %picture_ref.3, f32[24,1152]{1,0:T(8,128)} %caption_ref.3), custom_call_target="tpu_custom_call" | custom-call | tf_op jit(solution)/shard_map/pallas_call | solution.py:56
  3.7 16.3 %collective-permute-start.4 = (bf16[24,1152]{1,0:T(8,128)(2,1)}, bf16[24,1152]{1,0:T(8,128)(2,1)S(1)}, u32[]{:S(2)}, u32[]{:S(2)}) collective-permute-start(bf16[24,1152]{1,0:T(8,128)(2,1)} %get-tuple-element.13), channel_id=1, source_target_pairs={{0,1},{1,0},{2,3},{3,2},{4,5},{5,4},{6,7},{7,6},{8,9},{9,8},{10,11... | collective-permute-start | bytes 165896 | tf_op jit(solution)/shard_map/ppermute | solution.py:181
  20.0 4.0 %collective-permute-start = (bf16[24,1152]{1,0:T(8,128)(2,1)}, bf16[24,1152]{1,0:T(8,128)(2,1)S(1)}, u32[]{:S(2)}, u32[]{:S(2)}) collective-permute-start(bf16[24,1152]{1,0:T(8,128)(2,1)} %get-tuple-element.12), channel_id=1, source_target_pairs={{0,256},{64,320},{128,384},{192,448},{256,0},{320,64},{384,128},{4... | collective-permute-start | bytes 165896 | tf_op jit(solution)/shard_map/ppermute | solution.py:181
  24.0 0.0 collective-permute-done.4
  24.0 0.8 pad_maximum_fusion.2
  24.8 1.3 broadcast_in_dim.4
  26.2 0.0 copy-start.1
  26.2 0.0 copy-start
  26.2 6.9 %all-to-all-start = ((bf16[16,48,1152]{2,1,0:T(8,128)(2,1)}), bf16[16,48,1152]{2,1,0:T(8,128)(2,1)S(1)}, u32[]{:S(2)}, u32[]{:S(2)}) async-start(bf16[16,48,1152]{2,1,0:T(8,128)(2,1)} %broadcast_in_dim.4), calls=%async_computation | async-start | bytes 3538944 | tf_op jit(solution)/shard_map/all_to_all | solution.py:201
  33.1 0.0 copy-done.1
  33.1 0.0 collective-permute-done
  33.1 3.1 %collective-permute-start.1 = (bf16[48,1152]{1,0:T(8,128)(2,1)S(1)}, bf16[48,1152]{1,0:T(8,128)(2,1)S(1)}, u32[]{:S(2)}, u32[]{:S(2)}) collective-permute-start(bf16[48,1152]{1,0:T(8,128)(2,1)S(1)} %pad_maximum_fusion.1), channel_id=1, source_target_pairs={{0,128},{64,192},{128,0},{192,64},{256,384},{320,448},{384,256},{4... | collective-permute-start | bytes 331784 | tf_op jit(solution)/shard_map/ppermute | solution.py:181
  36.2 6.3 %collective-permute-done.1 = bf16[48,1152]{1,0:T(8,128)(2,1)S(1)} collective-permute-done((bf16[48,1152]{1,0:T(8,128)(2,1)S(1)}, bf16[48,1152]{1,0:T(8,128)(2,1)S(1)}, u32[]{:S(2)}, u32[]{:S(2)}) %collective-permute-start.1) | collective-permute-done | bytes 110624 | tf_op jit(solution)/shard_map/ppermute | solution.py:181
  42.5 1.9 %collective-permute-start.2 = (bf16[96,1152]{1,0:T(8,128)(2,1)S(1)}, bf16[96,1152]{1,0:T(8,128)(2,1)S(1)}, u32[]{:S(2)}, u32[]{:S(2)}) collective-permute-start(bf16[96,1152]{1,0:T(8,128)(2,1)S(1)} %pad_maximum_fusion), channel_id=1, source_target_pairs={{0,64},{64,0},{128,192},{192,128},{256,320},{320,256},{384,448},{4... | collective-permute-start | bytes 663560 | tf_op jit(solution)/shard_map/ppermute | solution.py:181
  44.5 5.6 %collective-permute-done.2 = bf16[96,1152]{1,0:T(8,128)(2,1)S(1)} collective-permute-done((bf16[96,1152]{1,0:T(8,128)(2,1)S(1)}, bf16[96,1152]{1,0:T(8,128)(2,1)S(1)}, u32[]{:S(2)}, u32[]{:S(2)}) %collective-permute-start.2) | collective-permute-done | bytes 221216 | tf_op jit(solution)/shard_map/ppermute | solution.py:181
  50.1 4.1 %collective-permute-start.3 = (bf16[192,1152]{1,0:T(8,128)(2,1)S(1)}, bf16[192,1152]{1,0:T(8,128)(2,1)S(1)}, u32[]{:S(2)}, u32[]{:S(2)}) collective-permute-start(bf16[192,1152]{1,0:T(8,128)(2,1)S(1)} %constant_dynamic-update-slice_fusion.near_ref), channel_id=1, source_target_pairs={{0,8},{8,0},{1,9},{9,1},{2,10},{10,2},{3,11},{11,3},{4,12},{12,4},... | collective-permute-start | bytes 1327112 | tf_op jit(solution)/shard_map/ppermute | solution.py:181
  54.2 1.4 collective-permute-done.3.far_ref
  55.6 0.0 all-to-all-done
  55.6 0.0 copy-done
  55.6 8.0 %shard_map.68 = (f32[192,1152]{1,0:T(8,128)S(1)}, f32[192,1152]{1,0:T(8,128)S(1)}, bf16[768,1280]{1,0:T(8,128)(2,1)}) custom-call(s32[1]{0:T(128)} %bitcast.place_ref, f32[1]{0:T(128)S(6)} %copy.12.heat_ref, f32[1]{0:T(128)S(6)} %copy.13.offset_ref, f32[24,1]{1,0:T(8,128)S(1)} %copy-done, bf16[192,1152]{1,0:T(8,128)(2,1)S(1)} %constant_dynamic-update-slice_fusion.near_ref, ...), custom_call_target="tpu_custom_call" | custom-call | flops 2038431744 | bytes 3538944 | tf_op jit(solution)/shard_map/pallas_call | solution.py:133
  63.7 6.3 %collective-permute-start.5 = (f32[192,1152]{1,0:T(8,128)S(1)}, f32[192,1152]{1,0:T(8,128)S(1)}, u32[]{:S(2)}, u32[]{:S(2)}) collective-permute-start(f32[192,1152]{1,0:T(8,128)S(1)} %get-tuple-element.16), channel_id=1, source_target_pairs={{0,8},{8,0},{1,9},{9,1},{2,10},{10,2},{3,11},{11,3},{4,12},{12,4},... | collective-permute-start | bytes 2654216 | tf_op jit(solution)/shard_map/ppermute | solution.py:181
  70.0 2.0 %collective-permute-done.5 = f32[192,1152]{1,0:T(8,128)S(1)} collective-permute-done((f32[192,1152]{1,0:T(8,128)S(1)}, f32[192,1152]{1,0:T(8,128)S(1)}, u32[]{:S(2)}, u32[]{:S(2)}) %collective-permute-start.5) | collective-permute-done | bytes 884768 | tf_op jit(solution)/shard_map/ppermute | solution.py:181
  72.0 0.1 add.19
  72.2 2.6 %collective-permute-start.6 = (f16[96,1152]{1,0:T(8,128)(2,1)S(1)}, f16[96,1152]{1,0:T(8,128)(2,1)S(1)}, u32[]{:S(2)}, u32[]{:S(2)}) collective-permute-start(f16[96,1152]{1,0:T(8,128)(2,1)S(1)} %fusion), channel_id=1, source_target_pairs={{0,64},{64,0},{128,192},{192,128},{256,320},{320,256},{384,448},{4... | collective-permute-start | bytes 663560 | tf_op jit(solution)/shard_map/ppermute | solution.py:181
  74.8 3.7 %all-to-all-start.1 = ((bf16[16,48,1280]{2,1,0:T(8,128)(2,1)}), bf16[16,48,1280]{2,1,0:T(8,128)(2,1)S(1)}, u32[]{:S(2)}, u32[]{:S(2)}) async-start(bf16[16,48,1280]{2,1,0:T(8,128)(2,1)} %bitcast.5), calls=%async_computation.1 | async-start | bytes 3932160 | tf_op jit(solution)/shard_map/all_to_all | solution.py:212
  78.6 2.1 %collective-permute-done.6 = f16[96,1152]{1,0:T(8,128)(2,1)S(1)} collective-permute-done((f16[96,1152]{1,0:T(8,128)(2,1)S(1)}, f16[96,1152]{1,0:T(8,128)(2,1)S(1)}, u32[]{:S(2)}, u32[]{:S(2)}) %collective-permute-start.6) | collective-permute-done | bytes 221216 | tf_op jit(solution)/shard_map/ppermute | solution.py:181
  80.7 0.1 slice_add_fusion
  80.8 3.1 %collective-permute-start.7 = (f16[48,1152]{1,0:T(8,128)(2,1)S(1)}, f16[48,1152]{1,0:T(8,128)(2,1)S(1)}, u32[]{:S(2)}, u32[]{:S(2)}) collective-permute-start(f16[48,1152]{1,0:T(8,128)(2,1)S(1)} %fusion.1), channel_id=1, source_target_pairs={{0,128},{64,192},{128,0},{192,64},{256,384},{320,448},{384,256},{4... | collective-permute-start | bytes 331784 | tf_op jit(solution)/shard_map/ppermute | solution.py:181
  83.9 6.5 %collective-permute-done.7 = f16[48,1152]{1,0:T(8,128)(2,1)S(1)} collective-permute-done((f16[48,1152]{1,0:T(8,128)(2,1)S(1)}, f16[48,1152]{1,0:T(8,128)(2,1)S(1)}, u32[]{:S(2)}, u32[]{:S(2)}) %collective-permute-start.7) | collective-permute-done | bytes 110624 | tf_op jit(solution)/shard_map/ppermute | solution.py:181
  90.5 8.0 %collective-permute-start.8 = (f16[24,1152]{1,0:T(8,128)(2,1)S(1)}, f16[24,1152]{1,0:T(8,128)(2,1)S(1)}, u32[]{:S(2)}, u32[]{:S(2)}) collective-permute-start(f16[24,1152]{1,0:T(8,128)(2,1)S(1)} %fusion.3), channel_id=1, source_target_pairs={{0,256},{64,320},{128,384},{192,448},{256,0},{320,64},{384,128},{4... | collective-permute-start | bytes 165896 | tf_op jit(solution)/shard_map/ppermute | solution.py:181
  98.5 7.7 %all-to-all-done.1 = bf16[16,48,1280]{2,1,0:T(8,128)(2,1)S(1)} async-done(((bf16[16,48,1280]{2,1,0:T(8,128)(2,1)}), bf16[16,48,1280]{2,1,0:T(8,128)(2,1)S(1)}, u32[]{:S(2)}, u32[]{:S(2)}) %all-to-all-start.1) | async-done | bytes 1966112 | tf_op jit(solution)/shard_map/all_to_all | solution.py:212
  106.2 0.2 convert_reduce_fusion
  106.5 9.9 %collective-permute-start.9 = (f16[24,1152]{1,0:T(8,128)(2,1)S(1)}, f16[24,1152]{1,0:T(8,128)(2,1)S(1)}, u32[]{:S(2)}, u32[]{:S(2)}) collective-permute-start(f16[24,1152]{1,0:T(8,128)(2,1)S(1)} %fusion.2), channel_id=1, source_target_pairs={{0,1},{1,0},{2,3},{3,2},{4,5},{5,4},{6,7},{7,6},{8,9},{9,8},{10,11... | collective-permute-start | bytes 165896 | tf_op jit(solution)/shard_map/ppermute | solution.py:181
  116.3 0.6 fusion.4
  117.0 1.3 broadcast_in_dim.10
  118.3 7.7 %all-to-all-start.2 = ((f32[32,8,128]{2,1,0:T(8,128)}), f32[32,8,128]{2,1,0:T(8,128)S(1)}, u32[]{:S(2)}, u32[]{:S(2)}) async-start(f32[32,8,128]{2,1,0:T(8,128)} %broadcast_in_dim.10), calls=%async_computation.2 | async-start | bytes 262144 | tf_op jit(solution)/shard_map/all_to_all | solution.py:219
  126.0 0.0 collective-permute-done.8
  126.0 0.7 slice_add_fusion.3.image_sum_ref
  126.7 0.0 collective-permute-done.9
  126.7 0.7 slice_add_fusion.2.text_sum_ref
  127.4 2.1 %shard_map.69 = (f32[24,1152]{1,0:T(8,128)}, f32[24,1152]{1,0:T(8,128)}) custom-call(f32[1]{0:T(128)S(6)} %copy.12.heat_ref, f32[1]{0:T(128)S(6)} %copy.13.offset_ref, f32[24,1152]{1,0:T(8,128)} %picture_ref.3, f32[24,1152]{1,0:T(8,128)} %caption_ref.3, f32[24,1152]{1,0:T(8,128)} %slice_add_fusion.3.image_sum_ref, f32[24,1152]{1,0:T(8,128)} %slice_add_fusion.2.text_sum_ref), custom_call_target="tpu_custom_call" | custom-call | tf_op jit(solution)/shard_map/pallas_call | solution.py:173
  129.4 11.3 %all-to-all-done.2 = f32[32,8,128]{2,1,0:T(8,128)S(1)} async-done(((f32[32,8,128]{2,1,0:T(8,128)}), f32[32,8,128]{2,1,0:T(8,128)S(1)}, u32[]{:S(2)}, u32[]{:S(2)}) %all-to-all-start.2) | async-done | bytes 131104 | tf_op jit(solution)/shard_map/all_to_all | solution.py:219
  140.7 0.6 slice_reduce_fusion
  (11 shorter events, 0.2 us)
Async XLA Ops:
  3.7 20.3 %collective-permute-start.4 = (bf16[24,1152]{1,0:T(8,128)(2,1)}, bf16[24,1152]{1,0:T(8,128)(2,1)S(1)}, u32[]{:S(2)}, u32[]{:S(2)}) collective-permute-start(bf16[24,1152]{1,0:T(8,128)(2,1)} %get-tuple-element.13), channel_id=1, source_target_pairs={{0,1},{1,0},{2,3},{3,2},{4,5},{5,4},{6,7},{7,6},{8,9},{9,8},{10,11... | collective-permute-start | bytes 165896 | tf_op jit(solution)/shard_map/ppermute | solution.py:181
  20.0 13.1 %collective-permute-start = (bf16[24,1152]{1,0:T(8,128)(2,1)}, bf16[24,1152]{1,0:T(8,128)(2,1)S(1)}, u32[]{:S(2)}, u32[]{:S(2)}) collective-permute-start(bf16[24,1152]{1,0:T(8,128)(2,1)} %get-tuple-element.12), channel_id=1, source_target_pairs={{0,256},{64,320},{128,384},{192,448},{256,0},{320,64},{384,128},{4... | collective-permute-start | bytes 165896 | tf_op jit(solution)/shard_map/ppermute | solution.py:181
  26.2 6.9 %copy-start.1 = (bf16[24,1152]{1,0:T(8,128)(2,1)S(1)}, bf16[24,1152]{1,0:T(8,128)(2,1)}, u32[]{:S(2)}) copy-start(bf16[24,1152]{1,0:T(8,128)(2,1)} %get-tuple-element.12) | copy-start | bytes 165892
  26.2 29.4 %copy-start = (f32[24,1]{1,0:T(8,128)S(1)}, f32[24,1]{1,0:T(8,128)}, u32[]{:S(2)}) copy-start(f32[24,1]{1,0:T(8,128)} %get-tuple-element.11.own_loss_ref) | copy-start | bytes 292
  26.2 29.4 %all-to-all-start = ((bf16[16,48,1152]{2,1,0:T(8,128)(2,1)}), bf16[16,48,1152]{2,1,0:T(8,128)(2,1)S(1)}, u32[]{:S(2)}, u32[]{:S(2)}) async-start(bf16[16,48,1152]{2,1,0:T(8,128)(2,1)} %broadcast_in_dim.4), calls=%async_computation | async-start | bytes 3538944 | tf_op jit(solution)/shard_map/all_to_all | solution.py:201
  33.1 9.4 %collective-permute-start.1 = (bf16[48,1152]{1,0:T(8,128)(2,1)S(1)}, bf16[48,1152]{1,0:T(8,128)(2,1)S(1)}, u32[]{:S(2)}, u32[]{:S(2)}) collective-permute-start(bf16[48,1152]{1,0:T(8,128)(2,1)S(1)} %pad_maximum_fusion.1), channel_id=1, source_target_pairs={{0,128},{64,192},{128,0},{192,64},{256,384},{320,448},{384,256},{4... | collective-permute-start | bytes 331784 | tf_op jit(solution)/shard_map/ppermute | solution.py:181
  42.5 7.6 %collective-permute-start.2 = (bf16[96,1152]{1,0:T(8,128)(2,1)S(1)}, bf16[96,1152]{1,0:T(8,128)(2,1)S(1)}, u32[]{:S(2)}, u32[]{:S(2)}) collective-permute-start(bf16[96,1152]{1,0:T(8,128)(2,1)S(1)} %pad_maximum_fusion), channel_id=1, source_target_pairs={{0,64},{64,0},{128,192},{192,128},{256,320},{320,256},{384,448},{4... | collective-permute-start | bytes 663560 | tf_op jit(solution)/shard_map/ppermute | solution.py:181
  50.1 5.5 %collective-permute-start.3 = (bf16[192,1152]{1,0:T(8,128)(2,1)S(1)}, bf16[192,1152]{1,0:T(8,128)(2,1)S(1)}, u32[]{:S(2)}, u32[]{:S(2)}) collective-permute-start(bf16[192,1152]{1,0:T(8,128)(2,1)S(1)} %constant_dynamic-update-slice_fusion.near_ref), channel_id=1, source_target_pairs={{0,8},{8,0},{1,9},{9,1},{2,10},{10,2},{3,11},{11,3},{4,12},{12,4},... | collective-permute-start | bytes 1327112 | tf_op jit(solution)/shard_map/ppermute | solution.py:181
  63.7 8.4 %collective-permute-start.5 = (f32[192,1152]{1,0:T(8,128)S(1)}, f32[192,1152]{1,0:T(8,128)S(1)}, u32[]{:S(2)}, u32[]{:S(2)}) collective-permute-start(f32[192,1152]{1,0:T(8,128)S(1)} %get-tuple-element.16), channel_id=1, source_target_pairs={{0,8},{8,0},{1,9},{9,1},{2,10},{10,2},{3,11},{11,3},{4,12},{12,4},... | collective-permute-start | bytes 2654216 | tf_op jit(solution)/shard_map/ppermute | solution.py:181
  72.2 8.5 %collective-permute-start.6 = (f16[96,1152]{1,0:T(8,128)(2,1)S(1)}, f16[96,1152]{1,0:T(8,128)(2,1)S(1)}, u32[]{:S(2)}, u32[]{:S(2)}) collective-permute-start(f16[96,1152]{1,0:T(8,128)(2,1)S(1)} %fusion), channel_id=1, source_target_pairs={{0,64},{64,0},{128,192},{192,128},{256,320},{320,256},{384,448},{4... | collective-permute-start | bytes 663560 | tf_op jit(solution)/shard_map/ppermute | solution.py:181
  74.8 31.4 %all-to-all-start.1 = ((bf16[16,48,1280]{2,1,0:T(8,128)(2,1)}), bf16[16,48,1280]{2,1,0:T(8,128)(2,1)S(1)}, u32[]{:S(2)}, u32[]{:S(2)}) async-start(bf16[16,48,1280]{2,1,0:T(8,128)(2,1)} %bitcast.5), calls=%async_computation.1 | async-start | bytes 3932160 | tf_op jit(solution)/shard_map/all_to_all | solution.py:212
  80.8 9.6 %collective-permute-start.7 = (f16[48,1152]{1,0:T(8,128)(2,1)S(1)}, f16[48,1152]{1,0:T(8,128)(2,1)S(1)}, u32[]{:S(2)}, u32[]{:S(2)}) collective-permute-start(f16[48,1152]{1,0:T(8,128)(2,1)S(1)} %fusion.1), channel_id=1, source_target_pairs={{0,128},{64,192},{128,0},{192,64},{256,384},{320,448},{384,256},{4... | collective-permute-start | bytes 331784 | tf_op jit(solution)/shard_map/ppermute | solution.py:181
  90.5 35.5 %collective-permute-start.8 = (f16[24,1152]{1,0:T(8,128)(2,1)S(1)}, f16[24,1152]{1,0:T(8,128)(2,1)S(1)}, u32[]{:S(2)}, u32[]{:S(2)}) collective-permute-start(f16[24,1152]{1,0:T(8,128)(2,1)S(1)} %fusion.3), channel_id=1, source_target_pairs={{0,256},{64,320},{128,384},{192,448},{256,0},{320,64},{384,128},{4... | collective-permute-start | bytes 165896 | tf_op jit(solution)/shard_map/ppermute | solution.py:181
  106.5 20.2 %collective-permute-start.9 = (f16[24,1152]{1,0:T(8,128)(2,1)S(1)}, f16[24,1152]{1,0:T(8,128)(2,1)S(1)}, u32[]{:S(2)}, u32[]{:S(2)}) collective-permute-start(f16[24,1152]{1,0:T(8,128)(2,1)S(1)} %fusion.2), channel_id=1, source_target_pairs={{0,1},{1,0},{2,3},{3,2},{4,5},{5,4},{6,7},{7,6},{8,9},{9,8},{10,11... | collective-permute-start | bytes 165896 | tf_op jit(solution)/shard_map/ppermute | solution.py:181
  118.3 22.5 %all-to-all-start.2 = ((f32[32,8,128]{2,1,0:T(8,128)}), f32[32,8,128]{2,1,0:T(8,128)S(1)}, u32[]{:S(2)}, u32[]{:S(2)}) async-start(f32[32,8,128]{2,1,0:T(8,128)} %broadcast_in_dim.10), calls=%async_computation.2 | async-start | bytes 262144 | tf_op jit(solution)/shard_map/all_to_all | solution.py:219

commit v3 on v2

v3 whole, which is shorter than its diff:
```python
import jax
import jax.numpy as jnp
from jax import lax
from jax.experimental import pallas as pl
from jax.experimental.pallas import tpu as pltpu
from jax.sharding import Mesh, PartitionSpec as P

epsilon = 1e-06
AXES = ("zl", "x", "c", "y", "zh")
SIZES = (8, 4, 2, 4, 2)
PLANE = ("x", "y")
COLUMN = ("zl", "c", "zh")
LANES = 128
LIMIT = 20 * 1024 * 1024
HALF = 0.5


def normalize(raw_rows):
    row_norm = jnp.sqrt(jnp.sum(raw_rows * raw_rows, axis=1, keepdims=True) + epsilon)
    return (raw_rows / row_norm, row_norm)


def back_norm(unit_rows, row_norm, gradient):
    return (gradient - unit_rows * jnp.sum(unit_rows * gradient, axis=1, keepdims=True)) / row_norm


def low(rows):
    return rows.astype(jnp.bfloat16).astype(jnp.float32)


def loss_and_sigmoid(values):
    small = jnp.exp(-jnp.abs(values))
    loss = jnp.maximum(values, 0.0) + jnp.log1p(small)
    return loss, jnp.where(values >= 0, 1.0, small) / (1.0 + small)


def own_pairs(image_low, text_low, heat, offset):
    return jnp.sum(image_low * text_low, axis=1, keepdims=True) * heat + offset


def unit_kernel(heat_ref, offset_ref, picture_ref, caption_ref, image_ref, text_ref, loss_ref):
    image_unit, _ = normalize(picture_ref[...])
    text_unit, _ = normalize(caption_ref[...])
    image_low, text_low = image_unit.astype(jnp.bfloat16), text_unit.astype(jnp.bfloat16)
    image_ref[...] = image_low
    text_ref[...] = text_low
    heat = jnp.exp(jnp.full((1, 1), heat_ref[0], jnp.float32))
    logits = own_pairs(image_low.astype(jnp.float32), text_low.astype(jnp.float32), heat, offset_ref[0])
    loss, _ = loss_and_sigmoid(-logits)
    loss_ref[...] = loss


def unit_rows(heat_exponent, offset_added, pictures, captions):
    rows = pictures.shape[0]
    return pl.pallas_call(
        unit_kernel,
        in_specs=[pl.BlockSpec(memory_space=pltpu.SMEM)] * 2 + [pl.BlockSpec(memory_space=pltpu.VMEM)] * 2,
        out_shape=[
            jax.ShapeDtypeStruct(pictures.shape, jnp.bfloat16),
            jax.ShapeDtypeStruct(captions.shape, jnp.bfloat16),
            jax.ShapeDtypeStruct((rows, 1), jnp.float32),
        ],
    )(heat_exponent, offset_added, pictures, captions)


def pieces(total, shape):
    first = low(total)
    second = low(total - first)
    third = total - first - second
    lane = lax.broadcasted_iota(jnp.int32, shape, len(shape) - 1)
    spread = jnp.where(lane == 0, first, jnp.where(lane == 1, second, jnp.where(lane == 2, third, 0.0)))
    return spread.astype(jnp.bfloat16)


def pair_kernel(
    place_ref, heat_ref, offset_ref, own_loss_ref, near_ref, far_ref, own_ref, other_ref,
    near_out_ref, far_out_ref, own_out_ref, other_out_ref, loss_ref,
):
    rows = own_loss_ref.shape[0]
    heat = jnp.exp(jnp.full((1, 1), heat_ref[0], jnp.float32))
    total = jnp.sum(own_loss_ref[...], axis=0, keepdims=True)
    for text_ref, text_out_ref in ((own_ref, own_out_ref), (other_ref, other_out_ref)):
        texts = text_ref[...]
        text_part = None
        for image_ref, image_out_ref in ((near_ref, near_out_ref), (far_ref, far_out_ref)):
            images = image_ref[...]
            logits = lax.dot_general(
                images, texts, (((1,), (1,)), ((), ())), preferred_element_type=jnp.float32
            )
            logits = logits * heat + offset_ref[0]
            loss, sigmoid = loss_and_sigmoid(logits)
            weights = heat * sigmoid
            if image_ref is near_ref and text_ref is own_ref:
                image_row = lax.broadcasted_iota(jnp.int32, logits.shape, 0)
                text_row = lax.broadcasted_iota(jnp.int32, logits.shape, 1) - place_ref[0]
                match = (image_row == text_row) & (image_row < rows)
                weights = jnp.where(match, 0.0, weights)
                loss = jnp.where(match, 0.0, loss)
            weights = weights.astype(jnp.bfloat16)
            total += jnp.sum(jnp.sum(loss, axis=0, keepdims=True), axis=1, keepdims=True)
            image_part = jnp.dot(weights, texts, preferred_element_type=jnp.float32)
            part = lax.dot_general(
                weights, images, (((0,), (0,)), ((), ())), preferred_element_type=jnp.float32
            )
            text_part = part if text_part is None else text_part + part
            if text_ref is own_ref:
                image_out_ref[...] = image_part
            else:
                image_out_ref[...] += image_part
        text_out_ref[...] = text_part.astype(jnp.bfloat16)
    loss_ref[...] = jnp.broadcast_to(total, loss_ref.shape)


def pair_terms(place, heat_exponent, offset_added, own_loss, near, far, own, other):
    half, width = near.shape
    count = own.shape[0]
    return pl.pallas_call(
        pair_kernel,
        in_specs=[pl.BlockSpec(memory_space=pltpu.SMEM)] * 3 + [pl.BlockSpec(memory_space=pltpu.VMEM)] * 5,
        out_shape=[
            jax.ShapeDtypeStruct((half, width), jnp.float32),
            jax.ShapeDtypeStruct((half, width), jnp.float32),
            jax.ShapeDtypeStruct((count, width), jnp.bfloat16),
            jax.ShapeDtypeStruct((count, width), jnp.bfloat16),
            jax.ShapeDtypeStruct((8, LANES), jnp.float32),
        ],
        compiler_params=pltpu.CompilerParams(vmem_limit_bytes=LIMIT),
        cost_estimate=pl.CostEstimate(
            flops=24 * half * count * width, bytes_accessed=24 * half * width, transcendentals=12 * half * count
        ),
    )(place, heat_exponent, offset_added, own_loss, near, far, own, other)


def grad_kernel(heat_ref, offset_ref, picture_ref, caption_ref, image_sum_ref, text_sum_ref, image_ref, text_ref):
    image_unit, image_norm = normalize(picture_ref[...])
    text_unit, text_norm = normalize(caption_ref[...])
    image_low, text_low = low(image_unit), low(text_unit)
    heat = jnp.exp(jnp.full((1, 1), heat_ref[0], jnp.float32))
    _, sigmoid = loss_and_sigmoid(-own_pairs(image_low, text_low, heat, offset_ref[0]))
    weights = low(-sigmoid * heat)
    image_ref[...] = back_norm(image_unit, image_norm, image_sum_ref[...] + weights * text_low)
    text_ref[...] = back_norm(text_unit, text_norm, text_sum_ref[...] + weights * image_low)


def gradients(heat_exponent, offset_added, pictures, captions, image_sum, text_sum):
    return pl.pallas_call(
        grad_kernel,
        in_specs=[pl.BlockSpec(memory_space=pltpu.SMEM)] * 2 + [pl.BlockSpec(memory_space=pltpu.VMEM)] * 4,
        out_shape=[jax.ShapeDtypeStruct(pictures.shape, jnp.float32)] * 2,
    )(heat_exponent, offset_added, pictures, captions, image_sum, text_sum)


def swapped(value, axis, step):
    return lax.ppermute(value, axis, [(i, i ^ step) for i in range(lax.axis_size(axis))])


def doubled(value, axis, step):
    return jnp.concatenate([value, swapped(value, axis, step)], axis=0)


def halved(value, axis, step):
    half = value.shape[0] // 2
    sent = (value[half:] * HALF).astype(jnp.float16)
    return value[:half] + swapped(sent, axis, step).astype(jnp.float32) * (1 / HALF)


def gathered(block, axes):
    count = lax.axis_size(axes)
    parts = lax.all_to_all(jnp.broadcast_to(block[None], (count, *block.shape)), axes, 0, 0)
    return parts.reshape(count * block.shape[0], *block.shape[1:])


def shards(picture_vectors, caption_vectors, heat_exponent, offset_added):
    rows, width = picture_vectors.shape
    plane, column = lax.axis_size(PLANE), lax.axis_size(COLUMN)
    steps = [1 << bit for bit in range(lax.axis_size("zl").bit_length() - 1)]
    image_low, text_low, own_loss = unit_rows(heat_exponent, offset_added, picture_vectors, caption_vectors)

    own = gathered(text_low, PLANE)
    other = gathered(swapped(text_low, "zh", 1), PLANE)
    near = image_low
    for step in reversed(steps):
        near = doubled(near, "zl", step)
    far = swapped(near, "c", 1)

    place = (lax.axis_index(PLANE) * rows).astype(jnp.int32).reshape(1)
    near_part, far_part, own_part, other_part, loss = pair_terms(
        place, heat_exponent, offset_added, own_loss, near, far, own, other
    )

    other_parts = lax.all_to_all(other_part.reshape(plane, rows, width), PLANE, 0, 0)
    losses = lax.all_to_all(jnp.broadcast_to(loss[None], (column, *loss.shape)), COLUMN, 0, 0)
    column_loss = pieces(jnp.sum(losses[:, 0, 0]), (plane, rows, LANES))
    own_parts = lax.all_to_all(
        jnp.concatenate([own_part.reshape(plane, rows, width), column_loss], axis=2), PLANE, 0, 0
    )
    image_sum = near_part + swapped(far_part, "c", 1)
    for step in steps:
        image_sum = halved(image_sum, "zl", step)
    other_sum = jnp.sum(other_parts.astype(jnp.float32), axis=0)
    own_sum = jnp.sum(own_parts[:, :, :width].astype(jnp.float32), axis=0)
    text_sum = halved(jnp.concatenate([own_sum, other_sum], axis=0), "zh", 1)

    total_loss = jnp.sum(own_parts[:, 0, width : width + 3].astype(jnp.float32))
    loss_mean = (total_loss / (rows * lax.axis_size(AXES))).reshape(1)
    image_grads, text_grads = gradients(
        heat_exponent, offset_added, picture_vectors, caption_vectors, image_sum, text_sum
    )
    return (loss_mean, image_grads, text_grads)


def solution(mesh):
    fine = Mesh(mesh.devices.reshape(SIZES), AXES)
    in_specs = (P(AXES, None), P(AXES, None), P(), P())
    out_specs = (P(), P(AXES, None), P(AXES, None))
    return jax.shard_map(shards, mesh=fine, in_specs=in_specs, out_specs=out_specs, check_vma=False)
```

time: 144 us -> 150 us (1.042)
  the two profiles are of different devices: /device:TPU:1 before, /device:TPU:2 now
where the time goes in v3:
time: 150 us; the launch traced here: 148 us
  starting transfers between devices  81.3 us (54%)
  waiting for transfers between devices  38.6 us (26%)
  Pallas kernels  9.24 us (6%)
  local copies, waits for them, and re-layouts  8.77 us (6%)
  between operations  5.28 us (4%)
  other arithmetic  5.17 us (3%)
    ppermute x10, starting transfers between devices, swapped(): lax.ppermute(value, axis, [(i, i ^ step) for i in range(lax.axis_size(axi...  48.3 us
    ppermute x10, waiting for transfers between devices, swapped(): lax.ppermute(value, axis, [(i, i ^ step) for i in range(lax.axis_size(axi...  15.7 us
    all_to_all x1, waiting for transfers between devices, shards(): lax.all_to_all(jnp.broadcast_to(loss[None], (column, *loss.shape)), COLUM...  14 us
    all_to_all x2, starting transfers between devices, gathered(): lax.all_to_all(jnp.broadcast_to(block[None], (count, *block.shape)), axes...  13.3 us
    all_to_all x2, waiting for transfers between devices, gathered(): lax.all_to_all(jnp.broadcast_to(block[None], (count, *block.shape)), axes...  8.87 us
    all_to_all x1, starting transfers between devices, shards(): lax.all_to_all(jnp.concatenate([own_part.reshape(plane, rows, width), col...  7.28 us
    all_to_all x1, starting transfers between devices, shards(): lax.all_to_all(jnp.broadcast_to(loss[None], (column, *loss.shape)), COLUM...  6.56 us
    all_to_all x1, starting transfers between devices, shards(): lax.all_to_all(other_part.reshape(plane, rows, width), PLANE, 0, 0)  5.87 us
  transfers between devices with their start and end apart: 15, of which 7 were waited for; matrix products, arithmetic and copies ran while one was open for 5% of the time, Pallas kernels for 0%

profile of v3, /device:TPU:2, one launch (start us, length us, event | category | flops | bytes accessed | tf_op | source)
XLA Modules:
  0.0 148.4 jit_solution(973752986108183545)
XLA Ops:
  1.9 1.8 %shard_map.67 = (bf16[24,1152]{1,0:T(8,128)(2,1)}, bf16[24,1152]{1,0:T(8,128)(2,1)}, f32[24,1]{1,0:T(8,128)}) custom-call(f32[1]{0:T(128)S(6)} %copy.12.heat_ref, f32[1]{0:T(128)S(6)} %copy.13.offset_ref, f32[24,1152]{1,0:T(8,128)} %picture_ref.3, f32[24,1152]{1,0:T(8,128)} %caption_ref.3), custom_call_target="tpu_custom_call" | custom-call | tf_op jit(solution)/shard_map/pallas_call | solution.py:55
  3.7 9.1 %collective-permute-start = (bf16[24,1152]{1,0:T(8,128)(2,1)}, bf16[24,1152]{1,0:T(8,128)(2,1)S(1)}, u32[]{:S(2)}, u32[]{:S(2)}) collective-permute-start(bf16[24,1152]{1,0:T(8,128)(2,1)} %get-tuple-element.14), channel_id=1, source_target_pairs={{0,256},{64,320},{128,384},{192,448},{256,0},{320,64},{384,128},{4... | collective-permute-start | bytes 165896 | tf_op jit(solution)/shard_map/ppermute | solution.py:154
  12.8 10.9 %collective-permute-start.4 = (bf16[24,1152]{1,0:T(8,128)(2,1)}, bf16[24,1152]{1,0:T(8,128)(2,1)S(1)}, u32[]{:S(2)}, u32[]{:S(2)}) collective-permute-start(bf16[24,1152]{1,0:T(8,128)(2,1)} %get-tuple-element.15), channel_id=1, source_target_pairs={{0,1},{1,0},{2,3},{3,2},{4,5},{5,4},{6,7},{7,6},{8,9},{9,8},{10,11... | collective-permute-start | bytes 165896 | tf_op jit(solution)/shard_map/ppermute | solution.py:154
  23.7 1.8 %broadcast_in_dim.33 = bf16[16,24,1152]{2,1,0:T(8,128)(2,1)} broadcast(bf16[24,1152]{1,0:T(8,128)(2,1)} %get-tuple-element.15), dimensions={1,2} | broadcast | bytes 940032 | tf_op jit(solution)/shard_map/broadcast_in_dim | solution.py:169
  25.5 0.0 copy-start.6
  25.5 7.6 %all-to-all-start = ((bf16[16,24,1152]{2,1,0:T(8,128)(2,1)}), bf16[16,24,1152]{2,1,0:T(8,128)(2,1)S(1)}, u32[]{:S(2)}, u32[]{:S(2)}) async-start(bf16[16,24,1152]{2,1,0:T(8,128)(2,1)} %broadcast_in_dim.33), calls=%async_computation | async-start | bytes 1769472 | tf_op jit(solution)/shard_map/all_to_all | solution.py:169
  33.1 0.0 copy-done.6
  33.2 0.0 collective-permute-done
  33.2 3.4 %collective-permute-start.1 = (bf16[48,1152]{1,0:T(8,128)(2,1)S(1)}, bf16[48,1152]{1,0:T(8,128)(2,1)S(1)}, u32[]{:S(2)}, u32[]{:S(2)}) collective-permute-start(bf16[48,1152]{1,0:T(8,128)(2,1)S(1)} %pad_maximum_fusion.2), channel_id=1, source_target_pairs={{0,128},{64,192},{128,0},{192,64},{256,384},{320,448},{384,256},{4... | collective-permute-start | bytes 331784 | tf_op jit(solution)/shard_map/ppermute | solution.py:154
  36.6 5.4 %collective-permute-done.1 = bf16[48,1152]{1,0:T(8,128)(2,1)S(1)} collective-permute-done((bf16[48,1152]{1,0:T(8,128)(2,1)S(1)}, bf16[48,1152]{1,0:T(8,128)(2,1)S(1)}, u32[]{:S(2)}, u32[]{:S(2)}) %collective-permute-start.1) | collective-permute-done | bytes 110624 | tf_op jit(solution)/shard_map/ppermute | solution.py:154
  42.0 1.9 %collective-permute-start.2 = (bf16[96,1152]{1,0:T(8,128)(2,1)S(1)}, bf16[96,1152]{1,0:T(8,128)(2,1)S(1)}, u32[]{:S(2)}, u32[]{:S(2)}) collective-permute-start(bf16[96,1152]{1,0:T(8,128)(2,1)S(1)} %pad_maximum_fusion.1), channel_id=1, source_target_pairs={{0,64},{64,0},{128,192},{192,128},{256,320},{320,256},{384,448},{4... | collective-permute-start | bytes 663560 | tf_op jit(solution)/shard_map/ppermute | solution.py:154
  44.0 0.0 collective-permute-done.4
  44.0 1.9 %all-to-all-done = bf16[16,24,1152]{2,1,0:T(8,128)(2,1)S(1)} async-done(((bf16[16,24,1152]{2,1,0:T(8,128)(2,1)}), bf16[16,24,1152]{2,1,0:T(8,128)(2,1)S(1)}, u32[]{:S(2)}, u32[]{:S(2)}) %all-to-all-start) | async-done | bytes 884768 | tf_op jit(solution)/shard_map/all_to_all | solution.py:169
  45.9 1.0 broadcast_in_dim.34
  46.9 0.0 copy-start.5
  46.9 5.7 %all-to-all-start.1 = ((bf16[16,24,1152]{2,1,0:T(8,128)(2,1)}), bf16[16,24,1152]{2,1,0:T(8,128)(2,1)S(1)}, u32[]{:S(2)}, u32[]{:S(2)}) async-start(bf16[16,24,1152]{2,1,0:T(8,128)(2,1)} %broadcast_in_dim.34), calls=%async_computation.1 | async-start | bytes 1769472 | tf_op jit(solution)/shard_map/all_to_all | solution.py:169
  52.6 0.0 collective-permute-done.2
  52.7 1.9 %collective-permute-start.3 = (bf16[192,1152]{1,0:T(8,128)(2,1)S(1)}, bf16[192,1152]{1,0:T(8,128)(2,1)S(1)}, u32[]{:S(2)}, u32[]{:S(2)}) collective-permute-start(bf16[192,1152]{1,0:T(8,128)(2,1)S(1)} %constant_dynamic-update-slice_fusion.near_ref), channel_id=1, source_target_pairs={{0,8},{8,0},{1,9},{9,1},{2,10},{10,2},{3,11},{11,3},{4,12},{12,4},... | collective-permute-start | bytes 1327112 | tf_op jit(solution)/shard_map/ppermute | solution.py:154
  54.6 0.0 copy-start
  54.6 0.8 copy-done
  55.4 1.0 collective-permute-done.3.far_ref
  56.4 0.0 copy-start.3
  56.4 0.8 copy-done.3
  57.1 7.0 %all-to-all-done.1 = bf16[16,24,1152]{2,1,0:T(8,128)(2,1)S(1)} async-done(((bf16[16,24,1152]{2,1,0:T(8,128)(2,1)}), bf16[16,24,1152]{2,1,0:T(8,128)(2,1)S(1)}, u32[]{:S(2)}, u32[]{:S(2)}) %all-to-all-start.1) | async-done | bytes 884768 | tf_op jit(solution)/shard_map/all_to_all | solution.py:169
  64.1 0.0 copy-done.5
  64.1 0.0 copy-start.1
  64.1 1.0 copy-done.1
  65.1 0.0 copy-start.4
  65.1 1.0 copy-done.4
  66.2 5.4 %shard_map.68 = (f32[192,1152]{1,0:T(8,128)S(1)}, f32[192,1152]{1,0:T(8,128)S(1)}, bf16[384,1152]{1,0:T(8,128)(2,1)S(1)}, bf16[384,1152]{1,0:T(8,128)(2,1)}, f32[8,128]{1,0:T(8,128)S(1)}) custom-call(s32[1]{0:T(128)} %bitcast.place_ref, f32[1]{0:T(128)S(6)} %copy.12.heat_ref, f32[1]{0:T(128)S(6)} %copy.13.offset_ref, f32[24,1]{1,0:T(8,128)S(1)} %copy-done.5, ...), custom_call_target="tpu_custom_call" | custom-call | flops 2038431744 | bytes 5308416 | tf_op jit(solution)/shard_map/pallas_call | solution.py:117
  71.6 0.0 copy-start.2
  71.6 1.0 copy-done.2
  72.5 0.7 broadcast_in_dim.35
  73.2 6.6 %all-to-all-start.2 = ((f32[32,8,128]{2,1,0:T(8,128)}), f32[32,8,128]{2,1,0:T(8,128)S(1)}, u32[]{:S(2)}, u32[]{:S(2)}) async-start(f32[32,8,128]{2,1,0:T(8,128)} %broadcast_in_dim.35), calls=%async_computation.2 | async-start | bytes 262144 | tf_op jit(solution)/shard_map/all_to_all | solution.py:192
  79.8 2.2 %collective-permute-start.5 = (f32[192,1152]{1,0:T(8,128)}, f32[192,1152]{1,0:T(8,128)S(1)}, u32[]{:S(2)}, u32[]{:S(2)}) collective-permute-start(f32[192,1152]{1,0:T(8,128)} %copy-done.2), channel_id=1, source_target_pairs={{0,8},{8,0},{1,9},{9,1},{2,10},{10,2},{3,11},{11,3},{4,12},{12,4},... | collective-permute-start | bytes 2654216 | tf_op jit(solution)/shard_map/ppermute | solution.py:154
  82.0 14.0 %all-to-all-done.2 = f32[32,8,128]{2,1,0:T(8,128)S(1)} async-done(((f32[32,8,128]{2,1,0:T(8,128)}), f32[32,8,128]{2,1,0:T(8,128)S(1)}, u32[]{:S(2)}, u32[]{:S(2)}) %all-to-all-start.2) | async-done | bytes 131104 | tf_op jit(solution)/shard_map/all_to_all | solution.py:192
  96.0 0.0 copy-start.7
  96.0 0.7 copy-done.7
  96.7 5.9 %all-to-all-start.4 = ((bf16[16,24,1152]{2,1,0:T(8,128)(2,1)}), bf16[16,24,1152]{2,1,0:T(8,128)(2,1)S(1)}, u32[]{:S(2)}, u32[]{:S(2)}) async-start(bf16[16,24,1152]{2,1,0:T(8,128)(2,1)} %bitcast.5), calls=%async_computation.4 | async-start | bytes 1769472 | tf_op jit(solution)/shard_map/all_to_all | solution.py:191
  102.6 1.5 %slice_reduce_fusion = f32[]{:T(128)} fusion(f32[32,8,128]{2,1,0:T(8,128)} %copy-done.7), kind=kLoop, calls=%fused_computation.17 | loop fusion | flops 31 | bytes 132 | tf_op jit(solution)/shard_map/reduce_sum | solution.py:193
  105.5 0.0 collective-permute-done.5
  105.5 0.1 add.19
  105.6 3.1 %collective-permute-start.6 = (f16[96,1152]{1,0:T(8,128)(2,1)S(1)}, f16[96,1152]{1,0:T(8,128)(2,1)S(1)}, u32[]{:S(2)}, u32[]{:S(2)}) collective-permute-start(f16[96,1152]{1,0:T(8,128)(2,1)S(1)} %fusion), channel_id=1, source_target_pairs={{0,64},{64,0},{128,192},{192,128},{256,320},{320,256},{384,448},{4... | collective-permute-start | bytes 663560 | tf_op jit(solution)/shard_map/ppermute | solution.py:154
  108.8 1.1 pad_maximum_fusion
  109.9 3.7 %collective-permute-done.6 = f16[96,1152]{1,0:T(8,128)(2,1)S(1)} collective-permute-done((f16[96,1152]{1,0:T(8,128)(2,1)S(1)}, f16[96,1152]{1,0:T(8,128)(2,1)S(1)}, u32[]{:S(2)}, u32[]{:S(2)}) %collective-permute-start.6) | collective-permute-done | bytes 221216 | tf_op jit(solution)/shard_map/ppermute | solution.py:154
  113.6 0.1 slice_add_fusion
  113.7 3.8 %collective-permute-start.7 = (f16[48,1152]{1,0:T(8,128)(2,1)S(1)}, f16[48,1152]{1,0:T(8,128)(2,1)S(1)}, u32[]{:S(2)}, u32[]{:S(2)}) collective-permute-start(f16[48,1152]{1,0:T(8,128)(2,1)S(1)} %fusion.1), channel_id=1, source_target_pairs={{0,128},{64,192},{128,0},{192,64},{256,384},{320,448},{384,256},{4... | collective-permute-start | bytes 331784 | tf_op jit(solution)/shard_map/ppermute | solution.py:154
  117.5 0.0 all-to-all-done.4
  117.6 7.3 %all-to-all-start.3 = ((bf16[16,24,1280]{2,1,0:T(8,128)(2,1)}), bf16[16,24,1280]{2,1,0:T(8,128)(2,1)S(1)}, u32[]{:S(2)}, u32[]{:S(2)}) async-start(bf16[16,24,1280]{2,1,0:T(8,128)(2,1)} %pad_maximum_fusion), calls=%async_computation.3 | async-start | bytes 1966080 | tf_op jit(solution)/shard_map/all_to_all | solution.py:194
  124.8 0.1 convert_reduce_fusion
  125.0 0.0 collective-permute-done.7
  125.0 3.0 %collective-permute-start.8 = (f16[24,1152]{1,0:T(8,128)(2,1)S(1)}, f16[24,1152]{1,0:T(8,128)(2,1)S(1)}, u32[]{:S(2)}, u32[]{:S(2)}) collective-permute-start(f16[24,1152]{1,0:T(8,128)(2,1)S(1)} %fusion.2), channel_id=1, source_target_pairs={{0,256},{64,320},{128,384},{192,448},{256,0},{320,64},{384,128},{4... | collective-permute-start | bytes 165896 | tf_op jit(solution)/shard_map/ppermute | solution.py:154
  128.0 8.9 %collective-permute-start.9 = (f16[24,1152]{1,0:T(8,128)(2,1)S(1)}, f16[24,1152]{1,0:T(8,128)(2,1)S(1)}, u32[]{:S(2)}, u32[]{:S(2)}) collective-permute-start(f16[24,1152]{1,0:T(8,128)(2,1)S(1)} %multiply_convert_fusion), channel_id=1, source_target_pairs={{0,1},{1,0},{2,3},{3,2},{4,5},{5,4},{6,7},{7,6},{8,9},{9,8},{10,11... | collective-permute-start | bytes 165896 | tf_op jit(solution)/shard_map/ppermute | solution.py:154
  137.0 0.0 collective-permute-done.8
  137.0 0.7 slice_add_fusion.2.image_sum_ref
  137.6 0.0 all-to-all-done.3
  137.6 0.1 convert_reduce_fusion.1
  137.8 5.5 %collective-permute-done.9 = f16[24,1152]{1,0:T(8,128)(2,1)S(1)} collective-permute-done((f16[24,1152]{1,0:T(8,128)(2,1)S(1)}, f16[24,1152]{1,0:T(8,128)(2,1)S(1)}, u32[]{:S(2)}, u32[]{:S(2)}) %collective-permute-start.9) | collective-permute-done | bytes 55328 | tf_op jit(solution)/shard_map/ppermute | solution.py:154
  143.2 0.7 multiply_add_fusion.text_sum_ref
  143.9 2.1 %shard_map.69 = (f32[24,1152]{1,0:T(8,128)}, f32[24,1152]{1,0:T(8,128)}) custom-call(f32[1]{0:T(128)S(6)} %copy.12.heat_ref, f32[1]{0:T(128)S(6)} %copy.13.offset_ref, f32[24,1152]{1,0:T(8,128)} %picture_ref.3, f32[24,1152]{1,0:T(8,128)} %caption_ref.3, f32[24,1152]{1,0:T(8,128)} %slice_add_fusion.2.image_sum_ref, f32[24,1152]{1,0:T(8,128)} %multiply_add_fusion.text_sum_ref), custom_call_target="tpu_custom_call" | custom-call | tf_op jit(solution)/shard_map/pallas_call | solution.py:146
  146.0 0.6 fusion.3
  (14 shorter events, 0.2 us)
Async XLA Ops:
  3.7 29.5 %collective-permute-start = (bf16[24,1152]{1,0:T(8,128)(2,1)}, bf16[24,1152]{1,0:T(8,128)(2,1)S(1)}, u32[]{:S(2)}, u32[]{:S(2)}) collective-permute-start(bf16[24,1152]{1,0:T(8,128)(2,1)} %get-tuple-element.14), channel_id=1, source_target_pairs={{0,256},{64,320},{128,384},{192,448},{256,0},{320,64},{384,128},{4... | collective-permute-start | bytes 165896 | tf_op jit(solution)/shard_map/ppermute | solution.py:154
  12.8 31.2 %collective-permute-start.4 = (bf16[24,1152]{1,0:T(8,128)(2,1)}, bf16[24,1152]{1,0:T(8,128)(2,1)S(1)}, u32[]{:S(2)}, u32[]{:S(2)}) collective-permute-start(bf16[24,1152]{1,0:T(8,128)(2,1)} %get-tuple-element.15), channel_id=1, source_target_pairs={{0,1},{1,0},{2,3},{3,2},{4,5},{5,4},{6,7},{7,6},{8,9},{9,8},{10,11... | collective-permute-start | bytes 165896 | tf_op jit(solution)/shard_map/ppermute | solution.py:154
  25.5 7.6 %copy-start.6 = (bf16[24,1152]{1,0:T(8,128)(2,1)S(1)}, bf16[24,1152]{1,0:T(8,128)(2,1)}, u32[]{:S(2)}) copy-start(bf16[24,1152]{1,0:T(8,128)(2,1)} %get-tuple-element.14) | copy-start | bytes 165892
  25.5 20.3 %all-to-all-start = ((bf16[16,24,1152]{2,1,0:T(8,128)(2,1)}), bf16[16,24,1152]{2,1,0:T(8,128)(2,1)S(1)}, u32[]{:S(2)}, u32[]{:S(2)}) async-start(bf16[16,24,1152]{2,1,0:T(8,128)(2,1)} %broadcast_in_dim.33), calls=%async_computation | async-start | bytes 1769472 | tf_op jit(solution)/shard_map/all_to_all | solution.py:169
  33.2 8.8 %collective-permute-start.1 = (bf16[48,1152]{1,0:T(8,128)(2,1)S(1)}, bf16[48,1152]{1,0:T(8,128)(2,1)S(1)}, u32[]{:S(2)}, u32[]{:S(2)}) collective-permute-start(bf16[48,1152]{1,0:T(8,128)(2,1)S(1)} %pad_maximum_fusion.2), channel_id=1, source_target_pairs={{0,128},{64,192},{128,0},{192,64},{256,384},{320,448},{384,256},{4... | collective-permute-start | bytes 331784 | tf_op jit(solution)/shard_map/ppermute | solution.py:154
  42.0 10.6 %collective-permute-start.2 = (bf16[96,1152]{1,0:T(8,128)(2,1)S(1)}, bf16[96,1152]{1,0:T(8,128)(2,1)S(1)}, u32[]{:S(2)}, u32[]{:S(2)}) collective-permute-start(bf16[96,1152]{1,0:T(8,128)(2,1)S(1)} %pad_maximum_fusion.1), channel_id=1, source_target_pairs={{0,64},{64,0},{128,192},{192,128},{256,320},{320,256},{384,448},{4... | collective-permute-start | bytes 663560 | tf_op jit(solution)/shard_map/ppermute | solution.py:154
  46.9 17.2 %copy-start.5 = (f32[24,1]{1,0:T(8,128)S(1)}, f32[24,1]{1,0:T(8,128)}, u32[]{:S(2)}) copy-start(f32[24,1]{1,0:T(8,128)} %get-tuple-element.13.own_loss_ref) | copy-start | bytes 292
  46.9 17.2 %all-to-all-start.1 = ((bf16[16,24,1152]{2,1,0:T(8,128)(2,1)}), bf16[16,24,1152]{2,1,0:T(8,128)(2,1)S(1)}, u32[]{:S(2)}, u32[]{:S(2)}) async-start(bf16[16,24,1152]{2,1,0:T(8,128)(2,1)} %broadcast_in_dim.34), calls=%async_computation.1 | async-start | bytes 1769472 | tf_op jit(solution)/shard_map/all_to_all | solution.py:169
  52.7 3.7 %collective-permute-start.3 = (bf16[192,1152]{1,0:T(8,128)(2,1)S(1)}, bf16[192,1152]{1,0:T(8,128)(2,1)S(1)}, u32[]{:S(2)}, u32[]{:S(2)}) collective-permute-start(bf16[192,1152]{1,0:T(8,128)(2,1)S(1)} %constant_dynamic-update-slice_fusion.near_ref), channel_id=1, source_target_pairs={{0,8},{8,0},{1,9},{9,1},{2,10},{10,2},{3,11},{11,3},{4,12},{12,4},... | collective-permute-start | bytes 1327112 | tf_op jit(solution)/shard_map/ppermute | solution.py:154
  54.6 0.8 copy-start
  56.4 0.8 copy-start.3
  64.1 1.0 copy-start.1
  65.1 1.0 copy-start.4
  71.6 1.0 copy-start.2
  73.2 22.8 %all-to-all-start.2 = ((f32[32,8,128]{2,1,0:T(8,128)}), f32[32,8,128]{2,1,0:T(8,128)S(1)}, u32[]{:S(2)}, u32[]{:S(2)}) async-start(f32[32,8,128]{2,1,0:T(8,128)} %broadcast_in_dim.35), calls=%async_computation.2 | async-start | bytes 262144 | tf_op jit(solution)/shard_map/all_to_all | solution.py:192
  79.8 25.7 %collective-permute-start.5 = (f32[192,1152]{1,0:T(8,128)}, f32[192,1152]{1,0:T(8,128)S(1)}, u32[]{:S(2)}, u32[]{:S(2)}) collective-permute-start(f32[192,1152]{1,0:T(8,128)} %copy-done.2), channel_id=1, source_target_pairs={{0,8},{8,0},{1,9},{9,1},{2,10},{10,2},{3,11},{11,3},{4,12},{12,4},... | collective-permute-start | bytes 2654216 | tf_op jit(solution)/shard_map/ppermute | solution.py:154
  96.0 0.7 copy-start.7
  96.7 20.8 %all-to-all-start.4 = ((bf16[16,24,1152]{2,1,0:T(8,128)(2,1)}), bf16[16,24,1152]{2,1,0:T(8,128)(2,1)S(1)}, u32[]{:S(2)}, u32[]{:S(2)}) async-start(bf16[16,24,1152]{2,1,0:T(8,128)(2,1)} %bitcast.5), calls=%async_computation.4 | async-start | bytes 1769472 | tf_op jit(solution)/shard_map/all_to_all | solution.py:191
  105.6 8.0 %collective-permute-start.6 = (f16[96,1152]{1,0:T(8,128)(2,1)S(1)}, f16[96,1152]{1,0:T(8,128)(2,1)S(1)}, u32[]{:S(2)}, u32[]{:S(2)}) collective-permute-start(f16[96,1152]{1,0:T(8,128)(2,1)S(1)} %fusion), channel_id=1, source_target_pairs={{0,64},{64,0},{128,192},{192,128},{256,320},{320,256},{384,448},{4... | collective-permute-start | bytes 663560 | tf_op jit(solution)/shard_map/ppermute | solution.py:154
  113.7 11.3 %collective-permute-start.7 = (f16[48,1152]{1,0:T(8,128)(2,1)S(1)}, f16[48,1152]{1,0:T(8,128)(2,1)S(1)}, u32[]{:S(2)}, u32[]{:S(2)}) collective-permute-start(f16[48,1152]{1,0:T(8,128)(2,1)S(1)} %fusion.1), channel_id=1, source_target_pairs={{0,128},{64,192},{128,0},{192,64},{256,384},{320,448},{384,256},{4... | collective-permute-start | bytes 331784 | tf_op jit(solution)/shard_map/ppermute | solution.py:154
  117.6 20.1 %all-to-all-start.3 = ((bf16[16,24,1280]{2,1,0:T(8,128)(2,1)}), bf16[16,24,1280]{2,1,0:T(8,128)(2,1)S(1)}, u32[]{:S(2)}, u32[]{:S(2)}) async-start(bf16[16,24,1280]{2,1,0:T(8,128)(2,1)} %pad_maximum_fusion), calls=%async_computation.3 | async-start | bytes 1966080 | tf_op jit(solution)/shard_map/all_to_all | solution.py:194
  125.0 11.9 %collective-permute-start.8 = (f16[24,1152]{1,0:T(8,128)(2,1)S(1)}, f16[24,1152]{1,0:T(8,128)(2,1)S(1)}, u32[]{:S(2)}, u32[]{:S(2)}) collective-permute-start(f16[24,1152]{1,0:T(8,128)(2,1)S(1)} %fusion.2), channel_id=1, source_target_pairs={{0,256},{64,320},{128,384},{192,448},{256,0},{320,64},{384,128},{4... | collective-permute-start | bytes 165896 | tf_op jit(solution)/shard_map/ppermute | solution.py:154
  128.0 15.2 %collective-permute-start.9 = (f16[24,1152]{1,0:T(8,128)(2,1)S(1)}, f16[24,1152]{1,0:T(8,128)(2,1)S(1)}, u32[]{:S(2)}, u32[]{:S(2)}) collective-permute-start(f16[24,1152]{1,0:T(8,128)(2,1)S(1)} %multiply_convert_fusion), channel_id=1, source_target_pairs={{0,1},{1,0},{2,3},{3,2},{4,5},{5,4},{6,7},{7,6},{8,9},{9,8},{10,11... | collective-permute-start | bytes 165896 | tf_op jit(solution)/shard_map/ppermute | solution.py:154

commit v4 on v3

v4 whole, which is shorter than its diff:
```python
import jax
import jax.numpy as jnp
from jax import lax
from jax.experimental import pallas as pl
from jax.experimental.pallas import tpu as pltpu
from jax.sharding import Mesh, PartitionSpec as P

epsilon = 1e-06
AXES = ("zl", "x", "c", "y", "zh")
SIZES = (8, 4, 2, 4, 2)
RING = ("zl", "zh")
PLANE = ("x", "y")
COLUMN = ("zl", "c", "zh")
LANES = 128
PARTS = 1
LIMIT = 20 * 1024 * 1024
HALF = 0.5


def normalize(raw_rows):
    row_norm = jnp.sqrt(jnp.sum(raw_rows * raw_rows, axis=1, keepdims=True) + epsilon)
    return (raw_rows / row_norm, row_norm)


def back_norm(unit_rows, row_norm, gradient):
    return (gradient - unit_rows * jnp.sum(unit_rows * gradient, axis=1, keepdims=True)) / row_norm


def low(rows):
    return rows.astype(jnp.bfloat16).astype(jnp.float32)


def loss_and_sigmoid(values):
    small = jnp.exp(-jnp.abs(values))
    loss = jnp.maximum(values, 0.0) + jnp.log1p(small)
    return loss, jnp.where(values >= 0, 1.0, small) / (1.0 + small)


def own_pairs(image_low, text_low, heat, offset):
    return jnp.sum(image_low * text_low, axis=1, keepdims=True) * heat + offset


def unit_kernel(heat_ref, offset_ref, picture_ref, caption_ref, image_ref, text_ref, loss_ref):
    image_unit, _ = normalize(picture_ref[...])
    text_unit, _ = normalize(caption_ref[...])
    image_low, text_low = image_unit.astype(jnp.bfloat16), text_unit.astype(jnp.bfloat16)
    image_ref[...] = image_low
    text_ref[...] = text_low
    heat = jnp.exp(jnp.full((1, 1), heat_ref[0], jnp.float32))
    logits = own_pairs(image_low.astype(jnp.float32), text_low.astype(jnp.float32), heat, offset_ref[0])
    loss, _ = loss_and_sigmoid(-logits)
    loss_ref[...] = loss


def unit_rows(heat_exponent, offset_added, pictures, captions):
    rows = pictures.shape[0]
    return pl.pallas_call(
        unit_kernel,
        in_specs=[pl.BlockSpec(memory_space=pltpu.SMEM)] * 2 + [pl.BlockSpec(memory_space=pltpu.VMEM)] * 2,
        out_shape=[
            jax.ShapeDtypeStruct(pictures.shape, jnp.bfloat16),
            jax.ShapeDtypeStruct(captions.shape, jnp.bfloat16),
            jax.ShapeDtypeStruct((rows, 1), jnp.float32),
        ],
    )(heat_exponent, offset_added, pictures, captions)


def pieces(total, shape):
    first = low(total)
    second = low(total - first)
    third = total - first - second
    lane = lax.broadcasted_iota(jnp.int32, shape, len(shape) - 1)
    spread = jnp.where(lane == 0, first, jnp.where(lane == 1, second, jnp.where(lane == 2, third, 0.0)))
    return spread.astype(jnp.bfloat16)


def pair_kernel(place_ref, heat_ref, offset_ref, own_loss_ref, near_ref, far_ref, text_ref, weight_ref, text_out_ref):
    rows = own_loss_ref.shape[0]
    half, width = near_ref.shape
    count = text_ref.shape[0] // PARTS
    heat = jnp.exp(jnp.full((1, 1), heat_ref[0], jnp.float32))
    total = jnp.sum(own_loss_ref[...], axis=0, keepdims=True)
    for part in range(PARTS):
        columns = slice(part * count, (part + 1) * count)
        texts = text_ref[columns]
        text_part = None
        for place, image_ref in enumerate((near_ref, far_ref)):
            images = image_ref[...]
            logits = lax.dot_general(
                images, texts, (((1,), (1,)), ((), ())), preferred_element_type=jnp.float32
            )
            logits = logits * heat + offset_ref[0]
            loss, sigmoid = loss_and_sigmoid(logits)
            weights = heat * sigmoid
            if image_ref is near_ref:
                image_row = lax.broadcasted_iota(jnp.int32, logits.shape, 0) - rows
                text_row = lax.broadcasted_iota(jnp.int32, logits.shape, 1) + (part * count - place_ref[0])
                match = (image_row == text_row) & (image_row >= 0) & (image_row < rows)
                weights = jnp.where(match, 0.0, weights)
                loss = jnp.where(match, 0.0, loss)
            weights = weights.astype(jnp.bfloat16)
            weight_ref[place * half : (place + 1) * half, columns] = weights
            total += jnp.sum(jnp.sum(loss, axis=0, keepdims=True), axis=1, keepdims=True)
            term = lax.dot_general(
                weights, images, (((0,), (0,)), ((), ())), preferred_element_type=jnp.float32
            )
            text_part = term if text_part is None else text_part + term
        text_out_ref[columns, :width] = text_part.astype(jnp.bfloat16)
    text_out_ref[:, width:] = pieces(total, (text_out_ref.shape[0], LANES))


def pair_terms(place, heat_exponent, offset_added, own_loss, near, far, texts):
    half, width = near.shape
    count = texts.shape[0]
    return pl.pallas_call(
        pair_kernel,
        in_specs=[pl.BlockSpec(memory_space=pltpu.SMEM)] * 3 + [pl.BlockSpec(memory_space=pltpu.VMEM)] * 4,
        out_shape=[
            jax.ShapeDtypeStruct((2 * half, count), jnp.bfloat16),
            jax.ShapeDtypeStruct((count, width + LANES), jnp.bfloat16),
        ],
        compiler_params=pltpu.CompilerParams(vmem_limit_bytes=LIMIT),
        cost_estimate=pl.CostEstimate(
            flops=8 * half * count * width, bytes_accessed=8 * half * width, transcendentals=6 * half * count
        ),
    )(place, heat_exponent, offset_added, own_loss, near, far, texts)


def image_kernel(weight_ref, text_ref, near_ref, far_ref):
    half = near_ref.shape[0]
    texts = text_ref[...]
    far_ref[...] = jnp.dot(weight_ref[half:], texts, preferred_element_type=jnp.float32)
    near_ref[...] = jnp.dot(weight_ref[:half], texts, preferred_element_type=jnp.float32)


def image_terms(weights, texts):
    half, width = weights.shape[0] // 2, texts.shape[1]
    return pl.pallas_call(
        image_kernel,
        in_specs=[pl.BlockSpec(memory_space=pltpu.VMEM)] * 2,
        out_shape=[jax.ShapeDtypeStruct((half, width), jnp.float32)] * 2,
        compiler_params=pltpu.CompilerParams(vmem_limit_bytes=LIMIT),
        cost_estimate=pl.CostEstimate(
            flops=4 * half * texts.shape[0] * width, bytes_accessed=16 * half * width, transcendentals=0
        ),
    )(weights, texts)


def grad_kernel(
    heat_ref, offset_ref, picture_ref, caption_ref, image_sum_ref, text_sum_ref, image_ref, text_ref
):
    image_unit, image_norm = normalize(picture_ref[...])
    text_unit, text_norm = normalize(caption_ref[...])
    image_low, text_low = low(image_unit), low(text_unit)
    heat = jnp.exp(jnp.full((1, 1), heat_ref[0], jnp.float32))
    _, sigmoid = loss_and_sigmoid(-own_pairs(image_low, text_low, heat, offset_ref[0]))
    weights = low(-sigmoid * heat)
    image_ref[...] = back_norm(image_unit, image_norm, image_sum_ref[...] + weights * text_low)
    text_ref[...] = back_norm(text_unit, text_norm, text_sum_ref[...] + weights * image_low)


def gradients(heat_exponent, offset_added, pictures, captions, image_sum, text_sum):
    return pl.pallas_call(
        grad_kernel,
        in_specs=[pl.BlockSpec(memory_space=pltpu.SMEM)] * 2 + [pl.BlockSpec(memory_space=pltpu.VMEM)] * 4,
        out_shape=[jax.ShapeDtypeStruct(pictures.shape, jnp.float32)] * 2,
    )(heat_exponent, offset_added, pictures, captions, image_sum, text_sum)


def moved(value, steps):
    halves = lax.axis_size("zh")
    count = lax.axis_size(RING)
    order = [low_place * halves + half for half in range(halves) for low_place in range(count // halves)]
    return lax.ppermute(value, RING, [(order[i], order[(i + steps) % count]) for i in range(count)])


def sent(value):
    return (value * HALF).astype(jnp.float16)


def received(value):
    return value.astype(jnp.float32) * (1 / HALF)


def swapped(value):
    return lax.ppermute(value, "c", [(0, 1), (1, 0)])


def ring_gathered(block, texts):
    rows = block.shape[0]
    same = jnp.concatenate([moved(block, 4), block, moved(block, -4), moved(block, 8)], axis=0)
    parts = [same, moved(same, -1), moved(same, 1)]
    parts += [moved(same[rows : 3 * rows], -2), moved(same[: 2 * rows], 2)]
    near = jnp.concatenate(parts, axis=0)
    return lax.optimization_barrier((near, texts))


def near_summed(value, rows):
    low_part = sent(value)
    up = received(moved(low_part[4 * rows : 8 * rows], 1))
    down = received(moved(low_part[8 * rows : 12 * rows], -1))
    up_two = received(moved(low_part[12 * rows : 14 * rows], 2))
    down_two = received(moved(low_part[14 * rows :], -2))
    same = value[: 4 * rows] + up + down
    own = same[rows : 2 * rows] + down_two[rows:] + up_two[:rows]
    others = (same[:rows] + down_two[:rows], same[2 * rows : 3 * rows] + up_two[rows:], same[3 * rows :])
    return own, [sent(other) for other in others]


def far_summed(own, others):
    for other, steps in zip(others, (-4, 4, 8)):
        own += received(moved(other, steps))
    return own


def shards(picture_vectors, caption_vectors, heat_exponent, offset_added):
    rows, width = picture_vectors.shape
    plane, column = lax.axis_size(PLANE), lax.axis_size(COLUMN)
    image_low, text_low, own_loss = unit_rows(heat_exponent, offset_added, picture_vectors, caption_vectors)

    texts = lax.all_to_all(jnp.broadcast_to(text_low[None], (plane, *text_low.shape)), PLANE, 0, 0)
    near, texts = ring_gathered(image_low, texts.reshape(plane * rows, width))
    far = swapped(near)

    place = (lax.axis_index(PLANE) * rows).astype(jnp.int32).reshape(1)
    weights, text_part = pair_terms(place, heat_exponent, offset_added, own_loss, near, far, texts)
    text_parts = lax.all_to_all(text_part.reshape(plane, rows, width + LANES), PLANE, 0, 0)
    near_part, far_part = image_terms(weights, texts)
    own, others = near_summed(near_part + swapped(far_part), rows)
    others, text_parts = lax.optimization_barrier((others, text_parts))
    plane_loss = jnp.sum(text_parts[:, 0, width : width + 3].astype(jnp.float32))
    losses = lax.all_to_all(jnp.broadcast_to(plane_loss, (column, 8, LANES)), COLUMN, 0, 0)
    loss_mean = (jnp.sum(losses[:, 0, 0]) / (rows * lax.axis_size(AXES))).reshape(1)
    text_sum = jnp.sum(text_parts[:, :, :width].astype(jnp.float32), axis=0)
    image_sum = far_summed(own, others)
    image_grads, text_grads = gradients(
        heat_exponent, offset_added, picture_vectors, caption_vectors, image_sum, text_sum
    )
    return (loss_mean, image_grads, text_grads)


def solution(mesh):
    fine = Mesh(mesh.devices.reshape(SIZES), AXES)
    in_specs = (P(AXES, None), P(AXES, None), P(), P())
    out_specs = (P(), P(AXES, None), P(AXES, None))
    return jax.shard_map(shards, mesh=fine, in_specs=in_specs, out_specs=out_specs, check_vma=False)
```

time: 150 us -> 145 us (0.967)
  the two profiles are of different devices: /device:TPU:2 before, /device:TPU:1 now
where the time goes in v4:
time: 145 us; the launch traced here: 143 us
  starting transfers between devices  102 us (70%)
  waiting for transfers between devices  19.2 us (13%)
  Pallas kernels  9.47 us (7%)
  other arithmetic  4.6 us (3%)
  between operations  4.05 us (3%)
  local copies, waits for them, and re-layouts  3.41 us (2%)
    ppermute x14, starting transfers between devices, moved(): lax.ppermute(value, RING, [(order[i], order[(i + steps) % count]) for i i...  69.9 us
    all_to_all x1, waiting for transfers between devices, shards(): lax.all_to_all(jnp.broadcast_to(plane_loss, (column, 8, LANES)), COLUMN,...  11.2 us
    all_to_all x1, starting transfers between devices, shards(): lax.all_to_all(jnp.broadcast_to(plane_loss, (column, 8, LANES)), COLUMN,...  10.9 us
    ppermute x2, starting transfers between devices, swapped(): return lax.ppermute(value, 'c', [(0, 1), (1, 0)])  7.9 us
    all_to_all x1, starting transfers between devices, shards(): lax.all_to_all(jnp.broadcast_to(text_low[None], (plane, *text_low.shape))...  6.89 us
    all_to_all x1, starting transfers between devices, shards(): lax.all_to_all(text_part.reshape(plane, rows, width + LANES), PLANE, 0, 0)  6.88 us
    ppermute x14, waiting for transfers between devices, moved(): lax.ppermute(value, RING, [(order[i], order[(i + steps) % count]) for i i...  5.99 us
    pallas_call x1, Pallas kernels, pair_terms(): pl.pallas_call(pair_kernel, in_specs=[pl.BlockSpec(memory_space=pltpu.SME...  3.71 us
  transfers between devices with their start and end apart: 19, of which 5 were waited for; matrix products, arithmetic and copies ran while one was open for 5% of the time, Pallas kernels for 1%

profile of v4, /device:TPU:1, one launch (start us, length us, event | category | flops | bytes accessed | tf_op | source)
XLA Modules:
  0.0 143.2 jit_solution(1360792243608460188)
XLA Ops:
  1.9 1.8 %shard_map.67 = (bf16[24,1152]{1,0:T(8,128)(2,1)}, bf16[24,1152]{1,0:T(8,128)(2,1)}, f32[24,1]{1,0:T(8,128)}) custom-call(f32[1]{0:T(128)S(6)} %copy.19.heat_ref, f32[1]{0:T(128)S(6)} %copy.20.offset_ref, f32[24,1152]{1,0:T(8,128)} %picture_ref.3, f32[24,1152]{1,0:T(8,128)} %caption_ref.3), custom_call_target="tpu_custom_call" | custom-call | tf_op jit(solution)/shard_map/pallas_call | solution.py:57
  3.7 0.0 copy-start.1
  3.7 9.8 %collective-permute-start = (bf16[24,1152]{1,0:T(8,128)(2,1)}, bf16[24,1152]{1,0:T(8,128)(2,1)S(1)}, u32[]{:S(2)}, u32[]{:S(2)}) collective-permute-start(bf16[24,1152]{1,0:T(8,128)(2,1)} %get-tuple-element.19), channel_id=1, source_target_pairs={{0,256},{64,320},{128,384},{192,448},{256,1},{320,65},{384,129},{4... | collective-permute-start | bytes 165896 | tf_op jit(solution)/shard_map/ppermute | solution.py:174
  13.5 10.6 %collective-permute-start.2 = (bf16[24,1152]{1,0:T(8,128)(2,1)}, bf16[24,1152]{1,0:T(8,128)(2,1)S(1)}, u32[]{:S(2)}, u32[]{:S(2)}) collective-permute-start(bf16[24,1152]{1,0:T(8,128)(2,1)} %get-tuple-element.19), channel_id=1, source_target_pairs={{0,1},{64,65},{128,129},{192,193},{256,257},{320,321},{384,385},{4... | collective-permute-start | bytes 165896 | tf_op jit(solution)/shard_map/ppermute | solution.py:174
  24.1 5.2 %collective-permute-start.1 = (bf16[24,1152]{1,0:T(8,128)(2,1)}, bf16[24,1152]{1,0:T(8,128)(2,1)S(1)}, u32[]{:S(2)}, u32[]{:S(2)}) collective-permute-start(bf16[24,1152]{1,0:T(8,128)(2,1)} %get-tuple-element.19), channel_id=1, source_target_pairs={{0,257},{64,321},{128,385},{192,449},{256,0},{320,64},{384,128},{4... | collective-permute-start | bytes 165896 | tf_op jit(solution)/shard_map/ppermute | solution.py:174
  29.3 1.8 %broadcast_in_dim.4 = bf16[16,24,1152]{2,1,0:T(8,128)(2,1)} broadcast(bf16[24,1152]{1,0:T(8,128)(2,1)} %get-tuple-element.20), dimensions={1,2} | broadcast | bytes 940032 | tf_op jit(solution)/shard_map/broadcast_in_dim | solution.py:221
  31.1 0.0 copy-start
  31.1 6.9 %all-to-all-start = ((bf16[16,24,1152]{2,1,0:T(8,128)(2,1)}), bf16[16,24,1152]{2,1,0:T(8,128)(2,1)S(1)}, u32[]{:S(2)}, u32[]{:S(2)}) async-start(bf16[16,24,1152]{2,1,0:T(8,128)(2,1)} %broadcast_in_dim.4), calls=%async_computation | async-start | bytes 1769472 | tf_op jit(solution)/shard_map/all_to_all | solution.py:221
  38.0 0.0 collective-permute-done
  38.0 0.0 copy-done.1
  38.1 0.0 collective-permute-done.1
  38.1 0.0 collective-permute-done.2
  38.1 2.6 %collective-permute-start.4 = (bf16[96,1152]{1,0:T(8,128)(2,1)S(1)}, bf16[96,1152]{1,0:T(8,128)(2,1)S(1)}, u32[]{:S(2)}, u32[]{:S(2)}) collective-permute-start(bf16[96,1152]{1,0:T(8,128)(2,1)S(1)} %get-tuple-element.44), channel_id=1, source_target_pairs={{0,64},{64,128},{128,192},{192,256},{256,320},{320,384},{384,448},... | collective-permute-start | bytes 663560 | tf_op jit(solution)/shard_map/ppermute | solution.py:174
  40.8 3.8 %collective-permute-start.3 = (bf16[96,1152]{1,0:T(8,128)(2,1)S(1)}, bf16[96,1152]{1,0:T(8,128)(2,1)S(1)}, u32[]{:S(2)}, u32[]{:S(2)}) collective-permute-start(bf16[96,1152]{1,0:T(8,128)(2,1)S(1)} %get-tuple-element.44), channel_id=1, source_target_pairs={{0,449},{64,0},{128,64},{192,128},{256,192},{320,256},{384,320},{4... | collective-permute-start | bytes 663560 | tf_op jit(solution)/shard_map/ppermute | solution.py:174
  44.7 1.9 %collective-permute-start.6 = (bf16[48,1152]{1,0:T(8,128)(2,1)S(1)}, bf16[48,1152]{1,0:T(8,128)(2,1)S(1)}, u32[]{:S(2)}, u32[]{:S(2)}) collective-permute-start(bf16[48,1152]{1,0:T(8,128)(2,1)S(1)} %get-tuple-element.42), channel_id=1, source_target_pairs={{0,128},{64,192},{128,256},{192,320},{256,384},{320,448},{384,1},{... | collective-permute-start | bytes 331784 | tf_op jit(solution)/shard_map/ppermute | solution.py:174
  46.6 5.5 %collective-permute-start.5 = (bf16[48,1152]{1,0:T(8,128)(2,1)S(1)}, bf16[48,1152]{1,0:T(8,128)(2,1)S(1)}, u32[]{:S(2)}, u32[]{:S(2)}) collective-permute-start(bf16[48,1152]{1,0:T(8,128)(2,1)S(1)} %get-tuple-element.43), channel_id=1, source_target_pairs={{0,385},{64,449},{128,0},{192,64},{256,128},{320,192},{384,256},{4... | collective-permute-start | bytes 331784 | tf_op jit(solution)/shard_map/ppermute | solution.py:174
  52.1 0.0 collective-permute-done.3
  52.1 0.0 collective-permute-done.4
  52.2 2.3 %collective-permute-done.5 = bf16[48,1152]{1,0:T(8,128)(2,1)S(1)} collective-permute-done((bf16[48,1152]{1,0:T(8,128)(2,1)S(1)}, bf16[48,1152]{1,0:T(8,128)(2,1)S(1)}, u32[]{:S(2)}, u32[]{:S(2)}) %collective-permute-start.5) | collective-permute-done | bytes 110624 | tf_op jit(solution)/shard_map/ppermute | solution.py:174
  54.5 0.0 collective-permute-done.6
  54.5 0.0 all-to-all-done
  54.6 5.6 %collective-permute-start.7 = (bf16[384,1152]{1,0:T(8,128)(2,1)S(1)}, bf16[384,1152]{1,0:T(8,128)(2,1)S(1)}, u32[]{:S(2)}, u32[]{:S(2)}) collective-permute-start(bf16[384,1152]{1,0:T(8,128)(2,1)S(1)} %constant_dynamic-update-slice_fusion.4.near_ref), channel_id=1, source_target_pairs={{0,8},{8,0},{1,9},{9,1},{2,10},{10,2},{3,11},{11,3},{4,12},{12,4},... | collective-permute-start | bytes 2654216 | tf_op jit(solution)/shard_map/ppermute | solution.py:186
  60.2 2.0 %collective-permute-done.7.far_ref = bf16[384,1152]{1,0:T(8,128)(2,1)S(1)} collective-permute-done((bf16[384,1152]{1,0:T(8,128)(2,1)S(1)}, bf16[384,1152]{1,0:T(8,128)(2,1)S(1)}, u32[]{:S(2)}, u32[]{:S(2)}) %collective-permute-start.7) | collective-permute-done | bytes 884768 | tf_op jit(solution)/shard_map/ppermute | solution.py:186
  62.2 0.0 copy-done
  62.2 3.7 %shard_map.68 = (bf16[768,384]{1,0:T(8,128)(2,1)S(1)}, bf16[384,1280]{1,0:T(8,128)(2,1)}) custom-call(s32[1]{0:T(128)} %bitcast.place_ref, f32[1]{0:T(128)S(6)} %copy.19.heat_ref, f32[1]{0:T(128)S(6)} %copy.20.offset_ref, f32[24,1]{1,0:T(8,128)S(1)} %copy-done, bf16[384,1152]{1,0:T(8,128)(2,1)S(1)} %constant_dynamic-update-slice_fusion.4.near_ref, ...), custom_call_target="tpu_custom_call" | custom-call | flops 1358954496 | bytes 3538944 | tf_op jit(solution)/shard_map/pallas_call | solution.py:115
  65.9 1.9 %shard_map.69 = (f32[384,1152]{1,0:T(8,128)S(1)}, f32[384,1152]{1,0:T(8,128)}) custom-call(bf16[768,384]{1,0:T(8,128)(2,1)S(1)} %get-tuple-element.23.weight_ref, bf16[384,1152]{1,0:T(8,128)(2,1)S(1)} %bitcast.5), custom_call_target="tpu_custom_call" | custom-call | flops 679477248 | bytes 7077888 | tf_op jit(solution)/shard_map/pallas_call | solution.py:138
  67.9 2.3 %collective-permute-start.8 = (f32[384,1152]{1,0:T(8,128)}, f32[384,1152]{1,0:T(8,128)}, u32[]{:S(2)}, u32[]{:S(2)}) collective-permute-start(f32[384,1152]{1,0:T(8,128)} %get-tuple-element.25), channel_id=1, source_target_pairs={{0,8},{8,0},{1,9},{9,1},{2,10},{10,2},{3,11},{11,3},{4,12},{12,4},... | collective-permute-start | bytes 5308424 | tf_op jit(solution)/shard_map/ppermute | solution.py:186
  70.1 6.9 %all-to-all-start.1 = ((bf16[16,24,1280]{2,1,0:T(8,128)(2,1)}), bf16[16,24,1280]{2,1,0:T(8,128)(2,1)S(1)}, u32[]{:S(2)}, u32[]{:S(2)}) async-start(bf16[16,24,1280]{2,1,0:T(8,128)(2,1)} %bitcast.2), calls=%async_computation.1 | async-start | bytes 1966080 | tf_op jit(solution)/shard_map/all_to_all | solution.py:227
  77.0 0.0 collective-permute-done.8
  77.0 1.7 %multiply_convert_fusion = (f16[384,1152]{1,0:T(8,128)(2,1)S(1)}, f32[384,1152]{1,0:T(8,128)S(1)}) fusion(f32[384,1152]{1,0:T(8,128)S(1)} %get-tuple-element.24, f32[384,1152]{1,0:T(8,128)} %collective-permute-done.8), kind=kLoop, calls=%fused_computation.1 | loop fusion | flops 1327104 | bytes 6193152 | tf_op jit(solution)/shard_map/convert_element_type | solution.py:178
  78.8 4.5 %collective-permute-start.12 = (f16[48,1152]{1,0:T(8,128)(2,1)S(1)}, f16[48,1152]{1,0:T(8,128)(2,1)S(1)}, u32[]{:S(2)}, u32[]{:S(2)}) collective-permute-start(f16[48,1152]{1,0:T(8,128)(2,1)S(1)} %get-tuple-element.35), channel_id=1, source_target_pairs={{0,128},{64,192},{128,256},{192,320},{256,384},{320,448},{384,1},{... | collective-permute-start | bytes 331784 | tf_op jit(solution)/shard_map/ppermute | solution.py:174
  83.2 0.1 fusion.10
  83.3 3.7 %collective-permute-start.11 = (f16[48,1152]{1,0:T(8,128)(2,1)S(1)}, f16[48,1152]{1,0:T(8,128)(2,1)S(1)}, u32[]{:S(2)}, u32[]{:S(2)}) collective-permute-start(f16[48,1152]{1,0:T(8,128)(2,1)S(1)} %get-tuple-element.36), channel_id=1, source_target_pairs={{0,385},{64,449},{128,0},{192,64},{256,128},{320,192},{384,256},{4... | collective-permute-start | bytes 331784 | tf_op jit(solution)/shard_map/ppermute | solution.py:174
  87.0 1.9 %collective-permute-start.9 = (f16[96,1152]{1,0:T(8,128)(2,1)S(1)}, f16[96,1152]{1,0:T(8,128)(2,1)S(1)}, u32[]{:S(2)}, u32[]{:S(2)}) collective-permute-start(f16[96,1152]{1,0:T(8,128)(2,1)S(1)} %get-tuple-element.37), channel_id=1, source_target_pairs={{0,64},{64,128},{128,192},{192,256},{256,320},{320,384},{384,448},... | collective-permute-start | bytes 663560 | tf_op jit(solution)/shard_map/ppermute | solution.py:174
  88.9 4.6 %collective-permute-start.10 = (f16[96,1152]{1,0:T(8,128)(2,1)S(1)}, f16[96,1152]{1,0:T(8,128)(2,1)S(1)}, u32[]{:S(2)}, u32[]{:S(2)}) collective-permute-start(f16[96,1152]{1,0:T(8,128)(2,1)S(1)} %get-tuple-element.38), channel_id=1, source_target_pairs={{0,449},{64,0},{128,64},{192,128},{256,192},{320,256},{384,320},{4... | collective-permute-start | bytes 663560 | tf_op jit(solution)/shard_map/ppermute | solution.py:174
  93.5 0.0 collective-permute-done.12
  93.5 0.0 collective-permute-done.11
  93.6 2.8 %collective-permute-done.9 = f16[96,1152]{1,0:T(8,128)(2,1)S(1)} collective-permute-done((f16[96,1152]{1,0:T(8,128)(2,1)S(1)}, f16[96,1152]{1,0:T(8,128)(2,1)S(1)}, u32[]{:S(2)}, u32[]{:S(2)}) %collective-permute-start.9) | collective-permute-done | bytes 221216 | tf_op jit(solution)/shard_map/ppermute | solution.py:174
  96.4 0.9 collective-permute-done.10
  97.2 0.1 fusion
  97.4 0.0 all-to-all-done.1
  97.4 0.6 convert_reduce_fusion.1
  98.0 4.7 %collective-permute-start.13 = (f16[24,1152]{1,0:T(8,128)(2,1)S(1)}, f16[24,1152]{1,0:T(8,128)(2,1)S(1)}, u32[]{:S(2)}, u32[]{:S(2)}) collective-permute-start(f16[24,1152]{1,0:T(8,128)(2,1)S(1)} %get-tuple-element.28), channel_id=1, source_target_pairs={{0,257},{64,321},{128,385},{192,449},{256,0},{320,64},{384,128},{4... | collective-permute-start | bytes 165896 | tf_op jit(solution)/shard_map/ppermute | solution.py:174
  102.7 4.5 %collective-permute-start.14 = (f16[24,1152]{1,0:T(8,128)(2,1)S(1)}, f16[24,1152]{1,0:T(8,128)(2,1)S(1)}, u32[]{:S(2)}, u32[]{:S(2)}) collective-permute-start(f16[24,1152]{1,0:T(8,128)(2,1)S(1)} %get-tuple-element.29), channel_id=1, source_target_pairs={{0,256},{64,320},{128,384},{192,448},{256,1},{320,65},{384,129},{4... | collective-permute-start | bytes 165896 | tf_op jit(solution)/shard_map/ppermute | solution.py:174
  107.2 6.7 %collective-permute-start.15 = (f16[24,1152]{1,0:T(8,128)(2,1)S(1)}, f16[24,1152]{1,0:T(8,128)(2,1)S(1)}, u32[]{:S(2)}, u32[]{:S(2)}) collective-permute-start(f16[24,1152]{1,0:T(8,128)(2,1)S(1)} %get-tuple-element.30), channel_id=1, source_target_pairs={{0,1},{64,65},{128,129},{192,193},{256,257},{320,321},{384,385},{4... | collective-permute-start | bytes 165896 | tf_op jit(solution)/shard_map/ppermute | solution.py:174
  113.9 1.3 broadcast_in_dim.10
  115.2 10.9 %all-to-all-start.2 = ((f32[32,8,128]{2,1,0:T(8,128)}), f32[32,8,128]{2,1,0:T(8,128)S(1)}, u32[]{:S(2)}, u32[]{:S(2)}) async-start(f32[32,8,128]{2,1,0:T(8,128)} %broadcast_in_dim.10), calls=%async_computation.2 | async-start | bytes 262144 | tf_op jit(solution)/shard_map/all_to_all | solution.py:232
  126.1 0.8 convert_reduce_fusion.text_sum_ref
  126.8 0.0 collective-permute-done.13
  126.8 0.0 collective-permute-done.14
  126.9 0.0 collective-permute-done.15
  126.9 0.7 fusion.3.image_sum_ref
  127.5 2.1 %shard_map.70 = (f32[24,1152]{1,0:T(8,128)}, f32[24,1152]{1,0:T(8,128)}) custom-call(f32[1]{0:T(128)S(6)} %copy.19.heat_ref, f32[1]{0:T(128)S(6)} %copy.20.offset_ref, f32[24,1152]{1,0:T(8,128)} %picture_ref.3, f32[24,1152]{1,0:T(8,128)} %caption_ref.3, f32[24,1152]{1,0:T(8,128)} %fusion.3.image_sum_ref, f32[24,1152]{1,0:T(8,128)} %convert_reduce_fusion.text_sum_ref), custom_call_target="tpu_custom_call" | custom-call | tf_op jit(solution)/shard_map/pallas_call | solution.py:163
  129.6 11.2 %all-to-all-done.2 = f32[32,8,128]{2,1,0:T(8,128)S(1)} async-done(((f32[32,8,128]{2,1,0:T(8,128)}), f32[32,8,128]{2,1,0:T(8,128)S(1)}, u32[]{:S(2)}, u32[]{:S(2)}) %all-to-all-start.2) | async-done | bytes 131104 | tf_op jit(solution)/shard_map/all_to_all | solution.py:232
  140.8 0.6 slice_reduce_fusion
  (13 shorter events, 0.3 us)
Async XLA Ops:
  3.7 34.3 %copy-start.1 = (bf16[24,1152]{1,0:T(8,128)(2,1)S(1)}, bf16[24,1152]{1,0:T(8,128)(2,1)}, u32[]{:S(2)}) copy-start(bf16[24,1152]{1,0:T(8,128)(2,1)} %get-tuple-element.19) | copy-start | bytes 165892
  3.7 34.3 %collective-permute-start = (bf16[24,1152]{1,0:T(8,128)(2,1)}, bf16[24,1152]{1,0:T(8,128)(2,1)S(1)}, u32[]{:S(2)}, u32[]{:S(2)}) collective-permute-start(bf16[24,1152]{1,0:T(8,128)(2,1)} %get-tuple-element.19), channel_id=1, source_target_pairs={{0,256},{64,320},{128,384},{192,448},{256,1},{320,65},{384,129},{4... | collective-permute-start | bytes 165896 | tf_op jit(solution)/shard_map/ppermute | solution.py:174
  13.5 24.6 %collective-permute-start.2 = (bf16[24,1152]{1,0:T(8,128)(2,1)}, bf16[24,1152]{1,0:T(8,128)(2,1)S(1)}, u32[]{:S(2)}, u32[]{:S(2)}) collective-permute-start(bf16[24,1152]{1,0:T(8,128)(2,1)} %get-tuple-element.19), channel_id=1, source_target_pairs={{0,1},{64,65},{128,129},{192,193},{256,257},{320,321},{384,385},{4... | collective-permute-start | bytes 165896 | tf_op jit(solution)/shard_map/ppermute | solution.py:174
  24.1 14.0 %collective-permute-start.1 = (bf16[24,1152]{1,0:T(8,128)(2,1)}, bf16[24,1152]{1,0:T(8,128)(2,1)S(1)}, u32[]{:S(2)}, u32[]{:S(2)}) collective-permute-start(bf16[24,1152]{1,0:T(8,128)(2,1)} %get-tuple-element.19), channel_id=1, source_target_pairs={{0,257},{64,321},{128,385},{192,449},{256,0},{320,64},{384,128},{4... | collective-permute-start | bytes 165896 | tf_op jit(solution)/shard_map/ppermute | solution.py:174
  31.1 31.1 %copy-start = (f32[24,1]{1,0:T(8,128)S(1)}, f32[24,1]{1,0:T(8,128)}, u32[]{:S(2)}) copy-start(f32[24,1]{1,0:T(8,128)} %get-tuple-element.18.own_loss_ref) | copy-start | bytes 292
  31.1 23.4 %all-to-all-start = ((bf16[16,24,1152]{2,1,0:T(8,128)(2,1)}), bf16[16,24,1152]{2,1,0:T(8,128)(2,1)S(1)}, u32[]{:S(2)}, u32[]{:S(2)}) async-start(bf16[16,24,1152]{2,1,0:T(8,128)(2,1)} %broadcast_in_dim.4), calls=%async_computation | async-start | bytes 1769472 | tf_op jit(solution)/shard_map/all_to_all | solution.py:221
  38.1 14.0 %collective-permute-start.4 = (bf16[96,1152]{1,0:T(8,128)(2,1)S(1)}, bf16[96,1152]{1,0:T(8,128)(2,1)S(1)}, u32[]{:S(2)}, u32[]{:S(2)}) collective-permute-start(bf16[96,1152]{1,0:T(8,128)(2,1)S(1)} %get-tuple-element.44), channel_id=1, source_target_pairs={{0,64},{64,128},{128,192},{192,256},{256,320},{320,384},{384,448},... | collective-permute-start | bytes 663560 | tf_op jit(solution)/shard_map/ppermute | solution.py:174
  40.8 11.3 %collective-permute-start.3 = (bf16[96,1152]{1,0:T(8,128)(2,1)S(1)}, bf16[96,1152]{1,0:T(8,128)(2,1)S(1)}, u32[]{:S(2)}, u32[]{:S(2)}) collective-permute-start(bf16[96,1152]{1,0:T(8,128)(2,1)S(1)} %get-tuple-element.44), channel_id=1, source_target_pairs={{0,449},{64,0},{128,64},{192,128},{256,192},{320,256},{384,320},{4... | collective-permute-start | bytes 663560 | tf_op jit(solution)/shard_map/ppermute | solution.py:174
  44.7 9.8 %collective-permute-start.6 = (bf16[48,1152]{1,0:T(8,128)(2,1)S(1)}, bf16[48,1152]{1,0:T(8,128)(2,1)S(1)}, u32[]{:S(2)}, u32[]{:S(2)}) collective-permute-start(bf16[48,1152]{1,0:T(8,128)(2,1)S(1)} %get-tuple-element.42), channel_id=1, source_target_pairs={{0,128},{64,192},{128,256},{192,320},{256,384},{320,448},{384,1},{... | collective-permute-start | bytes 331784 | tf_op jit(solution)/shard_map/ppermute | solution.py:174
  46.6 7.9 %collective-permute-start.5 = (bf16[48,1152]{1,0:T(8,128)(2,1)S(1)}, bf16[48,1152]{1,0:T(8,128)(2,1)S(1)}, u32[]{:S(2)}, u32[]{:S(2)}) collective-permute-start(bf16[48,1152]{1,0:T(8,128)(2,1)S(1)} %get-tuple-element.43), channel_id=1, source_target_pairs={{0,385},{64,449},{128,0},{192,64},{256,128},{320,192},{384,256},{4... | collective-permute-start | bytes 331784 | tf_op jit(solution)/shard_map/ppermute | solution.py:174
  54.6 7.7 %collective-permute-start.7 = (bf16[384,1152]{1,0:T(8,128)(2,1)S(1)}, bf16[384,1152]{1,0:T(8,128)(2,1)S(1)}, u32[]{:S(2)}, u32[]{:S(2)}) collective-permute-start(bf16[384,1152]{1,0:T(8,128)(2,1)S(1)} %constant_dynamic-update-slice_fusion.4.near_ref), channel_id=1, source_target_pairs={{0,8},{8,0},{1,9},{9,1},{2,10},{10,2},{3,11},{11,3},{4,12},{12,4},... | collective-permute-start | bytes 2654216 | tf_op jit(solution)/shard_map/ppermute | solution.py:186
  67.9 9.2 %collective-permute-start.8 = (f32[384,1152]{1,0:T(8,128)}, f32[384,1152]{1,0:T(8,128)}, u32[]{:S(2)}, u32[]{:S(2)}) collective-permute-start(f32[384,1152]{1,0:T(8,128)} %get-tuple-element.25), channel_id=1, source_target_pairs={{0,8},{8,0},{1,9},{9,1},{2,10},{10,2},{3,11},{11,3},{4,12},{12,4},... | collective-permute-start | bytes 5308424 | tf_op jit(solution)/shard_map/ppermute | solution.py:186
  70.1 27.2 %all-to-all-start.1 = ((bf16[16,24,1280]{2,1,0:T(8,128)(2,1)}), bf16[16,24,1280]{2,1,0:T(8,128)(2,1)S(1)}, u32[]{:S(2)}, u32[]{:S(2)}) async-start(bf16[16,24,1280]{2,1,0:T(8,128)(2,1)} %bitcast.2), calls=%async_computation.1 | async-start | bytes 1966080 | tf_op jit(solution)/shard_map/all_to_all | solution.py:227
  78.8 14.7 %collective-permute-start.12 = (f16[48,1152]{1,0:T(8,128)(2,1)S(1)}, f16[48,1152]{1,0:T(8,128)(2,1)S(1)}, u32[]{:S(2)}, u32[]{:S(2)}) collective-permute-start(f16[48,1152]{1,0:T(8,128)(2,1)S(1)} %get-tuple-element.35), channel_id=1, source_target_pairs={{0,128},{64,192},{128,256},{192,320},{256,384},{320,448},{384,1},{... | collective-permute-start | bytes 331784 | tf_op jit(solution)/shard_map/ppermute | solution.py:174
  83.3 10.2 %collective-permute-start.11 = (f16[48,1152]{1,0:T(8,128)(2,1)S(1)}, f16[48,1152]{1,0:T(8,128)(2,1)S(1)}, u32[]{:S(2)}, u32[]{:S(2)}) collective-permute-start(f16[48,1152]{1,0:T(8,128)(2,1)S(1)} %get-tuple-element.36), channel_id=1, source_target_pairs={{0,385},{64,449},{128,0},{192,64},{256,128},{320,192},{384,256},{4... | collective-permute-start | bytes 331784 | tf_op jit(solution)/shard_map/ppermute | solution.py:174
  87.0 9.4 %collective-permute-start.9 = (f16[96,1152]{1,0:T(8,128)(2,1)S(1)}, f16[96,1152]{1,0:T(8,128)(2,1)S(1)}, u32[]{:S(2)}, u32[]{:S(2)}) collective-permute-start(f16[96,1152]{1,0:T(8,128)(2,1)S(1)} %get-tuple-element.37), channel_id=1, source_target_pairs={{0,64},{64,128},{128,192},{192,256},{256,320},{320,384},{384,448},... | collective-permute-start | bytes 663560 | tf_op jit(solution)/shard_map/ppermute | solution.py:174
  88.9 8.3 %collective-permute-start.10 = (f16[96,1152]{1,0:T(8,128)(2,1)S(1)}, f16[96,1152]{1,0:T(8,128)(2,1)S(1)}, u32[]{:S(2)}, u32[]{:S(2)}) collective-permute-start(f16[96,1152]{1,0:T(8,128)(2,1)S(1)} %get-tuple-element.38), channel_id=1, source_target_pairs={{0,449},{64,0},{128,64},{192,128},{256,192},{320,256},{384,320},{4... | collective-permute-start | bytes 663560 | tf_op jit(solution)/shard_map/ppermute | solution.py:174
  98.0 28.9 %collective-permute-start.13 = (f16[24,1152]{1,0:T(8,128)(2,1)S(1)}, f16[24,1152]{1,0:T(8,128)(2,1)S(1)}, u32[]{:S(2)}, u32[]{:S(2)}) collective-permute-start(f16[24,1152]{1,0:T(8,128)(2,1)S(1)} %get-tuple-element.28), channel_id=1, source_target_pairs={{0,257},{64,321},{128,385},{192,449},{256,0},{320,64},{384,128},{4... | collective-permute-start | bytes 165896 | tf_op jit(solution)/shard_map/ppermute | solution.py:174
  102.7 24.2 %collective-permute-start.14 = (f16[24,1152]{1,0:T(8,128)(2,1)S(1)}, f16[24,1152]{1,0:T(8,128)(2,1)S(1)}, u32[]{:S(2)}, u32[]{:S(2)}) collective-permute-start(f16[24,1152]{1,0:T(8,128)(2,1)S(1)} %get-tuple-element.29), channel_id=1, source_target_pairs={{0,256},{64,320},{128,384},{192,448},{256,1},{320,65},{384,129},{4... | collective-permute-start | bytes 165896 | tf_op jit(solution)/shard_map/ppermute | solution.py:174
  107.2 19.7 %collective-permute-start.15 = (f16[24,1152]{1,0:T(8,128)(2,1)S(1)}, f16[24,1152]{1,0:T(8,128)(2,1)S(1)}, u32[]{:S(2)}, u32[]{:S(2)}) collective-permute-start(f16[24,1152]{1,0:T(8,128)(2,1)S(1)} %get-tuple-element.30), channel_id=1, source_target_pairs={{0,1},{64,65},{128,129},{192,193},{256,257},{320,321},{384,385},{4... | collective-permute-start | bytes 165896 | tf_op jit(solution)/shard_map/ppermute | solution.py:174
  115.2 25.6 %all-to-all-start.2 = ((f32[32,8,128]{2,1,0:T(8,128)}), f32[32,8,128]{2,1,0:T(8,128)S(1)}, u32[]{:S(2)}, u32[]{:S(2)}) async-start(f32[32,8,128]{2,1,0:T(8,128)} %broadcast_in_dim.10), calls=%async_computation.2 | async-start | bytes 262144 | tf_op jit(solution)/shard_map/all_to_all | solution.py:232

commit v5 on v4

--- a/solution.py
+++ b/solution.py
@@ -10,7 +10,6 @@
 SIZES = (8, 4, 2, 4, 2)
 RING = ("zl", "zh")
 PLANE = ("x", "y")
-COLUMN = ("zl", "c", "zh")
 LANES = 128
 PARTS = 1
 LIMIT = 20 * 1024 * 1024
@@ -45,21 +44,21 @@
     text_unit, _ = normalize(caption_ref[...])
     image_low, text_low = image_unit.astype(jnp.bfloat16), text_unit.astype(jnp.bfloat16)
     image_ref[...] = image_low
-    text_ref[...] = text_low
+    text_ref[...] = jnp.broadcast_to(text_low[None], text_ref.shape)
     heat = jnp.exp(jnp.full((1, 1), heat_ref[0], jnp.float32))
     logits = own_pairs(image_low.astype(jnp.float32), text_low.astype(jnp.float32), heat, offset_ref[0])
     loss, _ = loss_and_sigmoid(-logits)
     loss_ref[...] = loss
 
 
-def unit_rows(heat_exponent, offset_added, pictures, captions):
+def unit_rows(copies, heat_exponent, offset_added, pictures, captions):
     rows = pictures.shape[0]
     return pl.pallas_call(
         unit_kernel,
         in_specs=[pl.BlockSpec(memory_space=pltpu.SMEM)] * 2 + [pl.BlockSpec(memory_space=pltpu.VMEM)] * 2,
         out_shape=[
             jax.ShapeDtypeStruct(pictures.shape, jnp.bfloat16),
-            jax.ShapeDtypeStruct(captions.shape, jnp.bfloat16),
+            jax.ShapeDtypeStruct((copies, *captions.shape), jnp.bfloat16),
             jax.ShapeDtypeStruct((rows, 1), jnp.float32),
         ],
     )(heat_exponent, offset_added, pictures, captions)
@@ -195,44 +194,63 @@
     return lax.optimization_barrier((near, texts))
 
 
-def near_summed(value, rows):
-    low_part = sent(value)
-    up = received(moved(low_part[4 * rows : 8 * rows], 1))
-    down = received(moved(low_part[8 * rows : 12 * rows], -1))
-    up_two = received(moved(low_part[12 * rows : 14 * rows], 2))
-    down_two = received(moved(low_part[14 * rows :], -2))
-    same = value[: 4 * rows] + up + down
+LOSS_SCALE = 2.0**-15
+REST_SCALE = 2.0**11
+
+
+def with_loss(value, loss):
+    scaled = loss * LOSS_SCALE
+    first = scaled.astype(jnp.float16)
+    rest = ((scaled - first.astype(jnp.float32)) * REST_SCALE).astype(jnp.float16)
+    return jnp.concatenate([sent(value), first, rest], axis=0)
+
+
+def loss_of(arrived):
+    first, rest = arrived[-8:-4].astype(jnp.float32), arrived[-4:].astype(jnp.float32)
+    return (first + rest * (1 / REST_SCALE)) * (1 / LOSS_SCALE)
+
+
+def near_summed(value, rows, loss):
+    up = moved(with_loss(value[4 * rows : 8 * rows], loss), 1)
+    down = moved(with_loss(value[8 * rows : 12 * rows], loss), -1)
+    up_two = moved(with_loss(value[12 * rows : 14 * rows], loss), 2)
+    down_two = received(moved(sent(value[14 * rows :]), -2))
+    loss = loss + loss_of(up) + loss_of(down) + loss_of(up_two)
+    same = value[: 4 * rows] + received(up[:-8]) + received(down[:-8])
+    up_two = received(up_two[:-8])
     own = same[rows : 2 * rows] + down_two[rows:] + up_two[:rows]
     others = (same[:rows] + down_two[:rows], same[2 * rows : 3 * rows] + up_two[rows:], same[3 * rows :])
-    return own, [sent(other) for other in others]
-
-
-def far_summed(own, others):
-    for other, steps in zip(others, (-4, 4, 8)):
-        own += received(moved(other, steps))
-    return own
+    return own, others, loss
+
+
+def far_summed(own, others, loss):
+    arrived = [moved(with_loss(other, loss), steps) for other, steps in zip(others, (-4, 4, 8))]
+    for part in arrived:
+        own = own + received(part[:-8])
+        loss = loss + loss_of(part)
+    return own, loss
 
 
 def shards(picture_vectors, caption_vectors, heat_exponent, offset_added):
     rows, width = picture_vectors.shape
-    plane, column = lax.axis_size(PLANE), lax.axis_size(COLUMN)
-    image_low, text_low, own_loss = unit_rows(heat_exponent, offset_added, picture_vectors, caption_vectors)
-
-    texts = lax.all_to_all(jnp.broadcast_to(text_low[None], (plane, *text_low.shape)), PLANE, 0, 0)
-    near, texts = ring_gathered(image_low, texts.reshape(plane * rows, width))
+    plane = lax.axis_size(PLANE)
+    image_low, text_low, own_loss = unit_rows(plane, heat_exponent, offset_added, picture_vectors, caption_vectors)
+
+    texts = lax.all_to_all(text_low, PLANE, 0, 0).reshape(plane * rows, width)
+    near, texts = ring_gathered(image_low, texts)
     far = swapped(near)
 
     place = (lax.axis_index(PLANE) * rows).astype(jnp.int32).reshape(1)
     weights, text_part = pair_terms(place, heat_exponent, offset_added, own_loss, near, far, texts)
     text_parts = lax.all_to_all(text_part.reshape(plane, rows, width + LANES), PLANE, 0, 0)
     near_part, far_part = image_terms(weights, texts)
-    own, others = near_summed(near_part + swapped(far_part), rows)
-    others, text_parts = lax.optimization_barrier((others, text_parts))
-    plane_loss = jnp.sum(text_parts[:, 0, width : width + 3].astype(jnp.float32))
-    losses = lax.all_to_all(jnp.broadcast_to(plane_loss, (column, 8, LANES)), COLUMN, 0, 0)
-    loss_mean = (jnp.sum(losses[:, 0, 0]) / (rows * lax.axis_size(AXES))).reshape(1)
+    image_part = near_part + swapped(far_part)
+    loss = jnp.tile(jnp.sum(text_parts[:, :4, width:].astype(jnp.float32), axis=0), (1, width // LANES))
     text_sum = jnp.sum(text_parts[:, :, :width].astype(jnp.float32), axis=0)
-    image_sum = far_summed(own, others)
+    image_sum, loss = far_summed(*near_summed(image_part, rows, loss))
+    loss = loss[:, :LANES]
+    total = jnp.sum((loss + swapped(loss))[0, :3])
+    loss_mean = (total / (rows * lax.axis_size(AXES))).reshape(1)
     image_grads, text_grads = gradients(
         heat_exponent, offset_added, picture_vectors, caption_vectors, image_sum, text_sum
     )

time: 145 us -> 149 us (1.028)
  blocking collectives: 0 us -> 21.7 us
  starting transfers between devices: 102 us -> 86.6 us
  waiting for transfers between devices: 19.2 us -> 24.9 us
  local copies, waits for them, and re-layouts: 3.41 us -> 0.19 us
  other arithmetic: 4.6 us -> 2.98 us
    all_to_all x0 -> x1, blocking collectives: none -> 21.7 us  [shards(): lax.all_to_all(text_part.reshape(plane, rows, width + LANES), PLANE, 0, 0)]
    all_to_all x3 -> x1, starting transfers between devices: 24.7 us -> 6.77 us  [shards(): texts = lax.all_to_all(text_low, PLANE, 0, 0).reshape(plane * rows, width)]
    ppermute x14, waiting for transfers between devices: 5.99 us -> 22.9 us  [moved(): lax.ppermute(value, RING, [(order[i], order[(i + steps) % count]) for i i...]
    all_to_all x3 -> x1, waiting for transfers between devices: 11.2 us -> 0.01 us  [shards(): texts = lax.all_to_all(text_low, PLANE, 0, 0).reshape(plane * rows, width)]
    broadcast_in_dim x2 -> x0, local copies, waits for them, and re-layouts: 3.13 us -> none  [the longest x1 1.81 us: shards(): jnp.broadcast_to(text_low[None], (plane, *text_low.shape))]
    ppermute x14, starting transfers between devices: 69.9 us -> 71.6 us  [moved(): lax.ppermute(value, RING, [(order[i], order[(i + steps) % count]) for i i...]
    convert_element_type x2 -> x3, other arithmetic: 1.74 us -> 0.17 us  [sent(): return (value * HALF).astype(jnp.float16)]
    ppermute x2 -> x3, starting transfers between devices: 7.9 us -> 8.24 us  [swapped(): return lax.ppermute(value, 'c', [(0, 1), (1, 0)])]
  transfers between devices with their start and end apart: 19 -> 18, of which waited for: 5 -> 7; matrix products, arithmetic and copies ran while one was open for 5% -> 1% of each run, Pallas kernels for 1% -> 1%
where the time goes in v5:
time: 149 us
  starting transfers between devices  86.6 us (58%)
  waiting for transfers between devices  24.9 us (17%)
  blocking collectives  21.7 us (15%)
  Pallas kernels  8.01 us (5%)
  between operations  4.09 us (3%)
  other arithmetic  2.98 us (2%)
    ppermute x14, starting transfers between devices, moved(): lax.ppermute(value, RING, [(order[i], order[(i + steps) % count]) for i i...  71.6 us
    ppermute x14, waiting for transfers between devices, moved(): lax.ppermute(value, RING, [(order[i], order[(i + steps) % count]) for i i...  22.9 us
    all_to_all x1, blocking collectives, shards(): lax.all_to_all(text_part.reshape(plane, rows, width + LANES), PLANE, 0, 0)  21.7 us
    ppermute x3, starting transfers between devices, swapped(): return lax.ppermute(value, 'c', [(0, 1), (1, 0)])  8.24 us
    all_to_all x1, starting transfers between devices, shards(): texts = lax.all_to_all(text_low, PLANE, 0, 0).reshape(plane * rows, width)  6.77 us
  transfers between devices with their start and end apart: 18, of which 7 were waited for; matrix products, arithmetic and copies ran while one was open for 1% of the time, Pallas kernels for 1%

profile of v5, /device:TPU:1, one launch (start us, length us, event | category | flops | bytes accessed | tf_op | source)
XLA Modules:
  0.0 148.5 jit_solution(5248845555591348304)
XLA Ops:
  1.9 2.0 %shard_map.67 = (bf16[24,1152]{1,0:T(8,128)(2,1)}, bf16[16,24,1152]{2,1,0:T(8,128)(2,1)}, f32[24,1]{1,0:T(8,128)}) custom-call(f32[1]{0:T(128)S(6)} %copy.22.heat_ref, f32[1]{0:T(128)S(6)} %copy.23.offset_ref, f32[24,1152]{1,0:T(8,128)} %picture_ref.3, f32[24,1152]{1,0:T(8,128)} %caption_ref.3), custom_call_target="tpu_custom_call" | custom-call | tf_op jit(solution)/shard_map/pallas_call | solution.py:56
  4.0 0.0 copy-start.1
  4.0 9.8 %collective-permute-start = (bf16[24,1152]{1,0:T(8,128)(2,1)}, bf16[24,1152]{1,0:T(8,128)(2,1)S(1)}, u32[]{:S(2)}, u32[]{:S(2)}) collective-permute-start(bf16[24,1152]{1,0:T(8,128)(2,1)} %get-tuple-element.15), channel_id=1, source_target_pairs={{0,256},{64,320},{128,384},{192,448},{256,1},{320,65},{384,129},{4... | collective-permute-start | bytes 165896 | tf_op jit(solution)/shard_map/ppermute | solution.py:173
  13.7 10.6 %collective-permute-start.2 = (bf16[24,1152]{1,0:T(8,128)(2,1)}, bf16[24,1152]{1,0:T(8,128)(2,1)S(1)}, u32[]{:S(2)}, u32[]{:S(2)}) collective-permute-start(bf16[24,1152]{1,0:T(8,128)(2,1)} %get-tuple-element.15), channel_id=1, source_target_pairs={{0,1},{64,65},{128,129},{192,193},{256,257},{320,321},{384,385},{4... | collective-permute-start | bytes 165896 | tf_op jit(solution)/shard_map/ppermute | solution.py:173
  24.4 5.2 %collective-permute-start.1 = (bf16[24,1152]{1,0:T(8,128)(2,1)}, bf16[24,1152]{1,0:T(8,128)(2,1)S(1)}, u32[]{:S(2)}, u32[]{:S(2)}) collective-permute-start(bf16[24,1152]{1,0:T(8,128)(2,1)} %get-tuple-element.15), channel_id=1, source_target_pairs={{0,257},{64,321},{128,385},{192,449},{256,0},{320,64},{384,128},{4... | collective-permute-start | bytes 165896 | tf_op jit(solution)/shard_map/ppermute | solution.py:173
  29.6 0.0 copy-start
  29.6 6.8 %all-to-all-start = ((bf16[16,24,1152]{2,1,0:T(8,128)(2,1)}), bf16[16,24,1152]{2,1,0:T(8,128)(2,1)S(1)}, u32[]{:S(2)}, u32[]{:S(2)}) async-start(bf16[16,24,1152]{2,1,0:T(8,128)(2,1)} %get-tuple-element.16), calls=%async_computation | async-start | bytes 1769472 | tf_op jit(solution)/shard_map/all_to_all | solution.py:239
  36.4 0.0 collective-permute-done
  36.4 0.0 copy-done.1
  36.4 0.6 collective-permute-done.1
  37.0 0.0 collective-permute-done.2
  37.0 2.1 %collective-permute-start.4 = (bf16[96,1152]{1,0:T(8,128)(2,1)S(1)}, bf16[96,1152]{1,0:T(8,128)(2,1)S(1)}, u32[]{:S(2)}, u32[]{:S(2)}) collective-permute-start(bf16[96,1152]{1,0:T(8,128)(2,1)S(1)} %get-tuple-element.42), channel_id=1, source_target_pairs={{0,64},{64,128},{128,192},{192,256},{256,320},{320,384},{384,448},... | collective-permute-start | bytes 663560 | tf_op jit(solution)/shard_map/ppermute | solution.py:173
  39.1 4.4 %collective-permute-start.3 = (bf16[96,1152]{1,0:T(8,128)(2,1)S(1)}, bf16[96,1152]{1,0:T(8,128)(2,1)S(1)}, u32[]{:S(2)}, u32[]{:S(2)}) collective-permute-start(bf16[96,1152]{1,0:T(8,128)(2,1)S(1)} %get-tuple-element.42), channel_id=1, source_target_pairs={{0,449},{64,0},{128,64},{192,128},{256,192},{320,256},{384,320},{4... | collective-permute-start | bytes 663560 | tf_op jit(solution)/shard_map/ppermute | solution.py:173
  43.6 1.9 %collective-permute-start.6 = (bf16[48,1152]{1,0:T(8,128)(2,1)S(1)}, bf16[48,1152]{1,0:T(8,128)(2,1)S(1)}, u32[]{:S(2)}, u32[]{:S(2)}) collective-permute-start(bf16[48,1152]{1,0:T(8,128)(2,1)S(1)} %get-tuple-element.40), channel_id=1, source_target_pairs={{0,128},{64,192},{128,256},{192,320},{256,384},{320,448},{384,1},{... | collective-permute-start | bytes 331784 | tf_op jit(solution)/shard_map/ppermute | solution.py:173
  45.5 5.5 %collective-permute-start.5 = (bf16[48,1152]{1,0:T(8,128)(2,1)S(1)}, bf16[48,1152]{1,0:T(8,128)(2,1)S(1)}, u32[]{:S(2)}, u32[]{:S(2)}) collective-permute-start(bf16[48,1152]{1,0:T(8,128)(2,1)S(1)} %get-tuple-element.41), channel_id=1, source_target_pairs={{0,385},{64,449},{128,0},{192,64},{256,128},{320,192},{384,256},{4... | collective-permute-start | bytes 331784 | tf_op jit(solution)/shard_map/ppermute | solution.py:173
  51.0 0.0 collective-permute-done.3
  51.0 0.0 collective-permute-done.4
  51.1 4.5 %collective-permute-done.5 = bf16[48,1152]{1,0:T(8,128)(2,1)S(1)} collective-permute-done((bf16[48,1152]{1,0:T(8,128)(2,1)S(1)}, bf16[48,1152]{1,0:T(8,128)(2,1)S(1)}, u32[]{:S(2)}, u32[]{:S(2)}) %collective-permute-start.5) | collective-permute-done | bytes 110624 | tf_op jit(solution)/shard_map/ppermute | solution.py:173
  55.6 0.0 collective-permute-done.6
  55.6 0.0 all-to-all-done
  55.6 3.5 %collective-permute-start.7 = (bf16[384,1152]{1,0:T(8,128)(2,1)S(1)}, bf16[384,1152]{1,0:T(8,128)(2,1)S(1)}, u32[]{:S(2)}, u32[]{:S(2)}) collective-permute-start(bf16[384,1152]{1,0:T(8,128)(2,1)S(1)} %constant_dynamic-update-slice_fusion.4.near_ref), channel_id=1, source_target_pairs={{0,8},{8,0},{1,9},{9,1},{2,10},{10,2},{3,11},{11,3},{4,12},{12,4},... | collective-permute-start | bytes 2654216 | tf_op jit(solution)/shard_map/ppermute | solution.py:185
  59.1 2.0 %collective-permute-done.7.far_ref = bf16[384,1152]{1,0:T(8,128)(2,1)S(1)} collective-permute-done((bf16[384,1152]{1,0:T(8,128)(2,1)S(1)}, bf16[384,1152]{1,0:T(8,128)(2,1)S(1)}, u32[]{:S(2)}, u32[]{:S(2)}) %collective-permute-start.7) | collective-permute-done | bytes 884768 | tf_op jit(solution)/shard_map/ppermute | solution.py:185
  61.1 0.0 copy-done
  61.1 2.8 %shard_map.68 = (bf16[768,384]{1,0:T(8,128)(2,1)S(1)}, bf16[384,1280]{1,0:T(8,128)(2,1)S(1)}) custom-call(s32[1]{0:T(128)} %bitcast.place_ref, f32[1]{0:T(128)S(6)} %copy.22.heat_ref, f32[1]{0:T(128)S(6)} %copy.23.offset_ref, f32[24,1]{1,0:T(8,128)S(1)} %copy-done, bf16[384,1152]{1,0:T(8,128)(2,1)S(1)} %constant_dynamic-update-slice_fusion.4.near_ref, ...), custom_call_target="tpu_custom_call" | custom-call | flops 1358954496 | bytes 3538944 | tf_op jit(solution)/shard_map/pallas_call | solution.py:114
  63.9 1.1 shard_map.69
  65.0 2.3 %collective-permute-start.8 = (f32[384,1152]{1,0:T(8,128)S(1)}, f32[384,1152]{1,0:T(8,128)S(1)}, u32[]{:S(2)}, u32[]{:S(2)}) collective-permute-start(f32[384,1152]{1,0:T(8,128)S(1)} %get-tuple-element.22), channel_id=1, source_target_pairs={{0,8},{8,0},{1,9},{9,1},{2,10},{10,2},{3,11},{11,3},{4,12},{12,4},... | collective-permute-start | bytes 5308424 | tf_op jit(solution)/shard_map/ppermute | solution.py:185
  67.3 21.7 %all_to_all.10 = bf16[16,24,1280]{2,1,0:T(8,128)(2,1)S(1)} all-to-all(bf16[16,24,1280]{2,1,0:T(8,128)(2,1)S(1)} %bitcast.20), channel_id=1, replica_groups=mesh['zl'=8,'x'=4,'c'=2,'y'=4,'zh'=2] {'x','y'}, dimensions={0} | all-to-all | bytes 1966080 | tf_op jit(solution)/shard_map/all_to_all | solution.py:245
  89.1 0.0 collective-permute-done.8
  89.1 0.2 add.73
  89.4 0.1 fusion.2
  89.5 5.2 %collective-permute-start.12 = (f16[48,1152]{1,0:T(8,128)(2,1)S(1)}, f16[48,1152]{1,0:T(8,128)(2,1)S(1)}, u32[]{:S(2)}, u32[]{:S(2)}) collective-permute-start(f16[48,1152]{1,0:T(8,128)(2,1)S(1)} %get-tuple-element.27), channel_id=1, source_target_pairs={{0,385},{64,449},{128,0},{192,64},{256,128},{320,192},{384,256},{4... | collective-permute-start | bytes 331784 | tf_op jit(solution)/shard_map/ppermute | solution.py:173
  94.7 0.1 pad_maximum_fusion.4
  94.7 1.9 %collective-permute-start.11 = (f16[56,1152]{1,0:T(8,128)(2,1)S(1)}, f16[56,1152]{1,0:T(8,128)(2,1)S(1)}, u32[]{:S(2)}, u32[]{:S(2)}) collective-permute-start(f16[56,1152]{1,0:T(8,128)(2,1)S(1)} %pad_maximum_fusion.4), channel_id=1, source_target_pairs={{0,128},{64,192},{128,256},{192,320},{256,384},{320,448},{384,1},{... | collective-permute-start | bytes 387080 | tf_op jit(solution)/shard_map/ppermute | solution.py:173
  96.6 0.1 pad_maximum_fusion.1
  96.8 2.3 %collective-permute-start.9 = (f16[104,1152]{1,0:T(8,128)(2,1)S(1)}, f16[104,1152]{1,0:T(8,128)(2,1)S(1)}, u32[]{:S(2)}, u32[]{:S(2)}) collective-permute-start(f16[104,1152]{1,0:T(8,128)(2,1)S(1)} %get-tuple-element.55), channel_id=1, source_target_pairs={{0,64},{64,128},{128,192},{192,256},{256,320},{320,384},{384,448},... | collective-permute-start | bytes 718856 | tf_op jit(solution)/shard_map/ppermute | solution.py:173
  99.1 4.3 %collective-permute-start.10 = (f16[104,1152]{1,0:T(8,128)(2,1)S(1)}, f16[104,1152]{1,0:T(8,128)(2,1)S(1)}, u32[]{:S(2)}, u32[]{:S(2)}) collective-permute-start(f16[104,1152]{1,0:T(8,128)(2,1)S(1)} %get-tuple-element.56), channel_id=1, source_target_pairs={{0,449},{64,0},{128,64},{192,128},{256,192},{320,256},{384,320},{4... | collective-permute-start | bytes 718856 | tf_op jit(solution)/shard_map/ppermute | solution.py:173
  103.4 0.0 collective-permute-done.12
  103.5 0.5 collective-permute-done.11
  104.0 5.2 %collective-permute-done.9 = f16[104,1152]{1,0:T(8,128)(2,1)S(1)} collective-permute-done((f16[104,1152]{1,0:T(8,128)(2,1)S(1)}, f16[104,1152]{1,0:T(8,128)(2,1)S(1)}, u32[]{:S(2)}, u32[]{:S(2)}) %collective-permute-start.9) | collective-permute-done | bytes 239648 | tf_op jit(solution)/shard_map/ppermute | solution.py:173
  109.2 0.0 collective-permute-done.10
  109.3 0.1 fusion
  109.5 0.1 pad_maximum_fusion.6
  109.5 5.7 %collective-permute-start.14 = (f16[32,1152]{1,0:T(8,128)(2,1)S(1)}, f16[32,1152]{1,0:T(8,128)(2,1)S(1)}, u32[]{:S(2)}, u32[]{:S(2)}) collective-permute-start(f16[32,1152]{1,0:T(8,128)(2,1)S(1)} %get-tuple-element.52), channel_id=1, source_target_pairs={{0,256},{64,320},{128,384},{192,448},{256,1},{320,65},{384,129},{4... | collective-permute-start | bytes 221192 | tf_op jit(solution)/shard_map/ppermute | solution.py:173
  115.3 0.8 convert_reduce_fusion.text_sum_ref
  116.1 6.6 %collective-permute-start.15 = (f16[32,1152]{1,0:T(8,128)(2,1)S(1)}, f16[32,1152]{1,0:T(8,128)(2,1)S(1)}, u32[]{:S(2)}, u32[]{:S(2)}) collective-permute-start(f16[32,1152]{1,0:T(8,128)(2,1)S(1)} %get-tuple-element.53), channel_id=1, source_target_pairs={{0,1},{64,65},{128,129},{192,193},{256,257},{320,321},{384,385},{4... | collective-permute-start | bytes 221192 | tf_op jit(solution)/shard_map/ppermute | solution.py:173
  122.7 6.1 %collective-permute-start.13 = (f16[32,1152]{1,0:T(8,128)(2,1)S(1)}, f16[32,1152]{1,0:T(8,128)(2,1)S(1)}, u32[]{:S(2)}, u32[]{:S(2)}) collective-permute-start(f16[32,1152]{1,0:T(8,128)(2,1)S(1)} %get-tuple-element.54), channel_id=1, source_target_pairs={{0,257},{64,321},{128,385},{192,449},{256,0},{320,64},{384,128},{4... | collective-permute-start | bytes 221192 | tf_op jit(solution)/shard_map/ppermute | solution.py:173
  128.8 0.0 collective-permute-done.14
  128.8 1.4 collective-permute-done.15
  130.2 10.7 %collective-permute-done.13 = f16[32,1152]{1,0:T(8,128)(2,1)S(1)} collective-permute-done((f16[32,1152]{1,0:T(8,128)(2,1)S(1)}, f16[32,1152]{1,0:T(8,128)(2,1)S(1)}, u32[]{:S(2)}, u32[]{:S(2)}) %collective-permute-start.13) | collective-permute-done | bytes 73760 | tf_op jit(solution)/shard_map/ppermute | solution.py:173
  140.9 2.5 %collective-permute-start.16 = (f32[4,128]{1,0:T(4,128)S(1)}, f32[4,128]{1,0:T(4,128)S(1)}, u32[]{:S(2)}, u32[]{:S(2)}) collective-permute-start(f32[4,128]{1,0:T(4,128)S(1)} %fusion.17), channel_id=1, source_target_pairs={{0,8},{8,0},{1,9},{9,1},{2,10},{10,2},{3,11},{11,3},{4,12},{12,4},... | collective-permute-start | bytes 6152 | tf_op jit(solution)/shard_map/ppermute | solution.py:185
  143.4 0.7 fusion.7.image_sum_ref
  144.1 2.1 %shard_map.70 = (f32[24,1152]{1,0:T(8,128)}, f32[24,1152]{1,0:T(8,128)}) custom-call(f32[1]{0:T(128)S(6)} %copy.22.heat_ref, f32[1]{0:T(128)S(6)} %copy.23.offset_ref, f32[24,1152]{1,0:T(8,128)} %picture_ref.3, f32[24,1152]{1,0:T(8,128)} %caption_ref.3, f32[24,1152]{1,0:T(8,128)} %fusion.7.image_sum_ref, f32[24,1152]{1,0:T(8,128)} %convert_reduce_fusion.text_sum_ref), custom_call_target="tpu_custom_call" | custom-call | tf_op jit(solution)/shard_map/pallas_call | solution.py:162
  146.1 0.0 collective-permute-done.16
  146.2 0.6 slice_reduce_fusion
  (23 shorter events, 0.5 us)
Async XLA Ops:
  4.0 32.4 %copy-start.1 = (bf16[24,1152]{1,0:T(8,128)(2,1)S(1)}, bf16[24,1152]{1,0:T(8,128)(2,1)}, u32[]{:S(2)}) copy-start(bf16[24,1152]{1,0:T(8,128)(2,1)} %get-tuple-element.15) | copy-start | bytes 165892
  4.0 32.4 %collective-permute-start = (bf16[24,1152]{1,0:T(8,128)(2,1)}, bf16[24,1152]{1,0:T(8,128)(2,1)S(1)}, u32[]{:S(2)}, u32[]{:S(2)}) collective-permute-start(bf16[24,1152]{1,0:T(8,128)(2,1)} %get-tuple-element.15), channel_id=1, source_target_pairs={{0,256},{64,320},{128,384},{192,448},{256,1},{320,65},{384,129},{4... | collective-permute-start | bytes 165896 | tf_op jit(solution)/shard_map/ppermute | solution.py:173
  13.7 23.3 %collective-permute-start.2 = (bf16[24,1152]{1,0:T(8,128)(2,1)}, bf16[24,1152]{1,0:T(8,128)(2,1)S(1)}, u32[]{:S(2)}, u32[]{:S(2)}) collective-permute-start(bf16[24,1152]{1,0:T(8,128)(2,1)} %get-tuple-element.15), channel_id=1, source_target_pairs={{0,1},{64,65},{128,129},{192,193},{256,257},{320,321},{384,385},{4... | collective-permute-start | bytes 165896 | tf_op jit(solution)/shard_map/ppermute | solution.py:173
  24.4 12.6 %collective-permute-start.1 = (bf16[24,1152]{1,0:T(8,128)(2,1)}, bf16[24,1152]{1,0:T(8,128)(2,1)S(1)}, u32[]{:S(2)}, u32[]{:S(2)}) collective-permute-start(bf16[24,1152]{1,0:T(8,128)(2,1)} %get-tuple-element.15), channel_id=1, source_target_pairs={{0,257},{64,321},{128,385},{192,449},{256,0},{320,64},{384,128},{4... | collective-permute-start | bytes 165896 | tf_op jit(solution)/shard_map/ppermute | solution.py:173
  29.6 31.6 %copy-start = (f32[24,1]{1,0:T(8,128)S(1)}, f32[24,1]{1,0:T(8,128)}, u32[]{:S(2)}) copy-start(f32[24,1]{1,0:T(8,128)} %get-tuple-element.14.own_loss_ref) | copy-start | bytes 292
  29.6 26.0 %all-to-all-start = ((bf16[16,24,1152]{2,1,0:T(8,128)(2,1)}), bf16[16,24,1152]{2,1,0:T(8,128)(2,1)S(1)}, u32[]{:S(2)}, u32[]{:S(2)}) async-start(bf16[16,24,1152]{2,1,0:T(8,128)(2,1)} %get-tuple-element.16), calls=%async_computation | async-start | bytes 1769472 | tf_op jit(solution)/shard_map/all_to_all | solution.py:239
  37.0 14.0 %collective-permute-start.4 = (bf16[96,1152]{1,0:T(8,128)(2,1)S(1)}, bf16[96,1152]{1,0:T(8,128)(2,1)S(1)}, u32[]{:S(2)}, u32[]{:S(2)}) collective-permute-start(bf16[96,1152]{1,0:T(8,128)(2,1)S(1)} %get-tuple-element.42), channel_id=1, source_target_pairs={{0,64},{64,128},{128,192},{192,256},{256,320},{320,384},{384,448},... | collective-permute-start | bytes 663560 | tf_op jit(solution)/shard_map/ppermute | solution.py:173
  39.1 11.8 %collective-permute-start.3 = (bf16[96,1152]{1,0:T(8,128)(2,1)S(1)}, bf16[96,1152]{1,0:T(8,128)(2,1)S(1)}, u32[]{:S(2)}, u32[]{:S(2)}) collective-permute-start(bf16[96,1152]{1,0:T(8,128)(2,1)S(1)} %get-tuple-element.42), channel_id=1, source_target_pairs={{0,449},{64,0},{128,64},{192,128},{256,192},{320,256},{384,320},{4... | collective-permute-start | bytes 663560 | tf_op jit(solution)/shard_map/ppermute | solution.py:173
  43.6 12.0 %collective-permute-start.6 = (bf16[48,1152]{1,0:T(8,128)(2,1)S(1)}, bf16[48,1152]{1,0:T(8,128)(2,1)S(1)}, u32[]{:S(2)}, u32[]{:S(2)}) collective-permute-start(bf16[48,1152]{1,0:T(8,128)(2,1)S(1)} %get-tuple-element.40), channel_id=1, source_target_pairs={{0,128},{64,192},{128,256},{192,320},{256,384},{320,448},{384,1},{... | collective-permute-start | bytes 331784 | tf_op jit(solution)/shard_map/ppermute | solution.py:173
  45.5 10.1 %collective-permute-start.5 = (bf16[48,1152]{1,0:T(8,128)(2,1)S(1)}, bf16[48,1152]{1,0:T(8,128)(2,1)S(1)}, u32[]{:S(2)}, u32[]{:S(2)}) collective-permute-start(bf16[48,1152]{1,0:T(8,128)(2,1)S(1)} %get-tuple-element.41), channel_id=1, source_target_pairs={{0,385},{64,449},{128,0},{192,64},{256,128},{320,192},{384,256},{4... | collective-permute-start | bytes 331784 | tf_op jit(solution)/shard_map/ppermute | solution.py:173
  55.6 5.5 %collective-permute-start.7 = (bf16[384,1152]{1,0:T(8,128)(2,1)S(1)}, bf16[384,1152]{1,0:T(8,128)(2,1)S(1)}, u32[]{:S(2)}, u32[]{:S(2)}) collective-permute-start(bf16[384,1152]{1,0:T(8,128)(2,1)S(1)} %constant_dynamic-update-slice_fusion.4.near_ref), channel_id=1, source_target_pairs={{0,8},{8,0},{1,9},{9,1},{2,10},{10,2},{3,11},{11,3},{4,12},{12,4},... | collective-permute-start | bytes 2654216 | tf_op jit(solution)/shard_map/ppermute | solution.py:185
  65.0 24.1 %collective-permute-start.8 = (f32[384,1152]{1,0:T(8,128)S(1)}, f32[384,1152]{1,0:T(8,128)S(1)}, u32[]{:S(2)}, u32[]{:S(2)}) collective-permute-start(f32[384,1152]{1,0:T(8,128)S(1)} %get-tuple-element.22), channel_id=1, source_target_pairs={{0,8},{8,0},{1,9},{9,1},{2,10},{10,2},{3,11},{11,3},{4,12},{12,4},... | collective-permute-start | bytes 5308424 | tf_op jit(solution)/shard_map/ppermute | solution.py:185
  89.5 14.0 %collective-permute-start.12 = (f16[48,1152]{1,0:T(8,128)(2,1)S(1)}, f16[48,1152]{1,0:T(8,128)(2,1)S(1)}, u32[]{:S(2)}, u32[]{:S(2)}) collective-permute-start(f16[48,1152]{1,0:T(8,128)(2,1)S(1)} %get-tuple-element.27), channel_id=1, source_target_pairs={{0,385},{64,449},{128,0},{192,64},{256,128},{320,192},{384,256},{4... | collective-permute-start | bytes 331784 | tf_op jit(solution)/shard_map/ppermute | solution.py:173
  94.7 9.3 %collective-permute-start.11 = (f16[56,1152]{1,0:T(8,128)(2,1)S(1)}, f16[56,1152]{1,0:T(8,128)(2,1)S(1)}, u32[]{:S(2)}, u32[]{:S(2)}) collective-permute-start(f16[56,1152]{1,0:T(8,128)(2,1)S(1)} %pad_maximum_fusion.4), channel_id=1, source_target_pairs={{0,128},{64,192},{128,256},{192,320},{256,384},{320,448},{384,1},{... | collective-permute-start | bytes 387080 | tf_op jit(solution)/shard_map/ppermute | solution.py:173
  96.8 12.4 %collective-permute-start.9 = (f16[104,1152]{1,0:T(8,128)(2,1)S(1)}, f16[104,1152]{1,0:T(8,128)(2,1)S(1)}, u32[]{:S(2)}, u32[]{:S(2)}) collective-permute-start(f16[104,1152]{1,0:T(8,128)(2,1)S(1)} %get-tuple-element.55), channel_id=1, source_target_pairs={{0,64},{64,128},{128,192},{192,256},{256,320},{320,384},{384,448},... | collective-permute-start | bytes 718856 | tf_op jit(solution)/shard_map/ppermute | solution.py:173
  99.1 10.1 %collective-permute-start.10 = (f16[104,1152]{1,0:T(8,128)(2,1)S(1)}, f16[104,1152]{1,0:T(8,128)(2,1)S(1)}, u32[]{:S(2)}, u32[]{:S(2)}) collective-permute-start(f16[104,1152]{1,0:T(8,128)(2,1)S(1)} %get-tuple-element.56), channel_id=1, source_target_pairs={{0,449},{64,0},{128,64},{192,128},{256,192},{320,256},{384,320},{4... | collective-permute-start | bytes 718856 | tf_op jit(solution)/shard_map/ppermute | solution.py:173
  109.5 19.2 %collective-permute-start.14 = (f16[32,1152]{1,0:T(8,128)(2,1)S(1)}, f16[32,1152]{1,0:T(8,128)(2,1)S(1)}, u32[]{:S(2)}, u32[]{:S(2)}) collective-permute-start(f16[32,1152]{1,0:T(8,128)(2,1)S(1)} %get-tuple-element.52), channel_id=1, source_target_pairs={{0,256},{64,320},{128,384},{192,448},{256,1},{320,65},{384,129},{4... | collective-permute-start | bytes 221192 | tf_op jit(solution)/shard_map/ppermute | solution.py:173
  116.1 14.1 %collective-permute-start.15 = (f16[32,1152]{1,0:T(8,128)(2,1)S(1)}, f16[32,1152]{1,0:T(8,128)(2,1)S(1)}, u32[]{:S(2)}, u32[]{:S(2)}) collective-permute-start(f16[32,1152]{1,0:T(8,128)(2,1)S(1)} %get-tuple-element.53), channel_id=1, source_target_pairs={{0,1},{64,65},{128,129},{192,193},{256,257},{320,321},{384,385},{4... | collective-permute-start | bytes 221192 | tf_op jit(solution)/shard_map/ppermute | solution.py:173
  122.7 18.2 %collective-permute-start.13 = (f16[32,1152]{1,0:T(8,128)(2,1)S(1)}, f16[32,1152]{1,0:T(8,128)(2,1)S(1)}, u32[]{:S(2)}, u32[]{:S(2)}) collective-permute-start(f16[32,1152]{1,0:T(8,128)(2,1)S(1)} %get-tuple-element.54), channel_id=1, source_target_pairs={{0,257},{64,321},{128,385},{192,449},{256,0},{320,64},{384,128},{4... | collective-permute-start | bytes 221192 | tf_op jit(solution)/shard_map/ppermute | solution.py:173
  140.9 5.3 %collective-permute-start.16 = (f32[4,128]{1,0:T(4,128)S(1)}, f32[4,128]{1,0:T(4,128)S(1)}, u32[]{:S(2)}, u32[]{:S(2)}) collective-permute-start(f32[4,128]{1,0:T(4,128)S(1)} %fusion.17), channel_id=1, source_target_pairs={{0,8},{8,0},{1,9},{9,1},{2,10},{10,2},{3,11},{11,3},{4,12},{12,4},... | collective-permute-start | bytes 6152 | tf_op jit(solution)/shard_map/ppermute | solution.py:185

commit v6 on v3

v6 whole, which is shorter than its diff:
```python
import jax
import jax.numpy as jnp
from jax import lax
from jax.experimental import pallas as pl
from jax.experimental.pallas import tpu as pltpu
from jax.sharding import Mesh, PartitionSpec as P

epsilon = 1e-06
AXES = ("zl", "x", "c", "y", "zh")
SIZES = (8, 4, 2, 4, 2)
PLANE = ("x", "y")
LANES = 128
LIMIT = 20 * 1024 * 1024
HALF = 0.5


def normalize(raw_rows):
    row_norm = jnp.sqrt(jnp.sum(raw_rows * raw_rows, axis=1, keepdims=True) + epsilon)
    return (raw_rows / row_norm, row_norm)


def back_norm(unit_rows, row_norm, gradient):
    return (gradient - unit_rows * jnp.sum(unit_rows * gradient, axis=1, keepdims=True)) / row_norm


def low(rows):
    return rows.astype(jnp.bfloat16).astype(jnp.float32)


def loss_and_sigmoid(values):
    small = jnp.exp(-jnp.abs(values))
    loss = jnp.maximum(values, 0.0) + jnp.log1p(small)
    return loss, jnp.where(values >= 0, 1.0, small) / (1.0 + small)


def own_pairs(image_low, text_low, heat, offset):
    return jnp.sum(image_low * text_low, axis=1, keepdims=True) * heat + offset


def unit_kernel(heat_ref, offset_ref, picture_ref, caption_ref, image_ref, text_ref, loss_ref):
    image_unit, _ = normalize(picture_ref[...])
    text_unit, _ = normalize(caption_ref[...])
    image_low, text_low = image_unit.astype(jnp.bfloat16), text_unit.astype(jnp.bfloat16)
    image_ref[...] = image_low
    text_ref[...] = text_low
    heat = jnp.exp(jnp.full((1, 1), heat_ref[0], jnp.float32))
    logits = own_pairs(image_low.astype(jnp.float32), text_low.astype(jnp.float32), heat, offset_ref[0])
    loss, _ = loss_and_sigmoid(-logits)
    loss_ref[...] = loss


def unit_rows(heat_exponent, offset_added, pictures, captions):
    rows = pictures.shape[0]
    return pl.pallas_call(
        unit_kernel,
        in_specs=[pl.BlockSpec(memory_space=pltpu.SMEM)] * 2 + [pl.BlockSpec(memory_space=pltpu.VMEM)] * 2,
        out_shape=[
            jax.ShapeDtypeStruct(pictures.shape, jnp.bfloat16),
            jax.ShapeDtypeStruct(captions.shape, jnp.bfloat16),
            jax.ShapeDtypeStruct((rows, 1), jnp.float32),
        ],
    )(heat_exponent, offset_added, pictures, captions)


def pair_kernel(place_ref, heat_ref, offset_ref, own_loss_ref, near_ref, far_ref, text_ref, weight_ref, loss_ref):
    rows = own_loss_ref.shape[0]
    half = near_ref.shape[0]
    texts = text_ref[...]
    heat = jnp.exp(jnp.full((1, 1), heat_ref[0], jnp.float32))
    total = jnp.sum(own_loss_ref[...], axis=0, keepdims=True)
    for place, image_ref in enumerate((near_ref, far_ref)):
        logits = lax.dot_general(
            image_ref[...], texts, (((1,), (1,)), ((), ())), preferred_element_type=jnp.float32
        )
        logits = logits * heat + offset_ref[0]
        loss, sigmoid = loss_and_sigmoid(logits)
        weights = heat * sigmoid
        if image_ref is near_ref:
            image_row = lax.broadcasted_iota(jnp.int32, logits.shape, 0)
            text_row = lax.broadcasted_iota(jnp.int32, logits.shape, 1) - place_ref[0]
            match = (image_row == text_row) & (image_row < rows)
            weights = jnp.where(match, 0.0, weights)
            loss = jnp.where(match, 0.0, loss)
        weight_ref[place * half : (place + 1) * half] = weights.astype(jnp.bfloat16)
        total += jnp.sum(jnp.sum(loss, axis=0, keepdims=True), axis=1, keepdims=True)
    loss_ref[...] = jnp.broadcast_to(total[None], loss_ref.shape)


def pair_weights(copies, place, heat_exponent, offset_added, own_loss, near, far, texts):
    half, width = near.shape
    count = texts.shape[0]
    return pl.pallas_call(
        pair_kernel,
        in_specs=[pl.BlockSpec(memory_space=pltpu.SMEM)] * 3 + [pl.BlockSpec(memory_space=pltpu.VMEM)] * 4,
        out_shape=[
            jax.ShapeDtypeStruct((2 * half, count), jnp.bfloat16),
            jax.ShapeDtypeStruct((copies, 8, LANES), jnp.float32),
        ],
        compiler_params=pltpu.CompilerParams(vmem_limit_bytes=LIMIT),
        cost_estimate=pl.CostEstimate(
            flops=4 * half * count * width, bytes_accessed=8 * half * width, transcendentals=6 * half * count
        ),
    )(place, heat_exponent, offset_added, own_loss, near, far, texts)


def terms_kernel(weight_ref, near_ref, far_ref, text_ref, near_out_ref, far_out_ref, own_out_ref, other_out_ref):
    half = near_ref.shape[0]
    rows = own_out_ref.shape[1]
    texts = text_ref[...]
    far_out_ref[...] = jnp.dot(weight_ref[half:], texts, preferred_element_type=jnp.float32)
    near_out_ref[...] = jnp.dot(weight_ref[:half], texts, preferred_element_type=jnp.float32)
    text_part = lax.dot_general(
        weight_ref[:half], near_ref[...], (((0,), (0,)), ((), ())), preferred_element_type=jnp.float32
    )
    text_part += lax.dot_general(
        weight_ref[half:], far_ref[...], (((0,), (0,)), ((), ())), preferred_element_type=jnp.float32
    )
    for place in range(own_out_ref.shape[0]):
        start = 2 * place * rows
        own_out_ref[place] = text_part[start : start + rows].astype(jnp.bfloat16)
        other_out_ref[place] = text_part[start + rows : start + 2 * rows].astype(jnp.bfloat16)


def pair_terms(copies, weights, near, far, texts):
    block = jax.ShapeDtypeStruct((copies, texts.shape[0] // copies // 2, texts.shape[1]), jnp.bfloat16)
    return pl.pallas_call(
        terms_kernel,
        in_specs=[pl.BlockSpec(memory_space=pltpu.VMEM)] * 4,
        out_shape=[
            jax.ShapeDtypeStruct(near.shape, jnp.float32),
            jax.ShapeDtypeStruct(far.shape, jnp.float32),
            block,
            block,
        ],
        compiler_params=pltpu.CompilerParams(vmem_limit_bytes=LIMIT),
        cost_estimate=pl.CostEstimate(
            flops=4 * weights.size * near.shape[1], bytes_accessed=16 * near.size, transcendentals=0
        ),
    )(weights, near, far, texts)


def grad_kernel(
    heat_ref, offset_ref, picture_ref, caption_ref, image_sum_ref, text_sum_ref, image_ref, text_ref
):
    image_unit, image_norm = normalize(picture_ref[...])
    text_unit, text_norm = normalize(caption_ref[...])
    image_low, text_low = low(image_unit), low(text_unit)
    heat = jnp.exp(jnp.full((1, 1), heat_ref[0], jnp.float32))
    _, sigmoid = loss_and_sigmoid(-own_pairs(image_low, text_low, heat, offset_ref[0]))
    weights = low(-sigmoid * heat)
    image_ref[...] = back_norm(image_unit, image_norm, image_sum_ref[...] + weights * text_low)
    text_ref[...] = back_norm(text_unit, text_norm, text_sum_ref[...] + weights * image_low)


def gradients(heat_exponent, offset_added, pictures, captions, image_sum, text_sum):
    return pl.pallas_call(
        grad_kernel,
        in_specs=[pl.BlockSpec(memory_space=pltpu.SMEM)] * 2 + [pl.BlockSpec(memory_space=pltpu.VMEM)] * 4,
        out_shape=[jax.ShapeDtypeStruct(pictures.shape, jnp.float32)] * 2,
    )(heat_exponent, offset_added, pictures, captions, image_sum, text_sum)


def swapped(value, axis, step):
    return lax.ppermute(value, axis, [(i, i ^ step) for i in range(lax.axis_size(axis))])


def doubled(value, axis, step):
    return jnp.concatenate([value, swapped(value, axis, step)], axis=0)


def sent(value):
    return (value * HALF).astype(jnp.float16)


def received(value):
    return value.astype(jnp.float32) * (1 / HALF)


LOSS_SCALE = 2.0**-15
REST_SCALE = 2.0**11


def halved(value, loss, axis, step):
    half, width = value.shape[0] // 2, value.shape[1]
    scaled = loss * LOSS_SCALE
    first = scaled.astype(jnp.float16)
    rest = ((scaled - first.astype(jnp.float32)) * REST_SCALE).astype(jnp.float16)
    tail = jnp.pad(jnp.concatenate([first, rest], axis=0), ((0, 0), (0, width - LANES)))
    arrived = swapped(jnp.concatenate([sent(value[half:]), tail], axis=0), axis, step)
    first, rest = arrived[half : half + 4, :LANES], arrived[half + 4 :, :LANES]
    loss = loss + (first.astype(jnp.float32) + rest.astype(jnp.float32) * (1 / REST_SCALE)) * (1 / LOSS_SCALE)
    return value[:half] + received(arrived[:half]), loss


def shards(picture_vectors, caption_vectors, heat_exponent, offset_added):
    rows, width = picture_vectors.shape
    plane = lax.axis_size(PLANE)
    steps = [1 << bit for bit in range(lax.axis_size("zl").bit_length() - 1)]
    image_low, text_low, own_loss = unit_rows(heat_exponent, offset_added, picture_vectors, caption_vectors)

    other_low = swapped(text_low, "zh", 1)
    copies = [jnp.broadcast_to(part[None], (plane, rows, width)) for part in (text_low, other_low)]
    texts = lax.all_to_all(jnp.concatenate(copies, axis=1), PLANE, 0, 0)
    texts = texts.reshape(plane * 2 * rows, width)
    near = image_low
    for step in reversed(steps):
        near = doubled(near, "zl", step)
    far = swapped(near, "c", 1)

    place = (lax.axis_index(PLANE) * 2 * rows).astype(jnp.int32).reshape(1)
    weights, loss = pair_weights(plane, place, heat_exponent, offset_added, own_loss, near, far, texts)
    loss = jnp.sum(lax.all_to_all(loss, PLANE, 0, 0)[:, :4], axis=0)
    near_part, far_part, own_part, other_part = pair_terms(plane, weights, near, far, texts)
    other_parts = lax.all_to_all(other_part, PLANE, 0, 0)
    own_parts = lax.all_to_all(own_part, PLANE, 0, 0)

    image_sum = near_part + swapped(far_part, "c", 1)
    for step in steps:
        image_sum, loss = halved(image_sum, loss, "zl", step)
    loss += swapped(loss, "zh", 1)
    total = (loss + swapped(loss, "c", 1))[0, 0]
    loss_mean = (total / (rows * lax.axis_size(AXES))).reshape(1)
    other_sum = jnp.sum(other_parts.astype(jnp.float32), axis=0)
    text_sum = received(swapped(sent(other_sum), "zh", 1)) + jnp.sum(own_parts.astype(jnp.float32), axis=0)
    image_grads, text_grads = gradients(
        heat_exponent, offset_added, picture_vectors, caption_vectors, image_sum, text_sum
    )
    return (loss_mean, image_grads, text_grads)


def solution(mesh):
    fine = Mesh(mesh.devices.reshape(SIZES), AXES)
    in_specs = (P(AXES, None), P(AXES, None), P(), P())
    out_specs = (P(), P(AXES, None), P(AXES, None))
    return jax.shard_map(shards, mesh=fine, in_specs=in_specs, out_specs=out_specs, check_vma=False)
```

time: 150 us -> 150 us (level)
  the two profiles are of different devices: /device:TPU:2 before, /device:TPU:1 now
where the time goes in v6:
time: 150 us; the launch traced here: 149 us
  starting transfers between devices  80.6 us (54%)
  waiting for transfers between devices  41 us (27%)
  blocking collectives  9.6 us (6%)
  Pallas kernels  8.94 us (6%)
  between operations  4.04 us (3%)
  other arithmetic  3.52 us (2%)
  local copies, waits for them, and re-layouts  1.53 us (1%)
    ppermute x12, starting transfers between devices, swapped(): lax.ppermute(value, axis, [(i, i ^ step) for i in range(lax.axis_size(axi...  66.3 us
    ppermute x12, waiting for transfers between devices, swapped(): lax.ppermute(value, axis, [(i, i ^ step) for i in range(lax.axis_size(axi...  30.3 us
    all_to_all x1, waiting for transfers between devices, shards(): other_parts = lax.all_to_all(other_part, PLANE, 0, 0)  10.7 us
    all_to_all x1, blocking collectives, shards(): loss = jnp.sum(lax.all_to_all(loss, PLANE, 0, 0)[:, :4], axis=0)  9.6 us
    all_to_all x1, starting transfers between devices, shards(): texts = lax.all_to_all(jnp.concatenate(copies, axis=1), PLANE, 0, 0)  6.89 us
    all_to_all x1, starting transfers between devices, shards(): own_parts = lax.all_to_all(own_part, PLANE, 0, 0)  3.85 us
    all_to_all x1, starting transfers between devices, shards(): other_parts = lax.all_to_all(other_part, PLANE, 0, 0)  3.63 us
    pallas_call x1, Pallas kernels, pair_terms(): pl.pallas_call(terms_kernel, in_specs=[pl.BlockSpec(memory_space=pltpu.VM...  3.21 us
  transfers between devices with their start and end apart: 15, of which 6 were waited for; matrix products, arithmetic and copies ran while one was open for 3% of the time, Pallas kernels for 1%

profile of v6, /device:TPU:1, one launch (start us, length us, event | category | flops | bytes accessed | tf_op | source)
XLA Modules:
  0.0 149.3 jit_solution(8958179543714943242)
XLA Ops:
  1.9 1.8 %shard_map.67 = (bf16[24,1152]{1,0:T(8,128)(2,1)}, bf16[24,1152]{1,0:T(8,128)(2,1)}, f32[24,1]{1,0:T(8,128)}) custom-call(f32[1]{0:T(128)S(6)} %copy.10.heat_ref, f32[1]{0:T(128)S(6)} %copy.11.offset_ref, f32[24,1152]{1,0:T(8,128)} %picture_ref.3, f32[24,1152]{1,0:T(8,128)} %caption_ref.3), custom_call_target="tpu_custom_call" | custom-call | tf_op jit(solution)/shard_map/pallas_call | solution.py:54
  3.7 16.3 %collective-permute-start.4 = (bf16[24,1152]{1,0:T(8,128)(2,1)}, bf16[24,1152]{1,0:T(8,128)(2,1)S(1)}, u32[]{:S(2)}, u32[]{:S(2)}) collective-permute-start(bf16[24,1152]{1,0:T(8,128)(2,1)} %get-tuple-element.16), channel_id=1, source_target_pairs={{0,1},{1,0},{2,3},{3,2},{4,5},{5,4},{6,7},{7,6},{8,9},{9,8},{10,11... | collective-permute-start | bytes 165896 | tf_op jit(solution)/shard_map/ppermute | solution.py:164
  20.0 4.0 %collective-permute-start = (bf16[24,1152]{1,0:T(8,128)(2,1)}, bf16[24,1152]{1,0:T(8,128)(2,1)S(1)}, u32[]{:S(2)}, u32[]{:S(2)}) collective-permute-start(bf16[24,1152]{1,0:T(8,128)(2,1)} %get-tuple-element.15), channel_id=1, source_target_pairs={{0,256},{64,320},{128,384},{192,448},{256,0},{320,64},{384,128},{4... | collective-permute-start | bytes 165896 | tf_op jit(solution)/shard_map/ppermute | solution.py:164
  24.0 0.0 collective-permute-done.4
  24.0 0.1 broadcast_in_dim.5
  24.1 0.9 broadcast_in_dim.4
  25.0 1.4 pad_maximum_fusion
  26.3 0.0 copy-start.1
  26.4 0.0 copy-start
  26.4 6.9 %all-to-all-start = ((bf16[16,48,1152]{2,1,0:T(8,128)(2,1)}), bf16[16,48,1152]{2,1,0:T(8,128)(2,1)S(1)}, u32[]{:S(2)}, u32[]{:S(2)}) async-start(bf16[16,48,1152]{2,1,0:T(8,128)(2,1)} %pad_maximum_fusion), calls=%async_computation | async-start | bytes 3538944 | tf_op jit(solution)/shard_map/all_to_all | solution.py:203
  33.2 0.0 copy-done.1
  33.3 0.0 collective-permute-done
  33.3 3.1 %collective-permute-start.1 = (bf16[48,1152]{1,0:T(8,128)(2,1)S(1)}, bf16[48,1152]{1,0:T(8,128)(2,1)S(1)}, u32[]{:S(2)}, u32[]{:S(2)}) collective-permute-start(bf16[48,1152]{1,0:T(8,128)(2,1)S(1)} %pad_maximum_fusion.4), channel_id=1, source_target_pairs={{0,128},{64,192},{128,0},{192,64},{256,384},{320,448},{384,256},{4... | collective-permute-start | bytes 331784 | tf_op jit(solution)/shard_map/ppermute | solution.py:164
  36.4 6.3 %collective-permute-done.1 = bf16[48,1152]{1,0:T(8,128)(2,1)S(1)} collective-permute-done((bf16[48,1152]{1,0:T(8,128)(2,1)S(1)}, bf16[48,1152]{1,0:T(8,128)(2,1)S(1)}, u32[]{:S(2)}, u32[]{:S(2)}) %collective-permute-start.1) | collective-permute-done | bytes 110624 | tf_op jit(solution)/shard_map/ppermute | solution.py:164
  42.7 1.9 %collective-permute-start.2 = (bf16[96,1152]{1,0:T(8,128)(2,1)S(1)}, bf16[96,1152]{1,0:T(8,128)(2,1)S(1)}, u32[]{:S(2)}, u32[]{:S(2)}) collective-permute-start(bf16[96,1152]{1,0:T(8,128)(2,1)S(1)} %pad_maximum_fusion.2), channel_id=1, source_target_pairs={{0,64},{64,0},{128,192},{192,128},{256,320},{320,256},{384,448},{4... | collective-permute-start | bytes 663560 | tf_op jit(solution)/shard_map/ppermute | solution.py:164
  44.7 5.6 %collective-permute-done.2 = bf16[96,1152]{1,0:T(8,128)(2,1)S(1)} collective-permute-done((bf16[96,1152]{1,0:T(8,128)(2,1)S(1)}, bf16[96,1152]{1,0:T(8,128)(2,1)S(1)}, u32[]{:S(2)}, u32[]{:S(2)}) %collective-permute-start.2) | collective-permute-done | bytes 221216 | tf_op jit(solution)/shard_map/ppermute | solution.py:164
  50.3 4.1 %collective-permute-start.3 = (bf16[192,1152]{1,0:T(8,128)(2,1)S(1)}, bf16[192,1152]{1,0:T(8,128)(2,1)S(1)}, u32[]{:S(2)}, u32[]{:S(2)}) collective-permute-start(bf16[192,1152]{1,0:T(8,128)(2,1)S(1)} %constant_dynamic-update-slice_fusion.near_ref), channel_id=1, source_target_pairs={{0,8},{8,0},{1,9},{9,1},{2,10},{10,2},{3,11},{11,3},{4,12},{12,4},... | collective-permute-start | bytes 1327112 | tf_op jit(solution)/shard_map/ppermute | solution.py:164
  54.4 1.4 collective-permute-done.3.far_ref
  55.8 0.0 all-to-all-done
  55.8 0.0 copy-done
  55.8 1.9 %shard_map.68 = (bf16[384,768]{1,0:T(8,128)(2,1)S(1)}, f32[16,8,128]{2,1,0:T(8,128)S(1)}) custom-call(s32[1]{0:T(128)} %bitcast.place_ref, f32[1]{0:T(128)S(6)} %copy.10.heat_ref, f32[1]{0:T(128)S(6)} %copy.11.offset_ref, f32[24,1]{1,0:T(8,128)S(1)} %copy-done, bf16[192,1152]{1,0:T(8,128)(2,1)S(1)} %constant_dynamic-update-slice_fusion.near_ref, ...), custom_call_target="tpu_custom_call" | custom-call | flops 679477248 | bytes 1769472 | tf_op jit(solution)/shard_map/pallas_call | solution.py:92
  57.7 3.2 %shard_map.69 = (f32[192,1152]{1,0:T(8,128)S(1)}, f32[192,1152]{1,0:T(8,128)}, bf16[16,24,1152]{2,1,0:T(8,128)(2,1)}, bf16[16,24,1152]{2,1,0:T(8,128)(2,1)}) custom-call(bf16[384,768]{1,0:T(8,128)(2,1)S(1)} %get-tuple-element.18.weight_ref, bf16[192,1152]{1,0:T(8,128)(2,1)S(1)} %constant_dynamic-update-slice_fusion.near_ref, ...), custom_call_target="tpu_custom_call" | custom-call | flops 1358954496 | bytes 3538944 | tf_op jit(solution)/shard_map/pallas_call | solution.py:126
  60.9 6.3 %collective-permute-start.5 = (f32[192,1152]{1,0:T(8,128)}, f32[192,1152]{1,0:T(8,128)S(1)}, u32[]{:S(2)}, u32[]{:S(2)}) collective-permute-start(f32[192,1152]{1,0:T(8,128)} %get-tuple-element.20), channel_id=1, source_target_pairs={{0,8},{8,0},{1,9},{9,1},{2,10},{10,2},{3,11},{11,3},{4,12},{12,4},... | collective-permute-start | bytes 2654216 | tf_op jit(solution)/shard_map/ppermute | solution.py:164
  67.2 9.6 %all_to_all.20 = f32[16,8,128]{2,1,0:T(8,128)S(1)} all-to-all(f32[16,8,128]{2,1,0:T(8,128)S(1)} %get-tuple-element.17), channel_id=1, replica_groups=mesh['zl'=8,'x'=4,'c'=2,'y'=4,'zh'=2] {'x','y'}, dimensions={0} | all-to-all | bytes 131072 | tf_op jit(solution)/shard_map/all_to_all | solution.py:212
  76.8 3.6 %all-to-all-start.2 = ((bf16[16,24,1152]{2,1,0:T(8,128)(2,1)}), bf16[16,24,1152]{2,1,0:T(8,128)(2,1)S(1)}, u32[]{:S(2)}, u32[]{:S(2)}) async-start(bf16[16,24,1152]{2,1,0:T(8,128)(2,1)} %get-tuple-element.21), calls=%async_computation.2 | async-start | bytes 1769472 | tf_op jit(solution)/shard_map/all_to_all | solution.py:214
  80.5 0.0 collective-permute-done.5
  80.5 0.1 add.49
  80.7 0.1 pad_maximum_fusion.1
  80.7 2.7 %collective-permute-start.6 = (f16[104,1152]{1,0:T(8,128)(2,1)S(1)}, f16[104,1152]{1,0:T(8,128)(2,1)S(1)}, u32[]{:S(2)}, u32[]{:S(2)}) collective-permute-start(f16[104,1152]{1,0:T(8,128)(2,1)S(1)} %pad_maximum_fusion.1), channel_id=1, source_target_pairs={{0,64},{64,0},{128,192},{192,128},{256,320},{320,256},{384,448},{4... | collective-permute-start | bytes 718856 | tf_op jit(solution)/shard_map/ppermute | solution.py:164
  83.4 10.7 %all-to-all-done.2 = bf16[16,24,1152]{2,1,0:T(8,128)(2,1)S(1)} async-done(((bf16[16,24,1152]{2,1,0:T(8,128)(2,1)}), bf16[16,24,1152]{2,1,0:T(8,128)(2,1)S(1)}, u32[]{:S(2)}, u32[]{:S(2)}) %all-to-all-start.2) | async-done | bytes 884768 | tf_op jit(solution)/shard_map/all_to_all | solution.py:214
  94.1 3.9 %all-to-all-start.3 = ((bf16[16,24,1152]{2,1,0:T(8,128)(2,1)}), bf16[16,24,1152]{2,1,0:T(8,128)(2,1)S(1)}, u32[]{:S(2)}, u32[]{:S(2)}) async-start(bf16[16,24,1152]{2,1,0:T(8,128)(2,1)} %get-tuple-element.22), calls=%async_computation.3 | async-start | bytes 1769472 | tf_op jit(solution)/shard_map/all_to_all | solution.py:215
  97.9 0.1 convert_reduce_fusion.1
  98.1 0.0 collective-permute-done.6
  98.1 0.1 slice_add_fusion
  98.2 3.1 %collective-permute-start.7 = (f16[56,1152]{1,0:T(8,128)(2,1)S(1)}, f16[56,1152]{1,0:T(8,128)(2,1)S(1)}, u32[]{:S(2)}, u32[]{:S(2)}) collective-permute-start(f16[56,1152]{1,0:T(8,128)(2,1)S(1)} %pad_maximum_fusion.3), channel_id=1, source_target_pairs={{0,128},{64,192},{128,0},{192,64},{256,384},{320,448},{384,256},{4... | collective-permute-start | bytes 387080 | tf_op jit(solution)/shard_map/ppermute | solution.py:164
  101.4 11.1 %collective-permute-start.11 = (f16[24,1152]{1,0:T(8,128)(2,1)S(1)}, f16[24,1152]{1,0:T(8,128)(2,1)S(1)}, u32[]{:S(2)}, u32[]{:S(2)}) collective-permute-start(f16[24,1152]{1,0:T(8,128)(2,1)S(1)} %multiply_convert_fusion), channel_id=1, source_target_pairs={{0,1},{1,0},{2,3},{3,2},{4,5},{5,4},{6,7},{7,6},{8,9},{9,8},{10,11... | collective-permute-start | bytes 165896 | tf_op jit(solution)/shard_map/ppermute | solution.py:164
  112.5 0.0 collective-permute-done.7
  112.7 2.7 %collective-permute-start.8 = (f16[32,1152]{1,0:T(8,128)(2,1)S(1)}, f16[32,1152]{1,0:T(8,128)(2,1)S(1)}, u32[]{:S(2)}, u32[]{:S(2)}) collective-permute-start(f16[32,1152]{1,0:T(8,128)(2,1)S(1)} %pad_maximum_fusion.5), channel_id=1, source_target_pairs={{0,256},{64,320},{128,384},{192,448},{256,0},{320,64},{384,128},{4... | collective-permute-start | bytes 221192 | tf_op jit(solution)/shard_map/ppermute | solution.py:164
  115.4 0.0 all-to-all-done.3
  115.4 0.1 convert_reduce_fusion
  115.5 11.6 %collective-permute-done.8 = f16[32,1152]{1,0:T(8,128)(2,1)S(1)} collective-permute-done((f16[32,1152]{1,0:T(8,128)(2,1)S(1)}, f16[32,1152]{1,0:T(8,128)(2,1)S(1)}, u32[]{:S(2)}, u32[]{:S(2)}) %collective-permute-start.8) | collective-permute-done | bytes 73760 | tf_op jit(solution)/shard_map/ppermute | solution.py:164
  127.1 6.9 %collective-permute-start.9 = (f32[4,128]{1,0:T(4,128)S(1)}, f32[4,128]{1,0:T(4,128)S(1)}, u32[]{:S(2)}, u32[]{:S(2)}) collective-permute-start(f32[4,128]{1,0:T(4,128)S(1)} %multiply_add_fusion.1), channel_id=1, source_target_pairs={{0,1},{1,0},{2,3},{3,2},{4,5},{5,4},{6,7},{7,6},{8,9},{9,8},{10,11... | collective-permute-start | bytes 6152 | tf_op jit(solution)/shard_map/ppermute | solution.py:164
  134.0 0.0 collective-permute-done.11
  134.0 0.7 multiply_add_fusion.text_sum_ref
  134.7 5.4 %collective-permute-done.9 = f32[4,128]{1,0:T(4,128)S(1)} collective-permute-done((f32[4,128]{1,0:T(4,128)S(1)}, f32[4,128]{1,0:T(4,128)S(1)}, u32[]{:S(2)}, u32[]{:S(2)}) %collective-permute-start.9) | collective-permute-done | bytes 2080 | tf_op jit(solution)/shard_map/ppermute | solution.py:164
  140.2 4.1 %collective-permute-start.10 = (f32[4,128]{1,0:T(4,128)S(1)}, f32[4,128]{1,0:T(4,128)S(1)}, u32[]{:S(2)}, u32[]{:S(2)}) collective-permute-start(f32[4,128]{1,0:T(4,128)S(1)} %add.58), channel_id=1, source_target_pairs={{0,8},{8,0},{1,9},{9,1},{2,10},{10,2},{3,11},{11,3},{4,12},{12,4},... | collective-permute-start | bytes 6152 | tf_op jit(solution)/shard_map/ppermute | solution.py:164
  144.2 0.7 slice_add_fusion.2.image_sum_ref
  144.9 2.1 %shard_map.70 = (f32[24,1152]{1,0:T(8,128)}, f32[24,1152]{1,0:T(8,128)}) custom-call(f32[1]{0:T(128)S(6)} %copy.10.heat_ref, f32[1]{0:T(128)S(6)} %copy.11.offset_ref, f32[24,1152]{1,0:T(8,128)} %picture_ref.3, f32[24,1152]{1,0:T(8,128)} %caption_ref.3, f32[24,1152]{1,0:T(8,128)} %slice_add_fusion.2.image_sum_ref, f32[24,1152]{1,0:T(8,128)} %multiply_add_fusion.text_sum_ref), custom_call_target="tpu_custom_call" | custom-call | tf_op jit(solution)/shard_map/pallas_call | solution.py:156
  147.0 0.0 collective-permute-done.10
  147.0 0.5 slice.65
  (24 shorter events, 0.4 us)
Async XLA Ops:
  3.7 20.3 %collective-permute-start.4 = (bf16[24,1152]{1,0:T(8,128)(2,1)}, bf16[24,1152]{1,0:T(8,128)(2,1)S(1)}, u32[]{:S(2)}, u32[]{:S(2)}) collective-permute-start(bf16[24,1152]{1,0:T(8,128)(2,1)} %get-tuple-element.16), channel_id=1, source_target_pairs={{0,1},{1,0},{2,3},{3,2},{4,5},{5,4},{6,7},{7,6},{8,9},{9,8},{10,11... | collective-permute-start | bytes 165896 | tf_op jit(solution)/shard_map/ppermute | solution.py:164
  20.0 13.3 %collective-permute-start = (bf16[24,1152]{1,0:T(8,128)(2,1)}, bf16[24,1152]{1,0:T(8,128)(2,1)S(1)}, u32[]{:S(2)}, u32[]{:S(2)}) collective-permute-start(bf16[24,1152]{1,0:T(8,128)(2,1)} %get-tuple-element.15), channel_id=1, source_target_pairs={{0,256},{64,320},{128,384},{192,448},{256,0},{320,64},{384,128},{4... | collective-permute-start | bytes 165896 | tf_op jit(solution)/shard_map/ppermute | solution.py:164
  26.3 6.9 %copy-start.1 = (bf16[24,1152]{1,0:T(8,128)(2,1)S(1)}, bf16[24,1152]{1,0:T(8,128)(2,1)}, u32[]{:S(2)}) copy-start(bf16[24,1152]{1,0:T(8,128)(2,1)} %get-tuple-element.15) | copy-start | bytes 165892
  26.4 29.4 %copy-start = (f32[24,1]{1,0:T(8,128)S(1)}, f32[24,1]{1,0:T(8,128)}, u32[]{:S(2)}) copy-start(f32[24,1]{1,0:T(8,128)} %get-tuple-element.14.own_loss_ref) | copy-start | bytes 292
  26.4 29.4 %all-to-all-start = ((bf16[16,48,1152]{2,1,0:T(8,128)(2,1)}), bf16[16,48,1152]{2,1,0:T(8,128)(2,1)S(1)}, u32[]{:S(2)}, u32[]{:S(2)}) async-start(bf16[16,48,1152]{2,1,0:T(8,128)(2,1)} %pad_maximum_fusion), calls=%async_computation | async-start | bytes 3538944 | tf_op jit(solution)/shard_map/all_to_all | solution.py:203
  33.3 9.4 %collective-permute-start.1 = (bf16[48,1152]{1,0:T(8,128)(2,1)S(1)}, bf16[48,1152]{1,0:T(8,128)(2,1)S(1)}, u32[]{:S(2)}, u32[]{:S(2)}) collective-permute-start(bf16[48,1152]{1,0:T(8,128)(2,1)S(1)} %pad_maximum_fusion.4), channel_id=1, source_target_pairs={{0,128},{64,192},{128,0},{192,64},{256,384},{320,448},{384,256},{4... | collective-permute-start | bytes 331784 | tf_op jit(solution)/shard_map/ppermute | solution.py:164
  42.7 7.6 %collective-permute-start.2 = (bf16[96,1152]{1,0:T(8,128)(2,1)S(1)}, bf16[96,1152]{1,0:T(8,128)(2,1)S(1)}, u32[]{:S(2)}, u32[]{:S(2)}) collective-permute-start(bf16[96,1152]{1,0:T(8,128)(2,1)S(1)} %pad_maximum_fusion.2), channel_id=1, source_target_pairs={{0,64},{64,0},{128,192},{192,128},{256,320},{320,256},{384,448},{4... | collective-permute-start | bytes 663560 | tf_op jit(solution)/shard_map/ppermute | solution.py:164
  50.3 5.5 %collective-permute-start.3 = (bf16[192,1152]{1,0:T(8,128)(2,1)S(1)}, bf16[192,1152]{1,0:T(8,128)(2,1)S(1)}, u32[]{:S(2)}, u32[]{:S(2)}) collective-permute-start(bf16[192,1152]{1,0:T(8,128)(2,1)S(1)} %constant_dynamic-update-slice_fusion.near_ref), channel_id=1, source_target_pairs={{0,8},{8,0},{1,9},{9,1},{2,10},{10,2},{3,11},{11,3},{4,12},{12,4},... | collective-permute-start | bytes 1327112 | tf_op jit(solution)/shard_map/ppermute | solution.py:164
  60.9 19.6 %collective-permute-start.5 = (f32[192,1152]{1,0:T(8,128)}, f32[192,1152]{1,0:T(8,128)S(1)}, u32[]{:S(2)}, u32[]{:S(2)}) collective-permute-start(f32[192,1152]{1,0:T(8,128)} %get-tuple-element.20), channel_id=1, source_target_pairs={{0,8},{8,0},{1,9},{9,1},{2,10},{10,2},{3,11},{11,3},{4,12},{12,4},... | collective-permute-start | bytes 2654216 | tf_op jit(solution)/shard_map/ppermute | solution.py:164
  76.8 17.2 %all-to-all-start.2 = ((bf16[16,24,1152]{2,1,0:T(8,128)(2,1)}), bf16[16,24,1152]{2,1,0:T(8,128)(2,1)S(1)}, u32[]{:S(2)}, u32[]{:S(2)}) async-start(bf16[16,24,1152]{2,1,0:T(8,128)(2,1)} %get-tuple-element.21), calls=%async_computation.2 | async-start | bytes 1769472 | tf_op jit(solution)/shard_map/all_to_all | solution.py:214
  80.7 17.3 %collective-permute-start.6 = (f16[104,1152]{1,0:T(8,128)(2,1)S(1)}, f16[104,1152]{1,0:T(8,128)(2,1)S(1)}, u32[]{:S(2)}, u32[]{:S(2)}) collective-permute-start(f16[104,1152]{1,0:T(8,128)(2,1)S(1)} %pad_maximum_fusion.1), channel_id=1, source_target_pairs={{0,64},{64,0},{128,192},{192,128},{256,320},{320,256},{384,448},{4... | collective-permute-start | bytes 718856 | tf_op jit(solution)/shard_map/ppermute | solution.py:164
  94.1 21.3 %all-to-all-start.3 = ((bf16[16,24,1152]{2,1,0:T(8,128)(2,1)}), bf16[16,24,1152]{2,1,0:T(8,128)(2,1)S(1)}, u32[]{:S(2)}, u32[]{:S(2)}) async-start(bf16[16,24,1152]{2,1,0:T(8,128)(2,1)} %get-tuple-element.22), calls=%async_computation.3 | async-start | bytes 1769472 | tf_op jit(solution)/shard_map/all_to_all | solution.py:215
  98.2 14.3 %collective-permute-start.7 = (f16[56,1152]{1,0:T(8,128)(2,1)S(1)}, f16[56,1152]{1,0:T(8,128)(2,1)S(1)}, u32[]{:S(2)}, u32[]{:S(2)}) collective-permute-start(f16[56,1152]{1,0:T(8,128)(2,1)S(1)} %pad_maximum_fusion.3), channel_id=1, source_target_pairs={{0,128},{64,192},{128,0},{192,64},{256,384},{320,448},{384,256},{4... | collective-permute-start | bytes 387080 | tf_op jit(solution)/shard_map/ppermute | solution.py:164
  101.4 32.7 %collective-permute-start.11 = (f16[24,1152]{1,0:T(8,128)(2,1)S(1)}, f16[24,1152]{1,0:T(8,128)(2,1)S(1)}, u32[]{:S(2)}, u32[]{:S(2)}) collective-permute-start(f16[24,1152]{1,0:T(8,128)(2,1)S(1)} %multiply_convert_fusion), channel_id=1, source_target_pairs={{0,1},{1,0},{2,3},{3,2},{4,5},{5,4},{6,7},{7,6},{8,9},{9,8},{10,11... | collective-permute-start | bytes 165896 | tf_op jit(solution)/shard_map/ppermute | solution.py:164
  112.7 14.5 %collective-permute-start.8 = (f16[32,1152]{1,0:T(8,128)(2,1)S(1)}, f16[32,1152]{1,0:T(8,128)(2,1)S(1)}, u32[]{:S(2)}, u32[]{:S(2)}) collective-permute-start(f16[32,1152]{1,0:T(8,128)(2,1)S(1)} %pad_maximum_fusion.5), channel_id=1, source_target_pairs={{0,256},{64,320},{128,384},{192,448},{256,0},{320,64},{384,128},{4... | collective-permute-start | bytes 221192 | tf_op jit(solution)/shard_map/ppermute | solution.py:164
  127.1 13.0 %collective-permute-start.9 = (f32[4,128]{1,0:T(4,128)S(1)}, f32[4,128]{1,0:T(4,128)S(1)}, u32[]{:S(2)}, u32[]{:S(2)}) collective-permute-start(f32[4,128]{1,0:T(4,128)S(1)} %multiply_add_fusion.1), channel_id=1, source_target_pairs={{0,1},{1,0},{2,3},{3,2},{4,5},{5,4},{6,7},{7,6},{8,9},{9,8},{10,11... | collective-permute-start | bytes 6152 | tf_op jit(solution)/shard_map/ppermute | solution.py:164
  140.2 6.8 %collective-permute-start.10 = (f32[4,128]{1,0:T(4,128)S(1)}, f32[4,128]{1,0:T(4,128)S(1)}, u32[]{:S(2)}, u32[]{:S(2)}) collective-permute-start(f32[4,128]{1,0:T(4,128)S(1)} %add.58), channel_id=1, source_target_pairs={{0,8},{8,0},{1,9},{9,1},{2,10},{10,2},{3,11},{11,3},{4,12},{12,4},... | collective-permute-start | bytes 6152 | tf_op jit(solution)/shard_map/ppermute | solution.py:164

commit v7 on v4

--- a/solution.py
+++ b/solution.py
@@ -6,11 +6,10 @@
 from jax.sharding import Mesh, PartitionSpec as P
 
 epsilon = 1e-06
-AXES = ("zl", "x", "c", "y", "zh")
-SIZES = (8, 4, 2, 4, 2)
-RING = ("zl", "zh")
-PLANE = ("x", "y")
-COLUMN = ("zl", "c", "zh")
+AXES = ("zl", "xh", "xl", "c", "y", "zh")
+SIZES = (8, 2, 2, 2, 4, 2)
+PLANE = ("xh", "y")
+COLUMN = ("zl", "xl", "c", "zh")
 LANES = 128
 PARTS = 1
 LIMIT = 20 * 1024 * 1024
@@ -93,9 +92,9 @@
             loss, sigmoid = loss_and_sigmoid(logits)
             weights = heat * sigmoid
             if image_ref is near_ref:
-                image_row = lax.broadcasted_iota(jnp.int32, logits.shape, 0) - rows
+                image_row = lax.broadcasted_iota(jnp.int32, logits.shape, 0)
                 text_row = lax.broadcasted_iota(jnp.int32, logits.shape, 1) + (part * count - place_ref[0])
-                match = (image_row == text_row) & (image_row >= 0) & (image_row < rows)
+                match = (image_row == text_row) & (image_row < rows)
                 weights = jnp.where(match, 0.0, weights)
                 loss = jnp.where(match, 0.0, loss)
             weights = weights.astype(jnp.bfloat16)
@@ -167,72 +166,50 @@
     )(heat_exponent, offset_added, pictures, captions, image_sum, text_sum)
 
 
-def moved(value, steps):
-    halves = lax.axis_size("zh")
-    count = lax.axis_size(RING)
-    order = [low_place * halves + half for half in range(halves) for low_place in range(count // halves)]
-    return lax.ppermute(value, RING, [(order[i], order[(i + steps) % count]) for i in range(count)])
-
-
-def sent(value):
-    return (value * HALF).astype(jnp.float16)
-
-
-def received(value):
-    return value.astype(jnp.float32) * (1 / HALF)
-
-
-def swapped(value):
-    return lax.ppermute(value, "c", [(0, 1), (1, 0)])
-
-
-def ring_gathered(block, texts):
-    rows = block.shape[0]
-    same = jnp.concatenate([moved(block, 4), block, moved(block, -4), moved(block, 8)], axis=0)
-    parts = [same, moved(same, -1), moved(same, 1)]
-    parts += [moved(same[rows : 3 * rows], -2), moved(same[: 2 * rows], 2)]
-    near = jnp.concatenate(parts, axis=0)
-    return lax.optimization_barrier((near, texts))
-
-
-def near_summed(value, rows):
-    low_part = sent(value)
-    up = received(moved(low_part[4 * rows : 8 * rows], 1))
-    down = received(moved(low_part[8 * rows : 12 * rows], -1))
-    up_two = received(moved(low_part[12 * rows : 14 * rows], 2))
-    down_two = received(moved(low_part[14 * rows :], -2))
-    same = value[: 4 * rows] + up + down
-    own = same[rows : 2 * rows] + down_two[rows:] + up_two[:rows]
-    others = (same[:rows] + down_two[:rows], same[2 * rows : 3 * rows] + up_two[rows:], same[3 * rows :])
-    return own, [sent(other) for other in others]
-
-
-def far_summed(own, others):
-    for other, steps in zip(others, (-4, 4, 8)):
-        own += received(moved(other, steps))
-    return own
+def swapped(value, axis, step):
+    return lax.ppermute(value, axis, [(i, i ^ step) for i in range(lax.axis_size(axis))])
+
+
+def doubled(value, axis, step):
+    return jnp.concatenate([value, swapped(value, axis, step)], axis=0)
+
+
+def halved(value, axis, step):
+    half = value.shape[0] // 2
+    sent = (value[half:] * HALF).astype(jnp.float16)
+    return value[:half] + swapped(sent, axis, step).astype(jnp.float32) * (1 / HALF)
 
 
 def shards(picture_vectors, caption_vectors, heat_exponent, offset_added):
     rows, width = picture_vectors.shape
     plane, column = lax.axis_size(PLANE), lax.axis_size(COLUMN)
+    steps = [1 << bit for bit in range(lax.axis_size("zl").bit_length() - 1)]
     image_low, text_low, own_loss = unit_rows(heat_exponent, offset_added, picture_vectors, caption_vectors)
 
-    texts = lax.all_to_all(jnp.broadcast_to(text_low[None], (plane, *text_low.shape)), PLANE, 0, 0)
-    near, texts = ring_gathered(image_low, texts.reshape(plane * rows, width))
-    far = swapped(near)
-
-    place = (lax.axis_index(PLANE) * rows).astype(jnp.int32).reshape(1)
+    texts = doubled(text_low, "zh", 1)
+    texts = lax.all_to_all(jnp.broadcast_to(texts[None], (plane, *texts.shape)), PLANE, 0, 0)
+    texts = texts.reshape(plane * 2 * rows, width)
+    near = image_low
+    for step in reversed(steps):
+        near = doubled(near, "zl", step)
+    near = doubled(near, "xl", 1)
+    near, texts = lax.optimization_barrier((near, texts))
+    far = swapped(near, "c", 1)
+
+    place = (lax.axis_index(PLANE) * 2 * rows).astype(jnp.int32).reshape(1)
     weights, text_part = pair_terms(place, heat_exponent, offset_added, own_loss, near, far, texts)
-    text_parts = lax.all_to_all(text_part.reshape(plane, rows, width + LANES), PLANE, 0, 0)
+    text_parts = lax.all_to_all(text_part.reshape(plane, 2 * rows, width + LANES), PLANE, 0, 0)
+
     near_part, far_part = image_terms(weights, texts)
-    own, others = near_summed(near_part + swapped(far_part), rows)
-    others, text_parts = lax.optimization_barrier((others, text_parts))
+    image_sum = halved(near_part + swapped(far_part, "c", 1), "xl", 1)
+    for step in steps:
+        image_sum = halved(image_sum, "zl", step)
+
     plane_loss = jnp.sum(text_parts[:, 0, width : width + 3].astype(jnp.float32))
-    losses = lax.all_to_all(jnp.broadcast_to(plane_loss, (column, 8, LANES)), COLUMN, 0, 0)
+    losses = lax.all_to_all(jnp.broadcast_to(plane_loss, (column, 1, LANES)), COLUMN, 0, 0)
     loss_mean = (jnp.sum(losses[:, 0, 0]) / (rows * lax.axis_size(AXES))).reshape(1)
     text_sum = jnp.sum(text_parts[:, :, :width].astype(jnp.float32), axis=0)
-    image_sum = far_summed(own, others)
+    text_sum = halved(text_sum, "zh", 1)
     image_grads, text_grads = gradients(
         heat_exponent, offset_added, picture_vectors, caption_vectors, image_sum, text_sum
     )

time: 145 us -> 155 us (1.069)
  waiting for transfers between devices: 19.2 us -> 49 us
  starting transfers between devices: 102 us -> 78.8 us
  other arithmetic: 4.6 us -> 8.36 us
    ppermute x16 -> x12, waiting for transfers between devices: 8.01 us -> 39.7 us  [swapped(): lax.ppermute(value, axis, [(i, i ^ step) for i in range(lax.axis_size(axi...]
    ppermute x16 -> x12, starting transfers between devices: 77.8 us -> 55.5 us  [swapped(): lax.ppermute(value, axis, [(i, i ^ step) for i in range(lax.axis_size(axi...]
    add x2 -> x6, other arithmetic: 0.79 us -> 3.17 us  [the longest x1 1.65 us: shards(): image_sum = halved(near_part + swapped(far_part, 'c', 1), 'xl', 1)]
    unnamed x10, local copies, waits for them, and re-layouts: 0.12 us -> 2.12 us
    all_to_all x3, waiting for transfers between devices: 11.2 us -> 9.27 us  [the longest x1 9.27 us: shards(): lax.all_to_all(text_part.reshape(plane, 2 * rows, width + LANES), PLANE,...]
    concatenate x1 -> x4, other arithmetic: 0.02 us -> 1.71 us  [doubled(): return jnp.concatenate([value, swapped(value, axis, step)], axis=0)]
    convert_element_type x2 -> x5, other arithmetic: 1.74 us -> 0.17 us  [halved(): sent = (value[half:] * HALF).astype(jnp.float16)]
  transfers between devices with their start and end apart: 19 -> 15, of which waited for: 5 -> 8; matrix products, arithmetic and copies ran while one was open for 5% -> 7% of each run, Pallas kernels for 1% -> 0%
where the time goes in v7:
time: 155 us; the launch traced here: 154 us
  starting transfers between devices  78.8 us (51%)
  waiting for transfers between devices  49 us (32%)
  Pallas kernels  9.47 us (6%)
  other arithmetic  8.36 us (5%)
  local copies, waits for them, and re-layouts  4.42 us (3%)
  between operations  3.98 us (3%)
    ppermute x12, starting transfers between devices, swapped(): lax.ppermute(value, axis, [(i, i ^ step) for i in range(lax.axis_size(axi...  55.5 us
    ppermute x12, waiting for transfers between devices, swapped(): lax.ppermute(value, axis, [(i, i ^ step) for i in range(lax.axis_size(axi...  39.7 us
    all_to_all x1, starting transfers between devices, shards(): lax.all_to_all(jnp.broadcast_to(plane_loss, (column, 1, LANES)), COLUMN,...  9.86 us
    all_to_all x1, waiting for transfers between devices, shards(): lax.all_to_all(text_part.reshape(plane, 2 * rows, width + LANES), PLANE,...  9.27 us
    all_to_all x1, starting transfers between devices, shards(): lax.all_to_all(text_part.reshape(plane, 2 * rows, width + LANES), PLANE,...  6.76 us
    all_to_all x1, starting transfers between devices, shards(): lax.all_to_all(jnp.broadcast_to(texts[None], (plane, *texts.shape)), PLAN...  6.65 us
    pallas_call x1, Pallas kernels, pair_terms(): pl.pallas_call(pair_kernel, in_specs=[pl.BlockSpec(memory_space=pltpu.SME...  3.72 us
  transfers between devices with their start and end apart: 15, of which 8 were waited for; matrix products, arithmetic and copies ran while one was open for 7% of the time, Pallas kernels for 0%

profile of v7, /device:TPU:1, one launch (start us, length us, event | category | flops | bytes accessed | tf_op | source)
XLA Modules:
  0.0 154.0 jit_solution(6220323986617667401)
XLA Ops:
  1.9 1.8 %shard_map.67 = (bf16[24,1152]{1,0:T(8,128)(2,1)}, bf16[24,1152]{1,0:T(8,128)(2,1)}, f32[24,1]{1,0:T(8,128)}) custom-call(f32[1]{0:T(128)S(6)} %copy.13.heat_ref, f32[1]{0:T(128)S(6)} %copy.14.offset_ref, f32[24,1152]{1,0:T(8,128)} %picture_ref.3, f32[24,1152]{1,0:T(8,128)} %caption_ref.3), custom_call_target="tpu_custom_call" | custom-call | tf_op jit(solution)/shard_map/pallas_call | solution.py:56
  3.7 0.0 copy-start.2
  3.7 16.4 %collective-permute-start.4 = (bf16[24,1152]{1,0:T(8,128)(2,1)}, bf16[24,1152]{1,0:T(8,128)(2,1)S(1)}, u32[]{:S(2)}, u32[]{:S(2)}) collective-permute-start(bf16[24,1152]{1,0:T(8,128)(2,1)} %get-tuple-element.16), channel_id=1, source_target_pairs={{0,1},{1,0},{2,3},{3,2},{4,5},{5,4},{6,7},{7,6},{8,9},{9,8},{10,11... | collective-permute-start | bytes 165896 | tf_op jit(solution)/shard_map/ppermute | solution.py:170
  20.1 4.0 %collective-permute-start = (bf16[24,1152]{1,0:T(8,128)(2,1)}, bf16[24,1152]{1,0:T(8,128)(2,1)S(1)}, u32[]{:S(2)}, u32[]{:S(2)}) collective-permute-start(bf16[24,1152]{1,0:T(8,128)(2,1)} %get-tuple-element.15), channel_id=1, source_target_pairs={{0,256},{64,320},{128,384},{192,448},{256,0},{320,64},{384,128},{4... | collective-permute-start | bytes 165896 | tf_op jit(solution)/shard_map/ppermute | solution.py:170
  24.1 0.8 constant_dynamic-update-slice_fusion.4
  25.0 7.7 %collective-permute-done = bf16[24,1152]{1,0:T(8,128)(2,1)S(1)} collective-permute-done((bf16[24,1152]{1,0:T(8,128)(2,1)}, bf16[24,1152]{1,0:T(8,128)(2,1)S(1)}, u32[]{:S(2)}, u32[]{:S(2)}) %collective-permute-start) | collective-permute-done | bytes 55328 | tf_op jit(solution)/shard_map/ppermute | solution.py:170
  32.7 0.8 pad_maximum_fusion.2
  33.5 1.9 %collective-permute-start.1 = (bf16[48,1152]{1,0:T(8,128)(2,1)S(1)}, bf16[48,1152]{1,0:T(8,128)(2,1)S(1)}, u32[]{:S(2)}, u32[]{:S(2)}) collective-permute-start(bf16[48,1152]{1,0:T(8,128)(2,1)S(1)} %pad_maximum_fusion.2), channel_id=1, source_target_pairs={{0,128},{64,192},{128,0},{192,64},{256,384},{320,448},{384,256},{4... | collective-permute-start | bytes 331784 | tf_op jit(solution)/shard_map/ppermute | solution.py:170
  35.4 0.0 collective-permute-done.4
  35.4 0.8 pad_maximum_fusion.3
  36.3 1.0 broadcast_in_dim.4
  37.3 6.7 %all-to-all-start = ((bf16[8,48,1152]{2,1,0:T(8,128)(2,1)}), bf16[8,48,1152]{2,1,0:T(8,128)(2,1)S(1)}, u32[]{:S(2)}, u32[]{:S(2)}) async-start(bf16[8,48,1152]{2,1,0:T(8,128)(2,1)} %broadcast_in_dim.4), calls=%async_computation | async-start | bytes 1769472 | tf_op jit(solution)/shard_map/all_to_all | solution.py:190
  43.9 0.0 copy-start
  43.9 0.0 collective-permute-done.1
  43.9 0.0 copy-done.2
  44.0 1.9 %collective-permute-start.2 = (bf16[96,1152]{1,0:T(8,128)(2,1)S(1)}, bf16[96,1152]{1,0:T(8,128)(2,1)S(1)}, u32[]{:S(2)}, u32[]{:S(2)}) collective-permute-start(bf16[96,1152]{1,0:T(8,128)(2,1)S(1)} %pad_maximum_fusion.1), channel_id=1, source_target_pairs={{0,64},{64,0},{128,192},{192,128},{256,320},{320,256},{384,448},{4... | collective-permute-start | bytes 663560 | tf_op jit(solution)/shard_map/ppermute | solution.py:170
  45.9 5.3 %collective-permute-done.2 = bf16[96,1152]{1,0:T(8,128)(2,1)S(1)} collective-permute-done((bf16[96,1152]{1,0:T(8,128)(2,1)S(1)}, bf16[96,1152]{1,0:T(8,128)(2,1)S(1)}, u32[]{:S(2)}, u32[]{:S(2)}) %collective-permute-start.2) | collective-permute-done | bytes 221216 | tf_op jit(solution)/shard_map/ppermute | solution.py:170
  51.3 2.2 %collective-permute-start.3 = (bf16[192,1152]{1,0:T(8,128)(2,1)S(1)}, bf16[192,1152]{1,0:T(8,128)(2,1)S(1)}, u32[]{:S(2)}, u32[]{:S(2)}) collective-permute-start(bf16[192,1152]{1,0:T(8,128)(2,1)S(1)} %pad_maximum_fusion), channel_id=1, source_target_pairs={{0,16},{16,0},{1,17},{17,1},{2,18},{18,2},{3,19},{19,3},{4,20},{20... | collective-permute-start | bytes 1327112 | tf_op jit(solution)/shard_map/ppermute | solution.py:170
  53.5 8.8 %collective-permute-done.3 = bf16[192,1152]{1,0:T(8,128)(2,1)S(1)} collective-permute-done((bf16[192,1152]{1,0:T(8,128)(2,1)S(1)}, bf16[192,1152]{1,0:T(8,128)(2,1)S(1)}, u32[]{:S(2)}, u32[]{:S(2)}) %collective-permute-start.3) | collective-permute-done | bytes 442400 | tf_op jit(solution)/shard_map/ppermute | solution.py:170
  62.4 0.0 all-to-all-done
  62.4 5.3 %collective-permute-start.5 = (bf16[384,1152]{1,0:T(8,128)(2,1)S(1)}, bf16[384,1152]{1,0:T(8,128)(2,1)S(1)}, u32[]{:S(2)}, u32[]{:S(2)}) collective-permute-start(bf16[384,1152]{1,0:T(8,128)(2,1)S(1)} %constant_dynamic-update-slice_fusion.near_ref), channel_id=1, source_target_pairs={{0,8},{8,0},{1,9},{9,1},{2,10},{10,2},{3,11},{11,3},{4,12},{12,4},... | collective-permute-start | bytes 2654216 | tf_op jit(solution)/shard_map/ppermute | solution.py:170
  67.7 2.0 %collective-permute-done.5.far_ref = bf16[384,1152]{1,0:T(8,128)(2,1)S(1)} collective-permute-done((bf16[384,1152]{1,0:T(8,128)(2,1)S(1)}, bf16[384,1152]{1,0:T(8,128)(2,1)S(1)}, u32[]{:S(2)}, u32[]{:S(2)}) %collective-permute-start.5) | collective-permute-done | bytes 884768 | tf_op jit(solution)/shard_map/ppermute | solution.py:170
  69.7 0.0 copy-done
  69.7 3.7 %shard_map.68 = (bf16[768,384]{1,0:T(8,128)(2,1)S(1)}, bf16[384,1280]{1,0:T(8,128)(2,1)}) custom-call(s32[1]{0:T(128)} %bitcast.place_ref, f32[1]{0:T(128)S(6)} %copy.13.heat_ref, f32[1]{0:T(128)S(6)} %copy.14.offset_ref, f32[24,1]{1,0:T(8,128)S(1)} %copy-done, bf16[384,1152]{1,0:T(8,128)(2,1)S(1)} %constant_dynamic-update-slice_fusion.near_ref, ...), custom_call_target="tpu_custom_call" | custom-call | flops 1358954496 | bytes 3538944 | tf_op jit(solution)/shard_map/pallas_call | solution.py:114
  73.5 1.9 %shard_map.69 = (f32[384,1152]{1,0:T(8,128)S(1)}, f32[384,1152]{1,0:T(8,128)}) custom-call(bf16[768,384]{1,0:T(8,128)(2,1)S(1)} %get-tuple-element.20.weight_ref, bf16[384,1152]{1,0:T(8,128)(2,1)S(1)} %bitcast.5), custom_call_target="tpu_custom_call" | custom-call | flops 679477248 | bytes 7077888 | tf_op jit(solution)/shard_map/pallas_call | solution.py:137
  75.4 2.3 %collective-permute-start.6 = (f32[384,1152]{1,0:T(8,128)}, f32[384,1152]{1,0:T(8,128)S(1)}, u32[]{:S(2)}, u32[]{:S(2)}) collective-permute-start(f32[384,1152]{1,0:T(8,128)} %get-tuple-element.22), channel_id=1, source_target_pairs={{0,8},{8,0},{1,9},{9,1},{2,10},{10,2},{3,11},{11,3},{4,12},{12,4},... | collective-permute-start | bytes 5308424 | tf_op jit(solution)/shard_map/ppermute | solution.py:170
  77.6 6.8 %all-to-all-start.1 = ((bf16[8,48,1280]{2,1,0:T(8,128)(2,1)}), bf16[8,48,1280]{2,1,0:T(8,128)(2,1)}, u32[]{:S(2)}, u32[]{:S(2)}) async-start(bf16[8,48,1280]{2,1,0:T(8,128)(2,1)} %bitcast.2), calls=%async_computation.1 | async-start | bytes 1966080 | tf_op jit(solution)/shard_map/all_to_all | solution.py:201
  84.4 0.0 collective-permute-done.6
  84.4 0.0 copy-start.1
  84.4 1.2 copy-done.1
  85.6 1.7 %add.22 = f32[384,1152]{1,0:T(8,128)S(1)} add(f32[384,1152]{1,0:T(8,128)S(1)} %get-tuple-element.21, f32[384,1152]{1,0:T(8,128)} %copy-done.1) | non-fusion elementwise | flops 442368 | bytes 5308416 | tf_op jit(solution)/shard_map/add | solution.py:204
  87.3 0.1 fusion
  87.4 1.9 %collective-permute-start.7 = (f16[192,1152]{1,0:T(8,128)(2,1)S(1)}, f16[192,1152]{1,0:T(8,128)(2,1)S(1)}, u32[]{:S(2)}, u32[]{:S(2)}) collective-permute-start(f16[192,1152]{1,0:T(8,128)(2,1)S(1)} %fusion), channel_id=1, source_target_pairs={{0,16},{16,0},{1,17},{17,1},{2,18},{18,2},{3,19},{19,3},{4,20},{20... | collective-permute-start | bytes 1327112 | tf_op jit(solution)/shard_map/ppermute | solution.py:170
  89.3 9.3 %all-to-all-done.1 = bf16[8,48,1280]{2,1,0:T(8,128)(2,1)} async-done(((bf16[8,48,1280]{2,1,0:T(8,128)(2,1)}), bf16[8,48,1280]{2,1,0:T(8,128)(2,1)}, u32[]{:S(2)}, u32[]{:S(2)}) %all-to-all-start.1) | async-done | bytes 983072 | tf_op jit(solution)/shard_map/all_to_all | solution.py:201
  98.6 1.3 fusion.5
  99.9 1.3 broadcast_in_dim.10
  101.2 9.9 %all-to-all-start.2 = ((f32[64,1,128]{2,1,0:T(1,128)}), f32[64,1,128]{2,1,0:T(1,128)S(1)}, u32[]{:S(2)}, u32[]{:S(2)}) async-start(f32[64,1,128]{2,1,0:T(1,128)} %broadcast_in_dim.10), calls=%async_computation.2 | async-start | bytes 65536 | tf_op jit(solution)/shard_map/all_to_all | solution.py:209
  111.0 1.3 convert_reduce_fusion
  112.4 0.0 collective-permute-done.7
  112.4 0.1 slice_add_fusion
  112.5 3.3 %collective-permute-start.8 = (f16[96,1152]{1,0:T(8,128)(2,1)S(1)}, f16[96,1152]{1,0:T(8,128)(2,1)S(1)}, u32[]{:S(2)}, u32[]{:S(2)}) collective-permute-start(f16[96,1152]{1,0:T(8,128)(2,1)S(1)} %fusion.1), channel_id=1, source_target_pairs={{0,64},{64,0},{128,192},{192,128},{256,320},{320,256},{384,448},{4... | collective-permute-start | bytes 663560 | tf_op jit(solution)/shard_map/ppermute | solution.py:170
  115.9 10.9 %collective-permute-start.11 = (f16[24,1152]{1,0:T(8,128)(2,1)S(1)}, f16[24,1152]{1,0:T(8,128)(2,1)S(1)}, u32[]{:S(2)}, u32[]{:S(2)}) collective-permute-start(f16[24,1152]{1,0:T(8,128)(2,1)S(1)} %fusion.3), channel_id=1, source_target_pairs={{0,1},{1,0},{2,3},{3,2},{4,5},{5,4},{6,7},{7,6},{8,9},{9,8},{10,11... | collective-permute-start | bytes 165896 | tf_op jit(solution)/shard_map/ppermute | solution.py:170
  126.8 0.0 collective-permute-done.8
  126.8 0.1 slice_add_fusion.1
  126.9 2.2 %collective-permute-start.9 = (f16[48,1152]{1,0:T(8,128)(2,1)S(1)}, f16[48,1152]{1,0:T(8,128)(2,1)S(1)}, u32[]{:S(2)}, u32[]{:S(2)}) collective-permute-start(f16[48,1152]{1,0:T(8,128)(2,1)S(1)} %fusion.2), channel_id=1, source_target_pairs={{0,128},{64,192},{128,0},{192,64},{256,384},{320,448},{384,256},{4... | collective-permute-start | bytes 331784 | tf_op jit(solution)/shard_map/ppermute | solution.py:170
  129.1 1.9 %collective-permute-done.11 = f16[24,1152]{1,0:T(8,128)(2,1)S(1)} collective-permute-done((f16[24,1152]{1,0:T(8,128)(2,1)S(1)}, f16[24,1152]{1,0:T(8,128)(2,1)S(1)}, u32[]{:S(2)}, u32[]{:S(2)}) %collective-permute-start.11) | collective-permute-done | bytes 55328 | tf_op jit(solution)/shard_map/ppermute | solution.py:170
  131.0 0.7 slice_add_fusion.3.text_sum_ref
  131.6 6.9 %collective-permute-done.9 = f16[48,1152]{1,0:T(8,128)(2,1)S(1)} collective-permute-done((f16[48,1152]{1,0:T(8,128)(2,1)S(1)}, f16[48,1152]{1,0:T(8,128)(2,1)S(1)}, u32[]{:S(2)}, u32[]{:S(2)}) %collective-permute-start.9) | collective-permute-done | bytes 110624 | tf_op jit(solution)/shard_map/ppermute | solution.py:170
  138.5 3.1 %collective-permute-start.10 = (f16[24,1152]{1,0:T(8,128)(2,1)S(1)}, f16[24,1152]{1,0:T(8,128)(2,1)S(1)}, u32[]{:S(2)}, u32[]{:S(2)}) collective-permute-start(f16[24,1152]{1,0:T(8,128)(2,1)S(1)} %fusion.4), channel_id=1, source_target_pairs={{0,256},{64,320},{128,384},{192,448},{256,0},{320,64},{384,128},{4... | collective-permute-start | bytes 165896 | tf_op jit(solution)/shard_map/ppermute | solution.py:170
  141.6 0.0 all-to-all-done.2
  141.6 0.7 slice_reduce_fusion
  143.0 7.1 %collective-permute-done.10 = f16[24,1152]{1,0:T(8,128)(2,1)S(1)} collective-permute-done((f16[24,1152]{1,0:T(8,128)(2,1)S(1)}, f16[24,1152]{1,0:T(8,128)(2,1)S(1)}, u32[]{:S(2)}, u32[]{:S(2)}) %collective-permute-start.10) | collective-permute-done | bytes 55328 | tf_op jit(solution)/shard_map/ppermute | solution.py:170
  150.1 0.7 slice_add_fusion.4.image_sum_ref
  150.8 2.1 %shard_map.70 = (f32[24,1152]{1,0:T(8,128)}, f32[24,1152]{1,0:T(8,128)}) custom-call(f32[1]{0:T(128)S(6)} %copy.13.heat_ref, f32[1]{0:T(128)S(6)} %copy.14.offset_ref, f32[24,1152]{1,0:T(8,128)} %picture_ref.3, f32[24,1152]{1,0:T(8,128)} %caption_ref.3, f32[24,1152]{1,0:T(8,128)} %slice_add_fusion.4.image_sum_ref, f32[24,1152]{1,0:T(8,128)} %slice_add_fusion.3.text_sum_ref), custom_call_target="tpu_custom_call" | custom-call | tf_op jit(solution)/shard_map/pallas_call | solution.py:162
  (11 shorter events, 0.3 us)
Async XLA Ops:
  3.7 40.2 %copy-start.2 = (bf16[24,1152]{1,0:T(8,128)(2,1)S(1)}, bf16[24,1152]{1,0:T(8,128)(2,1)}, u32[]{:S(2)}) copy-start(bf16[24,1152]{1,0:T(8,128)(2,1)} %get-tuple-element.15) | copy-start | bytes 165892
  3.7 31.7 %collective-permute-start.4 = (bf16[24,1152]{1,0:T(8,128)(2,1)}, bf16[24,1152]{1,0:T(8,128)(2,1)S(1)}, u32[]{:S(2)}, u32[]{:S(2)}) collective-permute-start(bf16[24,1152]{1,0:T(8,128)(2,1)} %get-tuple-element.16), channel_id=1, source_target_pairs={{0,1},{1,0},{2,3},{3,2},{4,5},{5,4},{6,7},{7,6},{8,9},{9,8},{10,11... | collective-permute-start | bytes 165896 | tf_op jit(solution)/shard_map/ppermute | solution.py:170
  20.1 12.6 %collective-permute-start = (bf16[24,1152]{1,0:T(8,128)(2,1)}, bf16[24,1152]{1,0:T(8,128)(2,1)S(1)}, u32[]{:S(2)}, u32[]{:S(2)}) collective-permute-start(bf16[24,1152]{1,0:T(8,128)(2,1)} %get-tuple-element.15), channel_id=1, source_target_pairs={{0,256},{64,320},{128,384},{192,448},{256,0},{320,64},{384,128},{4... | collective-permute-start | bytes 165896 | tf_op jit(solution)/shard_map/ppermute | solution.py:170
  33.5 10.4 %collective-permute-start.1 = (bf16[48,1152]{1,0:T(8,128)(2,1)S(1)}, bf16[48,1152]{1,0:T(8,128)(2,1)S(1)}, u32[]{:S(2)}, u32[]{:S(2)}) collective-permute-start(bf16[48,1152]{1,0:T(8,128)(2,1)S(1)} %pad_maximum_fusion.2), channel_id=1, source_target_pairs={{0,128},{64,192},{128,0},{192,64},{256,384},{320,448},{384,256},{4... | collective-permute-start | bytes 331784 | tf_op jit(solution)/shard_map/ppermute | solution.py:170
  37.3 25.1 %all-to-all-start = ((bf16[8,48,1152]{2,1,0:T(8,128)(2,1)}), bf16[8,48,1152]{2,1,0:T(8,128)(2,1)S(1)}, u32[]{:S(2)}, u32[]{:S(2)}) async-start(bf16[8,48,1152]{2,1,0:T(8,128)(2,1)} %broadcast_in_dim.4), calls=%async_computation | async-start | bytes 1769472 | tf_op jit(solution)/shard_map/all_to_all | solution.py:190
  43.9 25.8 %copy-start = (f32[24,1]{1,0:T(8,128)S(1)}, f32[24,1]{1,0:T(8,128)}, u32[]{:S(2)}) copy-start(f32[24,1]{1,0:T(8,128)} %get-tuple-element.14.own_loss_ref) | copy-start | bytes 292
  44.0 7.3 %collective-permute-start.2 = (bf16[96,1152]{1,0:T(8,128)(2,1)S(1)}, bf16[96,1152]{1,0:T(8,128)(2,1)S(1)}, u32[]{:S(2)}, u32[]{:S(2)}) collective-permute-start(bf16[96,1152]{1,0:T(8,128)(2,1)S(1)} %pad_maximum_fusion.1), channel_id=1, source_target_pairs={{0,64},{64,0},{128,192},{192,128},{256,320},{320,256},{384,448},{4... | collective-permute-start | bytes 663560 | tf_op jit(solution)/shard_map/ppermute | solution.py:170
  51.3 11.1 %collective-permute-start.3 = (bf16[192,1152]{1,0:T(8,128)(2,1)S(1)}, bf16[192,1152]{1,0:T(8,128)(2,1)S(1)}, u32[]{:S(2)}, u32[]{:S(2)}) collective-permute-start(bf16[192,1152]{1,0:T(8,128)(2,1)S(1)} %pad_maximum_fusion), channel_id=1, source_target_pairs={{0,16},{16,0},{1,17},{17,1},{2,18},{18,2},{3,19},{19,3},{4,20},{20... | collective-permute-start | bytes 1327112 | tf_op jit(solution)/shard_map/ppermute | solution.py:170
  62.4 7.4 %collective-permute-start.5 = (bf16[384,1152]{1,0:T(8,128)(2,1)S(1)}, bf16[384,1152]{1,0:T(8,128)(2,1)S(1)}, u32[]{:S(2)}, u32[]{:S(2)}) collective-permute-start(bf16[384,1152]{1,0:T(8,128)(2,1)S(1)} %constant_dynamic-update-slice_fusion.near_ref), channel_id=1, source_target_pairs={{0,8},{8,0},{1,9},{9,1},{2,10},{10,2},{3,11},{11,3},{4,12},{12,4},... | collective-permute-start | bytes 2654216 | tf_op jit(solution)/shard_map/ppermute | solution.py:170
  75.4 9.0 %collective-permute-start.6 = (f32[384,1152]{1,0:T(8,128)}, f32[384,1152]{1,0:T(8,128)S(1)}, u32[]{:S(2)}, u32[]{:S(2)}) collective-permute-start(f32[384,1152]{1,0:T(8,128)} %get-tuple-element.22), channel_id=1, source_target_pairs={{0,8},{8,0},{1,9},{9,1},{2,10},{10,2},{3,11},{11,3},{4,12},{12,4},... | collective-permute-start | bytes 5308424 | tf_op jit(solution)/shard_map/ppermute | solution.py:170
  77.6 20.9 %all-to-all-start.1 = ((bf16[8,48,1280]{2,1,0:T(8,128)(2,1)}), bf16[8,48,1280]{2,1,0:T(8,128)(2,1)}, u32[]{:S(2)}, u32[]{:S(2)}) async-start(bf16[8,48,1280]{2,1,0:T(8,128)(2,1)} %bitcast.2), calls=%async_computation.1 | async-start | bytes 1966080 | tf_op jit(solution)/shard_map/all_to_all | solution.py:201
  84.4 1.2 copy-start.1
  87.4 25.0 %collective-permute-start.7 = (f16[192,1152]{1,0:T(8,128)(2,1)S(1)}, f16[192,1152]{1,0:T(8,128)(2,1)S(1)}, u32[]{:S(2)}, u32[]{:S(2)}) collective-permute-start(f16[192,1152]{1,0:T(8,128)(2,1)S(1)} %fusion), channel_id=1, source_target_pairs={{0,16},{16,0},{1,17},{17,1},{2,18},{18,2},{3,19},{19,3},{4,20},{20... | collective-permute-start | bytes 1327112 | tf_op jit(solution)/shard_map/ppermute | solution.py:170
  101.2 40.5 %all-to-all-start.2 = ((f32[64,1,128]{2,1,0:T(1,128)}), f32[64,1,128]{2,1,0:T(1,128)S(1)}, u32[]{:S(2)}, u32[]{:S(2)}) async-start(f32[64,1,128]{2,1,0:T(1,128)} %broadcast_in_dim.10), calls=%async_computation.2 | async-start | bytes 65536 | tf_op jit(solution)/shard_map/all_to_all | solution.py:209
  112.5 14.2 %collective-permute-start.8 = (f16[96,1152]{1,0:T(8,128)(2,1)S(1)}, f16[96,1152]{1,0:T(8,128)(2,1)S(1)}, u32[]{:S(2)}, u32[]{:S(2)}) collective-permute-start(f16[96,1152]{1,0:T(8,128)(2,1)S(1)} %fusion.1), channel_id=1, source_target_pairs={{0,64},{64,0},{128,192},{192,128},{256,320},{320,256},{384,448},{4... | collective-permute-start | bytes 663560 | tf_op jit(solution)/shard_map/ppermute | solution.py:170
  115.9 15.1 %collective-permute-start.11 = (f16[24,1152]{1,0:T(8,128)(2,1)S(1)}, f16[24,1152]{1,0:T(8,128)(2,1)S(1)}, u32[]{:S(2)}, u32[]{:S(2)}) collective-permute-start(f16[24,1152]{1,0:T(8,128)(2,1)S(1)} %fusion.3), channel_id=1, source_target_pairs={{0,1},{1,0},{2,3},{3,2},{4,5},{5,4},{6,7},{7,6},{8,9},{9,8},{10,11... | collective-permute-start | bytes 165896 | tf_op jit(solution)/shard_map/ppermute | solution.py:170
  126.9 11.6 %collective-permute-start.9 = (f16[48,1152]{1,0:T(8,128)(2,1)S(1)}, f16[48,1152]{1,0:T(8,128)(2,1)S(1)}, u32[]{:S(2)}, u32[]{:S(2)}) collective-permute-start(f16[48,1152]{1,0:T(8,128)(2,1)S(1)} %fusion.2), channel_id=1, source_target_pairs={{0,128},{64,192},{128,0},{192,64},{256,384},{320,448},{384,256},{4... | collective-permute-start | bytes 331784 | tf_op jit(solution)/shard_map/ppermute | solution.py:170
  138.5 11.5 %collective-permute-start.10 = (f16[24,1152]{1,0:T(8,128)(2,1)S(1)}, f16[24,1152]{1,0:T(8,128)(2,1)S(1)}, u32[]{:S(2)}, u32[]{:S(2)}) collective-permute-start(f16[24,1152]{1,0:T(8,128)(2,1)S(1)} %fusion.4), channel_id=1, source_target_pairs={{0,256},{64,320},{128,384},{192,448},{256,0},{320,64},{384,128},{4... | collective-permute-start | bytes 165896 | tf_op jit(solution)/shard_map/ppermute | solution.py:170

commit v8 on v6

v8 whole, which is shorter than its diff:
```python
import jax
import jax.numpy as jnp
from jax import lax
from jax.experimental import pallas as pl
from jax.experimental.pallas import tpu as pltpu
from jax.sharding import Mesh, PartitionSpec as P

epsilon = 1e-06
AXES = ("zl", "x", "c", "y", "zh")
SIZES = (8, 4, 2, 4, 2)
PLANE = ("x", "y")
COLUMN = ("zl", "c", "zh")
LANES = 128
LIMIT = 20 * 1024 * 1024
HALF = 0.5


def normalize(raw_rows):
    row_norm = jnp.sqrt(jnp.sum(raw_rows * raw_rows, axis=1, keepdims=True) + epsilon)
    return (raw_rows / row_norm, row_norm)


def back_norm(unit_rows, row_norm, gradient):
    return (gradient - unit_rows * jnp.sum(unit_rows * gradient, axis=1, keepdims=True)) / row_norm


def low(rows):
    return rows.astype(jnp.bfloat16).astype(jnp.float32)


def loss_and_sigmoid(values):
    small = jnp.exp(-jnp.abs(values))
    loss = jnp.maximum(values, 0.0) + jnp.log1p(small)
    return loss, jnp.where(values >= 0, 1.0, small) / (1.0 + small)


def own_pairs(image_low, text_low, heat, offset):
    return jnp.sum(image_low * text_low, axis=1, keepdims=True) * heat + offset


def unit_kernel(heat_ref, offset_ref, picture_ref, caption_ref, image_ref, own_ref, text_ref, loss_ref):
    image_unit, _ = normalize(picture_ref[...])
    text_unit, _ = normalize(caption_ref[...])
    image_low, text_low = image_unit.astype(jnp.bfloat16), text_unit.astype(jnp.bfloat16)
    image_ref[...] = image_low
    text_ref[...] = jnp.broadcast_to(jnp.concatenate([text_low, text_low], axis=0)[None], text_ref.shape)
    own_ref[...] = text_low
    heat = jnp.exp(jnp.full((1, 1), heat_ref[0], jnp.float32))
    logits = own_pairs(image_low.astype(jnp.float32), text_low.astype(jnp.float32), heat, offset_ref[0])
    loss, _ = loss_and_sigmoid(-logits)
    loss_ref[...] = loss


def unit_rows(copies, heat_exponent, offset_added, pictures, captions):
    rows, width = pictures.shape
    return pl.pallas_call(
        unit_kernel,
        in_specs=[pl.BlockSpec(memory_space=pltpu.SMEM)] * 2 + [pl.BlockSpec(memory_space=pltpu.VMEM)] * 2,
        out_shape=[
            jax.ShapeDtypeStruct(pictures.shape, jnp.bfloat16),
            jax.ShapeDtypeStruct(captions.shape, jnp.bfloat16),
            jax.ShapeDtypeStruct((copies, 2 * rows, width), jnp.bfloat16),
            jax.ShapeDtypeStruct((rows, 1), jnp.float32),
        ],
    )(heat_exponent, offset_added, pictures, captions)


def pieces(total, shape):
    first = low(total)
    second = low(total - first)
    third = total - first - second
    lane = lax.broadcasted_iota(jnp.int32, shape, len(shape) - 1)
    spread = jnp.where(lane == 0, first, jnp.where(lane == 1, second, jnp.where(lane == 2, third, 0.0)))
    return spread.astype(jnp.bfloat16)


def pair_kernel(
    place_ref, heat_ref, offset_ref, own_loss_ref, near_ref, far_ref, text_ref, weight_ref, far_out_ref, loss_ref
):
    rows = own_loss_ref.shape[0]
    texts = text_ref[...]
    heat = jnp.exp(jnp.full((1, 1), heat_ref[0], jnp.float32))
    total = jnp.sum(own_loss_ref[...], axis=0, keepdims=True)
    for place, image_ref in enumerate((near_ref, far_ref)):
        logits = lax.dot_general(
            image_ref[...], texts, (((1,), (1,)), ((), ())), preferred_element_type=jnp.float32
        )
        logits = logits * heat + offset_ref[0]
        loss, sigmoid = loss_and_sigmoid(logits)
        weights = heat * sigmoid
        if image_ref is near_ref:
            image_row = lax.broadcasted_iota(jnp.int32, logits.shape, 0)
            text_row = lax.broadcasted_iota(jnp.int32, logits.shape, 1) - place_ref[0]
            match = (image_row == text_row) & (image_row < rows)
            weights = jnp.where(match, 0.0, weights)
            loss = jnp.where(match, 0.0, loss)
        weights = weights.astype(jnp.bfloat16)
        weight_ref[place] = weights
        total += jnp.sum(jnp.sum(loss, axis=0, keepdims=True), axis=1, keepdims=True)
    far_out_ref[...] = jnp.dot(weights, texts, preferred_element_type=jnp.float32)
    loss_ref[...] = jnp.broadcast_to(total, loss_ref.shape)


def pair_weights(place, heat_exponent, offset_added, own_loss, near, far, texts):
    half, width = near.shape
    count = texts.shape[0]
    return pl.pallas_call(
        pair_kernel,
        in_specs=[pl.BlockSpec(memory_space=pltpu.SMEM)] * 3 + [pl.BlockSpec(memory_space=pltpu.VMEM)] * 4,
        out_shape=[
            jax.ShapeDtypeStruct((2, half, count), jnp.bfloat16),
            jax.ShapeDtypeStruct((half, width), jnp.float32),
            jax.ShapeDtypeStruct((8, LANES), jnp.float32),
        ],
        compiler_params=pltpu.CompilerParams(vmem_limit_bytes=LIMIT),
        cost_estimate=pl.CostEstimate(
            flops=6 * half * count * width, bytes_accessed=8 * half * width, transcendentals=6 * half * count
        ),
    )(place, heat_exponent, offset_added, own_loss, near, far, texts)


def terms_kernel(weight_ref, loss_ref, near_ref, far_ref, text_ref, near_out_ref, text_out_ref):
    width = near_ref.shape[1]
    text_part = lax.dot_general(
        weight_ref[0], near_ref[...], (((0,), (0,)), ((), ())), preferred_element_type=jnp.float32
    )
    text_part += lax.dot_general(
        weight_ref[1], far_ref[...], (((0,), (0,)), ((), ())), preferred_element_type=jnp.float32
    )
    text_out_ref[:, :width] = text_part.astype(jnp.bfloat16)
    text_out_ref[:, width:] = pieces(loss_ref[:1, :1], (text_out_ref.shape[0], LANES))
    near_out_ref[...] = jnp.dot(weight_ref[0], text_ref[...], preferred_element_type=jnp.float32)


def pair_terms(weights, loss, near, far, texts):
    count, width = texts.shape
    return pl.pallas_call(
        terms_kernel,
        in_specs=[pl.BlockSpec(memory_space=pltpu.VMEM)] * 5,
        out_shape=[
            jax.ShapeDtypeStruct(near.shape, jnp.float32),
            jax.ShapeDtypeStruct((count, width + LANES), jnp.bfloat16),
        ],
        compiler_params=pltpu.CompilerParams(vmem_limit_bytes=LIMIT),
        cost_estimate=pl.CostEstimate(flops=3 * weights.size * width, bytes_accessed=16 * near.size, transcendentals=0),
    )(weights, loss, near, far, texts)


def grad_kernel(
    heat_ref, offset_ref, picture_ref, caption_ref, image_sum_ref, text_sum_ref, image_ref, text_ref
):
    image_unit, image_norm = normalize(picture_ref[...])
    text_unit, text_norm = normalize(caption_ref[...])
    image_low, text_low = low(image_unit), low(text_unit)
    heat = jnp.exp(jnp.full((1, 1), heat_ref[0], jnp.float32))
    _, sigmoid = loss_and_sigmoid(-own_pairs(image_low, text_low, heat, offset_ref[0]))
    weights = low(-sigmoid * heat)
    image_ref[...] = back_norm(image_unit, image_norm, image_sum_ref[...] + weights * text_low)
    text_ref[...] = back_norm(text_unit, text_norm, text_sum_ref[...] + weights * image_low)


def gradients(heat_exponent, offset_added, pictures, captions, image_sum, text_sum):
    return pl.pallas_call(
        grad_kernel,
        in_specs=[pl.BlockSpec(memory_space=pltpu.SMEM)] * 2 + [pl.BlockSpec(memory_space=pltpu.VMEM)] * 4,
        out_shape=[jax.ShapeDtypeStruct(pictures.shape, jnp.float32)] * 2,
    )(heat_exponent, offset_added, pictures, captions, image_sum, text_sum)


def swapped(value, axis, step):
    return lax.ppermute(value, axis, [(i, i ^ step) for i in range(lax.axis_size(axis))])


def doubled(value, axis, step):
    return jnp.concatenate([value, swapped(value, axis, step)], axis=0)


def halved(value, axis, step):
    half = value.shape[0] // 2
    sent = (value[half:] * HALF).astype(jnp.float16)
    return value[:half] + swapped(sent, axis, step).astype(jnp.float32) * (1 / HALF)


def shards(picture_vectors, caption_vectors, heat_exponent, offset_added):
    rows, width = picture_vectors.shape
    plane, column = lax.axis_size(PLANE), lax.axis_size(COLUMN)
    steps = [1 << bit for bit in range(lax.axis_size("zl").bit_length() - 1)]
    image_low, text_low, copies, own_loss = unit_rows(
        plane, heat_exponent, offset_added, picture_vectors, caption_vectors
    )

    other_low = jnp.broadcast_to(swapped(text_low, "zh", 1)[None], (plane, rows, width))
    texts = lax.all_to_all(lax.dynamic_update_slice(copies, other_low, (0, rows, 0)), PLANE, 0, 0)
    texts = texts.reshape(plane * 2 * rows, width)
    near = image_low
    for step in reversed(steps):
        near = doubled(near, "zl", step)
    far = swapped(near, "c", 1)

    place = (lax.axis_index(PLANE) * 2 * rows).astype(jnp.int32).reshape(1)
    weights, far_part, loss = pair_weights(place, heat_exponent, offset_added, own_loss, near, far, texts)
    far_part = swapped(far_part, "c", 1)
    near_part, text_part = pair_terms(weights, loss, near, far, texts)
    text_parts = lax.all_to_all(text_part.reshape(plane, 2 * rows, width + LANES), PLANE, 0, 0)
    image_sum = near_part + far_part
    for step in steps:
        image_sum = halved(image_sum, "zl", step)

    plane_loss = jnp.sum(text_parts[:, 0, width : width + 3].astype(jnp.float32))
    losses = lax.all_to_all(jnp.broadcast_to(plane_loss, (column, 1, LANES)), COLUMN, 0, 0)
    loss_mean = (jnp.sum(losses[:, 0, 0]) / (rows * lax.axis_size(AXES))).reshape(1)
    text_sum = jnp.sum(text_parts[:, :, :width].astype(jnp.float32), axis=0)
    text_sum = halved(text_sum, "zh", 1)
    image_grads, text_grads = gradients(
        heat_exponent, offset_added, picture_vectors, caption_vectors, image_sum, text_sum
    )
    return (loss_mean, image_grads, text_grads)


def solution(mesh):
    fine = Mesh(mesh.devices.reshape(SIZES), AXES)
    in_specs = (P(AXES, None), P(AXES, None), P(), P())
    out_specs = (P(), P(AXES, None), P(AXES, None))
    return jax.shard_map(shards, mesh=fine, in_specs=in_specs, out_specs=out_specs, check_vma=False)
```

time: 150 us -> 136 us (0.907)
  blocking collectives: 9.6 us -> 0 us
  starting transfers between devices: 80.6 us -> 76.8 us
  waiting for transfers between devices: 41 us -> 39.2 us
    all_to_all x1 -> x0, blocking collectives: 9.6 us -> none  [shards(): loss = jnp.sum(lax.all_to_all(loss, PLANE, 0, 0)[:, :4], axis=0)]
    ppermute x12 -> x10, starting transfers between devices: 66.3 us -> 58 us  [swapped(): lax.ppermute(value, axis, [(i, i ^ step) for i in range(lax.axis_size(axi...]
    all_to_all x3, starting transfers between devices: 14.4 us -> 18.8 us  [the longest x1 8.19 us: shards(): lax.all_to_all(jnp.broadcast_to(plane_loss, (column, 1, LANES)), COLUMN,...]
    ppermute x12 -> x10, waiting for transfers between devices: 30.3 us -> 28.3 us  [swapped(): lax.ppermute(value, axis, [(i, i ^ step) for i in range(lax.axis_size(axi...]
    concatenate x7 -> x0, other arithmetic: 1.55 us -> none  [the longest x1 1.4 us: shards(): texts = lax.all_to_all(jnp.concatenate(copies, axis=1), PLANE, 0, 0)]
  transfers between devices with their start and end apart: 15 -> 13, of which waited for: 6 -> 9; matrix products, arithmetic and copies ran while one was open for 3% -> 3% of each run, Pallas kernels for 1% -> 4%
where the time goes in v8:
time: 136 us; the launch traced here: 135 us
  starting transfers between devices  76.8 us (56%)
  waiting for transfers between devices  39.2 us (29%)
  Pallas kernels  9.57 us (7%)
  between operations  3.92 us (3%)
  other arithmetic  3.1 us (2%)
  local copies, waits for them, and re-layouts  2.36 us (2%)
    ppermute x10, starting transfers between devices, swapped(): lax.ppermute(value, axis, [(i, i ^ step) for i in range(lax.axis_size(axi...  58 us
    ppermute x10, waiting for transfers between devices, swapped(): lax.ppermute(value, axis, [(i, i ^ step) for i in range(lax.axis_size(axi...  28.3 us
    all_to_all x1, waiting for transfers between devices, shards(): lax.all_to_all(jnp.broadcast_to(plane_loss, (column, 1, LANES)), COLUMN,...  8.79 us
    all_to_all x1, starting transfers between devices, shards(): lax.all_to_all(jnp.broadcast_to(plane_loss, (column, 1, LANES)), COLUMN,...  8.19 us
    all_to_all x1, starting transfers between devices, shards(): lax.all_to_all(lax.dynamic_update_slice(copies, other_low, (0, rows, 0)),...  6.89 us
    all_to_all x1, starting transfers between devices, shards(): lax.all_to_all(text_part.reshape(plane, 2 * rows, width + LANES), PLANE,...  3.73 us
    pallas_call x1, Pallas kernels, pair_terms(): pl.pallas_call(terms_kernel, in_specs=[pl.BlockSpec(memory_space=pltpu.VM...  2.86 us
  transfers between devices with their start and end apart: 13, of which 9 were waited for; matrix products, arithmetic and copies ran while one was open for 3% of the time, Pallas kernels for 4%

profile of v8, /device:TPU:1, one launch (start us, length us, event | category | flops | bytes accessed | tf_op | source)
XLA Modules:
  0.0 135.0 jit_solution(17061379978541741552)
XLA Ops:
  1.9 2.4 %shard_map.67 = (bf16[24,1152]{1,0:T(8,128)(2,1)}, bf16[24,1152]{1,0:T(8,128)(2,1)}, bf16[16,48,1152]{2,1,0:T(8,128)(2,1)}, f32[24,1]{1,0:T(8,128)}) custom-call(f32[1]{0:T(128)S(6)} %copy.13.heat_ref, f32[1]{0:T(128)S(6)} %copy.14.offset_ref, f32[24,1152]{1,0:T(8,128)} %picture_ref.3, f32[24,1152]{1,0:T(8,128)} %caption_ref.3), custom_call_target="tpu_custom_call" | custom-call | tf_op jit(solution)/shard_map/pallas_call | solution.py:56
  4.4 16.3 %collective-permute-start.4 = (bf16[24,1152]{1,0:T(8,128)(2,1)}, bf16[24,1152]{1,0:T(8,128)(2,1)S(1)}, u32[]{:S(2)}, u32[]{:S(2)}) collective-permute-start(bf16[24,1152]{1,0:T(8,128)(2,1)} %get-tuple-element.17), channel_id=1, source_target_pairs={{0,1},{1,0},{2,3},{3,2},{4,5},{5,4},{6,7},{7,6},{8,9},{9,8},{10,11... | collective-permute-start | bytes 165896 | tf_op jit(solution)/shard_map/ppermute | solution.py:171
  20.6 4.0 %collective-permute-start = (bf16[24,1152]{1,0:T(8,128)(2,1)}, bf16[24,1152]{1,0:T(8,128)(2,1)S(1)}, u32[]{:S(2)}, u32[]{:S(2)}) collective-permute-start(bf16[24,1152]{1,0:T(8,128)(2,1)} %get-tuple-element.15), channel_id=1, source_target_pairs={{0,256},{64,320},{128,384},{192,448},{256,0},{320,64},{384,128},{4... | collective-permute-start | bytes 165896 | tf_op jit(solution)/shard_map/ppermute | solution.py:171
  24.7 0.0 collective-permute-done.4
  24.7 1.0 broadcast_dynamic-update-slice_fusion
  25.7 0.0 copy-start.1
  25.7 0.0 copy-start
  25.7 6.9 %all-to-all-start = ((bf16[16,48,1152]{2,1,0:T(8,128)(2,1)}), bf16[16,48,1152]{2,1,0:T(8,128)(2,1)S(1)}, u32[]{:S(2)}, u32[]{:S(2)}) async-start(bf16[16,48,1152]{2,1,0:T(8,128)(2,1)} %broadcast_dynamic-update-slice_fusion), calls=%async_computation | async-start | bytes 3538944 | tf_op jit(solution)/shard_map/all_to_all | solution.py:193
  32.6 0.0 copy-done.1
  32.6 0.6 collective-permute-done
  33.2 2.5 %collective-permute-start.1 = (bf16[48,1152]{1,0:T(8,128)(2,1)S(1)}, bf16[48,1152]{1,0:T(8,128)(2,1)S(1)}, u32[]{:S(2)}, u32[]{:S(2)}) collective-permute-start(bf16[48,1152]{1,0:T(8,128)(2,1)S(1)} %pad_maximum_fusion.1), channel_id=1, source_target_pairs={{0,128},{64,192},{128,0},{192,64},{256,384},{320,448},{384,256},{4... | collective-permute-start | bytes 331784 | tf_op jit(solution)/shard_map/ppermute | solution.py:171
  35.8 6.8 %collective-permute-done.1 = bf16[48,1152]{1,0:T(8,128)(2,1)S(1)} collective-permute-done((bf16[48,1152]{1,0:T(8,128)(2,1)S(1)}, bf16[48,1152]{1,0:T(8,128)(2,1)S(1)}, u32[]{:S(2)}, u32[]{:S(2)}) %collective-permute-start.1) | collective-permute-done | bytes 110624 | tf_op jit(solution)/shard_map/ppermute | solution.py:171
  42.6 1.9 %collective-permute-start.2 = (bf16[96,1152]{1,0:T(8,128)(2,1)S(1)}, bf16[96,1152]{1,0:T(8,128)(2,1)S(1)}, u32[]{:S(2)}, u32[]{:S(2)}) collective-permute-start(bf16[96,1152]{1,0:T(8,128)(2,1)S(1)} %pad_maximum_fusion), channel_id=1, source_target_pairs={{0,64},{64,0},{128,192},{192,128},{256,320},{320,256},{384,448},{4... | collective-permute-start | bytes 663560 | tf_op jit(solution)/shard_map/ppermute | solution.py:171
  44.6 5.7 %collective-permute-done.2 = bf16[96,1152]{1,0:T(8,128)(2,1)S(1)} collective-permute-done((bf16[96,1152]{1,0:T(8,128)(2,1)S(1)}, bf16[96,1152]{1,0:T(8,128)(2,1)S(1)}, u32[]{:S(2)}, u32[]{:S(2)}) %collective-permute-start.2) | collective-permute-done | bytes 221216 | tf_op jit(solution)/shard_map/ppermute | solution.py:171
  50.4 4.0 %collective-permute-start.3 = (bf16[192,1152]{1,0:T(8,128)(2,1)S(1)}, bf16[192,1152]{1,0:T(8,128)(2,1)S(1)}, u32[]{:S(2)}, u32[]{:S(2)}) collective-permute-start(bf16[192,1152]{1,0:T(8,128)(2,1)S(1)} %constant_dynamic-update-slice_fusion.near_ref), channel_id=1, source_target_pairs={{0,8},{8,0},{1,9},{9,1},{2,10},{10,2},{3,11},{11,3},{4,12},{12,4},... | collective-permute-start | bytes 1327112 | tf_op jit(solution)/shard_map/ppermute | solution.py:171
  54.3 1.4 %collective-permute-done.3.far_ref = bf16[192,1152]{1,0:T(8,128)(2,1)S(1)} collective-permute-done((bf16[192,1152]{1,0:T(8,128)(2,1)S(1)}, bf16[192,1152]{1,0:T(8,128)(2,1)S(1)}, u32[]{:S(2)}, u32[]{:S(2)}) %collective-permute-start.3) | collective-permute-done | bytes 442400 | tf_op jit(solution)/shard_map/ppermute | solution.py:171
  55.7 0.0 all-to-all-done
  55.7 0.0 copy-done
  55.7 2.2 %shard_map.68 = (bf16[2,192,768]{2,1,0:T(8,128)(2,1)S(1)}, f32[192,1152]{1,0:T(8,128)S(1)}, f32[8,128]{1,0:T(8,128)S(1)}) custom-call(s32[1]{0:T(128)} %bitcast.place_ref, f32[1]{0:T(128)S(6)} %copy.13.heat_ref, f32[1]{0:T(128)S(6)} %copy.14.offset_ref, f32[24,1]{1,0:T(8,128)S(1)} %copy-done, ...), custom_call_target="tpu_custom_call" | custom-call | flops 1019215872 | bytes 1769472 | tf_op jit(solution)/shard_map/pallas_call | solution.py:107
  57.9 5.8 %collective-permute-start.5 = (f32[192,1152]{1,0:T(8,128)S(1)}, f32[192,1152]{1,0:T(8,128)S(1)}, u32[]{:S(2)}, u32[]{:S(2)}) collective-permute-start(f32[192,1152]{1,0:T(8,128)S(1)} %get-tuple-element.22), channel_id=1, source_target_pairs={{0,8},{8,0},{1,9},{9,1},{2,10},{10,2},{3,11},{11,3},{4,12},{12,4},... | collective-permute-start | bytes 2654216 | tf_op jit(solution)/shard_map/ppermute | solution.py:171
  63.7 2.9 %shard_map.69 = (f32[192,1152]{1,0:T(8,128)S(1)}, bf16[768,1280]{1,0:T(8,128)(2,1)}) custom-call(bf16[2,192,768]{2,1,0:T(8,128)(2,1)S(1)} %get-tuple-element.18.weight_ref, f32[8,128]{1,0:T(8,128)S(1)} %get-tuple-element.19.loss_ref, bf16[192,1152]{1,0:T(8,128)(2,1)S(1)} %constant_dynamic-update-slice_fusion.near_ref, ...), custom_call_target="tpu_custom_call" | custom-call | flops 1019215872 | bytes 3538944 | tf_op jit(solution)/shard_map/pallas_call | solution.py:137
  66.6 0.0 collective-permute-done.5
  66.6 0.1 add.19
  66.7 2.6 %collective-permute-start.6 = (f16[96,1152]{1,0:T(8,128)(2,1)S(1)}, f16[96,1152]{1,0:T(8,128)(2,1)S(1)}, u32[]{:S(2)}, u32[]{:S(2)}) collective-permute-start(f16[96,1152]{1,0:T(8,128)(2,1)S(1)} %fusion), channel_id=1, source_target_pairs={{0,64},{64,0},{128,192},{192,128},{256,320},{320,256},{384,448},{4... | collective-permute-start | bytes 663560 | tf_op jit(solution)/shard_map/ppermute | solution.py:171
  69.4 3.7 %all-to-all-start.1 = ((bf16[16,48,1280]{2,1,0:T(8,128)(2,1)}), bf16[16,48,1280]{2,1,0:T(8,128)(2,1)S(1)}, u32[]{:S(2)}, u32[]{:S(2)}) async-start(bf16[16,48,1280]{2,1,0:T(8,128)(2,1)} %bitcast.2), calls=%async_computation.1 | async-start | bytes 3932160 | tf_op jit(solution)/shard_map/all_to_all | solution.py:204
  73.1 2.6 %collective-permute-done.6 = f16[96,1152]{1,0:T(8,128)(2,1)S(1)} collective-permute-done((f16[96,1152]{1,0:T(8,128)(2,1)S(1)}, f16[96,1152]{1,0:T(8,128)(2,1)S(1)}, u32[]{:S(2)}, u32[]{:S(2)}) %collective-permute-start.6) | collective-permute-done | bytes 221216 | tf_op jit(solution)/shard_map/ppermute | solution.py:171
  75.7 0.1 slice_add_fusion
  75.8 3.1 %collective-permute-start.7 = (f16[48,1152]{1,0:T(8,128)(2,1)S(1)}, f16[48,1152]{1,0:T(8,128)(2,1)S(1)}, u32[]{:S(2)}, u32[]{:S(2)}) collective-permute-start(f16[48,1152]{1,0:T(8,128)(2,1)S(1)} %fusion.1), channel_id=1, source_target_pairs={{0,128},{64,192},{128,0},{192,64},{256,384},{320,448},{384,256},{4... | collective-permute-start | bytes 331784 | tf_op jit(solution)/shard_map/ppermute | solution.py:171
  78.9 6.5 %collective-permute-done.7 = f16[48,1152]{1,0:T(8,128)(2,1)S(1)} collective-permute-done((f16[48,1152]{1,0:T(8,128)(2,1)S(1)}, f16[48,1152]{1,0:T(8,128)(2,1)S(1)}, u32[]{:S(2)}, u32[]{:S(2)}) %collective-permute-start.7) | collective-permute-done | bytes 110624 | tf_op jit(solution)/shard_map/ppermute | solution.py:171
  85.5 8.0 %collective-permute-start.8 = (f16[24,1152]{1,0:T(8,128)(2,1)S(1)}, f16[24,1152]{1,0:T(8,128)(2,1)S(1)}, u32[]{:S(2)}, u32[]{:S(2)}) collective-permute-start(f16[24,1152]{1,0:T(8,128)(2,1)S(1)} %fusion.3), channel_id=1, source_target_pairs={{0,256},{64,320},{128,384},{192,448},{256,0},{320,64},{384,128},{4... | collective-permute-start | bytes 165896 | tf_op jit(solution)/shard_map/ppermute | solution.py:171
  93.4 4.6 %collective-permute-done.8 = f16[24,1152]{1,0:T(8,128)(2,1)S(1)} collective-permute-done((f16[24,1152]{1,0:T(8,128)(2,1)S(1)}, f16[24,1152]{1,0:T(8,128)(2,1)S(1)}, u32[]{:S(2)}, u32[]{:S(2)}) %collective-permute-start.8) | collective-permute-done | bytes 55328 | tf_op jit(solution)/shard_map/ppermute | solution.py:171
  98.1 0.6 slice_add_fusion.3.image_sum_ref
  98.7 2.1 %all-to-all-done.1 = bf16[16,48,1280]{2,1,0:T(8,128)(2,1)S(1)} async-done(((bf16[16,48,1280]{2,1,0:T(8,128)(2,1)}), bf16[16,48,1280]{2,1,0:T(8,128)(2,1)S(1)}, u32[]{:S(2)}, u32[]{:S(2)}) %all-to-all-start.1) | async-done | bytes 1966112 | tf_op jit(solution)/shard_map/all_to_all | solution.py:204
  100.8 0.2 convert_reduce_fusion
  101.1 9.9 %collective-permute-start.9 = (f16[24,1152]{1,0:T(8,128)(2,1)S(1)}, f16[24,1152]{1,0:T(8,128)(2,1)S(1)}, u32[]{:S(2)}, u32[]{:S(2)}) collective-permute-start(f16[24,1152]{1,0:T(8,128)(2,1)S(1)} %fusion.2), channel_id=1, source_target_pairs={{0,1},{1,0},{2,3},{3,2},{4,5},{5,4},{6,7},{7,6},{8,9},{9,8},{10,11... | collective-permute-start | bytes 165896 | tf_op jit(solution)/shard_map/ppermute | solution.py:171
  111.0 0.6 fusion.4
  111.6 1.2 broadcast_in_dim.10
  112.8 8.2 %all-to-all-start.2 = ((f32[32,1,128]{2,1,0:T(1,128)}), f32[32,1,128]{2,1,0:T(1,128)S(1)}, u32[]{:S(2)}, u32[]{:S(2)}) async-start(f32[32,1,128]{2,1,0:T(1,128)} %broadcast_in_dim.10), calls=%async_computation.2 | async-start | bytes 32768 | tf_op jit(solution)/shard_map/all_to_all | solution.py:210
  121.0 0.0 collective-permute-done.9
  121.0 0.6 slice_add_fusion.2.text_sum_ref
  121.7 2.1 %shard_map.70 = (f32[24,1152]{1,0:T(8,128)}, f32[24,1152]{1,0:T(8,128)}) custom-call(f32[1]{0:T(128)S(6)} %copy.13.heat_ref, f32[1]{0:T(128)S(6)} %copy.14.offset_ref, f32[24,1152]{1,0:T(8,128)} %picture_ref.3, f32[24,1152]{1,0:T(8,128)} %caption_ref.3, f32[24,1152]{1,0:T(8,128)} %slice_add_fusion.3.image_sum_ref, f32[24,1152]{1,0:T(8,128)} %slice_add_fusion.2.text_sum_ref), custom_call_target="tpu_custom_call" | custom-call | tf_op jit(solution)/shard_map/pallas_call | solution.py:163
  123.8 8.8 %all-to-all-done.2 = f32[32,1,128]{2,1,0:T(1,128)S(1)} async-done(((f32[32,1,128]{2,1,0:T(1,128)}), f32[32,1,128]{2,1,0:T(1,128)S(1)}, u32[]{:S(2)}, u32[]{:S(2)}) %all-to-all-start.2) | async-done | bytes 16416 | tf_op jit(solution)/shard_map/all_to_all | solution.py:210
  132.5 0.6 slice_reduce_fusion
  (11 shorter events, 0.2 us)
Async XLA Ops:
  4.4 20.3 %collective-permute-start.4 = (bf16[24,1152]{1,0:T(8,128)(2,1)}, bf16[24,1152]{1,0:T(8,128)(2,1)S(1)}, u32[]{:S(2)}, u32[]{:S(2)}) collective-permute-start(bf16[24,1152]{1,0:T(8,128)(2,1)} %get-tuple-element.17), channel_id=1, source_target_pairs={{0,1},{1,0},{2,3},{3,2},{4,5},{5,4},{6,7},{7,6},{8,9},{9,8},{10,11... | collective-permute-start | bytes 165896 | tf_op jit(solution)/shard_map/ppermute | solution.py:171
  20.6 12.6 %collective-permute-start = (bf16[24,1152]{1,0:T(8,128)(2,1)}, bf16[24,1152]{1,0:T(8,128)(2,1)S(1)}, u32[]{:S(2)}, u32[]{:S(2)}) collective-permute-start(bf16[24,1152]{1,0:T(8,128)(2,1)} %get-tuple-element.15), channel_id=1, source_target_pairs={{0,256},{64,320},{128,384},{192,448},{256,0},{320,64},{384,128},{4... | collective-permute-start | bytes 165896 | tf_op jit(solution)/shard_map/ppermute | solution.py:171
  25.7 6.9 %copy-start.1 = (bf16[24,1152]{1,0:T(8,128)(2,1)S(1)}, bf16[24,1152]{1,0:T(8,128)(2,1)}, u32[]{:S(2)}) copy-start(bf16[24,1152]{1,0:T(8,128)(2,1)} %get-tuple-element.15) | copy-start | bytes 165892
  25.7 30.0 %copy-start = (f32[24,1]{1,0:T(8,128)S(1)}, f32[24,1]{1,0:T(8,128)}, u32[]{:S(2)}) copy-start(f32[24,1]{1,0:T(8,128)} %get-tuple-element.14.own_loss_ref) | copy-start | bytes 292
  25.7 30.0 %all-to-all-start = ((bf16[16,48,1152]{2,1,0:T(8,128)(2,1)}), bf16[16,48,1152]{2,1,0:T(8,128)(2,1)S(1)}, u32[]{:S(2)}, u32[]{:S(2)}) async-start(bf16[16,48,1152]{2,1,0:T(8,128)(2,1)} %broadcast_dynamic-update-slice_fusion), calls=%async_computation | async-start | bytes 3538944 | tf_op jit(solution)/shard_map/all_to_all | solution.py:193
  33.2 9.4 %collective-permute-start.1 = (bf16[48,1152]{1,0:T(8,128)(2,1)S(1)}, bf16[48,1152]{1,0:T(8,128)(2,1)S(1)}, u32[]{:S(2)}, u32[]{:S(2)}) collective-permute-start(bf16[48,1152]{1,0:T(8,128)(2,1)S(1)} %pad_maximum_fusion.1), channel_id=1, source_target_pairs={{0,128},{64,192},{128,0},{192,64},{256,384},{320,448},{384,256},{4... | collective-permute-start | bytes 331784 | tf_op jit(solution)/shard_map/ppermute | solution.py:171
  42.6 7.7 %collective-permute-start.2 = (bf16[96,1152]{1,0:T(8,128)(2,1)S(1)}, bf16[96,1152]{1,0:T(8,128)(2,1)S(1)}, u32[]{:S(2)}, u32[]{:S(2)}) collective-permute-start(bf16[96,1152]{1,0:T(8,128)(2,1)S(1)} %pad_maximum_fusion), channel_id=1, source_target_pairs={{0,64},{64,0},{128,192},{192,128},{256,320},{320,256},{384,448},{4... | collective-permute-start | bytes 663560 | tf_op jit(solution)/shard_map/ppermute | solution.py:171
  50.4 5.4 %collective-permute-start.3 = (bf16[192,1152]{1,0:T(8,128)(2,1)S(1)}, bf16[192,1152]{1,0:T(8,128)(2,1)S(1)}, u32[]{:S(2)}, u32[]{:S(2)}) collective-permute-start(bf16[192,1152]{1,0:T(8,128)(2,1)S(1)} %constant_dynamic-update-slice_fusion.near_ref), channel_id=1, source_target_pairs={{0,8},{8,0},{1,9},{9,1},{2,10},{10,2},{3,11},{11,3},{4,12},{12,4},... | collective-permute-start | bytes 1327112 | tf_op jit(solution)/shard_map/ppermute | solution.py:171
  57.9 8.6 %collective-permute-start.5 = (f32[192,1152]{1,0:T(8,128)S(1)}, f32[192,1152]{1,0:T(8,128)S(1)}, u32[]{:S(2)}, u32[]{:S(2)}) collective-permute-start(f32[192,1152]{1,0:T(8,128)S(1)} %get-tuple-element.22), channel_id=1, source_target_pairs={{0,8},{8,0},{1,9},{9,1},{2,10},{10,2},{3,11},{11,3},{4,12},{12,4},... | collective-permute-start | bytes 2654216 | tf_op jit(solution)/shard_map/ppermute | solution.py:171
  66.7 8.9 %collective-permute-start.6 = (f16[96,1152]{1,0:T(8,128)(2,1)S(1)}, f16[96,1152]{1,0:T(8,128)(2,1)S(1)}, u32[]{:S(2)}, u32[]{:S(2)}) collective-permute-start(f16[96,1152]{1,0:T(8,128)(2,1)S(1)} %fusion), channel_id=1, source_target_pairs={{0,64},{64,0},{128,192},{192,128},{256,320},{320,256},{384,448},{4... | collective-permute-start | bytes 663560 | tf_op jit(solution)/shard_map/ppermute | solution.py:171
  69.4 31.5 %all-to-all-start.1 = ((bf16[16,48,1280]{2,1,0:T(8,128)(2,1)}), bf16[16,48,1280]{2,1,0:T(8,128)(2,1)S(1)}, u32[]{:S(2)}, u32[]{:S(2)}) async-start(bf16[16,48,1280]{2,1,0:T(8,128)(2,1)} %bitcast.2), calls=%async_computation.1 | async-start | bytes 3932160 | tf_op jit(solution)/shard_map/all_to_all | solution.py:204
  75.8 9.7 %collective-permute-start.7 = (f16[48,1152]{1,0:T(8,128)(2,1)S(1)}, f16[48,1152]{1,0:T(8,128)(2,1)S(1)}, u32[]{:S(2)}, u32[]{:S(2)}) collective-permute-start(f16[48,1152]{1,0:T(8,128)(2,1)S(1)} %fusion.1), channel_id=1, source_target_pairs={{0,128},{64,192},{128,0},{192,64},{256,384},{320,448},{384,256},{4... | collective-permute-start | bytes 331784 | tf_op jit(solution)/shard_map/ppermute | solution.py:171
  85.5 12.6 %collective-permute-start.8 = (f16[24,1152]{1,0:T(8,128)(2,1)S(1)}, f16[24,1152]{1,0:T(8,128)(2,1)S(1)}, u32[]{:S(2)}, u32[]{:S(2)}) collective-permute-start(f16[24,1152]{1,0:T(8,128)(2,1)S(1)} %fusion.3), channel_id=1, source_target_pairs={{0,256},{64,320},{128,384},{192,448},{256,0},{320,64},{384,128},{4... | collective-permute-start | bytes 165896 | tf_op jit(solution)/shard_map/ppermute | solution.py:171
  101.1 19.9 %collective-permute-start.9 = (f16[24,1152]{1,0:T(8,128)(2,1)S(1)}, f16[24,1152]{1,0:T(8,128)(2,1)S(1)}, u32[]{:S(2)}, u32[]{:S(2)}) collective-permute-start(f16[24,1152]{1,0:T(8,128)(2,1)S(1)} %fusion.2), channel_id=1, source_target_pairs={{0,1},{1,0},{2,3},{3,2},{4,5},{5,4},{6,7},{7,6},{8,9},{9,8},{10,11... | collective-permute-start | bytes 165896 | tf_op jit(solution)/shard_map/ppermute | solution.py:171
  112.8 19.7 %all-to-all-start.2 = ((f32[32,1,128]{2,1,0:T(1,128)}), f32[32,1,128]{2,1,0:T(1,128)S(1)}, u32[]{:S(2)}, u32[]{:S(2)}) async-start(f32[32,1,128]{2,1,0:T(1,128)} %broadcast_in_dim.10), calls=%async_computation.2 | async-start | bytes 32768 | tf_op jit(solution)/shard_map/all_to_all | solution.py:210

commit v9 on v8

--- a/solution.py
+++ b/solution.py
@@ -146,25 +146,21 @@
     )(weights, loss, near, far, texts)
 
 
-def grad_kernel(
-    heat_ref, offset_ref, picture_ref, caption_ref, image_sum_ref, text_sum_ref, image_ref, text_ref
-):
-    image_unit, image_norm = normalize(picture_ref[...])
-    text_unit, text_norm = normalize(caption_ref[...])
-    image_low, text_low = low(image_unit), low(text_unit)
+def grad_kernel(heat_ref, offset_ref, row_ref, low_ref, partner_ref, sum_ref, grad_ref):
+    unit, norm = normalize(row_ref[...])
+    partner_low = partner_ref[...].astype(jnp.float32)
     heat = jnp.exp(jnp.full((1, 1), heat_ref[0], jnp.float32))
-    _, sigmoid = loss_and_sigmoid(-own_pairs(image_low, text_low, heat, offset_ref[0]))
-    weights = low(-sigmoid * heat)
-    image_ref[...] = back_norm(image_unit, image_norm, image_sum_ref[...] + weights * text_low)
-    text_ref[...] = back_norm(text_unit, text_norm, text_sum_ref[...] + weights * image_low)
-
-
-def gradients(heat_exponent, offset_added, pictures, captions, image_sum, text_sum):
+    logits = own_pairs(low_ref[...].astype(jnp.float32), partner_low, heat, offset_ref[0])
+    _, sigmoid = loss_and_sigmoid(-logits)
+    grad_ref[...] = back_norm(unit, norm, sum_ref[...] + low(-sigmoid * heat) * partner_low)
+
+
+def gradients(heat_exponent, offset_added, vectors, lows, partners, sums):
     return pl.pallas_call(
         grad_kernel,
         in_specs=[pl.BlockSpec(memory_space=pltpu.SMEM)] * 2 + [pl.BlockSpec(memory_space=pltpu.VMEM)] * 4,
-        out_shape=[jax.ShapeDtypeStruct(pictures.shape, jnp.float32)] * 2,
-    )(heat_exponent, offset_added, pictures, captions, image_sum, text_sum)
+        out_shape=jax.ShapeDtypeStruct(vectors.shape, jnp.float32),
+    )(heat_exponent, offset_added, vectors, lows, partners, sums)
 
 
 def swapped(value, axis, step):
@@ -210,10 +206,11 @@
     losses = lax.all_to_all(jnp.broadcast_to(plane_loss, (column, 1, LANES)), COLUMN, 0, 0)
     loss_mean = (jnp.sum(losses[:, 0, 0]) / (rows * lax.axis_size(AXES))).reshape(1)
     text_sum = jnp.sum(text_parts[:, :, :width].astype(jnp.float32), axis=0)
-    text_sum = halved(text_sum, "zh", 1)
-    image_grads, text_grads = gradients(
-        heat_exponent, offset_added, picture_vectors, caption_vectors, image_sum, text_sum
-    )
+    arrived = swapped((text_sum[rows:] * HALF).astype(jnp.float16), "zh", 1)
+    arrived, loss_mean = lax.optimization_barrier((arrived, loss_mean))
+    text_sum = text_sum[:rows] + arrived.astype(jnp.float32) * (1 / HALF)
+    image_grads = gradients(heat_exponent, offset_added, picture_vectors, image_low, text_low, image_sum)
+    text_grads = gradients(heat_exponent, offset_added, caption_vectors, text_low, image_low, text_sum)
     return (loss_mean, image_grads, text_grads)
 
 

time: 136 us -> 135 us (level); the launches traced: 135 us -> 132 us
  waiting for transfers between devices: 39.2 us -> 28.9 us
  starting transfers between devices: 76.8 us -> 82.8 us
  Pallas kernels: 9.57 us -> 11.2 us
    all_to_all x1, waiting for transfers between devices: 8.79 us -> 0.01 us  [shards(): lax.all_to_all(jnp.broadcast_to(plane_loss, (column, 1, LANES)), COLUMN,...]
    all_to_all x1, starting transfers between devices: 8.19 us -> 12 us  [shards(): lax.all_to_all(jnp.broadcast_to(plane_loss, (column, 1, LANES)), COLUMN,...]
    ppermute x10, starting transfers between devices: 58 us -> 60.2 us  [swapped(): lax.ppermute(value, axis, [(i, i ^ step) for i in range(lax.axis_size(axi...]
    all_to_all x1, waiting for transfers between devices: 2.1 us -> 0.2 us  [shards(): lax.all_to_all(text_part.reshape(plane, 2 * rows, width + LANES), PLANE,...]
    pallas_call x1 -> x2, Pallas kernels: 2.07 us -> 3.75 us  [gradients(): pl.pallas_call(grad_kernel, in_specs=[pl.BlockSpec(memory_space=pltpu.SME...]
  transfers between devices with their start and end apart: 13 -> 13, of which waited for: 9 -> 9; matrix products, arithmetic and copies ran while one was open for 3% -> 2% of each run, Pallas kernels for 4% -> 4%
where the time goes in v9:
time: 135 us; the launch traced here: 132 us
  starting transfers between devices  82.8 us (61%)
  waiting for transfers between devices  28.9 us (21%)
  Pallas kernels  11.2 us (8%)
  between operations  3.92 us (3%)
  other arithmetic  3.12 us (2%)
  local copies, waits for them, and re-layouts  2.32 us (2%)
    ppermute x10, starting transfers between devices, swapped(): lax.ppermute(value, axis, [(i, i ^ step) for i in range(lax.axis_size(axi...  60.2 us
    ppermute x10, waiting for transfers between devices, swapped(): lax.ppermute(value, axis, [(i, i ^ step) for i in range(lax.axis_size(axi...  28.7 us
    all_to_all x1, starting transfers between devices, shards(): lax.all_to_all(jnp.broadcast_to(plane_loss, (column, 1, LANES)), COLUMN,...  12 us
    all_to_all x1, starting transfers between devices, shards(): lax.all_to_all(lax.dynamic_update_slice(copies, other_low, (0, rows, 0)),...  6.89 us
    pallas_call x2, Pallas kernels, gradients(): pl.pallas_call(grad_kernel, in_specs=[pl.BlockSpec(memory_space=pltpu.SME...  3.75 us
    all_to_all x1, starting transfers between devices, shards(): lax.all_to_all(text_part.reshape(plane, 2 * rows, width + LANES), PLANE,...  3.73 us
    pallas_call x1, Pallas kernels, pair_terms(): pl.pallas_call(terms_kernel, in_specs=[pl.BlockSpec(memory_space=pltpu.VM...  2.85 us
  transfers between devices with their start and end apart: 13, of which 9 were waited for; matrix products, arithmetic and copies ran while one was open for 2% of the time, Pallas kernels for 4%

profile of v9, /device:TPU:1, one launch (start us, length us, event | category | flops | bytes accessed | tf_op | source)
XLA Modules:
  0.0 132.3 jit_solution(8146852735252788464)
XLA Ops:
  1.9 2.4 %shard_map.67 = (bf16[24,1152]{1,0:T(8,128)(2,1)}, bf16[24,1152]{1,0:T(8,128)(2,1)}, bf16[16,48,1152]{2,1,0:T(8,128)(2,1)}, f32[24,1]{1,0:T(8,128)}) custom-call(f32[1]{0:T(128)S(6)} %copy.13.heat_ref, f32[1]{0:T(128)S(6)} %copy.14.offset_ref, f32[24,1152]{1,0:T(8,128)} %row_ref.2, f32[24,1152]{1,0:T(8,128)} %row_ref.3), custom_call_target="tpu_custom_call" | custom-call | tf_op jit(solution)/shard_map/pallas_call | solution.py:56
  4.3 16.3 %collective-permute-start.4 = (bf16[24,1152]{1,0:T(8,128)(2,1)}, bf16[24,1152]{1,0:T(8,128)(2,1)S(1)}, u32[]{:S(2)}, u32[]{:S(2)}) collective-permute-start(bf16[24,1152]{1,0:T(8,128)(2,1)} %get-tuple-element.17.partner_ref.low_ref), channel_id=1, source_target_pairs={{0,1},{1,0},{2,3},{3,2},{4,5},{5,4},{6,7},{7,6},{8,9},{9,8},{10,11... | collective-permute-start | bytes 165896 | tf_op jit(solution)/shard_map/ppermute | solution.py:167
  20.6 4.0 %collective-permute-start = (bf16[24,1152]{1,0:T(8,128)(2,1)}, bf16[24,1152]{1,0:T(8,128)(2,1)S(1)}, u32[]{:S(2)}, u32[]{:S(2)}) collective-permute-start(bf16[24,1152]{1,0:T(8,128)(2,1)} %get-tuple-element.15.low_ref.partner_ref), channel_id=1, source_target_pairs={{0,256},{64,320},{128,384},{192,448},{256,0},{320,64},{384,128},{4... | collective-permute-start | bytes 165896 | tf_op jit(solution)/shard_map/ppermute | solution.py:167
  24.6 0.0 collective-permute-done.4
  24.6 1.0 broadcast_dynamic-update-slice_fusion
  25.6 0.0 copy-start.1
  25.6 0.0 copy-start
  25.6 6.9 %all-to-all-start = ((bf16[16,48,1152]{2,1,0:T(8,128)(2,1)}), bf16[16,48,1152]{2,1,0:T(8,128)(2,1)S(1)}, u32[]{:S(2)}, u32[]{:S(2)}) async-start(bf16[16,48,1152]{2,1,0:T(8,128)(2,1)} %broadcast_dynamic-update-slice_fusion), calls=%async_computation | async-start | bytes 3538944 | tf_op jit(solution)/shard_map/all_to_all | solution.py:189
  32.5 0.0 copy-done.1
  32.6 0.6 collective-permute-done
  33.2 2.5 %collective-permute-start.1 = (bf16[48,1152]{1,0:T(8,128)(2,1)S(1)}, bf16[48,1152]{1,0:T(8,128)(2,1)S(1)}, u32[]{:S(2)}, u32[]{:S(2)}) collective-permute-start(bf16[48,1152]{1,0:T(8,128)(2,1)S(1)} %pad_maximum_fusion.1), channel_id=1, source_target_pairs={{0,128},{64,192},{128,0},{192,64},{256,384},{320,448},{384,256},{4... | collective-permute-start | bytes 331784 | tf_op jit(solution)/shard_map/ppermute | solution.py:167
  35.7 6.8 %collective-permute-done.1 = bf16[48,1152]{1,0:T(8,128)(2,1)S(1)} collective-permute-done((bf16[48,1152]{1,0:T(8,128)(2,1)S(1)}, bf16[48,1152]{1,0:T(8,128)(2,1)S(1)}, u32[]{:S(2)}, u32[]{:S(2)}) %collective-permute-start.1) | collective-permute-done | bytes 110624 | tf_op jit(solution)/shard_map/ppermute | solution.py:167
  42.5 1.9 %collective-permute-start.2 = (bf16[96,1152]{1,0:T(8,128)(2,1)S(1)}, bf16[96,1152]{1,0:T(8,128)(2,1)S(1)}, u32[]{:S(2)}, u32[]{:S(2)}) collective-permute-start(bf16[96,1152]{1,0:T(8,128)(2,1)S(1)} %pad_maximum_fusion), channel_id=1, source_target_pairs={{0,64},{64,0},{128,192},{192,128},{256,320},{320,256},{384,448},{4... | collective-permute-start | bytes 663560 | tf_op jit(solution)/shard_map/ppermute | solution.py:167
  44.5 5.7 %collective-permute-done.2 = bf16[96,1152]{1,0:T(8,128)(2,1)S(1)} collective-permute-done((bf16[96,1152]{1,0:T(8,128)(2,1)S(1)}, bf16[96,1152]{1,0:T(8,128)(2,1)S(1)}, u32[]{:S(2)}, u32[]{:S(2)}) %collective-permute-start.2) | collective-permute-done | bytes 221216 | tf_op jit(solution)/shard_map/ppermute | solution.py:167
  50.2 4.0 %collective-permute-start.3 = (bf16[192,1152]{1,0:T(8,128)(2,1)S(1)}, bf16[192,1152]{1,0:T(8,128)(2,1)S(1)}, u32[]{:S(2)}, u32[]{:S(2)}) collective-permute-start(bf16[192,1152]{1,0:T(8,128)(2,1)S(1)} %constant_dynamic-update-slice_fusion.near_ref), channel_id=1, source_target_pairs={{0,8},{8,0},{1,9},{9,1},{2,10},{10,2},{3,11},{11,3},{4,12},{12,4},... | collective-permute-start | bytes 1327112 | tf_op jit(solution)/shard_map/ppermute | solution.py:167
  54.2 1.4 %collective-permute-done.3.far_ref = bf16[192,1152]{1,0:T(8,128)(2,1)S(1)} collective-permute-done((bf16[192,1152]{1,0:T(8,128)(2,1)S(1)}, bf16[192,1152]{1,0:T(8,128)(2,1)S(1)}, u32[]{:S(2)}, u32[]{:S(2)}) %collective-permute-start.3) | collective-permute-done | bytes 442400 | tf_op jit(solution)/shard_map/ppermute | solution.py:167
  55.6 0.0 all-to-all-done
  55.6 0.0 copy-done
  55.6 2.2 %shard_map.68 = (bf16[2,192,768]{2,1,0:T(8,128)(2,1)S(1)}, f32[192,1152]{1,0:T(8,128)S(1)}, f32[8,128]{1,0:T(8,128)S(1)}) custom-call(s32[1]{0:T(128)} %bitcast.place_ref, f32[1]{0:T(128)S(6)} %copy.13.heat_ref, f32[1]{0:T(128)S(6)} %copy.14.offset_ref, f32[24,1]{1,0:T(8,128)S(1)} %copy-done, ...), custom_call_target="tpu_custom_call" | custom-call | flops 1019215872 | bytes 1769472 | tf_op jit(solution)/shard_map/pallas_call | solution.py:107
  57.8 5.8 %collective-permute-start.6 = (f32[192,1152]{1,0:T(8,128)S(1)}, f32[192,1152]{1,0:T(8,128)S(1)}, u32[]{:S(2)}, u32[]{:S(2)}) collective-permute-start(f32[192,1152]{1,0:T(8,128)S(1)} %get-tuple-element.23), channel_id=1, source_target_pairs={{0,8},{8,0},{1,9},{9,1},{2,10},{10,2},{3,11},{11,3},{4,12},{12,4},... | collective-permute-start | bytes 2654216 | tf_op jit(solution)/shard_map/ppermute | solution.py:167
  63.6 2.8 %shard_map.69 = (f32[192,1152]{1,0:T(8,128)S(1)}, bf16[768,1280]{1,0:T(8,128)(2,1)}) custom-call(bf16[2,192,768]{2,1,0:T(8,128)(2,1)S(1)} %get-tuple-element.18.weight_ref, f32[8,128]{1,0:T(8,128)S(1)} %get-tuple-element.19.loss_ref, bf16[192,1152]{1,0:T(8,128)(2,1)S(1)} %constant_dynamic-update-slice_fusion.near_ref, ...), custom_call_target="tpu_custom_call" | custom-call | flops 1019215872 | bytes 3538944 | tf_op jit(solution)/shard_map/pallas_call | solution.py:137
  66.5 0.0 collective-permute-done.6
  66.5 0.1 add.19
  66.6 2.6 %collective-permute-start.7 = (f16[96,1152]{1,0:T(8,128)(2,1)S(1)}, f16[96,1152]{1,0:T(8,128)(2,1)S(1)}, u32[]{:S(2)}, u32[]{:S(2)}) collective-permute-start(f16[96,1152]{1,0:T(8,128)(2,1)S(1)} %fusion), channel_id=1, source_target_pairs={{0,64},{64,0},{128,192},{192,128},{256,320},{320,256},{384,448},{4... | collective-permute-start | bytes 663560 | tf_op jit(solution)/shard_map/ppermute | solution.py:167
  69.3 3.7 %all-to-all-start.1 = ((bf16[16,48,1280]{2,1,0:T(8,128)(2,1)}), bf16[16,48,1280]{2,1,0:T(8,128)(2,1)S(1)}, u32[]{:S(2)}, u32[]{:S(2)}) async-start(bf16[16,48,1280]{2,1,0:T(8,128)(2,1)} %bitcast.2), calls=%async_computation.1 | async-start | bytes 3932160 | tf_op jit(solution)/shard_map/all_to_all | solution.py:200
  73.0 2.6 %collective-permute-done.7 = f16[96,1152]{1,0:T(8,128)(2,1)S(1)} collective-permute-done((f16[96,1152]{1,0:T(8,128)(2,1)S(1)}, f16[96,1152]{1,0:T(8,128)(2,1)S(1)}, u32[]{:S(2)}, u32[]{:S(2)}) %collective-permute-start.7) | collective-permute-done | bytes 221216 | tf_op jit(solution)/shard_map/ppermute | solution.py:167
  75.6 0.1 slice_add_fusion
  75.7 3.1 %collective-permute-start.8 = (f16[48,1152]{1,0:T(8,128)(2,1)S(1)}, f16[48,1152]{1,0:T(8,128)(2,1)S(1)}, u32[]{:S(2)}, u32[]{:S(2)}) collective-permute-start(f16[48,1152]{1,0:T(8,128)(2,1)S(1)} %fusion.1), channel_id=1, source_target_pairs={{0,128},{64,192},{128,0},{192,64},{256,384},{320,448},{384,256},{4... | collective-permute-start | bytes 331784 | tf_op jit(solution)/shard_map/ppermute | solution.py:167
  78.8 6.6 %collective-permute-done.8 = f16[48,1152]{1,0:T(8,128)(2,1)S(1)} collective-permute-done((f16[48,1152]{1,0:T(8,128)(2,1)S(1)}, f16[48,1152]{1,0:T(8,128)(2,1)S(1)}, u32[]{:S(2)}, u32[]{:S(2)}) %collective-permute-start.8) | collective-permute-done | bytes 110624 | tf_op jit(solution)/shard_map/ppermute | solution.py:167
  85.4 8.0 %collective-permute-start.9 = (f16[24,1152]{1,0:T(8,128)(2,1)S(1)}, f16[24,1152]{1,0:T(8,128)(2,1)S(1)}, u32[]{:S(2)}, u32[]{:S(2)}) collective-permute-start(f16[24,1152]{1,0:T(8,128)(2,1)S(1)} %fusion.2), channel_id=1, source_target_pairs={{0,256},{64,320},{128,384},{192,448},{256,0},{320,64},{384,128},{4... | collective-permute-start | bytes 165896 | tf_op jit(solution)/shard_map/ppermute | solution.py:167
  93.4 4.6 %collective-permute-done.9 = f16[24,1152]{1,0:T(8,128)(2,1)S(1)} collective-permute-done((f16[24,1152]{1,0:T(8,128)(2,1)S(1)}, f16[24,1152]{1,0:T(8,128)(2,1)S(1)}, u32[]{:S(2)}, u32[]{:S(2)}) %collective-permute-start.9) | collective-permute-done | bytes 55328 | tf_op jit(solution)/shard_map/ppermute | solution.py:167
  98.0 0.7 slice_add_fusion.3.sum_ref
  98.7 1.9 %shard_map.70 = f32[24,1152]{1,0:T(8,128)} custom-call(f32[1]{0:T(128)S(6)} %copy.13.heat_ref, f32[1]{0:T(128)S(6)} %copy.14.offset_ref, f32[24,1152]{1,0:T(8,128)} %row_ref.2, bf16[24,1152]{1,0:T(8,128)(2,1)} %get-tuple-element.15.low_ref.partner_ref, bf16[24,1152]{1,0:T(8,128)(2,1)} %get-tuple-element.17.partner_ref.low_ref, ...), custom_call_target="tpu_custom_call" | custom-call | tf_op jit(solution)/shard_map/pallas_call | solution.py:159
  100.5 0.2 all-to-all-done.1
  100.7 0.6 fusion.4
  101.4 1.3 broadcast_in_dim.10
  102.6 12.0 %all-to-all-start.2 = ((f32[32,1,128]{2,1,0:T(1,128)}), f32[32,1,128]{2,1,0:T(1,128)S(1)}, u32[]{:S(2)}, u32[]{:S(2)}) async-start(f32[32,1,128]{2,1,0:T(1,128)} %broadcast_in_dim.10), calls=%async_computation.2 | async-start | bytes 32768 | tf_op jit(solution)/shard_map/all_to_all | solution.py:206
  114.7 0.3 convert_reduce_fusion
  114.9 12.0 %collective-permute-start.5 = (f16[24,1152]{1,0:T(8,128)(2,1)S(1)}, f16[24,1152]{1,0:T(8,128)(2,1)S(1)}, u32[]{:S(2)}, u32[]{:S(2)}) collective-permute-start(f16[24,1152]{1,0:T(8,128)(2,1)S(1)} %fusion.3), channel_id=1, source_target_pairs={{0,1},{1,0},{2,3},{3,2},{4,5},{5,4},{6,7},{7,6},{8,9},{9,8},{10,11... | collective-permute-start | bytes 165896 | tf_op jit(solution)/shard_map/ppermute | solution.py:167
  126.9 0.0 all-to-all-done.2
  127.0 0.6 slice_reduce_fusion
  128.2 0.4 collective-permute-done.5
  128.7 0.7 slice_add_fusion.2.sum_ref
  129.3 1.9 %shard_map.71 = f32[24,1152]{1,0:T(8,128)} custom-call(f32[1]{0:T(128)S(6)} %copy.13.heat_ref, f32[1]{0:T(128)S(6)} %copy.14.offset_ref, f32[24,1152]{1,0:T(8,128)} %row_ref.3, bf16[24,1152]{1,0:T(8,128)(2,1)} %get-tuple-element.17.partner_ref.low_ref, bf16[24,1152]{1,0:T(8,128)(2,1)} %get-tuple-element.15.low_ref.partner_ref, ...), custom_call_target="tpu_custom_call" | custom-call | tf_op jit(solution)/shard_map/pallas_call | solution.py:159
  (11 shorter events, 0.2 us)
Async XLA Ops:
  4.3 20.3 %collective-permute-start.4 = (bf16[24,1152]{1,0:T(8,128)(2,1)}, bf16[24,1152]{1,0:T(8,128)(2,1)S(1)}, u32[]{:S(2)}, u32[]{:S(2)}) collective-permute-start(bf16[24,1152]{1,0:T(8,128)(2,1)} %get-tuple-element.17.partner_ref.low_ref), channel_id=1, source_target_pairs={{0,1},{1,0},{2,3},{3,2},{4,5},{5,4},{6,7},{7,6},{8,9},{9,8},{10,11... | collective-permute-start | bytes 165896 | tf_op jit(solution)/shard_map/ppermute | solution.py:167
  20.6 12.6 %collective-permute-start = (bf16[24,1152]{1,0:T(8,128)(2,1)}, bf16[24,1152]{1,0:T(8,128)(2,1)S(1)}, u32[]{:S(2)}, u32[]{:S(2)}) collective-permute-start(bf16[24,1152]{1,0:T(8,128)(2,1)} %get-tuple-element.15.low_ref.partner_ref), channel_id=1, source_target_pairs={{0,256},{64,320},{128,384},{192,448},{256,0},{320,64},{384,128},{4... | collective-permute-start | bytes 165896 | tf_op jit(solution)/shard_map/ppermute | solution.py:167
  25.6 6.9 %copy-start.1 = (bf16[24,1152]{1,0:T(8,128)(2,1)S(1)}, bf16[24,1152]{1,0:T(8,128)(2,1)}, u32[]{:S(2)}) copy-start(bf16[24,1152]{1,0:T(8,128)(2,1)} %get-tuple-element.15.low_ref.partner_ref) | copy-start | bytes 165892
  25.6 30.0 %copy-start = (f32[24,1]{1,0:T(8,128)S(1)}, f32[24,1]{1,0:T(8,128)}, u32[]{:S(2)}) copy-start(f32[24,1]{1,0:T(8,128)} %get-tuple-element.14.own_loss_ref) | copy-start | bytes 292
  25.6 30.0 %all-to-all-start = ((bf16[16,48,1152]{2,1,0:T(8,128)(2,1)}), bf16[16,48,1152]{2,1,0:T(8,128)(2,1)S(1)}, u32[]{:S(2)}, u32[]{:S(2)}) async-start(bf16[16,48,1152]{2,1,0:T(8,128)(2,1)} %broadcast_dynamic-update-slice_fusion), calls=%async_computation | async-start | bytes 3538944 | tf_op jit(solution)/shard_map/all_to_all | solution.py:189
  33.2 9.3 %collective-permute-start.1 = (bf16[48,1152]{1,0:T(8,128)(2,1)S(1)}, bf16[48,1152]{1,0:T(8,128)(2,1)S(1)}, u32[]{:S(2)}, u32[]{:S(2)}) collective-permute-start(bf16[48,1152]{1,0:T(8,128)(2,1)S(1)} %pad_maximum_fusion.1), channel_id=1, source_target_pairs={{0,128},{64,192},{128,0},{192,64},{256,384},{320,448},{384,256},{4... | collective-permute-start | bytes 331784 | tf_op jit(solution)/shard_map/ppermute | solution.py:167
  42.5 7.6 %collective-permute-start.2 = (bf16[96,1152]{1,0:T(8,128)(2,1)S(1)}, bf16[96,1152]{1,0:T(8,128)(2,1)S(1)}, u32[]{:S(2)}, u32[]{:S(2)}) collective-permute-start(bf16[96,1152]{1,0:T(8,128)(2,1)S(1)} %pad_maximum_fusion), channel_id=1, source_target_pairs={{0,64},{64,0},{128,192},{192,128},{256,320},{320,256},{384,448},{4... | collective-permute-start | bytes 663560 | tf_op jit(solution)/shard_map/ppermute | solution.py:167
  50.2 5.4 %collective-permute-start.3 = (bf16[192,1152]{1,0:T(8,128)(2,1)S(1)}, bf16[192,1152]{1,0:T(8,128)(2,1)S(1)}, u32[]{:S(2)}, u32[]{:S(2)}) collective-permute-start(bf16[192,1152]{1,0:T(8,128)(2,1)S(1)} %constant_dynamic-update-slice_fusion.near_ref), channel_id=1, source_target_pairs={{0,8},{8,0},{1,9},{9,1},{2,10},{10,2},{3,11},{11,3},{4,12},{12,4},... | collective-permute-start | bytes 1327112 | tf_op jit(solution)/shard_map/ppermute | solution.py:167
  57.8 8.7 %collective-permute-start.6 = (f32[192,1152]{1,0:T(8,128)S(1)}, f32[192,1152]{1,0:T(8,128)S(1)}, u32[]{:S(2)}, u32[]{:S(2)}) collective-permute-start(f32[192,1152]{1,0:T(8,128)S(1)} %get-tuple-element.23), channel_id=1, source_target_pairs={{0,8},{8,0},{1,9},{9,1},{2,10},{10,2},{3,11},{11,3},{4,12},{12,4},... | collective-permute-start | bytes 2654216 | tf_op jit(solution)/shard_map/ppermute | solution.py:167
  66.6 8.9 %collective-permute-start.7 = (f16[96,1152]{1,0:T(8,128)(2,1)S(1)}, f16[96,1152]{1,0:T(8,128)(2,1)S(1)}, u32[]{:S(2)}, u32[]{:S(2)}) collective-permute-start(f16[96,1152]{1,0:T(8,128)(2,1)S(1)} %fusion), channel_id=1, source_target_pairs={{0,64},{64,0},{128,192},{192,128},{256,320},{320,256},{384,448},{4... | collective-permute-start | bytes 663560 | tf_op jit(solution)/shard_map/ppermute | solution.py:167
  69.3 31.5 %all-to-all-start.1 = ((bf16[16,48,1280]{2,1,0:T(8,128)(2,1)}), bf16[16,48,1280]{2,1,0:T(8,128)(2,1)S(1)}, u32[]{:S(2)}, u32[]{:S(2)}) async-start(bf16[16,48,1280]{2,1,0:T(8,128)(2,1)} %bitcast.2), calls=%async_computation.1 | async-start | bytes 3932160 | tf_op jit(solution)/shard_map/all_to_all | solution.py:200
  75.7 9.7 %collective-permute-start.8 = (f16[48,1152]{1,0:T(8,128)(2,1)S(1)}, f16[48,1152]{1,0:T(8,128)(2,1)S(1)}, u32[]{:S(2)}, u32[]{:S(2)}) collective-permute-start(f16[48,1152]{1,0:T(8,128)(2,1)S(1)} %fusion.1), channel_id=1, source_target_pairs={{0,128},{64,192},{128,0},{192,64},{256,384},{320,448},{384,256},{4... | collective-permute-start | bytes 331784 | tf_op jit(solution)/shard_map/ppermute | solution.py:167
  85.4 12.6 %collective-permute-start.9 = (f16[24,1152]{1,0:T(8,128)(2,1)S(1)}, f16[24,1152]{1,0:T(8,128)(2,1)S(1)}, u32[]{:S(2)}, u32[]{:S(2)}) collective-permute-start(f16[24,1152]{1,0:T(8,128)(2,1)S(1)} %fusion.2), channel_id=1, source_target_pairs={{0,256},{64,320},{128,384},{192,448},{256,0},{320,64},{384,128},{4... | collective-permute-start | bytes 165896 | tf_op jit(solution)/shard_map/ppermute | solution.py:167
  102.6 24.3 %all-to-all-start.2 = ((f32[32,1,128]{2,1,0:T(1,128)}), f32[32,1,128]{2,1,0:T(1,128)S(1)}, u32[]{:S(2)}, u32[]{:S(2)}) async-start(f32[32,1,128]{2,1,0:T(1,128)} %broadcast_in_dim.10), calls=%async_computation.2 | async-start | bytes 32768 | tf_op jit(solution)/shard_map/all_to_all | solution.py:206
  114.9 13.7 %collective-permute-start.5 = (f16[24,1152]{1,0:T(8,128)(2,1)S(1)}, f16[24,1152]{1,0:T(8,128)(2,1)S(1)}, u32[]{:S(2)}, u32[]{:S(2)}) collective-permute-start(f16[24,1152]{1,0:T(8,128)(2,1)S(1)} %fusion.3), channel_id=1, source_target_pairs={{0,1},{1,0},{2,3},{3,2},{4,5},{5,4},{6,7},{7,6},{8,9},{9,8},{10,11... | collective-permute-start | bytes 165896 | tf_op jit(solution)/shard_map/ppermute | solution.py:167

commit v10 on v9

--- a/solution.py
+++ b/solution.py
@@ -6,10 +6,10 @@
 from jax.sharding import Mesh, PartitionSpec as P
 
 epsilon = 1e-06
-AXES = ("zl", "x", "c", "y", "zh")
-SIZES = (8, 4, 2, 4, 2)
+AXES = ("zm", "zl", "x", "c", "y", "zh")
+SIZES = (2, 4, 4, 2, 4, 2)
 PLANE = ("x", "y")
-COLUMN = ("zl", "c", "zh")
+COLUMN = ("zm", "zl", "c", "zh")
 LANES = 128
 LIMIT = 20 * 1024 * 1024
 HALF = 0.5
@@ -185,10 +185,10 @@
         plane, heat_exponent, offset_added, picture_vectors, caption_vectors
     )
 
-    other_low = jnp.broadcast_to(swapped(text_low, "zh", 1)[None], (plane, rows, width))
+    other_low = jnp.broadcast_to(swapped(text_low, "zm", 1)[None], (plane, rows, width))
     texts = lax.all_to_all(lax.dynamic_update_slice(copies, other_low, (0, rows, 0)), PLANE, 0, 0)
     texts = texts.reshape(plane * 2 * rows, width)
-    near = image_low
+    near = doubled(image_low, "zh", 1)
     for step in reversed(steps):
         near = doubled(near, "zl", step)
     far = swapped(near, "c", 1)
@@ -201,12 +201,13 @@
     image_sum = near_part + far_part
     for step in steps:
         image_sum = halved(image_sum, "zl", step)
+    image_sum = halved(image_sum, "zh", 1)
 
     plane_loss = jnp.sum(text_parts[:, 0, width : width + 3].astype(jnp.float32))
     losses = lax.all_to_all(jnp.broadcast_to(plane_loss, (column, 1, LANES)), COLUMN, 0, 0)
     loss_mean = (jnp.sum(losses[:, 0, 0]) / (rows * lax.axis_size(AXES))).reshape(1)
     text_sum = jnp.sum(text_parts[:, :, :width].astype(jnp.float32), axis=0)
-    arrived = swapped((text_sum[rows:] * HALF).astype(jnp.float16), "zh", 1)
+    arrived = swapped((text_sum[rows:] * HALF).astype(jnp.float16), "zm", 1)
     arrived, loss_mean = lax.optimization_barrier((arrived, loss_mean))
     text_sum = text_sum[:rows] + arrived.astype(jnp.float32) * (1 / HALF)
     image_grads = gradients(heat_exponent, offset_added, picture_vectors, image_low, text_low, image_sum)

time: 135 us -> 134 us (level); the launches traced: 132 us -> 133 us
  starting transfers between devices: 82.8 us -> 84.4 us
    ppermute x10, waiting for transfers between devices: 28.7 us -> 24.4 us  [swapped(): lax.ppermute(value, axis, [(i, i ^ step) for i in range(lax.axis_size(axi...]
    all_to_all x1, waiting for transfers between devices: 0.01 us -> 4.11 us  [shards(): lax.all_to_all(jnp.broadcast_to(plane_loss, (column, 1, LANES)), COLUMN,...]
    all_to_all x1, starting transfers between devices: 12 us -> 13.5 us  [shards(): lax.all_to_all(jnp.broadcast_to(plane_loss, (column, 1, LANES)), COLUMN,...]
  transfers between devices with their start and end apart: 13 -> 13, of which waited for: 9 -> 7; matrix products, arithmetic and copies ran while one was open for 2% -> 2% of each run, Pallas kernels for 4% -> 4%
where the time goes in v10:
time: 134 us; the launch traced here: 133 us
  starting transfers between devices  84.4 us (63%)
  waiting for transfers between devices  28.5 us (21%)
  Pallas kernels  11.2 us (8%)
  between operations  3.93 us (3%)
  other arithmetic  3.12 us (2%)
  local copies, waits for them, and re-layouts  2.32 us (2%)
    ppermute x10, starting transfers between devices, swapped(): lax.ppermute(value, axis, [(i, i ^ step) for i in range(lax.axis_size(axi...  60.3 us
    ppermute x10, waiting for transfers between devices, swapped(): lax.ppermute(value, axis, [(i, i ^ step) for i in range(lax.axis_size(axi...  24.4 us
    all_to_all x1, starting transfers between devices, shards(): lax.all_to_all(jnp.broadcast_to(plane_loss, (column, 1, LANES)), COLUMN,...  13.5 us
    all_to_all x1, starting transfers between devices, shards(): lax.all_to_all(lax.dynamic_update_slice(copies, other_low, (0, rows, 0)),...  6.89 us
    all_to_all x1, waiting for transfers between devices, shards(): lax.all_to_all(jnp.broadcast_to(plane_loss, (column, 1, LANES)), COLUMN,...  4.11 us
    pallas_call x2, Pallas kernels, gradients(): pl.pallas_call(grad_kernel, in_specs=[pl.BlockSpec(memory_space=pltpu.SME...  3.75 us
    all_to_all x1, starting transfers between devices, shards(): lax.all_to_all(text_part.reshape(plane, 2 * rows, width + LANES), PLANE,...  3.73 us
    pallas_call x1, Pallas kernels, pair_terms(): pl.pallas_call(terms_kernel, in_specs=[pl.BlockSpec(memory_space=pltpu.VM...  2.85 us
  transfers between devices with their start and end apart: 13, of which 7 were waited for; matrix products, arithmetic and copies ran while one was open for 2% of the time, Pallas kernels for 4%

profile of v10, /device:TPU:1, one launch (start us, length us, event | category | flops | bytes accessed | tf_op | source)
XLA Modules:
  0.0 133.5 jit_solution(18068068868508989921)
XLA Ops:
  1.9 2.4 %shard_map.67 = (bf16[24,1152]{1,0:T(8,128)(2,1)}, bf16[24,1152]{1,0:T(8,128)(2,1)}, bf16[16,48,1152]{2,1,0:T(8,128)(2,1)}, f32[24,1]{1,0:T(8,128)}) custom-call(f32[1]{0:T(128)S(6)} %copy.13.heat_ref, f32[1]{0:T(128)S(6)} %copy.14.offset_ref, f32[24,1152]{1,0:T(8,128)} %row_ref.2, f32[24,1152]{1,0:T(8,128)} %row_ref.3), custom_call_target="tpu_custom_call" | custom-call | tf_op jit(solution)/shard_map/pallas_call | solution.py:56
  4.3 9.6 %collective-permute-start.4 = (bf16[24,1152]{1,0:T(8,128)(2,1)}, bf16[24,1152]{1,0:T(8,128)(2,1)S(1)}, u32[]{:S(2)}, u32[]{:S(2)}) collective-permute-start(bf16[24,1152]{1,0:T(8,128)(2,1)} %get-tuple-element.17.partner_ref.low_ref), channel_id=1, source_target_pairs={{0,256},{256,0},{1,257},{257,1},{2,258},{258,2},{3,259},{259,3},{4... | collective-permute-start | bytes 165896 | tf_op jit(solution)/shard_map/ppermute | solution.py:167
  14.0 10.6 %collective-permute-start = (bf16[24,1152]{1,0:T(8,128)(2,1)}, bf16[24,1152]{1,0:T(8,128)(2,1)S(1)}, u32[]{:S(2)}, u32[]{:S(2)}) collective-permute-start(bf16[24,1152]{1,0:T(8,128)(2,1)} %get-tuple-element.15.low_ref.partner_ref), channel_id=1, source_target_pairs={{0,1},{1,0},{2,3},{3,2},{4,5},{5,4},{6,7},{7,6},{8,9},{9,8},{10,11... | collective-permute-start | bytes 165896 | tf_op jit(solution)/shard_map/ppermute | solution.py:167
  24.6 0.0 collective-permute-done.4
  24.6 1.0 broadcast_dynamic-update-slice_fusion
  25.6 0.0 copy-start.1
  25.6 0.0 copy-start
  25.6 6.9 %all-to-all-start = ((bf16[16,48,1152]{2,1,0:T(8,128)(2,1)}), bf16[16,48,1152]{2,1,0:T(8,128)(2,1)S(1)}, u32[]{:S(2)}, u32[]{:S(2)}) async-start(bf16[16,48,1152]{2,1,0:T(8,128)(2,1)} %broadcast_dynamic-update-slice_fusion), calls=%async_computation | async-start | bytes 3538944 | tf_op jit(solution)/shard_map/all_to_all | solution.py:189
  32.5 0.0 copy-done.1
  32.6 0.0 collective-permute-done
  32.6 3.1 %collective-permute-start.1 = (bf16[48,1152]{1,0:T(8,128)(2,1)S(1)}, bf16[48,1152]{1,0:T(8,128)(2,1)S(1)}, u32[]{:S(2)}, u32[]{:S(2)}) collective-permute-start(bf16[48,1152]{1,0:T(8,128)(2,1)S(1)} %pad_maximum_fusion.1), channel_id=1, source_target_pairs={{0,128},{64,192},{128,0},{192,64},{1,129},{65,193},{129,1},{193,65... | collective-permute-start | bytes 331784 | tf_op jit(solution)/shard_map/ppermute | solution.py:167
  35.7 6.3 %collective-permute-done.1 = bf16[48,1152]{1,0:T(8,128)(2,1)S(1)} collective-permute-done((bf16[48,1152]{1,0:T(8,128)(2,1)S(1)}, bf16[48,1152]{1,0:T(8,128)(2,1)S(1)}, u32[]{:S(2)}, u32[]{:S(2)}) %collective-permute-start.1) | collective-permute-done | bytes 110624 | tf_op jit(solution)/shard_map/ppermute | solution.py:167
  42.0 1.9 %collective-permute-start.2 = (bf16[96,1152]{1,0:T(8,128)(2,1)S(1)}, bf16[96,1152]{1,0:T(8,128)(2,1)S(1)}, u32[]{:S(2)}, u32[]{:S(2)}) collective-permute-start(bf16[96,1152]{1,0:T(8,128)(2,1)S(1)} %pad_maximum_fusion), channel_id=1, source_target_pairs={{0,64},{64,0},{128,192},{192,128},{1,65},{65,1},{129,193},{193,129... | collective-permute-start | bytes 663560 | tf_op jit(solution)/shard_map/ppermute | solution.py:167
  43.9 5.6 %collective-permute-done.2 = bf16[96,1152]{1,0:T(8,128)(2,1)S(1)} collective-permute-done((bf16[96,1152]{1,0:T(8,128)(2,1)S(1)}, bf16[96,1152]{1,0:T(8,128)(2,1)S(1)}, u32[]{:S(2)}, u32[]{:S(2)}) %collective-permute-start.2) | collective-permute-done | bytes 221216 | tf_op jit(solution)/shard_map/ppermute | solution.py:167
  49.6 4.1 %collective-permute-start.3 = (bf16[192,1152]{1,0:T(8,128)(2,1)S(1)}, bf16[192,1152]{1,0:T(8,128)(2,1)S(1)}, u32[]{:S(2)}, u32[]{:S(2)}) collective-permute-start(bf16[192,1152]{1,0:T(8,128)(2,1)S(1)} %constant_dynamic-update-slice_fusion.near_ref), channel_id=1, source_target_pairs={{0,8},{8,0},{1,9},{9,1},{2,10},{10,2},{3,11},{11,3},{4,12},{12,4},... | collective-permute-start | bytes 1327112 | tf_op jit(solution)/shard_map/ppermute | solution.py:167
  53.7 1.4 %collective-permute-done.3.far_ref = bf16[192,1152]{1,0:T(8,128)(2,1)S(1)} collective-permute-done((bf16[192,1152]{1,0:T(8,128)(2,1)S(1)}, bf16[192,1152]{1,0:T(8,128)(2,1)S(1)}, u32[]{:S(2)}, u32[]{:S(2)}) %collective-permute-start.3) | collective-permute-done | bytes 442400 | tf_op jit(solution)/shard_map/ppermute | solution.py:167
  55.1 0.0 all-to-all-done
  55.1 0.0 copy-done
  55.1 2.2 %shard_map.68 = (bf16[2,192,768]{2,1,0:T(8,128)(2,1)S(1)}, f32[192,1152]{1,0:T(8,128)S(1)}, f32[8,128]{1,0:T(8,128)S(1)}) custom-call(s32[1]{0:T(128)} %bitcast.place_ref, f32[1]{0:T(128)S(6)} %copy.13.heat_ref, f32[1]{0:T(128)S(6)} %copy.14.offset_ref, f32[24,1]{1,0:T(8,128)S(1)} %copy-done, ...), custom_call_target="tpu_custom_call" | custom-call | flops 1019215872 | bytes 1769472 | tf_op jit(solution)/shard_map/pallas_call | solution.py:107
  57.3 6.3 %collective-permute-start.6 = (f32[192,1152]{1,0:T(8,128)S(1)}, f32[192,1152]{1,0:T(8,128)S(1)}, u32[]{:S(2)}, u32[]{:S(2)}) collective-permute-start(f32[192,1152]{1,0:T(8,128)S(1)} %get-tuple-element.23), channel_id=1, source_target_pairs={{0,8},{8,0},{1,9},{9,1},{2,10},{10,2},{3,11},{11,3},{4,12},{12,4},... | collective-permute-start | bytes 2654216 | tf_op jit(solution)/shard_map/ppermute | solution.py:167
  63.6 2.8 %shard_map.69 = (f32[192,1152]{1,0:T(8,128)S(1)}, bf16[768,1280]{1,0:T(8,128)(2,1)}) custom-call(bf16[2,192,768]{2,1,0:T(8,128)(2,1)S(1)} %get-tuple-element.18.weight_ref, f32[8,128]{1,0:T(8,128)S(1)} %get-tuple-element.19.loss_ref, bf16[192,1152]{1,0:T(8,128)(2,1)S(1)} %constant_dynamic-update-slice_fusion.near_ref, ...), custom_call_target="tpu_custom_call" | custom-call | flops 1019215872 | bytes 3538944 | tf_op jit(solution)/shard_map/pallas_call | solution.py:137
  66.5 0.0 collective-permute-done.6
  66.5 0.1 add.19
  66.6 2.6 %collective-permute-start.7 = (f16[96,1152]{1,0:T(8,128)(2,1)S(1)}, f16[96,1152]{1,0:T(8,128)(2,1)S(1)}, u32[]{:S(2)}, u32[]{:S(2)}) collective-permute-start(f16[96,1152]{1,0:T(8,128)(2,1)S(1)} %fusion), channel_id=1, source_target_pairs={{0,64},{64,0},{128,192},{192,128},{1,65},{65,1},{129,193},{193,129... | collective-permute-start | bytes 663560 | tf_op jit(solution)/shard_map/ppermute | solution.py:167
  69.3 3.7 %all-to-all-start.1 = ((bf16[16,48,1280]{2,1,0:T(8,128)(2,1)}), bf16[16,48,1280]{2,1,0:T(8,128)(2,1)S(1)}, u32[]{:S(2)}, u32[]{:S(2)}) async-start(bf16[16,48,1280]{2,1,0:T(8,128)(2,1)} %bitcast.2), calls=%async_computation.1 | async-start | bytes 3932160 | tf_op jit(solution)/shard_map/all_to_all | solution.py:200
  73.0 2.6 %collective-permute-done.7 = f16[96,1152]{1,0:T(8,128)(2,1)S(1)} collective-permute-done((f16[96,1152]{1,0:T(8,128)(2,1)S(1)}, f16[96,1152]{1,0:T(8,128)(2,1)S(1)}, u32[]{:S(2)}, u32[]{:S(2)}) %collective-permute-start.7) | collective-permute-done | bytes 221216 | tf_op jit(solution)/shard_map/ppermute | solution.py:167
  75.6 0.1 slice_add_fusion
  75.7 3.1 %collective-permute-start.8 = (f16[48,1152]{1,0:T(8,128)(2,1)S(1)}, f16[48,1152]{1,0:T(8,128)(2,1)S(1)}, u32[]{:S(2)}, u32[]{:S(2)}) collective-permute-start(f16[48,1152]{1,0:T(8,128)(2,1)S(1)} %fusion.1), channel_id=1, source_target_pairs={{0,128},{64,192},{128,0},{192,64},{1,129},{65,193},{129,1},{193,65... | collective-permute-start | bytes 331784 | tf_op jit(solution)/shard_map/ppermute | solution.py:167
  78.8 6.6 %collective-permute-done.8 = f16[48,1152]{1,0:T(8,128)(2,1)S(1)} collective-permute-done((f16[48,1152]{1,0:T(8,128)(2,1)S(1)}, f16[48,1152]{1,0:T(8,128)(2,1)S(1)}, u32[]{:S(2)}, u32[]{:S(2)}) %collective-permute-start.8) | collective-permute-done | bytes 110624 | tf_op jit(solution)/shard_map/ppermute | solution.py:167
  85.4 11.6 %collective-permute-start.9 = (f16[24,1152]{1,0:T(8,128)(2,1)S(1)}, f16[24,1152]{1,0:T(8,128)(2,1)S(1)}, u32[]{:S(2)}, u32[]{:S(2)}) collective-permute-start(f16[24,1152]{1,0:T(8,128)(2,1)S(1)} %fusion.2), channel_id=1, source_target_pairs={{0,1},{1,0},{2,3},{3,2},{4,5},{5,4},{6,7},{7,6},{8,9},{9,8},{10,11... | collective-permute-start | bytes 165896 | tf_op jit(solution)/shard_map/ppermute | solution.py:167
  97.0 2.0 %collective-permute-done.9 = f16[24,1152]{1,0:T(8,128)(2,1)S(1)} collective-permute-done((f16[24,1152]{1,0:T(8,128)(2,1)S(1)}, f16[24,1152]{1,0:T(8,128)(2,1)S(1)}, u32[]{:S(2)}, u32[]{:S(2)}) %collective-permute-start.9) | collective-permute-done | bytes 55328 | tf_op jit(solution)/shard_map/ppermute | solution.py:167
  99.0 0.7 slice_add_fusion.3.sum_ref
  99.7 1.9 %shard_map.70 = f32[24,1152]{1,0:T(8,128)} custom-call(f32[1]{0:T(128)S(6)} %copy.13.heat_ref, f32[1]{0:T(128)S(6)} %copy.14.offset_ref, f32[24,1152]{1,0:T(8,128)} %row_ref.2, bf16[24,1152]{1,0:T(8,128)(2,1)} %get-tuple-element.15.low_ref.partner_ref, bf16[24,1152]{1,0:T(8,128)(2,1)} %get-tuple-element.17.partner_ref.low_ref, ...), custom_call_target="tpu_custom_call" | custom-call | tf_op jit(solution)/shard_map/pallas_call | solution.py:159
  101.6 0.0 all-to-all-done.1
  101.6 0.6 fusion.4
  102.2 1.3 broadcast_in_dim.10
  103.5 13.5 %all-to-all-start.2 = ((f32[32,1,128]{2,1,0:T(1,128)}), f32[32,1,128]{2,1,0:T(1,128)S(1)}, u32[]{:S(2)}, u32[]{:S(2)}) async-start(f32[32,1,128]{2,1,0:T(1,128)} %broadcast_in_dim.10), calls=%async_computation.2 | async-start | bytes 32768 | tf_op jit(solution)/shard_map/all_to_all | solution.py:207
  116.9 0.3 convert_reduce_fusion
  117.2 7.2 %collective-permute-start.5 = (f16[24,1152]{1,0:T(8,128)(2,1)S(1)}, f16[24,1152]{1,0:T(8,128)(2,1)S(1)}, u32[]{:S(2)}, u32[]{:S(2)}) collective-permute-start(f16[24,1152]{1,0:T(8,128)(2,1)S(1)} %fusion.3), channel_id=1, source_target_pairs={{0,256},{256,0},{1,257},{257,1},{2,258},{258,2},{3,259},{259,3},{4... | collective-permute-start | bytes 165896 | tf_op jit(solution)/shard_map/ppermute | solution.py:167
  124.4 4.1 %all-to-all-done.2 = f32[32,1,128]{2,1,0:T(1,128)S(1)} async-done(((f32[32,1,128]{2,1,0:T(1,128)}), f32[32,1,128]{2,1,0:T(1,128)S(1)}, u32[]{:S(2)}, u32[]{:S(2)}) %all-to-all-start.2) | async-done | bytes 16416 | tf_op jit(solution)/shard_map/all_to_all | solution.py:207
  128.5 0.6 slice_reduce_fusion
  129.8 0.0 collective-permute-done.5
  129.8 0.7 slice_add_fusion.2.sum_ref
  130.5 1.9 %shard_map.71 = f32[24,1152]{1,0:T(8,128)} custom-call(f32[1]{0:T(128)S(6)} %copy.13.heat_ref, f32[1]{0:T(128)S(6)} %copy.14.offset_ref, f32[24,1152]{1,0:T(8,128)} %row_ref.3, bf16[24,1152]{1,0:T(8,128)(2,1)} %get-tuple-element.17.partner_ref.low_ref, bf16[24,1152]{1,0:T(8,128)(2,1)} %get-tuple-element.15.low_ref.partner_ref, ...), custom_call_target="tpu_custom_call" | custom-call | tf_op jit(solution)/shard_map/pallas_call | solution.py:159
  (11 shorter events, 0.2 us)
Async XLA Ops:
  4.3 20.3 %collective-permute-start.4 = (bf16[24,1152]{1,0:T(8,128)(2,1)}, bf16[24,1152]{1,0:T(8,128)(2,1)S(1)}, u32[]{:S(2)}, u32[]{:S(2)}) collective-permute-start(bf16[24,1152]{1,0:T(8,128)(2,1)} %get-tuple-element.17.partner_ref.low_ref), channel_id=1, source_target_pairs={{0,256},{256,0},{1,257},{257,1},{2,258},{258,2},{3,259},{259,3},{4... | collective-permute-start | bytes 165896 | tf_op jit(solution)/shard_map/ppermute | solution.py:167
  14.0 18.6 %collective-permute-start = (bf16[24,1152]{1,0:T(8,128)(2,1)}, bf16[24,1152]{1,0:T(8,128)(2,1)S(1)}, u32[]{:S(2)}, u32[]{:S(2)}) collective-permute-start(bf16[24,1152]{1,0:T(8,128)(2,1)} %get-tuple-element.15.low_ref.partner_ref), channel_id=1, source_target_pairs={{0,1},{1,0},{2,3},{3,2},{4,5},{5,4},{6,7},{7,6},{8,9},{9,8},{10,11... | collective-permute-start | bytes 165896 | tf_op jit(solution)/shard_map/ppermute | solution.py:167
  25.6 6.9 %copy-start.1 = (bf16[24,1152]{1,0:T(8,128)(2,1)S(1)}, bf16[24,1152]{1,0:T(8,128)(2,1)}, u32[]{:S(2)}) copy-start(bf16[24,1152]{1,0:T(8,128)(2,1)} %get-tuple-element.15.low_ref.partner_ref) | copy-start | bytes 165892
  25.6 29.4 %copy-start = (f32[24,1]{1,0:T(8,128)S(1)}, f32[24,1]{1,0:T(8,128)}, u32[]{:S(2)}) copy-start(f32[24,1]{1,0:T(8,128)} %get-tuple-element.14.own_loss_ref) | copy-start | bytes 292
  25.6 29.4 %all-to-all-start = ((bf16[16,48,1152]{2,1,0:T(8,128)(2,1)}), bf16[16,48,1152]{2,1,0:T(8,128)(2,1)S(1)}, u32[]{:S(2)}, u32[]{:S(2)}) async-start(bf16[16,48,1152]{2,1,0:T(8,128)(2,1)} %broadcast_dynamic-update-slice_fusion), calls=%async_computation | async-start | bytes 3538944 | tf_op jit(solution)/shard_map/all_to_all | solution.py:189
  32.6 9.4 %collective-permute-start.1 = (bf16[48,1152]{1,0:T(8,128)(2,1)S(1)}, bf16[48,1152]{1,0:T(8,128)(2,1)S(1)}, u32[]{:S(2)}, u32[]{:S(2)}) collective-permute-start(bf16[48,1152]{1,0:T(8,128)(2,1)S(1)} %pad_maximum_fusion.1), channel_id=1, source_target_pairs={{0,128},{64,192},{128,0},{192,64},{1,129},{65,193},{129,1},{193,65... | collective-permute-start | bytes 331784 | tf_op jit(solution)/shard_map/ppermute | solution.py:167
  42.0 7.6 %collective-permute-start.2 = (bf16[96,1152]{1,0:T(8,128)(2,1)S(1)}, bf16[96,1152]{1,0:T(8,128)(2,1)S(1)}, u32[]{:S(2)}, u32[]{:S(2)}) collective-permute-start(bf16[96,1152]{1,0:T(8,128)(2,1)S(1)} %pad_maximum_fusion), channel_id=1, source_target_pairs={{0,64},{64,0},{128,192},{192,128},{1,65},{65,1},{129,193},{193,129... | collective-permute-start | bytes 663560 | tf_op jit(solution)/shard_map/ppermute | solution.py:167
  49.6 5.5 %collective-permute-start.3 = (bf16[192,1152]{1,0:T(8,128)(2,1)S(1)}, bf16[192,1152]{1,0:T(8,128)(2,1)S(1)}, u32[]{:S(2)}, u32[]{:S(2)}) collective-permute-start(bf16[192,1152]{1,0:T(8,128)(2,1)S(1)} %constant_dynamic-update-slice_fusion.near_ref), channel_id=1, source_target_pairs={{0,8},{8,0},{1,9},{9,1},{2,10},{10,2},{3,11},{11,3},{4,12},{12,4},... | collective-permute-start | bytes 1327112 | tf_op jit(solution)/shard_map/ppermute | solution.py:167
  57.3 9.2 %collective-permute-start.6 = (f32[192,1152]{1,0:T(8,128)S(1)}, f32[192,1152]{1,0:T(8,128)S(1)}, u32[]{:S(2)}, u32[]{:S(2)}) collective-permute-start(f32[192,1152]{1,0:T(8,128)S(1)} %get-tuple-element.23), channel_id=1, source_target_pairs={{0,8},{8,0},{1,9},{9,1},{2,10},{10,2},{3,11},{11,3},{4,12},{12,4},... | collective-permute-start | bytes 2654216 | tf_op jit(solution)/shard_map/ppermute | solution.py:167
  66.6 8.9 %collective-permute-start.7 = (f16[96,1152]{1,0:T(8,128)(2,1)S(1)}, f16[96,1152]{1,0:T(8,128)(2,1)S(1)}, u32[]{:S(2)}, u32[]{:S(2)}) collective-permute-start(f16[96,1152]{1,0:T(8,128)(2,1)S(1)} %fusion), channel_id=1, source_target_pairs={{0,64},{64,0},{128,192},{192,128},{1,65},{65,1},{129,193},{193,129... | collective-permute-start | bytes 663560 | tf_op jit(solution)/shard_map/ppermute | solution.py:167
  69.3 32.3 %all-to-all-start.1 = ((bf16[16,48,1280]{2,1,0:T(8,128)(2,1)}), bf16[16,48,1280]{2,1,0:T(8,128)(2,1)S(1)}, u32[]{:S(2)}, u32[]{:S(2)}) async-start(bf16[16,48,1280]{2,1,0:T(8,128)(2,1)} %bitcast.2), calls=%async_computation.1 | async-start | bytes 3932160 | tf_op jit(solution)/shard_map/all_to_all | solution.py:200
  75.7 9.7 %collective-permute-start.8 = (f16[48,1152]{1,0:T(8,128)(2,1)S(1)}, f16[48,1152]{1,0:T(8,128)(2,1)S(1)}, u32[]{:S(2)}, u32[]{:S(2)}) collective-permute-start(f16[48,1152]{1,0:T(8,128)(2,1)S(1)} %fusion.1), channel_id=1, source_target_pairs={{0,128},{64,192},{128,0},{192,64},{1,129},{65,193},{129,1},{193,65... | collective-permute-start | bytes 331784 | tf_op jit(solution)/shard_map/ppermute | solution.py:167
  85.4 13.6 %collective-permute-start.9 = (f16[24,1152]{1,0:T(8,128)(2,1)S(1)}, f16[24,1152]{1,0:T(8,128)(2,1)S(1)}, u32[]{:S(2)}, u32[]{:S(2)}) collective-permute-start(f16[24,1152]{1,0:T(8,128)(2,1)S(1)} %fusion.2), channel_id=1, source_target_pairs={{0,1},{1,0},{2,3},{3,2},{4,5},{5,4},{6,7},{7,6},{8,9},{9,8},{10,11... | collective-permute-start | bytes 165896 | tf_op jit(solution)/shard_map/ppermute | solution.py:167
  103.5 25.1 %all-to-all-start.2 = ((f32[32,1,128]{2,1,0:T(1,128)}), f32[32,1,128]{2,1,0:T(1,128)S(1)}, u32[]{:S(2)}, u32[]{:S(2)}) async-start(f32[32,1,128]{2,1,0:T(1,128)} %broadcast_in_dim.10), calls=%async_computation.2 | async-start | bytes 32768 | tf_op jit(solution)/shard_map/all_to_all | solution.py:207
  117.2 12.6 %collective-permute-start.5 = (f16[24,1152]{1,0:T(8,128)(2,1)S(1)}, f16[24,1152]{1,0:T(8,128)(2,1)S(1)}, u32[]{:S(2)}, u32[]{:S(2)}) collective-permute-start(f16[24,1152]{1,0:T(8,128)(2,1)S(1)} %fusion.3), channel_id=1, source_target_pairs={{0,256},{256,0},{1,257},{257,1},{2,258},{258,2},{3,259},{259,3},{4... | collective-permute-start | bytes 165896 | tf_op jit(solution)/shard_map/ppermute | solution.py:167

commit v11 on v10

--- a/solution.py
+++ b/solution.py
@@ -177,10 +177,17 @@
     return value[:half] + swapped(sent, axis, step).astype(jnp.float32) * (1 / HALF)
 
 
+def summed(value, axis, steps):
+    rows = value.shape[0] // (len(steps) + 1)
+    blocks = [value[step * rows : (step + 1) * rows] for step in steps]
+    arrived = [swapped((block * HALF).astype(jnp.float16), axis, step) for block, step in zip(blocks, steps)]
+    return value[:rows] + sum(part.astype(jnp.float32) for part in arrived) * (1 / HALF)
+
+
 def shards(picture_vectors, caption_vectors, heat_exponent, offset_added):
     rows, width = picture_vectors.shape
     plane, column = lax.axis_size(PLANE), lax.axis_size(COLUMN)
-    steps = [1 << bit for bit in range(lax.axis_size("zl").bit_length() - 1)]
+    steps = range(1, lax.axis_size("zl"))
     image_low, text_low, copies, own_loss = unit_rows(
         plane, heat_exponent, offset_added, picture_vectors, caption_vectors
     )
@@ -189,8 +196,7 @@
     texts = lax.all_to_all(lax.dynamic_update_slice(copies, other_low, (0, rows, 0)), PLANE, 0, 0)
     texts = texts.reshape(plane * 2 * rows, width)
     near = doubled(image_low, "zh", 1)
-    for step in reversed(steps):
-        near = doubled(near, "zl", step)
+    near = jnp.concatenate([near] + [swapped(near, "zl", step) for step in steps], axis=0)
     far = swapped(near, "c", 1)
 
     place = (lax.axis_index(PLANE) * 2 * rows).astype(jnp.int32).reshape(1)
@@ -199,17 +205,15 @@
     near_part, text_part = pair_terms(weights, loss, near, far, texts)
     text_parts = lax.all_to_all(text_part.reshape(plane, 2 * rows, width + LANES), PLANE, 0, 0)
     image_sum = near_part + far_part
-    for step in steps:
-        image_sum = halved(image_sum, "zl", step)
-    image_sum = halved(image_sum, "zh", 1)
+    image_sum = halved(summed(image_sum, "zl", steps), "zh", 1)
 
     plane_loss = jnp.sum(text_parts[:, 0, width : width + 3].astype(jnp.float32))
     losses = lax.all_to_all(jnp.broadcast_to(plane_loss, (column, 1, LANES)), COLUMN, 0, 0)
-    loss_mean = (jnp.sum(losses[:, 0, 0]) / (rows * lax.axis_size(AXES))).reshape(1)
     text_sum = jnp.sum(text_parts[:, :, :width].astype(jnp.float32), axis=0)
     arrived = swapped((text_sum[rows:] * HALF).astype(jnp.float16), "zm", 1)
-    arrived, loss_mean = lax.optimization_barrier((arrived, loss_mean))
+    arrived, losses = lax.optimization_barrier((arrived, losses))
     text_sum = text_sum[:rows] + arrived.astype(jnp.float32) * (1 / HALF)
+    loss_mean = (jnp.sum(losses[:, 0, 0]) / (rows * lax.axis_size(AXES))).reshape(1)
     image_grads = gradients(heat_exponent, offset_added, picture_vectors, image_low, text_low, image_sum)
     text_grads = gradients(heat_exponent, offset_added, caption_vectors, text_low, image_low, text_sum)
     return (loss_mean, image_grads, text_grads)

time: 134 us -> 135 us (level)
  the two profiles are of different devices: /device:TPU:1 before, /device:TPU:16 now
where the time goes in v11:
time: 135 us; the launch traced here: 134 us
  starting transfers between devices  86.1 us (64%)
  waiting for transfers between devices  22.6 us (17%)
  Pallas kernels  12.2 us (9%)
  other arithmetic  6.53 us (5%)
  between operations  3.93 us (3%)
  local copies, waits for them, and re-layouts  2.35 us (2%)
    ppermute x12, starting transfers between devices, swapped(): lax.ppermute(value, axis, [(i, i ^ step) for i in range(lax.axis_size(axi...  61.4 us
    ppermute x12, waiting for transfers between devices, swapped(): lax.ppermute(value, axis, [(i, i ^ step) for i in range(lax.axis_size(axi...  20.5 us
    all_to_all x1, starting transfers between devices, shards(): lax.all_to_all(jnp.broadcast_to(plane_loss, (column, 1, LANES)), COLUMN,...  9.96 us
    all_to_all x1, starting transfers between devices, shards(): lax.all_to_all(text_part.reshape(plane, 2 * rows, width + LANES), PLANE,...  7.41 us
    all_to_all x1, starting transfers between devices, shards(): lax.all_to_all(lax.dynamic_update_slice(copies, other_low, (0, rows, 0)),...  7.41 us
    pallas_call x2, Pallas kernels, gradients(): pl.pallas_call(grad_kernel, in_specs=[pl.BlockSpec(memory_space=pltpu.SME...  3.75 us
    pallas_call x1, Pallas kernels, pair_weights(): pl.pallas_call(pair_kernel, in_specs=[pl.BlockSpec(memory_space=pltpu.SME...  3.13 us
    pallas_call x1, Pallas kernels, pair_terms(): pl.pallas_call(terms_kernel, in_specs=[pl.BlockSpec(memory_space=pltpu.VM...  2.82 us
  transfers between devices with their start and end apart: 15, of which 6 were waited for; matrix products, arithmetic and copies ran while one was open for 6% of the time, Pallas kernels for 4%

profile of v11, /device:TPU:16, one launch (start us, length us, event | category | flops | bytes accessed | tf_op | source)
XLA Modules:
  0.0 133.7 jit_solution(871077049111146116)
XLA Ops:
  1.9 2.5 %shard_map.67 = (bf16[24,1152]{1,0:T(8,128)(2,1)}, bf16[24,1152]{1,0:T(8,128)(2,1)}, bf16[16,48,1152]{2,1,0:T(8,128)(2,1)}, f32[24,1]{1,0:T(8,128)}) custom-call(f32[1]{0:T(128)S(6)} %copy.15.heat_ref, f32[1]{0:T(128)S(6)} %copy.16.offset_ref, f32[24,1152]{1,0:T(8,128)} %row_ref.2, f32[24,1152]{1,0:T(8,128)} %row_ref.3), custom_call_target="tpu_custom_call" | custom-call | tf_op jit(solution)/shard_map/pallas_call | solution.py:56
  4.4 9.1 %collective-permute-start.5 = (bf16[24,1152]{1,0:T(8,128)(2,1)}, bf16[24,1152]{1,0:T(8,128)(2,1)S(1)}, u32[]{:S(2)}, u32[]{:S(2)}) collective-permute-start(bf16[24,1152]{1,0:T(8,128)(2,1)} %get-tuple-element.17.partner_ref.low_ref), channel_id=1, source_target_pairs={{0,256},{256,0},{1,257},{257,1},{2,258},{258,2},{3,259},{259,3},{4... | collective-permute-start | bytes 165896 | tf_op jit(solution)/shard_map/ppermute | solution.py:167
  13.5 10.9 %collective-permute-start = (bf16[24,1152]{1,0:T(8,128)(2,1)}, bf16[24,1152]{1,0:T(8,128)(2,1)S(1)}, u32[]{:S(2)}, u32[]{:S(2)}) collective-permute-start(bf16[24,1152]{1,0:T(8,128)(2,1)} %get-tuple-element.15.low_ref.partner_ref), channel_id=1, source_target_pairs={{0,1},{1,0},{2,3},{3,2},{4,5},{5,4},{6,7},{7,6},{8,9},{9,8},{10,11... | collective-permute-start | bytes 165896 | tf_op jit(solution)/shard_map/ppermute | solution.py:167
  24.4 0.0 collective-permute-done.5
  24.4 1.0 broadcast_dynamic-update-slice_fusion
  25.4 0.0 copy-start.1
  25.4 0.0 copy-start
  25.4 7.4 %all-to-all-start = ((bf16[16,48,1152]{2,1,0:T(8,128)(2,1)}), bf16[16,48,1152]{2,1,0:T(8,128)(2,1)S(1)}, u32[]{:S(2)}, u32[]{:S(2)}) async-start(bf16[16,48,1152]{2,1,0:T(8,128)(2,1)} %broadcast_dynamic-update-slice_fusion), calls=%async_computation | async-start | bytes 3538944 | tf_op jit(solution)/shard_map/all_to_all | solution.py:196
  32.8 0.0 copy-done.1
  32.9 0.0 collective-permute-done
  32.9 2.9 %collective-permute-start.1 = (bf16[48,1152]{1,0:T(8,128)(2,1)S(1)}, bf16[48,1152]{1,0:T(8,128)(2,1)S(1)}, u32[]{:S(2)}, u32[]{:S(2)}) collective-permute-start(bf16[48,1152]{1,0:T(8,128)(2,1)S(1)} %get-tuple-element.28), channel_id=1, source_target_pairs={{0,64},{64,0},{128,192},{192,128},{1,65},{65,1},{129,193},{193,129... | collective-permute-start | bytes 331784 | tf_op jit(solution)/shard_map/ppermute | solution.py:167
  35.8 3.8 %collective-permute-start.3 = (bf16[48,1152]{1,0:T(8,128)(2,1)S(1)}, bf16[48,1152]{1,0:T(8,128)(2,1)S(1)}, u32[]{:S(2)}, u32[]{:S(2)}) collective-permute-start(bf16[48,1152]{1,0:T(8,128)(2,1)S(1)} %get-tuple-element.28), channel_id=1, source_target_pairs={{0,192},{64,128},{128,64},{192,0},{1,193},{65,129},{129,65},{193,1... | collective-permute-start | bytes 331784 | tf_op jit(solution)/shard_map/ppermute | solution.py:167
  39.7 2.5 %collective-permute-start.2 = (bf16[48,1152]{1,0:T(8,128)(2,1)S(1)}, bf16[48,1152]{1,0:T(8,128)(2,1)S(1)}, u32[]{:S(2)}, u32[]{:S(2)}) collective-permute-start(bf16[48,1152]{1,0:T(8,128)(2,1)S(1)} %get-tuple-element.28), channel_id=1, source_target_pairs={{0,128},{64,192},{128,0},{192,64},{1,129},{65,193},{129,1},{193,65... | collective-permute-start | bytes 331784 | tf_op jit(solution)/shard_map/ppermute | solution.py:167
  42.1 0.0 collective-permute-done.1
  42.2 7.2 %collective-permute-done.2 = bf16[48,1152]{1,0:T(8,128)(2,1)S(1)} collective-permute-done((bf16[48,1152]{1,0:T(8,128)(2,1)S(1)}, bf16[48,1152]{1,0:T(8,128)(2,1)S(1)}, u32[]{:S(2)}, u32[]{:S(2)}) %collective-permute-start.2) | collective-permute-done | bytes 110624 | tf_op jit(solution)/shard_map/ppermute | solution.py:167
  49.4 0.0 collective-permute-done.3
  49.4 1.9 %collective-permute-start.4 = (bf16[192,1152]{1,0:T(8,128)(2,1)S(1)}, bf16[192,1152]{1,0:T(8,128)(2,1)S(1)}, u32[]{:S(2)}, u32[]{:S(2)}) collective-permute-start(bf16[192,1152]{1,0:T(8,128)(2,1)S(1)} %constant_dynamic-update-slice_fusion.2.near_ref), channel_id=1, source_target_pairs={{0,8},{8,0},{1,9},{9,1},{2,10},{10,2},{3,11},{11,3},{4,12},{12,4},... | collective-permute-start | bytes 1327112 | tf_op jit(solution)/shard_map/ppermute | solution.py:167
  51.4 1.8 %collective-permute-done.4.far_ref = bf16[192,1152]{1,0:T(8,128)(2,1)S(1)} collective-permute-done((bf16[192,1152]{1,0:T(8,128)(2,1)S(1)}, bf16[192,1152]{1,0:T(8,128)(2,1)S(1)}, u32[]{:S(2)}, u32[]{:S(2)}) %collective-permute-start.4) | collective-permute-done | bytes 442400 | tf_op jit(solution)/shard_map/ppermute | solution.py:167
  53.1 2.0 %all-to-all-done = bf16[16,48,1152]{2,1,0:T(8,128)(2,1)S(1)} async-done(((bf16[16,48,1152]{2,1,0:T(8,128)(2,1)}), bf16[16,48,1152]{2,1,0:T(8,128)(2,1)S(1)}, u32[]{:S(2)}, u32[]{:S(2)}) %all-to-all-start) | async-done | bytes 1769504 | tf_op jit(solution)/shard_map/all_to_all | solution.py:196
  55.1 0.0 copy-done
  55.1 3.1 %shard_map.68 = (bf16[2,192,768]{2,1,0:T(8,128)(2,1)S(1)}, f32[192,1152]{1,0:T(8,128)}, f32[8,128]{1,0:T(8,128)S(1)}) custom-call(s32[1]{0:T(128)} %bitcast.place_ref, f32[1]{0:T(128)S(6)} %copy.15.heat_ref, f32[1]{0:T(128)S(6)} %copy.16.offset_ref, f32[24,1]{1,0:T(8,128)S(1)} %copy-done, bf16[192,1152]{1,0:T(8,128)(2,1)S(1)} %constant_dynamic-update-slice_fusion.2.near_ref, ...), custom_call_target="tpu_custom_call" | custom-call | flops 1019215872 | bytes 1769472 | tf_op jit(solution)/shard_map/pallas_call | solution.py:107
  58.3 1.9 %collective-permute-start.7 = (f32[192,1152]{1,0:T(8,128)}, f32[192,1152]{1,0:T(8,128)}, u32[]{:S(2)}, u32[]{:S(2)}) collective-permute-start(f32[192,1152]{1,0:T(8,128)} %get-tuple-element.23), channel_id=1, source_target_pairs={{0,8},{8,0},{1,9},{9,1},{2,10},{10,2},{3,11},{11,3},{4,12},{12,4},... | collective-permute-start | bytes 2654216 | tf_op jit(solution)/shard_map/ppermute | solution.py:167
  60.2 2.8 %shard_map.69 = (f32[192,1152]{1,0:T(8,128)S(1)}, bf16[768,1280]{1,0:T(8,128)(2,1)}) custom-call(bf16[2,192,768]{2,1,0:T(8,128)(2,1)S(1)} %get-tuple-element.18.weight_ref, f32[8,128]{1,0:T(8,128)S(1)} %get-tuple-element.19.loss_ref, bf16[192,1152]{1,0:T(8,128)(2,1)S(1)} %constant_dynamic-update-slice_fusion.2.near_ref, ...), custom_call_target="tpu_custom_call" | custom-call | flops 1019215872 | bytes 3538944 | tf_op jit(solution)/shard_map/pallas_call | solution.py:137
  63.0 7.4 %all-to-all-start.1 = ((bf16[16,48,1280]{2,1,0:T(8,128)(2,1)}), bf16[16,48,1280]{2,1,0:T(8,128)(2,1)}, u32[]{:S(2)}, u32[]{:S(2)}) async-start(bf16[16,48,1280]{2,1,0:T(8,128)(2,1)} %bitcast.2), calls=%async_computation.1 | async-start | bytes 3932160 | tf_op jit(solution)/shard_map/all_to_all | solution.py:206
  70.4 0.0 collective-permute-done.7
  70.4 1.3 add.22
  71.7 0.1 fusion.2
  71.8 2.9 %collective-permute-start.8 = (f16[48,1152]{1,0:T(8,128)(2,1)S(1)}, f16[48,1152]{1,0:T(8,128)(2,1)S(1)}, u32[]{:S(2)}, u32[]{:S(2)}) collective-permute-start(f16[48,1152]{1,0:T(8,128)(2,1)S(1)} %get-tuple-element.25), channel_id=1, source_target_pairs={{0,64},{64,0},{128,192},{192,128},{1,65},{65,1},{129,193},{193,129... | collective-permute-start | bytes 331784 | tf_op jit(solution)/shard_map/ppermute | solution.py:167
  74.7 3.8 %collective-permute-start.10 = (f16[48,1152]{1,0:T(8,128)(2,1)S(1)}, f16[48,1152]{1,0:T(8,128)(2,1)S(1)}, u32[]{:S(2)}, u32[]{:S(2)}) collective-permute-start(f16[48,1152]{1,0:T(8,128)(2,1)S(1)} %get-tuple-element.26), channel_id=1, source_target_pairs={{0,192},{64,128},{128,64},{192,0},{1,193},{65,129},{129,65},{193,1... | collective-permute-start | bytes 331784 | tf_op jit(solution)/shard_map/ppermute | solution.py:167
  78.6 2.5 %collective-permute-start.9 = (f16[48,1152]{1,0:T(8,128)(2,1)S(1)}, f16[48,1152]{1,0:T(8,128)(2,1)S(1)}, u32[]{:S(2)}, u32[]{:S(2)}) collective-permute-start(f16[48,1152]{1,0:T(8,128)(2,1)S(1)} %get-tuple-element.27), channel_id=1, source_target_pairs={{0,128},{64,192},{128,0},{192,64},{1,129},{65,193},{129,1},{193,65... | collective-permute-start | bytes 331784 | tf_op jit(solution)/shard_map/ppermute | solution.py:167
  81.0 0.0 collective-permute-done.8
  81.1 2.5 %collective-permute-done.10 = f16[48,1152]{1,0:T(8,128)(2,1)S(1)} collective-permute-done((f16[48,1152]{1,0:T(8,128)(2,1)S(1)}, f16[48,1152]{1,0:T(8,128)(2,1)S(1)}, u32[]{:S(2)}, u32[]{:S(2)}) %collective-permute-start.10) | collective-permute-done | bytes 110624 | tf_op jit(solution)/shard_map/ppermute | solution.py:167
  83.6 5.5 %collective-permute-done.9 = f16[48,1152]{1,0:T(8,128)(2,1)S(1)} collective-permute-done((f16[48,1152]{1,0:T(8,128)(2,1)S(1)}, f16[48,1152]{1,0:T(8,128)(2,1)S(1)}, u32[]{:S(2)}, u32[]{:S(2)}) %collective-permute-start.9) | collective-permute-done | bytes 110624 | tf_op jit(solution)/shard_map/ppermute | solution.py:167
  89.1 0.1 slice_add_fusion
  89.2 11.5 %collective-permute-start.11 = (f16[24,1152]{1,0:T(8,128)(2,1)S(1)}, f16[24,1152]{1,0:T(8,128)(2,1)S(1)}, u32[]{:S(2)}, u32[]{:S(2)}) collective-permute-start(f16[24,1152]{1,0:T(8,128)(2,1)S(1)} %fusion.3), channel_id=1, source_target_pairs={{0,1},{1,0},{2,3},{3,2},{4,5},{5,4},{6,7},{7,6},{8,9},{9,8},{10,11... | collective-permute-start | bytes 165896 | tf_op jit(solution)/shard_map/ppermute | solution.py:167
  100.7 0.0 all-to-all-done.1
  100.7 1.4 %fusion.5 = f32[]{:T(128)} fusion(bf16[16,48,1280]{2,1,0:T(8,128)(2,1)} %all-to-all-done.1), kind=kLoop, calls=%fused_computation.24 | loop fusion | flops 95 | bytes 100 | tf_op jit(solution)/shard_map/reduce_sum | solution.py:210
  102.1 1.3 broadcast_in_dim.10
  103.3 10.0 %all-to-all-start.2 = ((f32[32,1,128]{2,1,0:T(1,128)}), f32[32,1,128]{2,1,0:T(1,128)S(1)}, u32[]{:S(2)}, u32[]{:S(2)}) async-start(f32[32,1,128]{2,1,0:T(1,128)} %broadcast_in_dim.10), calls=%async_computation.2 | async-start | bytes 32768 | tf_op jit(solution)/shard_map/all_to_all | solution.py:211
  113.3 1.7 %convert_reduce_fusion = f32[48,1152]{1,0:T(8,128)S(1)} fusion(bf16[16,48,1280]{2,1,0:T(8,128)(2,1)} %all-to-all-done.1), kind=kLoop, calls=%fused_computation | loop fusion | flops 1714176 | bytes 1990656 | tf_op jit(solution)/shard_map/reduce_sum | solution.py:212
  115.1 7.6 %collective-permute-start.6 = (f16[24,1152]{1,0:T(8,128)(2,1)S(1)}, f16[24,1152]{1,0:T(8,128)(2,1)S(1)}, u32[]{:S(2)}, u32[]{:S(2)}) collective-permute-start(f16[24,1152]{1,0:T(8,128)(2,1)S(1)} %fusion.4), channel_id=1, source_target_pairs={{0,256},{256,0},{1,257},{257,1},{2,258},{258,2},{3,259},{259,3},{4... | collective-permute-start | bytes 165896 | tf_op jit(solution)/shard_map/ppermute | solution.py:167
  122.7 0.0 collective-permute-done.11
  122.7 0.7 slice_add_fusion.2.sum_ref
  123.4 1.9 %shard_map.70 = f32[24,1152]{1,0:T(8,128)} custom-call(f32[1]{0:T(128)S(6)} %copy.15.heat_ref, f32[1]{0:T(128)S(6)} %copy.16.offset_ref, f32[24,1152]{1,0:T(8,128)} %row_ref.2, bf16[24,1152]{1,0:T(8,128)(2,1)} %get-tuple-element.15.low_ref.partner_ref, bf16[24,1152]{1,0:T(8,128)(2,1)} %get-tuple-element.17.partner_ref.low_ref, ...), custom_call_target="tpu_custom_call" | custom-call | tf_op jit(solution)/shard_map/pallas_call | solution.py:159
  125.2 3.5 %collective-permute-done.6 = f16[24,1152]{1,0:T(8,128)(2,1)S(1)} collective-permute-done((f16[24,1152]{1,0:T(8,128)(2,1)S(1)}, f16[24,1152]{1,0:T(8,128)(2,1)S(1)}, u32[]{:S(2)}, u32[]{:S(2)}) %collective-permute-start.6) | collective-permute-done | bytes 55328 | tf_op jit(solution)/shard_map/ppermute | solution.py:167
  128.7 0.0 all-to-all-done.2
  128.7 0.7 slice_add_fusion.1.sum_ref
  129.4 0.6 slice_reduce_fusion
  130.0 1.9 %shard_map.71 = f32[24,1152]{1,0:T(8,128)} custom-call(f32[1]{0:T(128)S(6)} %copy.15.heat_ref, f32[1]{0:T(128)S(6)} %copy.16.offset_ref, f32[24,1152]{1,0:T(8,128)} %row_ref.3, bf16[24,1152]{1,0:T(8,128)(2,1)} %get-tuple-element.17.partner_ref.low_ref, bf16[24,1152]{1,0:T(8,128)(2,1)} %get-tuple-element.15.low_ref.partner_ref, ...), custom_call_target="tpu_custom_call" | custom-call | tf_op jit(solution)/shard_map/pallas_call | solution.py:159
  (7 shorter events, 0.1 us)
Async XLA Ops:
  4.4 20.0 %collective-permute-start.5 = (bf16[24,1152]{1,0:T(8,128)(2,1)}, bf16[24,1152]{1,0:T(8,128)(2,1)S(1)}, u32[]{:S(2)}, u32[]{:S(2)}) collective-permute-start(bf16[24,1152]{1,0:T(8,128)(2,1)} %get-tuple-element.17.partner_ref.low_ref), channel_id=1, source_target_pairs={{0,256},{256,0},{1,257},{257,1},{2,258},{258,2},{3,259},{259,3},{4... | collective-permute-start | bytes 165896 | tf_op jit(solution)/shard_map/ppermute | solution.py:167
  13.5 19.4 %collective-permute-start = (bf16[24,1152]{1,0:T(8,128)(2,1)}, bf16[24,1152]{1,0:T(8,128)(2,1)S(1)}, u32[]{:S(2)}, u32[]{:S(2)}) collective-permute-start(bf16[24,1152]{1,0:T(8,128)(2,1)} %get-tuple-element.15.low_ref.partner_ref), channel_id=1, source_target_pairs={{0,1},{1,0},{2,3},{3,2},{4,5},{5,4},{6,7},{7,6},{8,9},{9,8},{10,11... | collective-permute-start | bytes 165896 | tf_op jit(solution)/shard_map/ppermute | solution.py:167
  25.4 7.4 %copy-start.1 = (bf16[24,1152]{1,0:T(8,128)(2,1)S(1)}, bf16[24,1152]{1,0:T(8,128)(2,1)}, u32[]{:S(2)}) copy-start(bf16[24,1152]{1,0:T(8,128)(2,1)} %get-tuple-element.15.low_ref.partner_ref) | copy-start | bytes 165892
  25.4 29.7 %copy-start = (f32[24,1]{1,0:T(8,128)S(1)}, f32[24,1]{1,0:T(8,128)}, u32[]{:S(2)}) copy-start(f32[24,1]{1,0:T(8,128)} %get-tuple-element.14.own_loss_ref) | copy-start | bytes 292
  25.4 29.7 %all-to-all-start = ((bf16[16,48,1152]{2,1,0:T(8,128)(2,1)}), bf16[16,48,1152]{2,1,0:T(8,128)(2,1)S(1)}, u32[]{:S(2)}, u32[]{:S(2)}) async-start(bf16[16,48,1152]{2,1,0:T(8,128)(2,1)} %broadcast_dynamic-update-slice_fusion), calls=%async_computation | async-start | bytes 3538944 | tf_op jit(solution)/shard_map/all_to_all | solution.py:196
  32.9 9.2 %collective-permute-start.1 = (bf16[48,1152]{1,0:T(8,128)(2,1)S(1)}, bf16[48,1152]{1,0:T(8,128)(2,1)S(1)}, u32[]{:S(2)}, u32[]{:S(2)}) collective-permute-start(bf16[48,1152]{1,0:T(8,128)(2,1)S(1)} %get-tuple-element.28), channel_id=1, source_target_pairs={{0,64},{64,0},{128,192},{192,128},{1,65},{65,1},{129,193},{193,129... | collective-permute-start | bytes 331784 | tf_op jit(solution)/shard_map/ppermute | solution.py:167
  35.8 13.6 %collective-permute-start.3 = (bf16[48,1152]{1,0:T(8,128)(2,1)S(1)}, bf16[48,1152]{1,0:T(8,128)(2,1)S(1)}, u32[]{:S(2)}, u32[]{:S(2)}) collective-permute-start(bf16[48,1152]{1,0:T(8,128)(2,1)S(1)} %get-tuple-element.28), channel_id=1, source_target_pairs={{0,192},{64,128},{128,64},{192,0},{1,193},{65,129},{129,65},{193,1... | collective-permute-start | bytes 331784 | tf_op jit(solution)/shard_map/ppermute | solution.py:167
  39.7 9.7 %collective-permute-start.2 = (bf16[48,1152]{1,0:T(8,128)(2,1)S(1)}, bf16[48,1152]{1,0:T(8,128)(2,1)S(1)}, u32[]{:S(2)}, u32[]{:S(2)}) collective-permute-start(bf16[48,1152]{1,0:T(8,128)(2,1)S(1)} %get-tuple-element.28), channel_id=1, source_target_pairs={{0,128},{64,192},{128,0},{192,64},{1,129},{65,193},{129,1},{193,65... | collective-permute-start | bytes 331784 | tf_op jit(solution)/shard_map/ppermute | solution.py:167
  49.4 3.7 %collective-permute-start.4 = (bf16[192,1152]{1,0:T(8,128)(2,1)S(1)}, bf16[192,1152]{1,0:T(8,128)(2,1)S(1)}, u32[]{:S(2)}, u32[]{:S(2)}) collective-permute-start(bf16[192,1152]{1,0:T(8,128)(2,1)S(1)} %constant_dynamic-update-slice_fusion.2.near_ref), channel_id=1, source_target_pairs={{0,8},{8,0},{1,9},{9,1},{2,10},{10,2},{3,11},{11,3},{4,12},{12,4},... | collective-permute-start | bytes 1327112 | tf_op jit(solution)/shard_map/ppermute | solution.py:167
  58.3 12.2 %collective-permute-start.7 = (f32[192,1152]{1,0:T(8,128)}, f32[192,1152]{1,0:T(8,128)}, u32[]{:S(2)}, u32[]{:S(2)}) collective-permute-start(f32[192,1152]{1,0:T(8,128)} %get-tuple-element.23), channel_id=1, source_target_pairs={{0,8},{8,0},{1,9},{9,1},{2,10},{10,2},{3,11},{11,3},{4,12},{12,4},... | collective-permute-start | bytes 2654216 | tf_op jit(solution)/shard_map/ppermute | solution.py:167
  63.0 37.7 %all-to-all-start.1 = ((bf16[16,48,1280]{2,1,0:T(8,128)(2,1)}), bf16[16,48,1280]{2,1,0:T(8,128)(2,1)}, u32[]{:S(2)}, u32[]{:S(2)}) async-start(bf16[16,48,1280]{2,1,0:T(8,128)(2,1)} %bitcast.2), calls=%async_computation.1 | async-start | bytes 3932160 | tf_op jit(solution)/shard_map/all_to_all | solution.py:206
  71.8 9.2 %collective-permute-start.8 = (f16[48,1152]{1,0:T(8,128)(2,1)S(1)}, f16[48,1152]{1,0:T(8,128)(2,1)S(1)}, u32[]{:S(2)}, u32[]{:S(2)}) collective-permute-start(f16[48,1152]{1,0:T(8,128)(2,1)S(1)} %get-tuple-element.25), channel_id=1, source_target_pairs={{0,64},{64,0},{128,192},{192,128},{1,65},{65,1},{129,193},{193,129... | collective-permute-start | bytes 331784 | tf_op jit(solution)/shard_map/ppermute | solution.py:167
  74.7 8.9 %collective-permute-start.10 = (f16[48,1152]{1,0:T(8,128)(2,1)S(1)}, f16[48,1152]{1,0:T(8,128)(2,1)S(1)}, u32[]{:S(2)}, u32[]{:S(2)}) collective-permute-start(f16[48,1152]{1,0:T(8,128)(2,1)S(1)} %get-tuple-element.26), channel_id=1, source_target_pairs={{0,192},{64,128},{128,64},{192,0},{1,193},{65,129},{129,65},{193,1... | collective-permute-start | bytes 331784 | tf_op jit(solution)/shard_map/ppermute | solution.py:167
  78.6 10.5 %collective-permute-start.9 = (f16[48,1152]{1,0:T(8,128)(2,1)S(1)}, f16[48,1152]{1,0:T(8,128)(2,1)S(1)}, u32[]{:S(2)}, u32[]{:S(2)}) collective-permute-start(f16[48,1152]{1,0:T(8,128)(2,1)S(1)} %get-tuple-element.27), channel_id=1, source_target_pairs={{0,128},{64,192},{128,0},{192,64},{1,129},{65,193},{129,1},{193,65... | collective-permute-start | bytes 331784 | tf_op jit(solution)/shard_map/ppermute | solution.py:167
  89.2 33.5 %collective-permute-start.11 = (f16[24,1152]{1,0:T(8,128)(2,1)S(1)}, f16[24,1152]{1,0:T(8,128)(2,1)S(1)}, u32[]{:S(2)}, u32[]{:S(2)}) collective-permute-start(f16[24,1152]{1,0:T(8,128)(2,1)S(1)} %fusion.3), channel_id=1, source_target_pairs={{0,1},{1,0},{2,3},{3,2},{4,5},{5,4},{6,7},{7,6},{8,9},{9,8},{10,11... | collective-permute-start | bytes 165896 | tf_op jit(solution)/shard_map/ppermute | solution.py:167
  103.3 25.4 %all-to-all-start.2 = ((f32[32,1,128]{2,1,0:T(1,128)}), f32[32,1,128]{2,1,0:T(1,128)S(1)}, u32[]{:S(2)}, u32[]{:S(2)}) async-start(f32[32,1,128]{2,1,0:T(1,128)} %broadcast_in_dim.10), calls=%async_computation.2 | async-start | bytes 32768 | tf_op jit(solution)/shard_map/all_to_all | solution.py:211
  115.1 13.7 %collective-permute-start.6 = (f16[24,1152]{1,0:T(8,128)(2,1)S(1)}, f16[24,1152]{1,0:T(8,128)(2,1)S(1)}, u32[]{:S(2)}, u32[]{:S(2)}) collective-permute-start(f16[24,1152]{1,0:T(8,128)(2,1)S(1)} %fusion.4), channel_id=1, source_target_pairs={{0,256},{256,0},{1,257},{257,1},{2,258},{258,2},{3,259},{259,3},{4... | collective-permute-start | bytes 165896 | tf_op jit(solution)/shard_map/ppermute | solution.py:167

commit v12 on v10

--- a/solution.py
+++ b/solution.py
@@ -205,11 +205,11 @@
 
     plane_loss = jnp.sum(text_parts[:, 0, width : width + 3].astype(jnp.float32))
     losses = lax.all_to_all(jnp.broadcast_to(plane_loss, (column, 1, LANES)), COLUMN, 0, 0)
-    loss_mean = (jnp.sum(losses[:, 0, 0]) / (rows * lax.axis_size(AXES))).reshape(1)
     text_sum = jnp.sum(text_parts[:, :, :width].astype(jnp.float32), axis=0)
     arrived = swapped((text_sum[rows:] * HALF).astype(jnp.float16), "zm", 1)
-    arrived, loss_mean = lax.optimization_barrier((arrived, loss_mean))
+    arrived, losses = lax.optimization_barrier((arrived, losses))
     text_sum = text_sum[:rows] + arrived.astype(jnp.float32) * (1 / HALF)
+    loss_mean = (jnp.sum(losses[:, 0, 0]) / (rows * lax.axis_size(AXES))).reshape(1)
     image_grads = gradients(heat_exponent, offset_added, picture_vectors, image_low, text_low, image_sum)
     text_grads = gradients(heat_exponent, offset_added, caption_vectors, text_low, image_low, text_sum)
     return (loss_mean, image_grads, text_grads)

time: 134 us -> 132 us (0.985)
    all_to_all x1, waiting for transfers between devices: 0.01 us -> 3.71 us  [shards(): lax.all_to_all(text_part.reshape(plane, 2 * rows, width + LANES), PLANE,...]
    all_to_all x1, waiting for transfers between devices: 4.11 us -> 1.48 us  [shards(): lax.all_to_all(jnp.broadcast_to(plane_loss, (column, 1, LANES)), COLUMN,...]
    ppermute x10, waiting for transfers between devices: 24.4 us -> 22.4 us  [swapped(): lax.ppermute(value, axis, [(i, i ^ step) for i in range(lax.axis_size(axi...]
  transfers between devices with their start and end apart: 13 -> 13, of which waited for: 7 -> 7; matrix products, arithmetic and copies ran while one was open for 2% -> 3% of each run, Pallas kernels for 4% -> 4%
where the time goes in v12:
time: 132 us
  starting transfers between devices  83.5 us (63%)
  waiting for transfers between devices  27.6 us (21%)
  Pallas kernels  11.2 us (8%)
  between operations  3.92 us (3%)
  other arithmetic  3.12 us (2%)
  local copies, waits for them, and re-layouts  2.31 us (2%)
    ppermute x10, starting transfers between devices, swapped(): lax.ppermute(value, axis, [(i, i ^ step) for i in range(lax.axis_size(axi...  60.3 us
    ppermute x10, waiting for transfers between devices, swapped(): lax.ppermute(value, axis, [(i, i ^ step) for i in range(lax.axis_size(axi...  22.4 us
    all_to_all x1, starting transfers between devices, shards(): lax.all_to_all(jnp.broadcast_to(plane_loss, (column, 1, LANES)), COLUMN,...  12.6 us
    all_to_all x1, starting transfers between devices, shards(): lax.all_to_all(lax.dynamic_update_slice(copies, other_low, (0, rows, 0)),...  6.89 us
    pallas_call x2, Pallas kernels, gradients(): pl.pallas_call(grad_kernel, in_specs=[pl.BlockSpec(memory_space=pltpu.SME...  3.75 us
    all_to_all x1, starting transfers between devices, shards(): lax.all_to_all(text_part.reshape(plane, 2 * rows, width + LANES), PLANE,...  3.73 us
    all_to_all x1, waiting for transfers between devices, shards(): lax.all_to_all(text_part.reshape(plane, 2 * rows, width + LANES), PLANE,...  3.71 us
    pallas_call x1, Pallas kernels, pair_terms(): pl.pallas_call(terms_kernel, in_specs=[pl.BlockSpec(memory_space=pltpu.VM...  2.85 us
  transfers between devices with their start and end apart: 13, of which 7 were waited for; matrix products, arithmetic and copies ran while one was open for 3% of the time, Pallas kernels for 4%

profile of v12, /device:TPU:1, one launch (start us, length us, event | category | flops | bytes accessed | tf_op | source)
XLA Modules:
  0.0 131.6 jit_solution(7621327910663832365)
XLA Ops:
  1.9 2.4 %shard_map.67 = (bf16[24,1152]{1,0:T(8,128)(2,1)}, bf16[24,1152]{1,0:T(8,128)(2,1)}, bf16[16,48,1152]{2,1,0:T(8,128)(2,1)}, f32[24,1]{1,0:T(8,128)}) custom-call(f32[1]{0:T(128)S(6)} %copy.13.heat_ref, f32[1]{0:T(128)S(6)} %copy.14.offset_ref, f32[24,1152]{1,0:T(8,128)} %row_ref.2, f32[24,1152]{1,0:T(8,128)} %row_ref.3), custom_call_target="tpu_custom_call" | custom-call | tf_op jit(solution)/shard_map/pallas_call | solution.py:56
  4.3 9.6 %collective-permute-start.4 = (bf16[24,1152]{1,0:T(8,128)(2,1)}, bf16[24,1152]{1,0:T(8,128)(2,1)S(1)}, u32[]{:S(2)}, u32[]{:S(2)}) collective-permute-start(bf16[24,1152]{1,0:T(8,128)(2,1)} %get-tuple-element.17.partner_ref.low_ref), channel_id=1, source_target_pairs={{0,256},{256,0},{1,257},{257,1},{2,258},{258,2},{3,259},{259,3},{4... | collective-permute-start | bytes 165896 | tf_op jit(solution)/shard_map/ppermute | solution.py:167
  14.0 10.6 %collective-permute-start = (bf16[24,1152]{1,0:T(8,128)(2,1)}, bf16[24,1152]{1,0:T(8,128)(2,1)S(1)}, u32[]{:S(2)}, u32[]{:S(2)}) collective-permute-start(bf16[24,1152]{1,0:T(8,128)(2,1)} %get-tuple-element.15.low_ref.partner_ref), channel_id=1, source_target_pairs={{0,1},{1,0},{2,3},{3,2},{4,5},{5,4},{6,7},{7,6},{8,9},{9,8},{10,11... | collective-permute-start | bytes 165896 | tf_op jit(solution)/shard_map/ppermute | solution.py:167
  24.6 0.0 collective-permute-done.4
  24.6 1.0 broadcast_dynamic-update-slice_fusion
  25.6 0.0 copy-start.1
  25.6 0.0 copy-start
  25.6 6.9 %all-to-all-start = ((bf16[16,48,1152]{2,1,0:T(8,128)(2,1)}), bf16[16,48,1152]{2,1,0:T(8,128)(2,1)S(1)}, u32[]{:S(2)}, u32[]{:S(2)}) async-start(bf16[16,48,1152]{2,1,0:T(8,128)(2,1)} %broadcast_dynamic-update-slice_fusion), calls=%async_computation | async-start | bytes 3538944 | tf_op jit(solution)/shard_map/all_to_all | solution.py:189
  32.5 0.0 copy-done.1
  32.6 0.0 collective-permute-done
  32.6 3.1 %collective-permute-start.1 = (bf16[48,1152]{1,0:T(8,128)(2,1)S(1)}, bf16[48,1152]{1,0:T(8,128)(2,1)S(1)}, u32[]{:S(2)}, u32[]{:S(2)}) collective-permute-start(bf16[48,1152]{1,0:T(8,128)(2,1)S(1)} %pad_maximum_fusion.1), channel_id=1, source_target_pairs={{0,128},{64,192},{128,0},{192,64},{1,129},{65,193},{129,1},{193,65... | collective-permute-start | bytes 331784 | tf_op jit(solution)/shard_map/ppermute | solution.py:167
  35.7 6.3 %collective-permute-done.1 = bf16[48,1152]{1,0:T(8,128)(2,1)S(1)} collective-permute-done((bf16[48,1152]{1,0:T(8,128)(2,1)S(1)}, bf16[48,1152]{1,0:T(8,128)(2,1)S(1)}, u32[]{:S(2)}, u32[]{:S(2)}) %collective-permute-start.1) | collective-permute-done | bytes 110624 | tf_op jit(solution)/shard_map/ppermute | solution.py:167
  42.0 1.9 %collective-permute-start.2 = (bf16[96,1152]{1,0:T(8,128)(2,1)S(1)}, bf16[96,1152]{1,0:T(8,128)(2,1)S(1)}, u32[]{:S(2)}, u32[]{:S(2)}) collective-permute-start(bf16[96,1152]{1,0:T(8,128)(2,1)S(1)} %pad_maximum_fusion), channel_id=1, source_target_pairs={{0,64},{64,0},{128,192},{192,128},{1,65},{65,1},{129,193},{193,129... | collective-permute-start | bytes 663560 | tf_op jit(solution)/shard_map/ppermute | solution.py:167
  43.9 5.6 %collective-permute-done.2 = bf16[96,1152]{1,0:T(8,128)(2,1)S(1)} collective-permute-done((bf16[96,1152]{1,0:T(8,128)(2,1)S(1)}, bf16[96,1152]{1,0:T(8,128)(2,1)S(1)}, u32[]{:S(2)}, u32[]{:S(2)}) %collective-permute-start.2) | collective-permute-done | bytes 221216 | tf_op jit(solution)/shard_map/ppermute | solution.py:167
  49.6 4.1 %collective-permute-start.3 = (bf16[192,1152]{1,0:T(8,128)(2,1)S(1)}, bf16[192,1152]{1,0:T(8,128)(2,1)S(1)}, u32[]{:S(2)}, u32[]{:S(2)}) collective-permute-start(bf16[192,1152]{1,0:T(8,128)(2,1)S(1)} %constant_dynamic-update-slice_fusion.near_ref), channel_id=1, source_target_pairs={{0,8},{8,0},{1,9},{9,1},{2,10},{10,2},{3,11},{11,3},{4,12},{12,4},... | collective-permute-start | bytes 1327112 | tf_op jit(solution)/shard_map/ppermute | solution.py:167
  53.7 1.4 %collective-permute-done.3.far_ref = bf16[192,1152]{1,0:T(8,128)(2,1)S(1)} collective-permute-done((bf16[192,1152]{1,0:T(8,128)(2,1)S(1)}, bf16[192,1152]{1,0:T(8,128)(2,1)S(1)}, u32[]{:S(2)}, u32[]{:S(2)}) %collective-permute-start.3) | collective-permute-done | bytes 442400 | tf_op jit(solution)/shard_map/ppermute | solution.py:167
  55.1 0.0 all-to-all-done
  55.1 0.0 copy-done
  55.1 2.2 %shard_map.68 = (bf16[2,192,768]{2,1,0:T(8,128)(2,1)S(1)}, f32[192,1152]{1,0:T(8,128)S(1)}, f32[8,128]{1,0:T(8,128)S(1)}) custom-call(s32[1]{0:T(128)} %bitcast.place_ref, f32[1]{0:T(128)S(6)} %copy.13.heat_ref, f32[1]{0:T(128)S(6)} %copy.14.offset_ref, f32[24,1]{1,0:T(8,128)S(1)} %copy-done, ...), custom_call_target="tpu_custom_call" | custom-call | flops 1019215872 | bytes 1769472 | tf_op jit(solution)/shard_map/pallas_call | solution.py:107
  57.3 6.3 %collective-permute-start.6 = (f32[192,1152]{1,0:T(8,128)S(1)}, f32[192,1152]{1,0:T(8,128)S(1)}, u32[]{:S(2)}, u32[]{:S(2)}) collective-permute-start(f32[192,1152]{1,0:T(8,128)S(1)} %get-tuple-element.23), channel_id=1, source_target_pairs={{0,8},{8,0},{1,9},{9,1},{2,10},{10,2},{3,11},{11,3},{4,12},{12,4},... | collective-permute-start | bytes 2654216 | tf_op jit(solution)/shard_map/ppermute | solution.py:167
  63.6 2.8 %shard_map.69 = (f32[192,1152]{1,0:T(8,128)S(1)}, bf16[768,1280]{1,0:T(8,128)(2,1)}) custom-call(bf16[2,192,768]{2,1,0:T(8,128)(2,1)S(1)} %get-tuple-element.18.weight_ref, f32[8,128]{1,0:T(8,128)S(1)} %get-tuple-element.19.loss_ref, bf16[192,1152]{1,0:T(8,128)(2,1)S(1)} %constant_dynamic-update-slice_fusion.near_ref, ...), custom_call_target="tpu_custom_call" | custom-call | flops 1019215872 | bytes 3538944 | tf_op jit(solution)/shard_map/pallas_call | solution.py:137
  66.5 0.0 collective-permute-done.6
  66.5 0.1 add.19
  66.6 2.6 %collective-permute-start.7 = (f16[96,1152]{1,0:T(8,128)(2,1)S(1)}, f16[96,1152]{1,0:T(8,128)(2,1)S(1)}, u32[]{:S(2)}, u32[]{:S(2)}) collective-permute-start(f16[96,1152]{1,0:T(8,128)(2,1)S(1)} %fusion), channel_id=1, source_target_pairs={{0,64},{64,0},{128,192},{192,128},{1,65},{65,1},{129,193},{193,129... | collective-permute-start | bytes 663560 | tf_op jit(solution)/shard_map/ppermute | solution.py:167
  69.3 3.7 %all-to-all-start.1 = ((bf16[16,48,1280]{2,1,0:T(8,128)(2,1)}), bf16[16,48,1280]{2,1,0:T(8,128)(2,1)S(1)}, u32[]{:S(2)}, u32[]{:S(2)}) async-start(bf16[16,48,1280]{2,1,0:T(8,128)(2,1)} %bitcast.2), calls=%async_computation.1 | async-start | bytes 3932160 | tf_op jit(solution)/shard_map/all_to_all | solution.py:200
  73.0 2.6 %collective-permute-done.7 = f16[96,1152]{1,0:T(8,128)(2,1)S(1)} collective-permute-done((f16[96,1152]{1,0:T(8,128)(2,1)S(1)}, f16[96,1152]{1,0:T(8,128)(2,1)S(1)}, u32[]{:S(2)}, u32[]{:S(2)}) %collective-permute-start.7) | collective-permute-done | bytes 221216 | tf_op jit(solution)/shard_map/ppermute | solution.py:167
  75.6 0.1 slice_add_fusion
  75.7 3.1 %collective-permute-start.8 = (f16[48,1152]{1,0:T(8,128)(2,1)S(1)}, f16[48,1152]{1,0:T(8,128)(2,1)S(1)}, u32[]{:S(2)}, u32[]{:S(2)}) collective-permute-start(f16[48,1152]{1,0:T(8,128)(2,1)S(1)} %fusion.1), channel_id=1, source_target_pairs={{0,128},{64,192},{128,0},{192,64},{1,129},{65,193},{129,1},{193,65... | collective-permute-start | bytes 331784 | tf_op jit(solution)/shard_map/ppermute | solution.py:167
  78.8 6.6 %collective-permute-done.8 = f16[48,1152]{1,0:T(8,128)(2,1)S(1)} collective-permute-done((f16[48,1152]{1,0:T(8,128)(2,1)S(1)}, f16[48,1152]{1,0:T(8,128)(2,1)S(1)}, u32[]{:S(2)}, u32[]{:S(2)}) %collective-permute-start.8) | collective-permute-done | bytes 110624 | tf_op jit(solution)/shard_map/ppermute | solution.py:167
  85.4 11.6 %collective-permute-start.9 = (f16[24,1152]{1,0:T(8,128)(2,1)S(1)}, f16[24,1152]{1,0:T(8,128)(2,1)S(1)}, u32[]{:S(2)}, u32[]{:S(2)}) collective-permute-start(f16[24,1152]{1,0:T(8,128)(2,1)S(1)} %fusion.2), channel_id=1, source_target_pairs={{0,1},{1,0},{2,3},{3,2},{4,5},{5,4},{6,7},{7,6},{8,9},{9,8},{10,11... | collective-permute-start | bytes 165896 | tf_op jit(solution)/shard_map/ppermute | solution.py:167
  97.0 3.7 %all-to-all-done.1 = bf16[16,48,1280]{2,1,0:T(8,128)(2,1)S(1)} async-done(((bf16[16,48,1280]{2,1,0:T(8,128)(2,1)}), bf16[16,48,1280]{2,1,0:T(8,128)(2,1)S(1)}, u32[]{:S(2)}, u32[]{:S(2)}) %all-to-all-start.1) | async-done | bytes 1966112 | tf_op jit(solution)/shard_map/all_to_all | solution.py:200
  100.7 0.6 fusion.4
  101.4 1.2 broadcast_in_dim.10
  102.6 12.6 %all-to-all-start.2 = ((f32[32,1,128]{2,1,0:T(1,128)}), f32[32,1,128]{2,1,0:T(1,128)S(1)}, u32[]{:S(2)}, u32[]{:S(2)}) async-start(f32[32,1,128]{2,1,0:T(1,128)} %broadcast_in_dim.10), calls=%async_computation.2 | async-start | bytes 32768 | tf_op jit(solution)/shard_map/all_to_all | solution.py:207
  115.2 0.3 convert_reduce_fusion
  115.5 7.2 %collective-permute-start.5 = (f16[24,1152]{1,0:T(8,128)(2,1)S(1)}, f16[24,1152]{1,0:T(8,128)(2,1)S(1)}, u32[]{:S(2)}, u32[]{:S(2)}) collective-permute-start(f16[24,1152]{1,0:T(8,128)(2,1)S(1)} %fusion.3), channel_id=1, source_target_pairs={{0,256},{256,0},{1,257},{257,1},{2,258},{258,2},{3,259},{259,3},{4... | collective-permute-start | bytes 165896 | tf_op jit(solution)/shard_map/ppermute | solution.py:167
  122.7 0.0 collective-permute-done.9
  122.7 0.7 slice_add_fusion.3.sum_ref
  123.3 1.9 %shard_map.70 = f32[24,1152]{1,0:T(8,128)} custom-call(f32[1]{0:T(128)S(6)} %copy.13.heat_ref, f32[1]{0:T(128)S(6)} %copy.14.offset_ref, f32[24,1152]{1,0:T(8,128)} %row_ref.2, bf16[24,1152]{1,0:T(8,128)(2,1)} %get-tuple-element.15.low_ref.partner_ref, bf16[24,1152]{1,0:T(8,128)(2,1)} %get-tuple-element.17.partner_ref.low_ref, ...), custom_call_target="tpu_custom_call" | custom-call | tf_op jit(solution)/shard_map/pallas_call | solution.py:159
  125.2 0.0 collective-permute-done.5
  125.2 1.5 %all-to-all-done.2 = f32[32,1,128]{2,1,0:T(1,128)S(1)} async-done(((f32[32,1,128]{2,1,0:T(1,128)}), f32[32,1,128]{2,1,0:T(1,128)S(1)}, u32[]{:S(2)}, u32[]{:S(2)}) %all-to-all-start.2) | async-done | bytes 16416 | tf_op jit(solution)/shard_map/all_to_all | solution.py:207
  126.7 0.6 slice_add_fusion.2.sum_ref
  127.4 0.6 slice_reduce_fusion
  128.0 1.9 %shard_map.71 = f32[24,1152]{1,0:T(8,128)} custom-call(f32[1]{0:T(128)S(6)} %copy.13.heat_ref, f32[1]{0:T(128)S(6)} %copy.14.offset_ref, f32[24,1152]{1,0:T(8,128)} %row_ref.3, bf16[24,1152]{1,0:T(8,128)(2,1)} %get-tuple-element.17.partner_ref.low_ref, bf16[24,1152]{1,0:T(8,128)(2,1)} %get-tuple-element.15.low_ref.partner_ref, ...), custom_call_target="tpu_custom_call" | custom-call | tf_op jit(solution)/shard_map/pallas_call | solution.py:159
  (11 shorter events, 0.2 us)
Async XLA Ops:
  4.3 20.3 %collective-permute-start.4 = (bf16[24,1152]{1,0:T(8,128)(2,1)}, bf16[24,1152]{1,0:T(8,128)(2,1)S(1)}, u32[]{:S(2)}, u32[]{:S(2)}) collective-permute-start(bf16[24,1152]{1,0:T(8,128)(2,1)} %get-tuple-element.17.partner_ref.low_ref), channel_id=1, source_target_pairs={{0,256},{256,0},{1,257},{257,1},{2,258},{258,2},{3,259},{259,3},{4... | collective-permute-start | bytes 165896 | tf_op jit(solution)/shard_map/ppermute | solution.py:167
  14.0 18.6 %collective-permute-start = (bf16[24,1152]{1,0:T(8,128)(2,1)}, bf16[24,1152]{1,0:T(8,128)(2,1)S(1)}, u32[]{:S(2)}, u32[]{:S(2)}) collective-permute-start(bf16[24,1152]{1,0:T(8,128)(2,1)} %get-tuple-element.15.low_ref.partner_ref), channel_id=1, source_target_pairs={{0,1},{1,0},{2,3},{3,2},{4,5},{5,4},{6,7},{7,6},{8,9},{9,8},{10,11... | collective-permute-start | bytes 165896 | tf_op jit(solution)/shard_map/ppermute | solution.py:167
  25.6 6.9 %copy-start.1 = (bf16[24,1152]{1,0:T(8,128)(2,1)S(1)}, bf16[24,1152]{1,0:T(8,128)(2,1)}, u32[]{:S(2)}) copy-start(bf16[24,1152]{1,0:T(8,128)(2,1)} %get-tuple-element.15.low_ref.partner_ref) | copy-start | bytes 165892
  25.6 29.4 %copy-start = (f32[24,1]{1,0:T(8,128)S(1)}, f32[24,1]{1,0:T(8,128)}, u32[]{:S(2)}) copy-start(f32[24,1]{1,0:T(8,128)} %get-tuple-element.14.own_loss_ref) | copy-start | bytes 292
  25.6 29.4 %all-to-all-start = ((bf16[16,48,1152]{2,1,0:T(8,128)(2,1)}), bf16[16,48,1152]{2,1,0:T(8,128)(2,1)S(1)}, u32[]{:S(2)}, u32[]{:S(2)}) async-start(bf16[16,48,1152]{2,1,0:T(8,128)(2,1)} %broadcast_dynamic-update-slice_fusion), calls=%async_computation | async-start | bytes 3538944 | tf_op jit(solution)/shard_map/all_to_all | solution.py:189
  32.6 9.4 %collective-permute-start.1 = (bf16[48,1152]{1,0:T(8,128)(2,1)S(1)}, bf16[48,1152]{1,0:T(8,128)(2,1)S(1)}, u32[]{:S(2)}, u32[]{:S(2)}) collective-permute-start(bf16[48,1152]{1,0:T(8,128)(2,1)S(1)} %pad_maximum_fusion.1), channel_id=1, source_target_pairs={{0,128},{64,192},{128,0},{192,64},{1,129},{65,193},{129,1},{193,65... | collective-permute-start | bytes 331784 | tf_op jit(solution)/shard_map/ppermute | solution.py:167
  42.0 7.6 %collective-permute-start.2 = (bf16[96,1152]{1,0:T(8,128)(2,1)S(1)}, bf16[96,1152]{1,0:T(8,128)(2,1)S(1)}, u32[]{:S(2)}, u32[]{:S(2)}) collective-permute-start(bf16[96,1152]{1,0:T(8,128)(2,1)S(1)} %pad_maximum_fusion), channel_id=1, source_target_pairs={{0,64},{64,0},{128,192},{192,128},{1,65},{65,1},{129,193},{193,129... | collective-permute-start | bytes 663560 | tf_op jit(solution)/shard_map/ppermute | solution.py:167
  49.6 5.5 %collective-permute-start.3 = (bf16[192,1152]{1,0:T(8,128)(2,1)S(1)}, bf16[192,1152]{1,0:T(8,128)(2,1)S(1)}, u32[]{:S(2)}, u32[]{:S(2)}) collective-permute-start(bf16[192,1152]{1,0:T(8,128)(2,1)S(1)} %constant_dynamic-update-slice_fusion.near_ref), channel_id=1, source_target_pairs={{0,8},{8,0},{1,9},{9,1},{2,10},{10,2},{3,11},{11,3},{4,12},{12,4},... | collective-permute-start | bytes 1327112 | tf_op jit(solution)/shard_map/ppermute | solution.py:167
  57.3 9.2 %collective-permute-start.6 = (f32[192,1152]{1,0:T(8,128)S(1)}, f32[192,1152]{1,0:T(8,128)S(1)}, u32[]{:S(2)}, u32[]{:S(2)}) collective-permute-start(f32[192,1152]{1,0:T(8,128)S(1)} %get-tuple-element.23), channel_id=1, source_target_pairs={{0,8},{8,0},{1,9},{9,1},{2,10},{10,2},{3,11},{11,3},{4,12},{12,4},... | collective-permute-start | bytes 2654216 | tf_op jit(solution)/shard_map/ppermute | solution.py:167
  66.6 8.9 %collective-permute-start.7 = (f16[96,1152]{1,0:T(8,128)(2,1)S(1)}, f16[96,1152]{1,0:T(8,128)(2,1)S(1)}, u32[]{:S(2)}, u32[]{:S(2)}) collective-permute-start(f16[96,1152]{1,0:T(8,128)(2,1)S(1)} %fusion), channel_id=1, source_target_pairs={{0,64},{64,0},{128,192},{192,128},{1,65},{65,1},{129,193},{193,129... | collective-permute-start | bytes 663560 | tf_op jit(solution)/shard_map/ppermute | solution.py:167
  69.3 31.5 %all-to-all-start.1 = ((bf16[16,48,1280]{2,1,0:T(8,128)(2,1)}), bf16[16,48,1280]{2,1,0:T(8,128)(2,1)S(1)}, u32[]{:S(2)}, u32[]{:S(2)}) async-start(bf16[16,48,1280]{2,1,0:T(8,128)(2,1)} %bitcast.2), calls=%async_computation.1 | async-start | bytes 3932160 | tf_op jit(solution)/shard_map/all_to_all | solution.py:200
  75.7 9.7 %collective-permute-start.8 = (f16[48,1152]{1,0:T(8,128)(2,1)S(1)}, f16[48,1152]{1,0:T(8,128)(2,1)S(1)}, u32[]{:S(2)}, u32[]{:S(2)}) collective-permute-start(f16[48,1152]{1,0:T(8,128)(2,1)S(1)} %fusion.1), channel_id=1, source_target_pairs={{0,128},{64,192},{128,0},{192,64},{1,129},{65,193},{129,1},{193,65... | collective-permute-start | bytes 331784 | tf_op jit(solution)/shard_map/ppermute | solution.py:167
  85.4 37.3 %collective-permute-start.9 = (f16[24,1152]{1,0:T(8,128)(2,1)S(1)}, f16[24,1152]{1,0:T(8,128)(2,1)S(1)}, u32[]{:S(2)}, u32[]{:S(2)}) collective-permute-start(f16[24,1152]{1,0:T(8,128)(2,1)S(1)} %fusion.2), channel_id=1, source_target_pairs={{0,1},{1,0},{2,3},{3,2},{4,5},{5,4},{6,7},{7,6},{8,9},{9,8},{10,11... | collective-permute-start | bytes 165896 | tf_op jit(solution)/shard_map/ppermute | solution.py:167
  102.6 24.1 %all-to-all-start.2 = ((f32[32,1,128]{2,1,0:T(1,128)}), f32[32,1,128]{2,1,0:T(1,128)S(1)}, u32[]{:S(2)}, u32[]{:S(2)}) async-start(f32[32,1,128]{2,1,0:T(1,128)} %broadcast_in_dim.10), calls=%async_computation.2 | async-start | bytes 32768 | tf_op jit(solution)/shard_map/all_to_all | solution.py:207
  115.5 9.8 %collective-permute-start.5 = (f16[24,1152]{1,0:T(8,128)(2,1)S(1)}, f16[24,1152]{1,0:T(8,128)(2,1)S(1)}, u32[]{:S(2)}, u32[]{:S(2)}) collective-permute-start(f16[24,1152]{1,0:T(8,128)(2,1)S(1)} %fusion.3), channel_id=1, source_target_pairs={{0,256},{256,0},{1,257},{257,1},{2,258},{258,2},{3,259},{259,3},{4... | collective-permute-start | bytes 165896 | tf_op jit(solution)/shard_map/ppermute | solution.py:167

commit v13 on v12

--- a/solution.py
+++ b/solution.py
@@ -185,12 +185,13 @@
         plane, heat_exponent, offset_added, picture_vectors, caption_vectors
     )
 
-    other_low = jnp.broadcast_to(swapped(text_low, "zm", 1)[None], (plane, rows, width))
+    other_low = swapped(text_low, "zm", 1)
+    other_low, near = lax.optimization_barrier((other_low, image_low))
+    other_low = jnp.broadcast_to(other_low[None], (plane, rows, width))
     texts = lax.all_to_all(lax.dynamic_update_slice(copies, other_low, (0, rows, 0)), PLANE, 0, 0)
     texts = texts.reshape(plane * 2 * rows, width)
-    near = doubled(image_low, "zh", 1)
-    for step in reversed(steps):
-        near = doubled(near, "zl", step)
+    near = doubled(near, "zh", 1)
+    near = jnp.concatenate([near] + [swapped(near, "zl", step) for step in (2, 1, 3)], axis=0)
     far = swapped(near, "c", 1)
 
     place = (lax.axis_index(PLANE) * 2 * rows).astype(jnp.int32).reshape(1)

time: 132 us -> 140 us (1.061)
  starting transfers between devices: 83.5 us -> 94.9 us
  waiting for transfers between devices: 27.6 us -> 23.5 us
    ppermute x10 -> x11, starting transfers between devices: 60.3 us -> 67.6 us  [swapped(): lax.ppermute(value, axis, [(i, i ^ step) for i in range(lax.axis_size(axi...]
    ppermute x10 -> x11, waiting for transfers between devices: 22.4 us -> 15.4 us  [swapped(): lax.ppermute(value, axis, [(i, i ^ step) for i in range(lax.axis_size(axi...]
    all_to_all x1, starting transfers between devices: 3.73 us -> 6.63 us  [shards(): lax.all_to_all(text_part.reshape(plane, 2 * rows, width + LANES), PLANE,...]
    all_to_all x1, waiting for transfers between devices: 3.71 us -> 6.46 us  [shards(): lax.all_to_all(text_part.reshape(plane, 2 * rows, width + LANES), PLANE,...]
  transfers between devices with their start and end apart: 13 -> 14, of which waited for: 7 -> 8; matrix products, arithmetic and copies ran while one was open for 3% -> 2% of each run, Pallas kernels for 4% -> 3%
where the time goes in v13:
time: 140 us; the launch traced here: 139 us
  starting transfers between devices  94.9 us (68%)
  waiting for transfers between devices  23.5 us (17%)
  Pallas kernels  11.3 us (8%)
  between operations  3.93 us (3%)
  other arithmetic  3.1 us (2%)
  local copies, waits for them, and re-layouts  2.34 us (2%)
    ppermute x11, starting transfers between devices, swapped(): lax.ppermute(value, axis, [(i, i ^ step) for i in range(lax.axis_size(axi...  67.6 us
    ppermute x11, waiting for transfers between devices, swapped(): lax.ppermute(value, axis, [(i, i ^ step) for i in range(lax.axis_size(axi...  15.4 us
    all_to_all x1, starting transfers between devices, shards(): lax.all_to_all(jnp.broadcast_to(plane_loss, (column, 1, LANES)), COLUMN,...  13.8 us
    all_to_all x1, starting transfers between devices, shards(): lax.all_to_all(lax.dynamic_update_slice(copies, other_low, (0, rows, 0)),...  6.89 us
    all_to_all x1, starting transfers between devices, shards(): lax.all_to_all(text_part.reshape(plane, 2 * rows, width + LANES), PLANE,...  6.63 us
    all_to_all x1, waiting for transfers between devices, shards(): lax.all_to_all(text_part.reshape(plane, 2 * rows, width + LANES), PLANE,...  6.46 us
    pallas_call x2, Pallas kernels, gradients(): pl.pallas_call(grad_kernel, in_specs=[pl.BlockSpec(memory_space=pltpu.SME...  3.75 us
    pallas_call x1, Pallas kernels, pair_terms(): pl.pallas_call(terms_kernel, in_specs=[pl.BlockSpec(memory_space=pltpu.VM...  2.87 us
  transfers between devices with their start and end apart: 14, of which 8 were waited for; matrix products, arithmetic and copies ran while one was open for 2% of the time, Pallas kernels for 3%

profile of v13, /device:TPU:1, one launch (start us, length us, event | category | flops | bytes accessed | tf_op | source)
XLA Modules:
  0.0 139.1 jit_solution(14528030526467519226)
XLA Ops:
  1.9 2.4 %shard_map.67 = (bf16[24,1152]{1,0:T(8,128)(2,1)}, bf16[24,1152]{1,0:T(8,128)(2,1)}, bf16[16,48,1152]{2,1,0:T(8,128)(2,1)}, f32[24,1]{1,0:T(8,128)}) custom-call(f32[1]{0:T(128)S(6)} %copy.15.heat_ref, f32[1]{0:T(128)S(6)} %copy.16.offset_ref, f32[24,1152]{1,0:T(8,128)} %row_ref.2, f32[24,1152]{1,0:T(8,128)} %row_ref.3), custom_call_target="tpu_custom_call" | custom-call | tf_op jit(solution)/shard_map/pallas_call | solution.py:56
  4.4 9.6 %collective-permute-start = (bf16[24,1152]{1,0:T(8,128)(2,1)}, bf16[24,1152]{1,0:T(8,128)(2,1)S(1)}, u32[]{:S(2)}, u32[]{:S(2)}) collective-permute-start(bf16[24,1152]{1,0:T(8,128)(2,1)} %get-tuple-element.17.partner_ref.low_ref), channel_id=1, source_target_pairs={{0,256},{256,0},{1,257},{257,1},{2,258},{258,2},{3,259},{259,3},{4... | collective-permute-start | bytes 165896 | tf_op jit(solution)/shard_map/ppermute | solution.py:167
  14.0 1.7 %collective-permute-done = bf16[24,1152]{1,0:T(8,128)(2,1)S(1)} collective-permute-done((bf16[24,1152]{1,0:T(8,128)(2,1)}, bf16[24,1152]{1,0:T(8,128)(2,1)S(1)}, u32[]{:S(2)}, u32[]{:S(2)}) %collective-permute-start) | collective-permute-done | bytes 55328 | tf_op jit(solution)/shard_map/ppermute | solution.py:167
  15.8 1.0 broadcast_dynamic-update-slice_fusion
  16.8 0.0 copy-start.1
  16.8 0.0 copy-start
  16.8 6.9 %all-to-all-start = ((bf16[16,48,1152]{2,1,0:T(8,128)(2,1)}), bf16[16,48,1152]{2,1,0:T(8,128)(2,1)S(1)}, u32[]{:S(2)}, u32[]{:S(2)}) async-start(bf16[16,48,1152]{2,1,0:T(8,128)(2,1)} %broadcast_dynamic-update-slice_fusion), calls=%async_computation | async-start | bytes 3538944 | tf_op jit(solution)/shard_map/all_to_all | solution.py:191
  23.7 0.0 copy-done.1
  23.7 17.8 %collective-permute-start.1 = (bf16[24,1152]{1,0:T(8,128)(2,1)S(1)}, bf16[24,1152]{1,0:T(8,128)(2,1)S(1)}, u32[]{:S(2)}, u32[]{:S(2)}) collective-permute-start(bf16[24,1152]{1,0:T(8,128)(2,1)S(1)} %copy-done.1), channel_id=1, source_target_pairs={{0,1},{1,0},{2,3},{3,2},{4,5},{5,4},{6,7},{7,6},{8,9},{9,8},{10,11... | collective-permute-start | bytes 165896 | tf_op jit(solution)/shard_map/ppermute | solution.py:167
  41.5 1.5 %collective-permute-done.1 = bf16[24,1152]{1,0:T(8,128)(2,1)S(1)} collective-permute-done((bf16[24,1152]{1,0:T(8,128)(2,1)S(1)}, bf16[24,1152]{1,0:T(8,128)(2,1)S(1)}, u32[]{:S(2)}, u32[]{:S(2)}) %collective-permute-start.1) | collective-permute-done | bytes 55328 | tf_op jit(solution)/shard_map/ppermute | solution.py:167
  43.0 1.9 %collective-permute-start.2 = (bf16[48,1152]{1,0:T(8,128)(2,1)S(1)}, bf16[48,1152]{1,0:T(8,128)(2,1)S(1)}, u32[]{:S(2)}, u32[]{:S(2)}) collective-permute-start(bf16[48,1152]{1,0:T(8,128)(2,1)S(1)} %get-tuple-element.29), channel_id=1, source_target_pairs={{0,128},{64,192},{128,0},{192,64},{1,129},{65,193},{129,1},{193,65... | collective-permute-start | bytes 331784 | tf_op jit(solution)/shard_map/ppermute | solution.py:167
  44.9 3.6 %collective-permute-start.4 = (bf16[48,1152]{1,0:T(8,128)(2,1)S(1)}, bf16[48,1152]{1,0:T(8,128)(2,1)S(1)}, u32[]{:S(2)}, u32[]{:S(2)}) collective-permute-start(bf16[48,1152]{1,0:T(8,128)(2,1)S(1)} %get-tuple-element.29), channel_id=1, source_target_pairs={{0,192},{64,128},{128,64},{192,0},{1,193},{65,129},{129,65},{193,1... | collective-permute-start | bytes 331784 | tf_op jit(solution)/shard_map/ppermute | solution.py:167
  48.5 2.9 %collective-permute-start.3 = (bf16[48,1152]{1,0:T(8,128)(2,1)S(1)}, bf16[48,1152]{1,0:T(8,128)(2,1)S(1)}, u32[]{:S(2)}, u32[]{:S(2)}) collective-permute-start(bf16[48,1152]{1,0:T(8,128)(2,1)S(1)} %get-tuple-element.29), channel_id=1, source_target_pairs={{0,64},{64,0},{128,192},{192,128},{1,65},{65,1},{129,193},{193,129... | collective-permute-start | bytes 331784 | tf_op jit(solution)/shard_map/ppermute | solution.py:167
  51.4 0.0 collective-permute-done.2
  51.4 4.4 %collective-permute-done.3 = bf16[48,1152]{1,0:T(8,128)(2,1)S(1)} collective-permute-done((bf16[48,1152]{1,0:T(8,128)(2,1)S(1)}, bf16[48,1152]{1,0:T(8,128)(2,1)S(1)}, u32[]{:S(2)}, u32[]{:S(2)}) %collective-permute-start.3) | collective-permute-done | bytes 110624 | tf_op jit(solution)/shard_map/ppermute | solution.py:167
  55.8 0.0 collective-permute-done.4
  55.8 5.6 %collective-permute-start.5 = (bf16[192,1152]{1,0:T(8,128)(2,1)S(1)}, bf16[192,1152]{1,0:T(8,128)(2,1)S(1)}, u32[]{:S(2)}, u32[]{:S(2)}) collective-permute-start(bf16[192,1152]{1,0:T(8,128)(2,1)S(1)} %constant_dynamic-update-slice_fusion.2.near_ref), channel_id=1, source_target_pairs={{0,8},{8,0},{1,9},{9,1},{2,10},{10,2},{3,11},{11,3},{4,12},{12,4},... | collective-permute-start | bytes 1327112 | tf_op jit(solution)/shard_map/ppermute | solution.py:167
  61.5 1.4 %collective-permute-done.5.far_ref = bf16[192,1152]{1,0:T(8,128)(2,1)S(1)} collective-permute-done((bf16[192,1152]{1,0:T(8,128)(2,1)S(1)}, bf16[192,1152]{1,0:T(8,128)(2,1)S(1)}, u32[]{:S(2)}, u32[]{:S(2)}) %collective-permute-start.5) | collective-permute-done | bytes 442400 | tf_op jit(solution)/shard_map/ppermute | solution.py:167
  62.9 0.0 all-to-all-done
  62.9 0.0 copy-done
  62.9 2.2 %shard_map.68 = (bf16[2,192,768]{2,1,0:T(8,128)(2,1)S(1)}, f32[192,1152]{1,0:T(8,128)S(1)}, f32[8,128]{1,0:T(8,128)S(1)}) custom-call(s32[1]{0:T(128)} %bitcast.place_ref, f32[1]{0:T(128)S(6)} %copy.15.heat_ref, f32[1]{0:T(128)S(6)} %copy.16.offset_ref, f32[24,1]{1,0:T(8,128)S(1)} %copy-done, ...), custom_call_target="tpu_custom_call" | custom-call | flops 1019215872 | bytes 1769472 | tf_op jit(solution)/shard_map/pallas_call | solution.py:107
  65.1 2.3 %collective-permute-start.7 = (f32[192,1152]{1,0:T(8,128)S(1)}, f32[192,1152]{1,0:T(8,128)S(1)}, u32[]{:S(2)}, u32[]{:S(2)}) collective-permute-start(f32[192,1152]{1,0:T(8,128)S(1)} %get-tuple-element.27), channel_id=1, source_target_pairs={{0,8},{8,0},{1,9},{9,1},{2,10},{10,2},{3,11},{11,3},{4,12},{12,4},... | collective-permute-start | bytes 2654216 | tf_op jit(solution)/shard_map/ppermute | solution.py:167
  67.4 2.9 %shard_map.69 = (f32[192,1152]{1,0:T(8,128)S(1)}, bf16[768,1280]{1,0:T(8,128)(2,1)}) custom-call(bf16[2,192,768]{2,1,0:T(8,128)(2,1)S(1)} %get-tuple-element.22.weight_ref, f32[8,128]{1,0:T(8,128)S(1)} %get-tuple-element.23.loss_ref, bf16[192,1152]{1,0:T(8,128)(2,1)S(1)} %constant_dynamic-update-slice_fusion.2.near_ref, ...), custom_call_target="tpu_custom_call" | custom-call | flops 1019215872 | bytes 3538944 | tf_op jit(solution)/shard_map/pallas_call | solution.py:137
  70.2 0.0 collective-permute-done.7
  70.2 0.1 add.19
  70.4 1.9 %collective-permute-start.8 = (f16[96,1152]{1,0:T(8,128)(2,1)S(1)}, f16[96,1152]{1,0:T(8,128)(2,1)S(1)}, u32[]{:S(2)}, u32[]{:S(2)}) collective-permute-start(f16[96,1152]{1,0:T(8,128)(2,1)S(1)} %fusion), channel_id=1, source_target_pairs={{0,64},{64,0},{128,192},{192,128},{1,65},{65,1},{129,193},{193,129... | collective-permute-start | bytes 663560 | tf_op jit(solution)/shard_map/ppermute | solution.py:167
  72.3 6.6 %all-to-all-start.1 = ((bf16[16,48,1280]{2,1,0:T(8,128)(2,1)}), bf16[16,48,1280]{2,1,0:T(8,128)(2,1)S(1)}, u32[]{:S(2)}, u32[]{:S(2)}) async-start(bf16[16,48,1280]{2,1,0:T(8,128)(2,1)} %bitcast.2), calls=%async_computation.1 | async-start | bytes 3932160 | tf_op jit(solution)/shard_map/all_to_all | solution.py:201
  79.0 0.2 collective-permute-done.8
  79.2 0.1 slice_add_fusion
  79.3 2.9 %collective-permute-start.9 = (f16[48,1152]{1,0:T(8,128)(2,1)S(1)}, f16[48,1152]{1,0:T(8,128)(2,1)S(1)}, u32[]{:S(2)}, u32[]{:S(2)}) collective-permute-start(f16[48,1152]{1,0:T(8,128)(2,1)S(1)} %fusion.1), channel_id=1, source_target_pairs={{0,128},{64,192},{128,0},{192,64},{1,129},{65,193},{129,1},{193,65... | collective-permute-start | bytes 331784 | tf_op jit(solution)/shard_map/ppermute | solution.py:167
  82.2 6.2 %collective-permute-done.9 = f16[48,1152]{1,0:T(8,128)(2,1)S(1)} collective-permute-done((f16[48,1152]{1,0:T(8,128)(2,1)S(1)}, f16[48,1152]{1,0:T(8,128)(2,1)S(1)}, u32[]{:S(2)}, u32[]{:S(2)}) %collective-permute-start.9) | collective-permute-done | bytes 110624 | tf_op jit(solution)/shard_map/ppermute | solution.py:167
  88.4 11.9 %collective-permute-start.10 = (f16[24,1152]{1,0:T(8,128)(2,1)S(1)}, f16[24,1152]{1,0:T(8,128)(2,1)S(1)}, u32[]{:S(2)}, u32[]{:S(2)}) collective-permute-start(f16[24,1152]{1,0:T(8,128)(2,1)S(1)} %fusion.2), channel_id=1, source_target_pairs={{0,1},{1,0},{2,3},{3,2},{4,5},{5,4},{6,7},{7,6},{8,9},{9,8},{10,11... | collective-permute-start | bytes 165896 | tf_op jit(solution)/shard_map/ppermute | solution.py:167
  100.3 6.5 %all-to-all-done.1 = bf16[16,48,1280]{2,1,0:T(8,128)(2,1)S(1)} async-done(((bf16[16,48,1280]{2,1,0:T(8,128)(2,1)}), bf16[16,48,1280]{2,1,0:T(8,128)(2,1)S(1)}, u32[]{:S(2)}, u32[]{:S(2)}) %all-to-all-start.1) | async-done | bytes 1966112 | tf_op jit(solution)/shard_map/all_to_all | solution.py:201
  106.8 0.6 fusion.4
  107.4 1.3 broadcast_in_dim.10
  108.6 13.8 %all-to-all-start.2 = ((f32[32,1,128]{2,1,0:T(1,128)}), f32[32,1,128]{2,1,0:T(1,128)S(1)}, u32[]{:S(2)}, u32[]{:S(2)}) async-start(f32[32,1,128]{2,1,0:T(1,128)} %broadcast_in_dim.10), calls=%async_computation.2 | async-start | bytes 32768 | tf_op jit(solution)/shard_map/all_to_all | solution.py:208
  122.5 0.3 convert_reduce_fusion
  122.7 7.2 %collective-permute-start.6 = (f16[24,1152]{1,0:T(8,128)(2,1)S(1)}, f16[24,1152]{1,0:T(8,128)(2,1)S(1)}, u32[]{:S(2)}, u32[]{:S(2)}) collective-permute-start(f16[24,1152]{1,0:T(8,128)(2,1)S(1)} %fusion.3), channel_id=1, source_target_pairs={{0,256},{256,0},{1,257},{257,1},{2,258},{258,2},{3,259},{259,3},{4... | collective-permute-start | bytes 165896 | tf_op jit(solution)/shard_map/ppermute | solution.py:167
  130.0 0.0 collective-permute-done.10
  130.0 0.7 slice_add_fusion.3.sum_ref
  130.6 1.9 %shard_map.70 = f32[24,1152]{1,0:T(8,128)} custom-call(f32[1]{0:T(128)S(6)} %copy.15.heat_ref, f32[1]{0:T(128)S(6)} %copy.16.offset_ref, f32[24,1152]{1,0:T(8,128)} %row_ref.2, bf16[24,1152]{1,0:T(8,128)(2,1)} %get-tuple-element.19.low_ref.partner_ref, bf16[24,1152]{1,0:T(8,128)(2,1)} %get-tuple-element.17.partner_ref.low_ref, ...), custom_call_target="tpu_custom_call" | custom-call | tf_op jit(solution)/shard_map/pallas_call | solution.py:159
  132.5 0.0 collective-permute-done.6
  132.5 1.6 %all-to-all-done.2 = f32[32,1,128]{2,1,0:T(1,128)S(1)} async-done(((f32[32,1,128]{2,1,0:T(1,128)}), f32[32,1,128]{2,1,0:T(1,128)S(1)}, u32[]{:S(2)}, u32[]{:S(2)}) %all-to-all-start.2) | async-done | bytes 16416 | tf_op jit(solution)/shard_map/all_to_all | solution.py:208
  134.1 0.7 slice_add_fusion.2.sum_ref
  134.8 0.6 slice_reduce_fusion
  135.4 1.9 %shard_map.71 = f32[24,1152]{1,0:T(8,128)} custom-call(f32[1]{0:T(128)S(6)} %copy.15.heat_ref, f32[1]{0:T(128)S(6)} %copy.16.offset_ref, f32[24,1152]{1,0:T(8,128)} %row_ref.3, bf16[24,1152]{1,0:T(8,128)(2,1)} %get-tuple-element.17.partner_ref.low_ref, bf16[24,1152]{1,0:T(8,128)(2,1)} %get-tuple-element.19.low_ref.partner_ref, ...), custom_call_target="tpu_custom_call" | custom-call | tf_op jit(solution)/shard_map/pallas_call | solution.py:159
  (10 shorter events, 0.2 us)
Async XLA Ops:
  4.4 11.4 %collective-permute-start = (bf16[24,1152]{1,0:T(8,128)(2,1)}, bf16[24,1152]{1,0:T(8,128)(2,1)S(1)}, u32[]{:S(2)}, u32[]{:S(2)}) collective-permute-start(bf16[24,1152]{1,0:T(8,128)(2,1)} %get-tuple-element.17.partner_ref.low_ref), channel_id=1, source_target_pairs={{0,256},{256,0},{1,257},{257,1},{2,258},{258,2},{3,259},{259,3},{4... | collective-permute-start | bytes 165896 | tf_op jit(solution)/shard_map/ppermute | solution.py:167
  16.8 6.9 %copy-start.1 = (bf16[24,1152]{1,0:T(8,128)(2,1)S(1)}, bf16[24,1152]{1,0:T(8,128)(2,1)}, u32[]{:S(2)}) copy-start(bf16[24,1152]{1,0:T(8,128)(2,1)} %get-tuple-element.19.low_ref.partner_ref) | copy-start | bytes 165892
  16.8 46.1 %copy-start = (f32[24,1]{1,0:T(8,128)S(1)}, f32[24,1]{1,0:T(8,128)}, u32[]{:S(2)}) copy-start(f32[24,1]{1,0:T(8,128)} %get-tuple-element.16.own_loss_ref) | copy-start | bytes 292
  16.8 46.1 %all-to-all-start = ((bf16[16,48,1152]{2,1,0:T(8,128)(2,1)}), bf16[16,48,1152]{2,1,0:T(8,128)(2,1)S(1)}, u32[]{:S(2)}, u32[]{:S(2)}) async-start(bf16[16,48,1152]{2,1,0:T(8,128)(2,1)} %broadcast_dynamic-update-slice_fusion), calls=%async_computation | async-start | bytes 3538944 | tf_op jit(solution)/shard_map/all_to_all | solution.py:191
  23.7 19.3 %collective-permute-start.1 = (bf16[24,1152]{1,0:T(8,128)(2,1)S(1)}, bf16[24,1152]{1,0:T(8,128)(2,1)S(1)}, u32[]{:S(2)}, u32[]{:S(2)}) collective-permute-start(bf16[24,1152]{1,0:T(8,128)(2,1)S(1)} %copy-done.1), channel_id=1, source_target_pairs={{0,1},{1,0},{2,3},{3,2},{4,5},{5,4},{6,7},{7,6},{8,9},{9,8},{10,11... | collective-permute-start | bytes 165896 | tf_op jit(solution)/shard_map/ppermute | solution.py:167
  43.0 8.4 %collective-permute-start.2 = (bf16[48,1152]{1,0:T(8,128)(2,1)S(1)}, bf16[48,1152]{1,0:T(8,128)(2,1)S(1)}, u32[]{:S(2)}, u32[]{:S(2)}) collective-permute-start(bf16[48,1152]{1,0:T(8,128)(2,1)S(1)} %get-tuple-element.29), channel_id=1, source_target_pairs={{0,128},{64,192},{128,0},{192,64},{1,129},{65,193},{129,1},{193,65... | collective-permute-start | bytes 331784 | tf_op jit(solution)/shard_map/ppermute | solution.py:167
  44.9 10.9 %collective-permute-start.4 = (bf16[48,1152]{1,0:T(8,128)(2,1)S(1)}, bf16[48,1152]{1,0:T(8,128)(2,1)S(1)}, u32[]{:S(2)}, u32[]{:S(2)}) collective-permute-start(bf16[48,1152]{1,0:T(8,128)(2,1)S(1)} %get-tuple-element.29), channel_id=1, source_target_pairs={{0,192},{64,128},{128,64},{192,0},{1,193},{65,129},{129,65},{193,1... | collective-permute-start | bytes 331784 | tf_op jit(solution)/shard_map/ppermute | solution.py:167
  48.5 7.3 %collective-permute-start.3 = (bf16[48,1152]{1,0:T(8,128)(2,1)S(1)}, bf16[48,1152]{1,0:T(8,128)(2,1)S(1)}, u32[]{:S(2)}, u32[]{:S(2)}) collective-permute-start(bf16[48,1152]{1,0:T(8,128)(2,1)S(1)} %get-tuple-element.29), channel_id=1, source_target_pairs={{0,64},{64,0},{128,192},{192,128},{1,65},{65,1},{129,193},{193,129... | collective-permute-start | bytes 331784 | tf_op jit(solution)/shard_map/ppermute | solution.py:167
  55.8 7.0 %collective-permute-start.5 = (bf16[192,1152]{1,0:T(8,128)(2,1)S(1)}, bf16[192,1152]{1,0:T(8,128)(2,1)S(1)}, u32[]{:S(2)}, u32[]{:S(2)}) collective-permute-start(bf16[192,1152]{1,0:T(8,128)(2,1)S(1)} %constant_dynamic-update-slice_fusion.2.near_ref), channel_id=1, source_target_pairs={{0,8},{8,0},{1,9},{9,1},{2,10},{10,2},{3,11},{11,3},{4,12},{12,4},... | collective-permute-start | bytes 1327112 | tf_op jit(solution)/shard_map/ppermute | solution.py:167
  65.1 5.2 %collective-permute-start.7 = (f32[192,1152]{1,0:T(8,128)S(1)}, f32[192,1152]{1,0:T(8,128)S(1)}, u32[]{:S(2)}, u32[]{:S(2)}) collective-permute-start(f32[192,1152]{1,0:T(8,128)S(1)} %get-tuple-element.27), channel_id=1, source_target_pairs={{0,8},{8,0},{1,9},{9,1},{2,10},{10,2},{3,11},{11,3},{4,12},{12,4},... | collective-permute-start | bytes 2654216 | tf_op jit(solution)/shard_map/ppermute | solution.py:167
  70.4 8.8 %collective-permute-start.8 = (f16[96,1152]{1,0:T(8,128)(2,1)S(1)}, f16[96,1152]{1,0:T(8,128)(2,1)S(1)}, u32[]{:S(2)}, u32[]{:S(2)}) collective-permute-start(f16[96,1152]{1,0:T(8,128)(2,1)S(1)} %fusion), channel_id=1, source_target_pairs={{0,64},{64,0},{128,192},{192,128},{1,65},{65,1},{129,193},{193,129... | collective-permute-start | bytes 663560 | tf_op jit(solution)/shard_map/ppermute | solution.py:167
  72.3 34.4 %all-to-all-start.1 = ((bf16[16,48,1280]{2,1,0:T(8,128)(2,1)}), bf16[16,48,1280]{2,1,0:T(8,128)(2,1)S(1)}, u32[]{:S(2)}, u32[]{:S(2)}) async-start(bf16[16,48,1280]{2,1,0:T(8,128)(2,1)} %bitcast.2), calls=%async_computation.1 | async-start | bytes 3932160 | tf_op jit(solution)/shard_map/all_to_all | solution.py:201
  79.3 9.1 %collective-permute-start.9 = (f16[48,1152]{1,0:T(8,128)(2,1)S(1)}, f16[48,1152]{1,0:T(8,128)(2,1)S(1)}, u32[]{:S(2)}, u32[]{:S(2)}) collective-permute-start(f16[48,1152]{1,0:T(8,128)(2,1)S(1)} %fusion.1), channel_id=1, source_target_pairs={{0,128},{64,192},{128,0},{192,64},{1,129},{65,193},{129,1},{193,65... | collective-permute-start | bytes 331784 | tf_op jit(solution)/shard_map/ppermute | solution.py:167
  88.4 41.5 %collective-permute-start.10 = (f16[24,1152]{1,0:T(8,128)(2,1)S(1)}, f16[24,1152]{1,0:T(8,128)(2,1)S(1)}, u32[]{:S(2)}, u32[]{:S(2)}) collective-permute-start(f16[24,1152]{1,0:T(8,128)(2,1)S(1)} %fusion.2), channel_id=1, source_target_pairs={{0,1},{1,0},{2,3},{3,2},{4,5},{5,4},{6,7},{7,6},{8,9},{9,8},{10,11... | collective-permute-start | bytes 165896 | tf_op jit(solution)/shard_map/ppermute | solution.py:167
  108.6 25.5 %all-to-all-start.2 = ((f32[32,1,128]{2,1,0:T(1,128)}), f32[32,1,128]{2,1,0:T(1,128)S(1)}, u32[]{:S(2)}, u32[]{:S(2)}) async-start(f32[32,1,128]{2,1,0:T(1,128)} %broadcast_in_dim.10), calls=%async_computation.2 | async-start | bytes 32768 | tf_op jit(solution)/shard_map/all_to_all | solution.py:208
  122.7 9.8 %collective-permute-start.6 = (f16[24,1152]{1,0:T(8,128)(2,1)S(1)}, f16[24,1152]{1,0:T(8,128)(2,1)S(1)}, u32[]{:S(2)}, u32[]{:S(2)}) collective-permute-start(f16[24,1152]{1,0:T(8,128)(2,1)S(1)} %fusion.3), channel_id=1, source_target_pairs={{0,256},{256,0},{1,257},{257,1},{2,258},{258,2},{3,259},{259,3},{4... | collective-permute-start | bytes 165896 | tf_op jit(solution)/shard_map/ppermute | solution.py:167

commit v14 on v12

--- a/solution.py
+++ b/solution.py
@@ -163,6 +163,23 @@
     )(heat_exponent, offset_added, vectors, lows, partners, sums)
 
 
+def loss_kernel(part_ref, loss_ref):
+    width = part_ref.shape[2] - LANES
+    terms = jnp.sum(part_ref[:, :16, width:].astype(jnp.float32), axis=0)[:8]
+    lane = lax.broadcasted_iota(jnp.int32, terms.shape, 1)
+    total = jnp.sum(jnp.where(lane < 3, terms, 0.0), axis=1, keepdims=True)
+    loss_ref[...] = jnp.broadcast_to(total[None], loss_ref.shape)
+
+
+def loss_copies(count, parts):
+    return pl.pallas_call(
+        loss_kernel,
+        in_specs=[pl.BlockSpec(memory_space=pltpu.VMEM)],
+        out_shape=jax.ShapeDtypeStruct((count, 8, LANES), jnp.float32),
+        compiler_params=pltpu.CompilerParams(vmem_limit_bytes=LIMIT),
+    )(parts)
+
+
 def swapped(value, axis, step):
     return lax.ppermute(value, axis, [(i, i ^ step) for i in range(lax.axis_size(axis))])
 
@@ -203,8 +220,7 @@
         image_sum = halved(image_sum, "zl", step)
     image_sum = halved(image_sum, "zh", 1)
 
-    plane_loss = jnp.sum(text_parts[:, 0, width : width + 3].astype(jnp.float32))
-    losses = lax.all_to_all(jnp.broadcast_to(plane_loss, (column, 1, LANES)), COLUMN, 0, 0)
+    losses = lax.all_to_all(loss_copies(column, text_parts), COLUMN, 0, 0)
     text_sum = jnp.sum(text_parts[:, :, :width].astype(jnp.float32), axis=0)
     arrived = swapped((text_sum[rows:] * HALF).astype(jnp.float16), "zm", 1)
     arrived, losses = lax.optimization_barrier((arrived, losses))

time: 132 us -> 136 us (1.030)
  waiting for transfers between devices: 27.6 us -> 33.2 us
    ppermute x10, waiting for transfers between devices: 22.4 us -> 29.2 us  [swapped(): lax.ppermute(value, axis, [(i, i ^ step) for i in range(lax.axis_size(axi...]
    all_to_all x1, waiting for transfers between devices: 1.48 us -> 0.01 us  [shards(): losses = lax.all_to_all(loss_copies(column, text_parts), COLUMN, 0, 0)]
  transfers between devices with their start and end apart: 13 -> 13, of which waited for: 7 -> 8; matrix products, arithmetic and copies ran while one was open for 3% -> 2% of each run, Pallas kernels for 4% -> 3%
where the time goes in v14:
time: 136 us; the launch traced here: 135 us
  starting transfers between devices  83.7 us (62%)
  waiting for transfers between devices  33.2 us (24%)
  Pallas kernels  10.8 us (8%)
  between operations  3.94 us (3%)
  other arithmetic  2.53 us (2%)
    ppermute x10, starting transfers between devices, swapped(): lax.ppermute(value, axis, [(i, i ^ step) for i in range(lax.axis_size(axi...  60.3 us
    ppermute x10, waiting for transfers between devices, swapped(): lax.ppermute(value, axis, [(i, i ^ step) for i in range(lax.axis_size(axi...  29.2 us
    all_to_all x1, starting transfers between devices, shards(): losses = lax.all_to_all(loss_copies(column, text_parts), COLUMN, 0, 0)  12.8 us
    all_to_all x1, starting transfers between devices, shards(): lax.all_to_all(lax.dynamic_update_slice(copies, other_low, (0, rows, 0)),...  6.89 us
    all_to_all x1, waiting for transfers between devices, shards(): lax.all_to_all(text_part.reshape(plane, 2 * rows, width + LANES), PLANE,...  4.08 us
    pallas_call x2, Pallas kernels, gradients(): pl.pallas_call(grad_kernel, in_specs=[pl.BlockSpec(memory_space=pltpu.SME...  3.75 us
    all_to_all x1, starting transfers between devices, shards(): lax.all_to_all(text_part.reshape(plane, 2 * rows, width + LANES), PLANE,...  3.73 us
  transfers between devices with their start and end apart: 13, of which 8 were waited for; matrix products, arithmetic and copies ran while one was open for 2% of the time, Pallas kernels for 3%

profile of v14, /device:TPU:1, one launch (start us, length us, event | category | flops | bytes accessed | tf_op | source)
XLA Modules:
  0.0 135.3 jit_solution(16809987669063539737)
XLA Ops:
  1.9 2.4 %shard_map.67 = (bf16[24,1152]{1,0:T(8,128)(2,1)}, bf16[24,1152]{1,0:T(8,128)(2,1)}, bf16[16,48,1152]{2,1,0:T(8,128)(2,1)}, f32[24,1]{1,0:T(8,128)}) custom-call(f32[1]{0:T(128)S(6)} %copy.11.heat_ref, f32[1]{0:T(128)S(6)} %copy.12.offset_ref, f32[24,1152]{1,0:T(8,128)} %row_ref.2, f32[24,1152]{1,0:T(8,128)} %row_ref.3), custom_call_target="tpu_custom_call" | custom-call | tf_op jit(solution)/shard_map/pallas_call | solution.py:56
  4.4 9.6 %collective-permute-start.4 = (bf16[24,1152]{1,0:T(8,128)(2,1)}, bf16[24,1152]{1,0:T(8,128)(2,1)S(1)}, u32[]{:S(2)}, u32[]{:S(2)}) collective-permute-start(bf16[24,1152]{1,0:T(8,128)(2,1)} %get-tuple-element.17.partner_ref.low_ref), channel_id=1, source_target_pairs={{0,256},{256,0},{1,257},{257,1},{2,258},{258,2},{3,259},{259,3},{4... | collective-permute-start | bytes 165896 | tf_op jit(solution)/shard_map/ppermute | solution.py:184
  14.0 10.6 %collective-permute-start = (bf16[24,1152]{1,0:T(8,128)(2,1)}, bf16[24,1152]{1,0:T(8,128)(2,1)S(1)}, u32[]{:S(2)}, u32[]{:S(2)}) collective-permute-start(bf16[24,1152]{1,0:T(8,128)(2,1)} %get-tuple-element.15.low_ref.partner_ref), channel_id=1, source_target_pairs={{0,1},{1,0},{2,3},{3,2},{4,5},{5,4},{6,7},{7,6},{8,9},{9,8},{10,11... | collective-permute-start | bytes 165896 | tf_op jit(solution)/shard_map/ppermute | solution.py:184
  24.7 0.0 collective-permute-done.4
  24.7 1.0 broadcast_dynamic-update-slice_fusion
  25.7 0.0 copy-start.2
  25.7 0.0 copy-start.1
  25.7 6.9 %all-to-all-start = ((bf16[16,48,1152]{2,1,0:T(8,128)(2,1)}), bf16[16,48,1152]{2,1,0:T(8,128)(2,1)S(1)}, u32[]{:S(2)}, u32[]{:S(2)}) async-start(bf16[16,48,1152]{2,1,0:T(8,128)(2,1)} %broadcast_dynamic-update-slice_fusion), calls=%async_computation | async-start | bytes 3538944 | tf_op jit(solution)/shard_map/all_to_all | solution.py:206
  32.6 0.0 copy-done.2
  32.6 0.0 collective-permute-done
  32.6 3.1 %collective-permute-start.1 = (bf16[48,1152]{1,0:T(8,128)(2,1)S(1)}, bf16[48,1152]{1,0:T(8,128)(2,1)S(1)}, u32[]{:S(2)}, u32[]{:S(2)}) collective-permute-start(bf16[48,1152]{1,0:T(8,128)(2,1)S(1)} %pad_maximum_fusion.1), channel_id=1, source_target_pairs={{0,128},{64,192},{128,0},{192,64},{1,129},{65,193},{129,1},{193,65... | collective-permute-start | bytes 331784 | tf_op jit(solution)/shard_map/ppermute | solution.py:184
  35.8 6.3 %collective-permute-done.1 = bf16[48,1152]{1,0:T(8,128)(2,1)S(1)} collective-permute-done((bf16[48,1152]{1,0:T(8,128)(2,1)S(1)}, bf16[48,1152]{1,0:T(8,128)(2,1)S(1)}, u32[]{:S(2)}, u32[]{:S(2)}) %collective-permute-start.1) | collective-permute-done | bytes 110624 | tf_op jit(solution)/shard_map/ppermute | solution.py:184
  42.0 1.9 %collective-permute-start.2 = (bf16[96,1152]{1,0:T(8,128)(2,1)S(1)}, bf16[96,1152]{1,0:T(8,128)(2,1)S(1)}, u32[]{:S(2)}, u32[]{:S(2)}) collective-permute-start(bf16[96,1152]{1,0:T(8,128)(2,1)S(1)} %pad_maximum_fusion), channel_id=1, source_target_pairs={{0,64},{64,0},{128,192},{192,128},{1,65},{65,1},{129,193},{193,129... | collective-permute-start | bytes 663560 | tf_op jit(solution)/shard_map/ppermute | solution.py:184
  44.0 5.6 %collective-permute-done.2 = bf16[96,1152]{1,0:T(8,128)(2,1)S(1)} collective-permute-done((bf16[96,1152]{1,0:T(8,128)(2,1)S(1)}, bf16[96,1152]{1,0:T(8,128)(2,1)S(1)}, u32[]{:S(2)}, u32[]{:S(2)}) %collective-permute-start.2) | collective-permute-done | bytes 221216 | tf_op jit(solution)/shard_map/ppermute | solution.py:184
  49.6 4.1 %collective-permute-start.3 = (bf16[192,1152]{1,0:T(8,128)(2,1)S(1)}, bf16[192,1152]{1,0:T(8,128)(2,1)S(1)}, u32[]{:S(2)}, u32[]{:S(2)}) collective-permute-start(bf16[192,1152]{1,0:T(8,128)(2,1)S(1)} %constant_dynamic-update-slice_fusion.near_ref), channel_id=1, source_target_pairs={{0,8},{8,0},{1,9},{9,1},{2,10},{10,2},{3,11},{11,3},{4,12},{12,4},... | collective-permute-start | bytes 1327112 | tf_op jit(solution)/shard_map/ppermute | solution.py:184
  53.7 1.4 %collective-permute-done.3.far_ref = bf16[192,1152]{1,0:T(8,128)(2,1)S(1)} collective-permute-done((bf16[192,1152]{1,0:T(8,128)(2,1)S(1)}, bf16[192,1152]{1,0:T(8,128)(2,1)S(1)}, u32[]{:S(2)}, u32[]{:S(2)}) %collective-permute-start.3) | collective-permute-done | bytes 442400 | tf_op jit(solution)/shard_map/ppermute | solution.py:184
  55.1 0.0 all-to-all-done
  55.1 0.0 copy-done.1
  55.1 2.2 %shard_map.68 = (bf16[2,192,768]{2,1,0:T(8,128)(2,1)S(1)}, f32[192,1152]{1,0:T(8,128)S(1)}, f32[8,128]{1,0:T(8,128)S(1)}) custom-call(s32[1]{0:T(128)} %bitcast.place_ref, f32[1]{0:T(128)S(6)} %copy.11.heat_ref, f32[1]{0:T(128)S(6)} %copy.12.offset_ref, f32[24,1]{1,0:T(8,128)S(1)} %copy-done.1, ...), custom_call_target="tpu_custom_call" | custom-call | flops 1019215872 | bytes 1769472 | tf_op jit(solution)/shard_map/pallas_call | solution.py:107
  57.3 6.3 %collective-permute-start.6 = (f32[192,1152]{1,0:T(8,128)S(1)}, f32[192,1152]{1,0:T(8,128)S(1)}, u32[]{:S(2)}, u32[]{:S(2)}) collective-permute-start(f32[192,1152]{1,0:T(8,128)S(1)} %get-tuple-element.23), channel_id=1, source_target_pairs={{0,8},{8,0},{1,9},{9,1},{2,10},{10,2},{3,11},{11,3},{4,12},{12,4},... | collective-permute-start | bytes 2654216 | tf_op jit(solution)/shard_map/ppermute | solution.py:184
  63.7 1.6 %shard_map.69 = (f32[192,1152]{1,0:T(8,128)S(1)}, bf16[768,1280]{1,0:T(8,128)(2,1)S(1)}) custom-call(bf16[2,192,768]{2,1,0:T(8,128)(2,1)S(1)} %get-tuple-element.18.weight_ref, f32[8,128]{1,0:T(8,128)S(1)} %get-tuple-element.19.loss_ref, bf16[192,1152]{1,0:T(8,128)(2,1)S(1)} %constant_dynamic-update-slice_fusion.near_ref, ...), custom_call_target="tpu_custom_call" | custom-call | flops 1019215872 | bytes 3538944 | tf_op jit(solution)/shard_map/pallas_call | solution.py:137
  65.3 0.0 copy-start
  65.3 0.4 collective-permute-done.6
  65.7 0.1 add.19
  65.9 2.6 %collective-permute-start.7 = (f16[96,1152]{1,0:T(8,128)(2,1)S(1)}, f16[96,1152]{1,0:T(8,128)(2,1)S(1)}, u32[]{:S(2)}, u32[]{:S(2)}) collective-permute-start(f16[96,1152]{1,0:T(8,128)(2,1)S(1)} %fusion), channel_id=1, source_target_pairs={{0,64},{64,0},{128,192},{192,128},{1,65},{65,1},{129,193},{193,129... | collective-permute-start | bytes 663560 | tf_op jit(solution)/shard_map/ppermute | solution.py:184
  68.5 0.0 copy-done
  68.5 3.7 %all-to-all-start.1 = ((bf16[16,48,1280]{2,1,0:T(8,128)(2,1)}), bf16[16,48,1280]{2,1,0:T(8,128)(2,1)S(1)}, u32[]{:S(2)}, u32[]{:S(2)}) async-start(bf16[16,48,1280]{2,1,0:T(8,128)(2,1)} %bitcast.4), calls=%async_computation.1 | async-start | bytes 3932160 | tf_op jit(solution)/shard_map/all_to_all | solution.py:217
  72.2 2.1 %collective-permute-done.7 = f16[96,1152]{1,0:T(8,128)(2,1)S(1)} collective-permute-done((f16[96,1152]{1,0:T(8,128)(2,1)S(1)}, f16[96,1152]{1,0:T(8,128)(2,1)S(1)}, u32[]{:S(2)}, u32[]{:S(2)}) %collective-permute-start.7) | collective-permute-done | bytes 221216 | tf_op jit(solution)/shard_map/ppermute | solution.py:184
  74.4 0.1 slice_add_fusion
  74.5 3.1 %collective-permute-start.8 = (f16[48,1152]{1,0:T(8,128)(2,1)S(1)}, f16[48,1152]{1,0:T(8,128)(2,1)S(1)}, u32[]{:S(2)}, u32[]{:S(2)}) collective-permute-start(f16[48,1152]{1,0:T(8,128)(2,1)S(1)} %fusion.1), channel_id=1, source_target_pairs={{0,128},{64,192},{128,0},{192,64},{1,129},{65,193},{129,1},{193,65... | collective-permute-start | bytes 331784 | tf_op jit(solution)/shard_map/ppermute | solution.py:184
  77.6 6.5 %collective-permute-done.8 = f16[48,1152]{1,0:T(8,128)(2,1)S(1)} collective-permute-done((f16[48,1152]{1,0:T(8,128)(2,1)S(1)}, f16[48,1152]{1,0:T(8,128)(2,1)S(1)}, u32[]{:S(2)}, u32[]{:S(2)}) %collective-permute-start.8) | collective-permute-done | bytes 110624 | tf_op jit(solution)/shard_map/ppermute | solution.py:184
  84.2 11.6 %collective-permute-start.9 = (f16[24,1152]{1,0:T(8,128)(2,1)S(1)}, f16[24,1152]{1,0:T(8,128)(2,1)S(1)}, u32[]{:S(2)}, u32[]{:S(2)}) collective-permute-start(f16[24,1152]{1,0:T(8,128)(2,1)S(1)} %fusion.2), channel_id=1, source_target_pairs={{0,1},{1,0},{2,3},{3,2},{4,5},{5,4},{6,7},{7,6},{8,9},{9,8},{10,11... | collective-permute-start | bytes 165896 | tf_op jit(solution)/shard_map/ppermute | solution.py:184
  95.8 4.1 %all-to-all-done.1.part_ref = bf16[16,48,1280]{2,1,0:T(8,128)(2,1)S(1)} async-done(((bf16[16,48,1280]{2,1,0:T(8,128)(2,1)}), bf16[16,48,1280]{2,1,0:T(8,128)(2,1)S(1)}, u32[]{:S(2)}, u32[]{:S(2)}) %all-to-all-start.1) | async-done | bytes 1966112 | tf_op jit(solution)/shard_map/all_to_all | solution.py:217
  99.9 0.8 shard_map.70
  100.6 12.8 %all-to-all-start.2 = ((f32[32,8,128]{2,1,0:T(8,128)}), f32[32,8,128]{2,1,0:T(8,128)S(1)}, u32[]{:S(2)}, u32[]{:S(2)}) async-start(f32[32,8,128]{2,1,0:T(8,128)} %shard_map.70), calls=%async_computation.2 | async-start | bytes 262144 | tf_op jit(solution)/shard_map/all_to_all | solution.py:223
  113.4 0.3 convert_reduce_fusion
  113.7 7.2 %collective-permute-start.5 = (f16[24,1152]{1,0:T(8,128)(2,1)S(1)}, f16[24,1152]{1,0:T(8,128)(2,1)S(1)}, u32[]{:S(2)}, u32[]{:S(2)}) collective-permute-start(f16[24,1152]{1,0:T(8,128)(2,1)S(1)} %fusion.3), channel_id=1, source_target_pairs={{0,256},{256,0},{1,257},{257,1},{2,258},{258,2},{3,259},{259,3},{4... | collective-permute-start | bytes 165896 | tf_op jit(solution)/shard_map/ppermute | solution.py:184
  120.9 0.0 collective-permute-done.9
  120.9 0.7 slice_add_fusion.3.sum_ref
  121.6 1.9 %shard_map.71 = f32[24,1152]{1,0:T(8,128)} custom-call(f32[1]{0:T(128)S(6)} %copy.11.heat_ref, f32[1]{0:T(128)S(6)} %copy.12.offset_ref, f32[24,1152]{1,0:T(8,128)} %row_ref.2, bf16[24,1152]{1,0:T(8,128)(2,1)} %get-tuple-element.15.low_ref.partner_ref, bf16[24,1152]{1,0:T(8,128)(2,1)} %get-tuple-element.17.partner_ref.low_ref, ...), custom_call_target="tpu_custom_call" | custom-call | tf_op jit(solution)/shard_map/pallas_call | solution.py:159
  123.5 6.8 %collective-permute-done.5 = f16[24,1152]{1,0:T(8,128)(2,1)S(1)} collective-permute-done((f16[24,1152]{1,0:T(8,128)(2,1)S(1)}, f16[24,1152]{1,0:T(8,128)(2,1)S(1)}, u32[]{:S(2)}, u32[]{:S(2)}) %collective-permute-start.5) | collective-permute-done | bytes 55328 | tf_op jit(solution)/shard_map/ppermute | solution.py:184
  130.3 0.0 all-to-all-done.2
  130.3 0.7 slice_add_fusion.2.sum_ref
  131.0 0.6 slice_reduce_fusion
  131.6 1.9 %shard_map.72 = f32[24,1152]{1,0:T(8,128)} custom-call(f32[1]{0:T(128)S(6)} %copy.11.heat_ref, f32[1]{0:T(128)S(6)} %copy.12.offset_ref, f32[24,1152]{1,0:T(8,128)} %row_ref.3, bf16[24,1152]{1,0:T(8,128)(2,1)} %get-tuple-element.17.partner_ref.low_ref, bf16[24,1152]{1,0:T(8,128)(2,1)} %get-tuple-element.15.low_ref.partner_ref, ...), custom_call_target="tpu_custom_call" | custom-call | tf_op jit(solution)/shard_map/pallas_call | solution.py:159
  (11 shorter events, 0.2 us)
Async XLA Ops:
  4.4 20.3 %collective-permute-start.4 = (bf16[24,1152]{1,0:T(8,128)(2,1)}, bf16[24,1152]{1,0:T(8,128)(2,1)S(1)}, u32[]{:S(2)}, u32[]{:S(2)}) collective-permute-start(bf16[24,1152]{1,0:T(8,128)(2,1)} %get-tuple-element.17.partner_ref.low_ref), channel_id=1, source_target_pairs={{0,256},{256,0},{1,257},{257,1},{2,258},{258,2},{3,259},{259,3},{4... | collective-permute-start | bytes 165896 | tf_op jit(solution)/shard_map/ppermute | solution.py:184
  14.0 18.6 %collective-permute-start = (bf16[24,1152]{1,0:T(8,128)(2,1)}, bf16[24,1152]{1,0:T(8,128)(2,1)S(1)}, u32[]{:S(2)}, u32[]{:S(2)}) collective-permute-start(bf16[24,1152]{1,0:T(8,128)(2,1)} %get-tuple-element.15.low_ref.partner_ref), channel_id=1, source_target_pairs={{0,1},{1,0},{2,3},{3,2},{4,5},{5,4},{6,7},{7,6},{8,9},{9,8},{10,11... | collective-permute-start | bytes 165896 | tf_op jit(solution)/shard_map/ppermute | solution.py:184
  25.7 6.9 %copy-start.2 = (bf16[24,1152]{1,0:T(8,128)(2,1)S(1)}, bf16[24,1152]{1,0:T(8,128)(2,1)}, u32[]{:S(2)}) copy-start(bf16[24,1152]{1,0:T(8,128)(2,1)} %get-tuple-element.15.low_ref.partner_ref) | copy-start | bytes 165892
  25.7 29.4 %copy-start.1 = (f32[24,1]{1,0:T(8,128)S(1)}, f32[24,1]{1,0:T(8,128)}, u32[]{:S(2)}) copy-start(f32[24,1]{1,0:T(8,128)} %get-tuple-element.14.own_loss_ref) | copy-start | bytes 292
  25.7 29.4 %all-to-all-start = ((bf16[16,48,1152]{2,1,0:T(8,128)(2,1)}), bf16[16,48,1152]{2,1,0:T(8,128)(2,1)S(1)}, u32[]{:S(2)}, u32[]{:S(2)}) async-start(bf16[16,48,1152]{2,1,0:T(8,128)(2,1)} %broadcast_dynamic-update-slice_fusion), calls=%async_computation | async-start | bytes 3538944 | tf_op jit(solution)/shard_map/all_to_all | solution.py:206
  32.6 9.4 %collective-permute-start.1 = (bf16[48,1152]{1,0:T(8,128)(2,1)S(1)}, bf16[48,1152]{1,0:T(8,128)(2,1)S(1)}, u32[]{:S(2)}, u32[]{:S(2)}) collective-permute-start(bf16[48,1152]{1,0:T(8,128)(2,1)S(1)} %pad_maximum_fusion.1), channel_id=1, source_target_pairs={{0,128},{64,192},{128,0},{192,64},{1,129},{65,193},{129,1},{193,65... | collective-permute-start | bytes 331784 | tf_op jit(solution)/shard_map/ppermute | solution.py:184
  42.0 7.6 %collective-permute-start.2 = (bf16[96,1152]{1,0:T(8,128)(2,1)S(1)}, bf16[96,1152]{1,0:T(8,128)(2,1)S(1)}, u32[]{:S(2)}, u32[]{:S(2)}) collective-permute-start(bf16[96,1152]{1,0:T(8,128)(2,1)S(1)} %pad_maximum_fusion), channel_id=1, source_target_pairs={{0,64},{64,0},{128,192},{192,128},{1,65},{65,1},{129,193},{193,129... | collective-permute-start | bytes 663560 | tf_op jit(solution)/shard_map/ppermute | solution.py:184
  49.6 5.5 %collective-permute-start.3 = (bf16[192,1152]{1,0:T(8,128)(2,1)S(1)}, bf16[192,1152]{1,0:T(8,128)(2,1)S(1)}, u32[]{:S(2)}, u32[]{:S(2)}) collective-permute-start(bf16[192,1152]{1,0:T(8,128)(2,1)S(1)} %constant_dynamic-update-slice_fusion.near_ref), channel_id=1, source_target_pairs={{0,8},{8,0},{1,9},{9,1},{2,10},{10,2},{3,11},{11,3},{4,12},{12,4},... | collective-permute-start | bytes 1327112 | tf_op jit(solution)/shard_map/ppermute | solution.py:184
  57.3 8.4 %collective-permute-start.6 = (f32[192,1152]{1,0:T(8,128)S(1)}, f32[192,1152]{1,0:T(8,128)S(1)}, u32[]{:S(2)}, u32[]{:S(2)}) collective-permute-start(f32[192,1152]{1,0:T(8,128)S(1)} %get-tuple-element.23), channel_id=1, source_target_pairs={{0,8},{8,0},{1,9},{9,1},{2,10},{10,2},{3,11},{11,3},{4,12},{12,4},... | collective-permute-start | bytes 2654216 | tf_op jit(solution)/shard_map/ppermute | solution.py:184
  65.3 3.2 %copy-start = (bf16[768,1280]{1,0:T(8,128)(2,1)}, bf16[768,1280]{1,0:T(8,128)(2,1)S(1)}, u32[]{:S(2)}) copy-start(bf16[768,1280]{1,0:T(8,128)(2,1)S(1)} %get-tuple-element.20) | copy-start | bytes 5898244
  65.9 8.5 %collective-permute-start.7 = (f16[96,1152]{1,0:T(8,128)(2,1)S(1)}, f16[96,1152]{1,0:T(8,128)(2,1)S(1)}, u32[]{:S(2)}, u32[]{:S(2)}) collective-permute-start(f16[96,1152]{1,0:T(8,128)(2,1)S(1)} %fusion), channel_id=1, source_target_pairs={{0,64},{64,0},{128,192},{192,128},{1,65},{65,1},{129,193},{193,129... | collective-permute-start | bytes 663560 | tf_op jit(solution)/shard_map/ppermute | solution.py:184
  68.5 31.4 %all-to-all-start.1 = ((bf16[16,48,1280]{2,1,0:T(8,128)(2,1)}), bf16[16,48,1280]{2,1,0:T(8,128)(2,1)S(1)}, u32[]{:S(2)}, u32[]{:S(2)}) async-start(bf16[16,48,1280]{2,1,0:T(8,128)(2,1)} %bitcast.4), calls=%async_computation.1 | async-start | bytes 3932160 | tf_op jit(solution)/shard_map/all_to_all | solution.py:217
  74.5 9.6 %collective-permute-start.8 = (f16[48,1152]{1,0:T(8,128)(2,1)S(1)}, f16[48,1152]{1,0:T(8,128)(2,1)S(1)}, u32[]{:S(2)}, u32[]{:S(2)}) collective-permute-start(f16[48,1152]{1,0:T(8,128)(2,1)S(1)} %fusion.1), channel_id=1, source_target_pairs={{0,128},{64,192},{128,0},{192,64},{1,129},{65,193},{129,1},{193,65... | collective-permute-start | bytes 331784 | tf_op jit(solution)/shard_map/ppermute | solution.py:184
  84.2 36.8 %collective-permute-start.9 = (f16[24,1152]{1,0:T(8,128)(2,1)S(1)}, f16[24,1152]{1,0:T(8,128)(2,1)S(1)}, u32[]{:S(2)}, u32[]{:S(2)}) collective-permute-start(f16[24,1152]{1,0:T(8,128)(2,1)S(1)} %fusion.2), channel_id=1, source_target_pairs={{0,1},{1,0},{2,3},{3,2},{4,5},{5,4},{6,7},{7,6},{8,9},{9,8},{10,11... | collective-permute-start | bytes 165896 | tf_op jit(solution)/shard_map/ppermute | solution.py:184
  100.6 29.7 %all-to-all-start.2 = ((f32[32,8,128]{2,1,0:T(8,128)}), f32[32,8,128]{2,1,0:T(8,128)S(1)}, u32[]{:S(2)}, u32[]{:S(2)}) async-start(f32[32,8,128]{2,1,0:T(8,128)} %shard_map.70), calls=%async_computation.2 | async-start | bytes 262144 | tf_op jit(solution)/shard_map/all_to_all | solution.py:223
  113.7 16.6 %collective-permute-start.5 = (f16[24,1152]{1,0:T(8,128)(2,1)S(1)}, f16[24,1152]{1,0:T(8,128)(2,1)S(1)}, u32[]{:S(2)}, u32[]{:S(2)}) collective-permute-start(f16[24,1152]{1,0:T(8,128)(2,1)S(1)} %fusion.3), channel_id=1, source_target_pairs={{0,256},{256,0},{1,257},{257,1},{2,258},{258,2},{3,259},{259,3},{4... | collective-permute-start | bytes 165896 | tf_op jit(solution)/shard_map/ppermute | solution.py:184
